TPU v7x, 32 devices: a whole 2x2x4 slice. The times are simulated.
32 devices in a mesh: pipe: 2 (over core), dp: 16 (over z, y, x).
Axes of the slice: x: 2, y: 2, z: 4, core: 2. Of those that a mesh axis runs over, the one named last changes fastest.
Arguments:
- images: bfloat16 [128, 16, 24, 1024], P('dp'), may hold values from -6 to 6
- cotangent: bfloat16 [128, 8, 12, 2048], P('dp'), may hold values from -6 to 6
- heights: int32 [128], P('dp'), may hold values from 4 to 8, as said below
- widths: int32 [128], P('dp'), may hold values from 6 to 12, as said below
- assign: int32 [16, 8], P('dp'), may hold values from 0 to 7, each once within a row
- w_narrow: float32 [12288, 512], P(('pipe', 'dp')), may hold values from -0.09375 to 0.09375
- w_wide: float32 [2048, 2048], P(('pipe', 'dp')), may hold values from -0.1875 to 0.1875
- bn_mid: float32 [8, 512], P(None, ('pipe', 'dp')), may hold values from -1 to 1.6, as said below
- bn_wide: float32 [6, 2048], P(None, ('pipe', 'dp')), may hold values from -1 to 1.6, as said below
- mom_narrow: float32 [12288, 512], P(('pipe', 'dp')), may hold values from -0.015625 to 0.015625
- mom_wide: float32 [2048, 2048], P(('pipe', 'dp')), may hold values from -0.03125 to 0.03125
- mom_bn_mid: float32 [8, 512], P(None, ('pipe', 'dp')), may hold values from -2 to 2
- mom_bn_wide: float32 [6, 2048], P(None, ('pipe', 'dp')), may hold values from -2 to 2
Outputs:
- block_out: bfloat16 [128, 8, 12, 2048], P('dp', None, None, 'pipe')
- grad_input: bfloat16 [128, 16, 24, 1024], P('dp', None, None, 'pipe')
- grad_narrow: float32 [12288, 512], P(('pipe', 'dp'))
- grad_wide: float32 [2048, 2048], P(('pipe', 'dp'))
- grad_bn_mid: float32 [8, 512], P(None, ('pipe', 'dp'))
- grad_bn_wide: float32 [6, 2048], P(None, ('pipe', 'dp'))
- new_mom_narrow: float32 [12288, 512], P(('pipe', 'dp'))
- new_mom_wide: float32 [2048, 2048], P(('pipe', 'dp'))
- new_mom_bn_mid: float32 [8, 512], P(None, ('pipe', 'dp'))
- new_mom_bn_wide: float32 [6, 2048], P(None, ('pipe', 'dp'))
- new_narrow: float32 [12288, 512], P(('pipe', 'dp'))
- new_wide: float32 [2048, 2048], P(('pipe', 'dp'))
- new_bn_mid: float32 [8, 512], P(None, ('pipe', 'dp'))
- new_bn_wide: float32 [6, 2048], P(None, ('pipe', 'dp'))
Inputs may be any that keep to these rules, and one draw needn't show every extreme that they name: `heights`: some image has height 8. `widths`: some image has width 12. `assign`: each row is a permutation of 0 to 7. `bn_mid`: even rows are gains, odd rows biases. `bn_wide`: even rows are gains, odd rows biases.
All inputs are finite; a program needn't handle non-finite values.
Results may differ from a plain program's by a relative error of at most 0.018.
Values may be sent and summed in bfloat16 or wider, within the bound.
No kernel may reach another device: no remote copies, remote signals or barrier semaphores. Data moves between devices by JAX's collectives and lax.ppermute only.
A program may use at most 384 MiB of HBM per device.

v0:
```python
import jax
import jax.numpy as jnp
from jax import lax
from jax.sharding import PartitionSpec as P

C_IN = 1024
C_MID = 512
C_OUT = 2048
HB = 8
WB = 12
MB = 4
IMG_MB = 2
IMG_DEV = 8


EPS = 1e-05
MOMENTUM = 0.9
DECAY = 5e-05
TRUST = 0.001
RATE = 29.0
PRECISE = lax.Precision.HIGHEST
BFLOAT = jnp.bfloat16
SINGLE = jnp.float32


def from_behind(shard, axis, by):
    size = lax.axis_size(axis)
    pairs = [(i, i + by) for i in range(size) if 0 <= i + by < size]
    return lax.ppermute(shard, axis, pairs)


def smooth_gate(values):
    return values * jax.nn.sigmoid(values)


def gate_slope(values):
    logistic = jax.nn.sigmoid(values)
    return logistic * (1.0 + values * (1.0 - logistic))


def patches(feature, stride):
    padded = jnp.pad(feature, ((0, 0), (1, 1), (1, 1), (0, 0)))
    rows_out = feature.shape[1] // stride
    cols_out = feature.shape[2] // stride
    tap_list = []
    for tap_row in range(3):
        for tap_col in range(3):
            tap_list.append(
                padded[
                    :,
                    tap_row : tap_row + stride * rows_out : stride,
                    tap_col : tap_col + stride * cols_out : stride,
                    :,
                ]
            )
    return jnp.concatenate(tap_list, axis=3)


def unpatch(columns, shape_spec, stride):
    blank_feature = jnp.zeros(shape_spec, SINGLE)
    unused_out, pullback = jax.vjp(lambda feature: patches(feature, stride), blank_feature)
    return pullback(columns)[0]


def project(feature, weight):
    return jnp.einsum("bhwc,cd->bhwd", feature, weight, preferred_element_type=SINGLE)


def project_back(gradient, weight):
    return jnp.einsum("bhwd,cd->bhwc", gradient, weight, preferred_element_type=SINGLE)


def weight_grad(feature, gradient):
    return jnp.einsum("bhwc,bhwd->cd", feature, gradient, preferred_element_type=SINGLE)


def pixel_masks(heights, widths, rows, cols):
    row_ids = jnp.arange(rows, dtype=jnp.int32)
    col_ids = jnp.arange(cols, dtype=jnp.int32)
    inside = (row_ids[:, None] < heights[..., None, None]) & (
        col_ids[None, :] < widths[..., None, None]
    )
    return inside.astype(SINGLE)[..., None]


def zeros_of(specs):
    return tuple((jnp.zeros(shape_spec, dtype_spec) for shape_spec, dtype_spec in specs))


def run_on(flag, function, operand):
    result = function(operand)
    return jax.tree.map(lambda value: jnp.where(flag, value, jnp.zeros_like(value)), result)


def norm_stats(values_list, pixel_mask):
    sum_rows = jnp.stack([jnp.sum(values * pixel_mask, axis=(0, 1, 2)) for values in values_list])
    square_rows = jnp.stack(
        [jnp.sum(values * values * pixel_mask, axis=(0, 1, 2)) for values in values_list]
    )
    pixel_total, sum_total, square_total = lax.psum(
        (jnp.sum(pixel_mask), sum_rows, square_rows), "dp"
    )
    mean_rows = sum_total / pixel_total
    scale_rows = lax.rsqrt(square_total / pixel_total - mean_rows * mean_rows + EPS)
    return (mean_rows, scale_rows, pixel_total)


def norm_back(grad_list, normed_list):
    first_rows = jnp.stack([jnp.sum(grad_z, axis=(0, 1, 2)) for grad_z in grad_list])
    second_rows = jnp.stack(
        [jnp.sum(grad_z * normed, axis=(0, 1, 2)) for grad_z, normed in zip(grad_list, normed_list)]
    )
    first_total, second_total = lax.psum((first_rows, second_rows), "dp")
    return (first_total, second_total, first_rows, second_rows)


def norm_grad(grad_z, normed, pixel_mask, scale_row, gain_row, first_row, second_row, pixel_total):
    inner_term = grad_z - first_row / pixel_total - normed * second_row / pixel_total
    return (pixel_mask * scale_row * gain_row * inner_term).astype(BFLOAT)


def group_table(start_index, rows_local, bounds):
    global_rows = start_index * rows_local + jnp.arange(rows_local, dtype=jnp.int32)
    group_ids = jnp.zeros((rows_local,), jnp.int32)
    for boundary in bounds:
        group_ids = group_ids + (global_rows >= boundary).astype(jnp.int32)
    return (group_ids[:, None] == jnp.arange(len(bounds) + 1, dtype=jnp.int32)[None, :]).astype(
        SINGLE
    )


def on_device(
    images,
    cotangent,
    heights,
    widths,
    assign,
    w_narrow,
    w_wide,
    bn_mid,
    bn_wide,
    mom_narrow,
    mom_wide,
    mom_bn_mid,
    mom_bn_wide,
):
    pipe_rank = lax.axis_index("pipe")
    is_first = pipe_rank == 0
    is_second = jnp.logical_not(is_first)
    shard_index = lax.axis_index(("pipe", "dp"))
    hot_narrow = group_table(
        shard_index, w_narrow.shape[0], (C_IN, C_IN + 9 * C_MID, C_IN + 9 * C_MID + C_OUT)
    )
    hot_wide = group_table(shard_index, w_wide.shape[0], (C_MID, C_MID + C_IN))

    def square_vector(narrow, wide, mid_rows, wide_rows):
        return jnp.concatenate(
            [
                jnp.dot(jnp.sum(narrow * narrow, axis=1), hot_narrow, precision=PRECISE),
                jnp.dot(jnp.sum(wide * wide, axis=1), hot_wide, precision=PRECISE),
                jnp.sum(mid_rows * mid_rows, axis=1),
                jnp.sum(wide_rows * wide_rows, axis=1),
            ]
        )

    full_narrow, full_wide, full_mid, full_table = (
        lax.all_gather(w_narrow.astype(BFLOAT), ("pipe", "dp"), axis=0, tiled=True),
        lax.all_gather(w_wide.astype(BFLOAT), ("pipe", "dp"), axis=0, tiled=True),
        lax.all_gather(bn_mid.astype(BFLOAT), ("pipe", "dp"), axis=1, tiled=True),
        lax.all_gather(bn_wide.astype(BFLOAT), ("pipe", "dp"), axis=1, tiled=True),
    )
    second_edge = C_IN + 9 * C_MID
    third_edge = second_edge + C_OUT
    weight_one = full_narrow[:C_IN]
    weight_two = full_narrow[C_IN:second_edge]
    weight_four = full_narrow[second_edge:third_edge]
    weight_five = full_narrow[third_edge:]
    weight_three = full_wide[:C_MID]
    weight_short = full_wide[C_MID : C_MID + C_IN]
    weight_six = full_wide[C_MID + C_IN :]
    table_mid = full_mid.astype(SINGLE)
    table_wide = full_table.astype(SINGLE)
    row_mid = (1, C_MID)
    row_wide = (1, C_OUT)
    pair_wide = (2, C_OUT)
    front_row_specs = [
        (row_mid, SINGLE),
        (row_mid, SINGLE),
        (row_mid, SINGLE),
        (row_mid, SINGLE),
        (pair_wide, SINGLE),
        (pair_wide, SINGLE),
    ]
    back_row_specs = [
        (row_mid, SINGLE),
        (row_mid, SINGLE),
        (row_mid, SINGLE),
        (row_mid, SINGLE),
        (row_wide, SINGLE),
        (row_wide, SINGLE),
    ]
    front_weight_specs = [
        ((C_IN, C_MID), SINGLE),
        ((9 * C_MID, C_MID), SINGLE),
        ((C_MID, C_OUT), SINGLE),
        ((C_IN, C_OUT), SINGLE),
    ]
    back_weight_specs = [
        ((C_OUT, C_MID), SINGLE),
        ((9 * C_MID, C_MID), SINGLE),
        ((C_MID, C_OUT), SINGLE),
    ]

    def front_forward(operand):
        image_block, mask_in, mask_out = operand
        masked = image_block * mask_in.astype(BFLOAT)
        conv_one = project(masked, weight_one)
        mean_one, scale_one, count_in = norm_stats([conv_one], mask_in)
        act_one = (
            smooth_gate((conv_one - mean_one[0]) * scale_one[0] * table_mid[0] + table_mid[1])
            * mask_in
        ).astype(BFLOAT)
        conv_two = project(patches(act_one, 2), weight_two)
        mean_two, scale_two, count_out = norm_stats([conv_two], mask_out)
        act_two = (
            smooth_gate((conv_two - mean_two[0]) * scale_two[0] * table_mid[2] + table_mid[3])
            * mask_out
        ).astype(BFLOAT)
        conv_three = project(act_two, weight_three)
        conv_short = project(masked[:, ::2, ::2], weight_short)
        mean_pair, scale_pair, unused_total = norm_stats([conv_three, conv_short], mask_out)
        joined = (
            (conv_three - mean_pair[0]) * scale_pair[0] * table_wide[0]
            + table_wide[1]
            + (conv_short - mean_pair[1]) * scale_pair[1] * table_wide[2]
            + table_wide[3]
        )
        middle = (smooth_gate(joined) * mask_out).astype(BFLOAT)
        return (
            middle,
            conv_one,
            conv_two,
            conv_three,
            conv_short,
            mean_one,
            scale_one,
            mean_two,
            scale_two,
            mean_pair,
            scale_pair,
            count_in,
            count_out,
        )

    def back_forward(operand):
        middle_in, mask_out = operand
        conv_four = project(middle_in, weight_four)
        mean_four, scale_four, count_out = norm_stats([conv_four], mask_out)
        act_four = (
            smooth_gate((conv_four - mean_four[0]) * scale_four[0] * table_mid[4] + table_mid[5])
            * mask_out
        ).astype(BFLOAT)
        conv_five = project(patches(act_four, 1), weight_five)
        mean_five, scale_five, unused_five = norm_stats([conv_five], mask_out)
        act_five = (
            smooth_gate((conv_five - mean_five[0]) * scale_five[0] * table_mid[6] + table_mid[7])
            * mask_out
        ).astype(BFLOAT)
        conv_six = project(act_five, weight_six)
        mean_six, scale_six, unused_six = norm_stats([conv_six], mask_out)
        joined_six = (
            (conv_six - mean_six[0]) * scale_six[0] * table_wide[4]
            + table_wide[5]
            + middle_in.astype(SINGLE)
        )
        block_part = (smooth_gate(joined_six) * mask_out).astype(BFLOAT)
        return (
            middle_in,
            conv_four,
            conv_five,
            conv_six,
            mean_four,
            scale_four,
            mean_five,
            scale_five,
            mean_six,
            scale_six,
            count_out,
            block_part,
        )

    def back_grad(operand):
        kept_state, mask_out, cot_block = operand
        (
            middle_in,
            conv_four,
            conv_five,
            conv_six,
            mean_four,
            scale_four,
            mean_five,
            scale_five,
            mean_six,
            scale_six,
            count_out,
            block_part,
        ) = kept_state
        normed_six = (conv_six - mean_six[0]) * scale_six[0]
        joined_six = normed_six * table_wide[4] + table_wide[5] + middle_in.astype(SINGLE)
        grad_six = cot_block.astype(SINGLE) * mask_out * gate_slope(joined_six)
        first_total, second_total, first_six, second_six = norm_back([grad_six], [normed_six])
        grad_conv_six = norm_grad(
            grad_six,
            normed_six,
            mask_out,
            scale_six[0],
            table_wide[4],
            first_total[0],
            second_total[0],
            count_out,
        )
        normed_five = (conv_five - mean_five[0]) * scale_five[0]
        joined_five = normed_five * table_mid[6] + table_mid[7]
        act_five = (smooth_gate(joined_five) * mask_out).astype(BFLOAT)
        grad_five = project_back(grad_conv_six, weight_six) * mask_out * gate_slope(joined_five)
        first_total, second_total, first_five, second_five = norm_back([grad_five], [normed_five])
        grad_conv_five = norm_grad(
            grad_five,
            normed_five,
            mask_out,
            scale_five[0],
            table_mid[6],
            first_total[0],
            second_total[0],
            count_out,
        )
        normed_four = (conv_four - mean_four[0]) * scale_four[0]
        joined_four = normed_four * table_mid[4] + table_mid[5]
        act_four = (smooth_gate(joined_four) * mask_out).astype(BFLOAT)
        grad_act_four = unpatch(project_back(grad_conv_five, weight_five), act_four.shape, 1)
        grad_four = grad_act_four * mask_out * gate_slope(joined_four)
        first_total, second_total, first_four, second_four = norm_back([grad_four], [normed_four])
        grad_conv_four = norm_grad(
            grad_four,
            normed_four,
            mask_out,
            scale_four[0],
            table_mid[4],
            first_total[0],
            second_total[0],
            count_out,
        )
        grad_middle = (project_back(grad_conv_four, weight_four) + grad_six).astype(BFLOAT)
        return (
            grad_middle,
            block_part[..., : C_OUT // 2],
            grad_conv_four,
            grad_conv_five,
            grad_conv_six,
            act_four,
            act_five,
            middle_in,
            first_four,
            second_four,
            first_five,
            second_five,
            first_six,
            second_six,
        )

    def front_grad(operand):
        grad_middle, kept_state, image_block, mask_in, mask_out = operand
        (
            conv_one,
            conv_two,
            conv_three,
            conv_short,
            mean_one,
            scale_one,
            mean_two,
            scale_two,
            mean_pair,
            scale_pair,
            count_in,
            count_out,
        ) = kept_state
        normed_three = (conv_three - mean_pair[0]) * scale_pair[0]
        normed_short = (conv_short - mean_pair[1]) * scale_pair[1]
        joined = (
            normed_three * table_wide[0]
            + table_wide[1]
            + normed_short * table_wide[2]
            + table_wide[3]
        )
        grad_joined = grad_middle.astype(SINGLE) * mask_out * gate_slope(joined)
        first_total, second_total, first_pair, second_pair = norm_back(
            [grad_joined, grad_joined], [normed_three, normed_short]
        )
        grad_conv_three = norm_grad(
            grad_joined,
            normed_three,
            mask_out,
            scale_pair[0],
            table_wide[0],
            first_total[0],
            second_total[0],
            count_out,
        )
        grad_conv_short = norm_grad(
            grad_joined,
            normed_short,
            mask_out,
            scale_pair[1],
            table_wide[2],
            first_total[1],
            second_total[1],
            count_out,
        )
        normed_two = (conv_two - mean_two[0]) * scale_two[0]
        joined_two = normed_two * table_mid[2] + table_mid[3]
        act_two = (smooth_gate(joined_two) * mask_out).astype(BFLOAT)
        grad_two = project_back(grad_conv_three, weight_three) * mask_out * gate_slope(joined_two)
        first_total, second_total, first_two, second_two = norm_back([grad_two], [normed_two])
        grad_conv_two = norm_grad(
            grad_two,
            normed_two,
            mask_out,
            scale_two[0],
            table_mid[2],
            first_total[0],
            second_total[0],
            count_out,
        )
        normed_one = (conv_one - mean_one[0]) * scale_one[0]
        joined_one = normed_one * table_mid[0] + table_mid[1]
        act_one = (smooth_gate(joined_one) * mask_in).astype(BFLOAT)
        grad_act_one = unpatch(project_back(grad_conv_two, weight_two), act_one.shape, 2)
        grad_one = grad_act_one * mask_in * gate_slope(joined_one)
        first_total, second_total, first_one, second_one = norm_back([grad_one], [normed_one])
        grad_conv_one = norm_grad(
            grad_one,
            normed_one,
            mask_in,
            scale_one[0],
            table_mid[0],
            first_total[0],
            second_total[0],
            count_in,
        )
        grad_image = project_back(grad_conv_one, weight_one)
        grad_image = grad_image.at[:, ::2, ::2, :].add(project_back(grad_conv_short, weight_short))
        grad_image = (grad_image * mask_in).astype(BFLOAT)
        return (
            grad_image,
            grad_conv_one,
            grad_conv_two,
            grad_conv_three,
            grad_conv_short,
            act_one,
            act_two,
            first_one,
            second_one,
            first_two,
            second_two,
            first_pair,
            second_pair,
        )

    def front_weights(operand):
        (
            image_block,
            mask_in,
            grad_conv_one,
            grad_conv_two,
            grad_conv_three,
            grad_conv_short,
            act_one,
            act_two,
        ) = operand
        masked = image_block * mask_in.astype(BFLOAT)
        return (
            weight_grad(masked, grad_conv_one),
            weight_grad(patches(act_one, 2), grad_conv_two),
            weight_grad(act_two, grad_conv_three),
            weight_grad(masked[:, ::2, ::2], grad_conv_short),
        )

    def back_weights(operand):
        middle_in, act_four, act_five, grad_conv_four, grad_conv_five, grad_conv_six = operand
        return (
            weight_grad(middle_in, grad_conv_four),
            weight_grad(patches(act_four, 1), grad_conv_five),
            weight_grad(act_five, grad_conv_six),
        )

    image_order = assign[0]
    masks_in_all = pixel_masks(2 * heights, 2 * widths, 2 * HB, 2 * WB)
    masks_out_all = pixel_masks(heights, widths, HB, WB)
    chosen_rows = []
    for batch_index in range(MB):
        chosen_rows.append(image_order[batch_index * IMG_MB : (batch_index + 1) * IMG_MB])
    image_blocks = [images[chosen] for chosen in chosen_rows]
    inner_blocks = [masks_in_all[chosen] for chosen in chosen_rows]
    outer_blocks = [masks_out_all[chosen] for chosen in chosen_rows]
    cot_blocks = [cotangent[chosen] for chosen in chosen_rows]
    kept_front = [None] * MB
    kept_back = [None] * MB
    received = None
    for tick_now in range(MB + 1):
        if tick_now < MB:
            front_result = run_on(
                is_first,
                front_forward,
                (image_blocks[tick_now], inner_blocks[tick_now], outer_blocks[tick_now]),
            )
            kept_front[tick_now] = front_result[1:]
            outgoing = front_result[0]
        if tick_now >= 1:
            kept_back[tick_now - 1] = run_on(
                is_second, back_forward, (received, outer_blocks[tick_now - 1])
            )
        if tick_now < MB:
            received = from_behind(outgoing, "pipe", 1)
    lower_parts = [None] * MB
    image_grad_parts = [None] * MB
    grad_shards = None
    front_acc = zeros_of(front_weight_specs)
    back_acc = zeros_of(back_weight_specs)
    front_rows_acc = zeros_of(front_row_specs)
    back_rows_acc = zeros_of(back_row_specs)
    grad_received = None
    for tick_now in range(MB + 1):
        tick_front = zeros_of(front_weight_specs)
        tick_back = zeros_of(back_weight_specs)
        tick_front_rows = zeros_of(front_row_specs)
        tick_back_rows = zeros_of(back_row_specs)
        if tick_now < MB:
            back_result = run_on(
                is_second,
                back_grad,
                (kept_back[tick_now], outer_blocks[tick_now], cot_blocks[tick_now]),
            )
        if tick_now >= 1:
            earlier = tick_now - 1
            front_result = run_on(
                is_first,
                front_grad,
                (
                    grad_received,
                    kept_front[earlier],
                    image_blocks[earlier],
                    inner_blocks[earlier],
                    outer_blocks[earlier],
                ),
            )
            image_grad_parts[earlier] = front_result[0]
            tick_front_rows = front_result[7:]
        if tick_now < MB:
            grad_received, lower_parts[tick_now] = from_behind(
                (back_result[0], back_result[1]), "pipe", -1
            )
            tick_back_rows = back_result[8:]
            tick_back = run_on(
                is_second,
                back_weights,
                (
                    back_result[7],
                    back_result[5],
                    back_result[6],
                    back_result[2],
                    back_result[3],
                    back_result[4],
                ),
            )
        if tick_now >= 1:
            earlier = tick_now - 1
            tick_front = run_on(
                is_first,
                front_weights,
                (
                    image_blocks[earlier],
                    inner_blocks[earlier],
                    front_result[1],
                    front_result[2],
                    front_result[3],
                    front_result[4],
                    front_result[5],
                    front_result[6],
                ),
            )
        front_acc = jax.tree.map(lambda total, extra: total + extra, front_acc, tick_front)
        back_acc = jax.tree.map(lambda total, extra: total + extra, back_acc, tick_back)
        front_rows_acc = jax.tree.map(
            lambda total, extra: total + extra, front_rows_acc, tick_front_rows
        )
        back_rows_acc = jax.tree.map(
            lambda total, extra: total + extra, back_rows_acc, tick_back_rows
        )
    narrow_term = jnp.concatenate([front_acc[0], front_acc[1], back_acc[0], back_acc[1]], axis=0)
    wide_term = jnp.concatenate([front_acc[2], front_acc[3], back_acc[2]], axis=0)
    mid_term = jnp.stack(
        [
            front_rows_acc[1][0],
            front_rows_acc[0][0],
            front_rows_acc[3][0],
            front_rows_acc[2][0],
            back_rows_acc[1][0],
            back_rows_acc[0][0],
            back_rows_acc[3][0],
            back_rows_acc[2][0],
        ]
    )
    table_term = jnp.stack(
        [
            front_rows_acc[5][0],
            front_rows_acc[4][0],
            front_rows_acc[5][1],
            front_rows_acc[4][1],
            back_rows_acc[5][0],
            back_rows_acc[4][0],
        ]
    )
    narrow_term, wide_term, mid_term, table_term = (narrow_term, wide_term, mid_term, table_term)
    grad_shards = (
        lax.psum_scatter(narrow_term, ("pipe", "dp"), scatter_dimension=0, tiled=True),
        lax.psum_scatter(wide_term, ("pipe", "dp"), scatter_dimension=0, tiled=True),
        lax.psum_scatter(mid_term, ("pipe", "dp"), scatter_dimension=1, tiled=True),
        lax.psum_scatter(table_term, ("pipe", "dp"), scatter_dimension=1, tiled=True),
    )
    grad_narrow, grad_wide, grad_mid, grad_table = grad_shards
    block_lower = jnp.zeros((IMG_DEV, HB, WB, C_OUT // 2), BFLOAT)
    block_own = jnp.zeros((IMG_DEV, HB, WB, C_OUT), BFLOAT)
    image_grads = jnp.zeros((IMG_DEV, 2 * HB, 2 * WB, C_IN), BFLOAT)
    for batch_index in range(MB):
        chosen = chosen_rows[batch_index]
        block_lower = block_lower.at[chosen].set(lower_parts[batch_index])
        block_own = block_own.at[chosen].set(kept_back[batch_index][11])
        image_grads = image_grads.at[chosen].set(image_grad_parts[batch_index])
    block_local = jnp.where(is_first, block_lower, block_own[..., C_OUT // 2 :])
    upper_grads = from_behind(image_grads[..., C_IN // 2 :], "pipe", 1)
    grad_local = jnp.where(is_first, image_grads[..., : C_IN // 2], upper_grads)
    weight_squares, grad_squares = lax.psum(
        (
            square_vector(w_narrow, w_wide, bn_mid, bn_wide),
            square_vector(grad_narrow, grad_wide, grad_mid, grad_table),
        ),
        ("pipe", "dp"),
    )
    weight_norms = jnp.sqrt(weight_squares)
    grad_norms = jnp.sqrt(grad_squares)
    ratios = TRUST * weight_norms / (grad_norms + DECAY * weight_norms)
    ratio_narrow = jnp.dot(hot_narrow, ratios[:4], precision=PRECISE)
    ratio_wide = jnp.dot(hot_wide, ratios[4:7], precision=PRECISE)

    def lars_step(weight, gradient, moment, ratio_rows):
        new_moment = MOMENTUM * moment + RATE * ratio_rows[:, None] * (gradient + DECAY * weight)
        return (weight - new_moment, new_moment)

    new_narrow, new_mom_narrow = lars_step(w_narrow, grad_narrow, mom_narrow, ratio_narrow)
    new_wide, new_mom_wide = lars_step(w_wide, grad_wide, mom_wide, ratio_wide)
    new_mid, new_mom_mid = lars_step(bn_mid, grad_mid, mom_bn_mid, ratios[7:15])
    new_table, new_mom_table = lars_step(bn_wide, grad_table, mom_bn_wide, ratios[15:21])
    return (
        block_local,
        grad_local,
        grad_narrow,
        grad_wide,
        grad_mid,
        grad_table,
        new_mom_narrow,
        new_mom_wide,
        new_mom_mid,
        new_mom_table,
        new_narrow,
        new_wide,
        new_mid,
        new_table,
    )


def solution(mesh):
    placed = (
        P("dp", None, None, None),
        P("dp", None, None, None),
        P("dp"),
        P("dp"),
        P("dp", None),
        P(("pipe", "dp"), None),
        P(("pipe", "dp"), None),
        P(None, ("pipe", "dp")),
        P(None, ("pipe", "dp")),
        P(("pipe", "dp"), None),
        P(("pipe", "dp"), None),
        P(None, ("pipe", "dp")),
        P(None, ("pipe", "dp")),
    )
    return jax.shard_map(
        on_device,
        mesh=mesh,
        in_specs=placed,
        out_specs=(
            P("dp", None, None, "pipe"),
            P("dp", None, None, "pipe"),
            P(("pipe", "dp"), None),
            P(("pipe", "dp"), None),
            P(None, ("pipe", "dp")),
            P(None, ("pipe", "dp")),
            P(("pipe", "dp"), None),
            P(("pipe", "dp"), None),
            P(None, ("pipe", "dp")),
            P(None, ("pipe", "dp")),
            P(("pipe", "dp"), None),
            P(("pipe", "dp"), None),
            P(None, ("pipe", "dp")),
            P(None, ("pipe", "dp")),
        ),
        check_vma=False,
    )
```

profile of v0, /device:TPU:0, one launch (start us, length us, event | category | flops | bytes accessed | tf_op | source)
XLA Modules:
  0.0 3282.3 jit_solution(3266336633815868768)
XLA Ops:
  43.8 71.4 %all-gather.1 = bf16[32,64,6]{1,2,0:T(8,128)(2,1)S(1)} all-gather(bf16[1,64,6]{1,2,0:T(8,128)(2,1)S(1)} %get-tuple-element.540), channel_id=1, replica_groups=mesh['pipe'=2,'dp'=16] {'pipe','dp'}, dimensions={0}, use_global_device_ids=true | all-gather | bytes 25344 | tf_op jit(solution)/shard_map/all_gather | solution.py:170
  123.7 65.0 %all-gather = bf16[32,16,8]{1,2,0:T(8,128)(2,1)S(1)} all-gather(bf16[1,16,8]{1,2,0:T(8,128)(2,1)S(1)} %get-tuple-element.538), channel_id=1, replica_groups=mesh['pipe'=2,'dp'=16] {'pipe','dp'}, dimensions={0}, use_global_device_ids=true | all-gather | bytes 8448 | tf_op jit(solution)/shard_map/all_gather | solution.py:169
  242.3 74.8 %all-reduce.100 = (f32[1,512]{1,0:T(1,128)S(1)}, f32[]{:T(128)}, f32[1,512]{1,0:T(1,128)S(1)}, f32[1,512]{1,0:T(1,128)S(1)}, f32[]{:T(128)}, /*index=5*/f32[1,51...) all-reduce(f32[1,512]{1,0:T(1,128)S(1)} %bitcast.1177, ...), channel_id=1, replica_groups=mesh['pipe'=2,'dp'=16] {'dp'}, use_global_device_ids=true, to_apply=%region_1.0 | all-reduce | flops 4100 | bytes 32800 | tf_op jit(solution)/shard_map/psum | solution.py:100
  831.9 72.0 %all-reduce.99 = (f32[1,512]{1,0:T(1,128)S(1)}, f32[]{:T(128)}, f32[1,512]{1,0:T(1,128)}, f32[1,512]{1,0:T(1,128)S(1)}, f32[]{:T(128)}, /*index=5*/f32[1,512]{1,...) all-reduce(f32[1,512]{1,0:T(1,128)S(1)} %bitcast.1175, ...), channel_id=1, replica_groups=mesh['pipe'=2,'dp'=16] {'dp'}, use_global_device_ids=true, to_apply=%region_7.8 | all-reduce | flops 4100 | bytes 32800 | tf_op jit(solution)/shard_map/psum | solution.py:100
  968.4 86.5 %all-reduce.112.cloned.1.call-done = (f32[2,2048]{1,0:T(2,128)}, f32[2,2048]{1,0:T(2,128)}, f32[2,2048]{1,0:T(2,128)}, f32[2,2048]{1,0:T(2,128)}, f32[2,2048]{1,...) async-done(((f32[2,2048]{1,0:T(2,128)}, f32[2,2048]{1,0:T(2,128)}, f32[2,2048]{1,0:T(2,128)}, f32[2,2048]{1,0:T(2,128)}, f32[2,2048]{1,0:T(2,128)}, ...) | async-done | bytes 131088 | tf_op jit(solution)/shard_map/psum | solution.py:100
  1088.4 75.0 %all-reduce.97 = (f32[1,512]{1,0:T(1,128)S(1)}, f32[1,512]{1,0:T(1,128)S(1)}, f32[1,512]{1,0:T(1,128)S(1)}, f32[1,512]{1,0:T(1,128)S(1)}, f32[1,512]{1,0:T(1,128...) all-reduce(f32[1,512]{1,0:T(1,128)S(1)} %bitcast.1199, ...), channel_id=1, replica_groups=mesh['pipe'=2,'dp'=16] {'dp'}, use_global_device_ids=true, to_apply=%region_19.20 | all-reduce | flops 4096 | bytes 32768 | tf_op jit(solution)/shard_map/psum | solution.py:100
  1184.1 72.2 %all-reduce.96 = (f32[1,512]{1,0:T(1,128)S(1)}, f32[1,512]{1,0:T(1,128)S(1)}, f32[1,512]{1,0:T(1,128)S(1)}, f32[1,512]{1,0:T(1,128)S(1)}, f32[1,512]{1,0:T(1,128...) all-reduce(f32[1,512]{1,0:T(1,128)S(1)} %bitcast.1201, ...), channel_id=1, replica_groups=mesh['pipe'=2,'dp'=16] {'dp'}, use_global_device_ids=true, to_apply=%region_23.24 | all-reduce | flops 4096 | bytes 32768 | tf_op jit(solution)/shard_map/psum | solution.py:100
  1282.8 99.8 %all-reduce.110.cloned.1.call-done = (f32[1,2048]{1,0:T(1,128)}, f32[1,2048]{1,0:T(1,128)}, f32[1,2048]{1,0:T(1,128)}, f32[1,2048]{1,0:T(1,128)}, f32[1,2048]{1,...) async-done(((f32[1,2048]{1,0:T(1,128)}, f32[1,2048]{1,0:T(1,128)}, f32[1,2048]{1,0:T(1,128)}, f32[1,2048]{1,0:T(1,128)}, f32[1,2048]{1,0:T(1,128)}, ...) | async-done | bytes 65552 | tf_op jit(solution)/shard_map/psum | solution.py:100
  1407.3 110.3 %all-reduce.108.cloned.1.call-done = (f32[2048]{0:T(1024)}, f32[1,2048]{1,0:T(1,128)}, f32[2048]{0:T(1024)}, f32[1,2048]{1,0:T(1,128)}, f32[2048]{0:T(1024)}, /*...) async-done(((f32[2048]{0:T(1024)}, f32[1,2048]{1,0:T(1,128)}, f32[2048]{0:T(1024)}, f32[1,2048]{1,0:T(1,128)}, f32[2048]{0:T(1024)}, ...) | async-done | bytes 65552 | tf_op jit(solution)/shard_map/psum | solution.py:113
  1539.4 75.3 %all-reduce.93 = (f32[512]{0:T(512)S(1)}, f32[1,512]{1,0:T(1,128)S(1)}, f32[512]{0:T(512)S(1)}, f32[1,512]{1,0:T(1,128)S(1)}, f32[512]{0:T(512)S(1)}, /*index=5*...) all-reduce(f32[512]{0:T(512)S(1)} %get-tuple-element.121, ...), channel_id=1, replica_groups=mesh['pipe'=2,'dp'=16] {'dp'}, use_global_device_ids=true, to_apply=%region_135.136 | all-reduce | flops 4096 | bytes 32768 | tf_op jit(solution)/shard_map/psum | solution.py:113
  1638.8 72.3 %all-reduce.92 = (f32[512]{0:T(512)S(1)}, f32[1,512]{1,0:T(1,128)S(1)}, f32[512]{0:T(512)S(1)}, f32[1,512]{1,0:T(1,128)S(1)}, f32[512]{0:T(512)S(1)}, /*index=5*...) all-reduce(f32[512]{0:T(512)S(1)} %get-tuple-element.119, ...), channel_id=1, replica_groups=mesh['pipe'=2,'dp'=16] {'dp'}, use_global_device_ids=true, to_apply=%region_139.140 | all-reduce | flops 4096 | bytes 32768 | tf_op jit(solution)/shard_map/psum | solution.py:113
  1745.9 15.2 fusion
  1788.2 102.0 %all-reduce.106.cloned.1.call-done = (f32[2,2048]{1,0:T(2,128)}, f32[2,2048]{1,0:T(2,128)}, f32[2,2048]{1,0:T(2,128)}, f32[2,2048]{1,0:T(2,128)}, f32[2,2048]{1,...) async-done(((f32[2,2048]{1,0:T(2,128)}, f32[2,2048]{1,0:T(2,128)}, f32[2,2048]{1,0:T(2,128)}, f32[2,2048]{1,0:T(2,128)}, f32[2,2048]{1,0:T(2,128)}, ...) | async-done | bytes 131088 | tf_op jit(solution)/shard_map/psum | solution.py:113
  1918.6 75.5 %all-reduce.90 = (f32[512]{0:T(512)S(1)}, f32[1,512]{1,0:T(1,128)S(1)}, f32[512]{0:T(512)S(1)}, f32[1,512]{1,0:T(1,128)S(1)}, f32[512]{0:T(512)S(1)}, /*index=5*...) all-reduce(f32[512]{0:T(512)S(1)} %get-tuple-element.117, ...), channel_id=1, replica_groups=mesh['pipe'=2,'dp'=16] {'dp'}, use_global_device_ids=true, to_apply=%region_148.149 | all-reduce | flops 4096 | bytes 32768 | tf_op jit(solution)/shard_map/psum | solution.py:113
  2019.6 9.8 pad.378
  2029.4 9.9 pad.379
  2118.5 9.8 pad.319
  2153.6 9.8 pad.946
  2200.5 9.8 pad.338
  2299.0 9.8 pad.359
  2308.8 9.8 pad.957
  2334.3 9.9 pad.954
  2377.4 72.0 %all-reduce.89 = (f32[512]{0:T(512)}, f32[1,512]{1,0:T(1,128)}, f32[512]{0:T(512)}, f32[1,512]{1,0:T(1,128)}, f32[512]{0:T(512)}, /*index=5*/f32[1,512]{1,0:T(1,128)}, f32[512]{0:T(512)}, f32[1,512]{1,0:T(1,128)}) all-reduce(f32[512]{0:T(512)S(1)} %get-tuple-element.73, ...), channel_id=1, replica_groups=mesh['pipe'=2,'dp'=16] {'dp'}, use_global_device_ids=true, to_apply=%region_152.153 | all-reduce | flops 4096 | bytes 32768 | tf_op jit(solution)/shard_map/psum | solution.py:113
  2478.8 11.6 fusion.3
  2494.2 21.6 pad_maximum_fusion
  2578.9 14.0 scatter_fusion.8
  2608.2 13.8 scatter_fusion.10
  2638.7 14.1 scatter_fusion.12
  2669.9 13.8 scatter_fusion.14
  2767.4 93.5 %reduce-scatter.9.cloned.1.call-done = f32[384,512]{1,0:T(8,128)} async-done(((f32[12288,512]{1,0:T(8,128)}), f32[384,512]{1,0:T(8,128)}) %reduce-scatter.9.cloned.1.call-update) | async-done | bytes 786448 | tf_op jit(solution)/shard_map/reduce_scatter | solution.py:625
  2862.2 358.5 %reduce-scatter.11.cloned.1.call-done = f32[64,2048]{1,0:T(8,128)} async-done(((f32[2048,2048]{1,0:T(8,128)}), f32[64,2048]{1,0:T(8,128)}) %reduce-scatter.11.cloned.1.call-update) | async-done | bytes 524304 | tf_op jit(solution)/shard_map/reduce_scatter | solution.py:626
  3226.4 42.5 %all-reduce.88 = (f32[21]{0:T(128)S(1)}, f32[21]{0:T(128)S(1)}) all-reduce(f32[21]{0:T(128)S(1)} %pad_maximum_fusion.19, f32[21]{0:T(128)S(1)} %copy-done.490), channel_id=1, replica_groups=mesh['pipe'=2,'dp'=16] {'pipe','dp'}, use_global_device_ids=true, to_apply=%region_249.250 | all-reduce | flops 42 | bytes 336 | tf_op jit(solution)/shard_map/psum | solution.py:642
  (1740 shorter events, 1452.0 us)
Async XLA Ops:
  7.2 208.8 %all-gather.7.cloned.1.call-start = ((), (), s32[]{:S(2)}) async-start(), calls=%async_computation.5 | async-start | bytes 8650752 | tf_op jit(solution)/shard_map/all_gather | solution.py:168
  10.1 219.3 %all-gather.5.cloned.1.call-start = ((), (), s32[]{:S(2)}) async-start(), calls=%async_computation.4 | async-start | bytes 12976128 | tf_op jit(solution)/shard_map/all_gather | solution.py:167
  12.9 1042.0 %all-reduce.112.cloned.1.call-start = ((), (), s32[]{:S(2)}) async-start(), calls=%async_computation.13 | async-start | bytes 262144 | tf_op jit(solution)/shard_map/psum | solution.py:100
  30.3 1963.9 %copy-start.146 = (f32[2,8,12]{2,1,0:T(8,128)}, f32[2,8,12]{2,1,0:T(8,128)S(1)}, u32[]{:S(2)}) copy-start(f32[2,8,12]{2,1,0:T(8,128)S(1)} %gather_fusion.2) | copy-start | bytes 2308
  30.8 2132.6 %copy-start.148 = (f32[2,8,12]{2,1,0:T(8,128)}, f32[2,8,12]{2,1,0:T(8,128)S(1)}, u32[]{:S(2)}) copy-start(f32[2,8,12]{2,1,0:T(8,128)S(1)} %gather_fusion.8) | copy-start | bytes 2308
  36.6 2126.9 %copy-start.151 = (f32[2,8,12]{2,1,0:T(8,128)}, f32[2,8,12]{2,1,0:T(8,128)S(1)}, u32[]{:S(2)}) copy-start(f32[2,8,12]{2,1,0:T(8,128)S(1)} %gather_fusion.5) | copy-start | bytes 2308
  37.1 1957.0 %copy-start.154 = (f32[2,8,12]{2,1,0:T(8,128)}, f32[2,8,12]{2,1,0:T(8,128)S(1)}, u32[]{:S(2)}) copy-start(f32[2,8,12]{2,1,0:T(8,128)S(1)} %gather_fusion.11) | copy-start | bytes 2308
  215.9 853.6 %copy-start.241 = (f32[1,2048]{1,0:T(1,128)}, f32[1,2048]{1,0:T(1,128)S(1)}, u32[]{:S(2)}) copy-start(f32[1,2048]{1,0:T(1,128)S(1)} %get-tuple-element.439) | copy-start | bytes 24580
  216.0 853.6 %copy-start.243 = (f32[1,2048]{1,0:T(1,128)}, f32[1,2048]{1,0:T(1,128)S(1)}, u32[]{:S(2)}) copy-start(f32[1,2048]{1,0:T(1,128)S(1)} %get-tuple-element.441) | copy-start | bytes 24580
  216.0 853.6 %copy-start.297 = (f32[1,2048]{1,0:T(1,128)}, f32[1,2048]{1,0:T(1,128)S(1)}, u32[]{:S(2)}) copy-start(f32[1,2048]{1,0:T(1,128)S(1)} %get-tuple-element.438) | copy-start | bytes 24580
  216.0 1182.3 %copy-start.303 = (f32[1,2048]{1,0:T(1,128)}, f32[1,2048]{1,0:T(1,128)S(1)}, u32[]{:S(2)}) copy-start(f32[1,2048]{1,0:T(1,128)S(1)} %get-tuple-element.437) | copy-start | bytes 24580
  216.0 1307.8 %copy-start.301 = (f32[1,2048]{1,0:T(1,128)}, f32[1,2048]{1,0:T(1,128)S(1)}, u32[]{:S(2)}) copy-start(f32[1,2048]{1,0:T(1,128)S(1)} %get-tuple-element.436) | copy-start | bytes 24580
  952.2 430.4 %all-reduce.110.cloned.1.call-start = ((), (), s32[]{:S(2)}) async-start(), calls=%async_computation.12 | async-start | bytes 131072 | tf_op jit(solution)/shard_map/psum | solution.py:100
  1065.1 20.0 collective-permute-start
  1074.2 10.0 collective-permute-start.6
  1076.2 10.4 collective-permute-start.2
  1078.0 9.6 collective-permute-start.4
  1405.8 111.8 %all-reduce.108.cloned.1.call-start = ((), (), s32[]{:S(2)}) async-start(), calls=%async_computation.11 | async-start | bytes 131072 | tf_op jit(solution)/shard_map/psum | solution.py:113
  1406.4 483.8 %all-reduce.106.cloned.1.call-start = ((), (), s32[]{:S(2)}) async-start(), calls=%async_computation.10 | async-start | bytes 262144 | tf_op jit(solution)/shard_map/psum | solution.py:113
  1715.7 55.3 %collective-permute-start.11 = (bf16[2,8,12,2048]{3,1,2,0:T(8,128)(2,1)S(1)}, bf16[2,8,12,2048]{3,1,2,0:T(8,128)(2,1)S(1)}, u32[]{:S(2)}, u32[]{:S(2)}) collective-permute-start(bf16[2,8,12,2048]{3,1,2,0:T(8,128)(2,1)S(1)} %copy.180), channel_id=1, source_target_pairs={{16,0},{17,1},{18,2},{19,3},{20,4},{21,5},{22,6},{23,7},{24,8},{25... | collective-permute-start | bytes 2359304 | tf_op jit(solution)/shard_map/ppermute | solution.py:29
  1720.6 53.9 %collective-permute-start.10 = (bf16[2,8,12,2048]{3,1,2,0:T(8,128)(2,1)S(1)}, bf16[2,8,12,2048]{3,1,2,0:T(8,128)(2,1)S(1)}, u32[]{:S(2)}, u32[]{:S(2)}) collective-permute-start(bf16[2,8,12,2048]{3,1,2,0:T(8,128)(2,1)S(1)} %copy.172), channel_id=1, source_target_pairs={{16,0},{17,1},{18,2},{19,3},{20,4},{21,5},{22,6},{23,7},{24,8},{25... | collective-permute-start | bytes 2359304 | tf_op jit(solution)/shard_map/ppermute | solution.py:29
  1725.0 53.1 %collective-permute-start.9 = (bf16[2,8,12,2048]{3,1,2,0:T(8,128)(2,1)S(1)}, bf16[2,8,12,2048]{3,1,2,0:T(8,128)(2,1)S(1)}, u32[]{:S(2)}, u32[]{:S(2)}) collective-permute-start(bf16[2,8,12,2048]{3,1,2,0:T(8,128)(2,1)S(1)} %copy.164), channel_id=1, source_target_pairs={{16,0},{17,1},{18,2},{19,3},{20,4},{21,5},{22,6},{23,7},{24,8},{25... | collective-permute-start | bytes 2359304 | tf_op jit(solution)/shard_map/ppermute | solution.py:29
  1729.3 52.2 %collective-permute-start.8 = (bf16[2,8,12,2048]{3,1,2,0:T(8,128)(2,1)S(1)}, bf16[2,8,12,2048]{3,1,2,0:T(8,128)(2,1)S(1)}, u32[]{:S(2)}, u32[]{:S(2)}) collective-permute-start(bf16[2,8,12,2048]{3,1,2,0:T(8,128)(2,1)S(1)} %copy.156), channel_id=1, source_target_pairs={{16,0},{17,1},{18,2},{19,3},{20,4},{21,5},{22,6},{23,7},{24,8},{25... | collective-permute-start | bytes 2359304 | tf_op jit(solution)/shard_map/ppermute | solution.py:29
  1786.4 979.2 %reduce-scatter.15.cloned.1.call-start = ((), (), s32[]{:S(2)}) async-start(), calls=%async_computation.9 | async-start | bytes 1081344
  1787.9 978.6 %reduce-scatter.13.cloned.1.call-start = ((), (), s32[]{:S(2)}) async-start(), calls=%async_computation.8 | async-start | bytes 270336
  2478.8 382.2 %reduce-scatter.9.cloned.1.call-start = ((), (), s32[]{:S(2)}) async-start(), calls=%async_computation.6 | async-start | bytes 25952256 | tf_op jit(solution)/shard_map/reduce_scatter | solution.py:625
  2515.9 704.8 %reduce-scatter.11.cloned.1.call-start = ((), (), s32[]{:S(2)}) async-start(), calls=%async_computation.7 | async-start | bytes 17301504 | tf_op jit(solution)/shard_map/reduce_scatter | solution.py:626
  2567.0 179.8 %collective-permute-start.1 = (bf16[2,8,12,1024]{3,2,1,0:T(8,128)(2,1)}, bf16[2,8,12,1024]{3,2,1,0:T(8,128)(2,1)}, u32[]{:S(2)}, u32[]{:S(2)}) collective-permute-start(bf16[2,8,12,1024]{3,2,1,0:T(8,128)(2,1)} %slice_select_fusion.5), channel_id=1, source_target_pairs={{16,0},{17,1},{18,2},{19,3},{20,4},{21,5},{22,6},{23,7},{24,8},{25... | collective-permute-start | bytes 1179656 | tf_op jit(solution)/shard_map/ppermute | solution.py:29
  2715.7 506.7 %collective-permute-start.12 = (bf16[8,16,24,512]{3,2,1,0:T(8,128)(2,1)}, bf16[8,16,24,512]{3,2,1,0:T(8,128)(2,1)}, u32[]{:S(2)}, u32[]{:S(2)}) collective-permute-start(bf16[8,16,24,512]{3,2,1,0:T(8,128)(2,1)} %slice.1197), channel_id=1, source_target_pairs={{0,16},{1,17},{2,18},{3,19},{4,20},{5,21},{6,22},{7,23},{8,24},{9,... | collective-permute-start | bytes 9437192 | tf_op jit(solution)/shard_map/ppermute | solution.py:29
  2727.0 24.8 collective-permute-start.3
  2729.1 26.3 collective-permute-start.5
  2731.3 27.8 collective-permute-start.7
  (508 other events, 17760.1 us)
Sparse Core Ops, SparseCore 0:
  11.5 80.6 all-gather.6
  95.6 95.3 all-gather.4
  952.3 102.5 all-reduce.111
  1282.1 100.3 all-reduce.109
  1413.8 103.7 all-reduce.107
  1786.5 103.6 all-reduce.105
  1892.4 138.2 reduce-scatter.14
  2478.9 132.9 reduce-scatter.12
  2618.8 242.0 reduce-scatter.8
  2863.7 356.9 reduce-scatter.10
where the time goes:
time: 3340 us; the launch traced here: 3280 us
  local copies, waits for them, and re-layouts  1030 us (31%)
  waiting for transfers between devices  851 us (25%)
  blocking collectives  768 us (23%)
  other arithmetic  307 us (9%)
  matrix products  269 us (8%)
    slice x72, local copies, waits for them, and re-layouts, patches(): padded[:, tap_row:tap_row + stride * rows_out:stride, tap_col:tap_col + s...  476 us
    reduce_scatter x1, waiting for transfers between devices, on_device(): lax.psum_scatter(wide_term, ('pipe', 'dp'), scatter_dimension=0, tiled=True)  358 us
    psum x4, blocking collectives, norm_back(): first_total, second_total = lax.psum((first_rows, second_rows), 'dp')  295 us
    psum x4, blocking collectives, norm_stats(): lax.psum((jnp.sum(pixel_mask), sum_rows, square_rows), 'dp')  294 us
    psum x2, waiting for transfers between devices, norm_back(): first_total, second_total = lax.psum((first_rows, second_rows), 'dp')  212 us
    unnamed x1182, local copies, waits for them, and re-layouts  204 us
    psum x2, waiting for transfers between devices, norm_stats(): lax.psum((jnp.sum(pixel_mask), sum_rows, square_rows), 'dp')  186 us
    pad x12, local copies, waits for them, and re-layouts, patches(): padded[:, tap_row:tap_row + stride * rows_out:stride, tap_col:tap_col + s...  114 us
  transfers between devices with their start and end apart: 23, of which 6 were waited for; matrix products, arithmetic and copies ran while one was open for 26% of the time, Pallas kernels for 0%

commit v1 on v0

v1 whole, which is shorter than its diff:
```python
import jax
import jax.numpy as jnp
import numpy as np
from jax import lax
from jax.experimental import pallas as pl
from jax.experimental.pallas import tpu as pltpu
from jax.sharding import PartitionSpec as P

C_IN = 1024
C_MID = 512
C_OUT = 2048
HB = 8
WB = 12
IMG_DEV = 8
SLOTS = 4
PIX = HB * WB
ROWS = SLOTS * PIX
HALF = ROWS // 2
PAD = 16
TILE = 512

EPS = 1e-05
MOMENTUM = 0.9
DECAY = 5e-05
TRUST = 0.001
RATE = 29.0
PRECISE = lax.Precision.HIGHEST
BFLOAT = jnp.bfloat16
SINGLE = jnp.float32
VMEM_LIMIT = 56 * 1024 * 1024


def dp_sum(value):
    size = lax.axis_size("dp")
    step = 1
    while step < size:
        value = value + lax.ppermute(value, "dp", [(i, i ^ step) for i in range(size)])
        step *= 2
    return value


def swap_pipe(value):
    return lax.ppermute(value, "pipe", [(0, 1), (1, 0)])


def dot(left, right):
    return jnp.dot(left, right, preferred_element_type=SINGLE)


def dot_back(left, right):
    return lax.dot_general(left, right, (((1,), (1,)), ((), ())), preferred_element_type=SINGLE)


def silu(value):
    return value * jax.nn.sigmoid(value)


def slope(value):
    gate = jax.nn.sigmoid(value)
    return gate * (1.0 + value * (1.0 - gate))


def put_sums(ref, values, first):
    for k, value in enumerate(values):
        for m in range(2):
            total = jnp.sum(value[m * HALF : (m + 1) * HALF], axis=0, keepdims=True)
            row = 2 * k + m
            ref[row : row + 1, :] = total if first else ref[row : row + 1, :] + total


def both(function):
    return jnp.concatenate([function(0), function(1)], axis=0)


def part(m):
    return slice(m * HALF, (m + 1) * HALF)


def moments(total_ref, inv_ref, m, scale=1.0):
    inv = inv_ref[m] * scale
    mean = total_ref[m : m + 1, :] * inv
    var = total_ref[2 + m : 3 + m, :] * inv - mean * mean
    return mean, lax.rsqrt(var + EPS)


def normed(a, total_ref, inv_ref, m, scale=1.0):
    mean, rstd = moments(total_ref, inv_ref, m, scale)
    return (a - mean) * rstd, rstd


def conv_grad(gz, xhat, rstd, gain, mask, sum_ref, inv_ref, m, scale=1.0, second=2):
    inv = inv_ref[m] * scale
    first_row = sum_ref[m : m + 1, :] * inv
    second_row = sum_ref[second + m : second + m + 1, :] * inv
    return (mask * ((rstd * gain) * (gz - first_row - xhat * second_row))).astype(BFLOAT)


def k_prep(slot_ref, img_ref, perm_ref, mask_ref, out_ref):
    planes = dot(perm_ref[...], img_ref[0])
    mask = mask_ref[...]
    for k in range(4):
        out_ref[k] = (planes[k * PIX : (k + 1) * PIX] * mask).astype(BFLOAT)


def k_first(x_ref, w_ref, a_ref, sum_ref):
    a = dot(x_ref[0], w_ref[...])
    a_ref[0] = a

    @pl.when(pl.program_id(0) == 0)
    def _():
        sum_ref[...] = jnp.zeros_like(sum_ref)

    put_sums(sum_ref, [a, a * a], False)


def shift_mask(edge_ref, di, dj):
    mask = None
    if di:
        mask = edge_ref[0 if di < 0 else 1]
    if dj:
        column = edge_ref[2 if dj < 0 else 3]
        mask = column if mask is None else mask * column
    return mask


def shifted(pad, edge_ref, di, dj):
    start = PAD + HB * dj + di
    rows = pad[start : start + ROWS, :]
    mask = shift_mask(edge_ref, di, dj)
    return (rows if mask is None else rows * mask).astype(BFLOAT)


def clear_pad(pad):
    pad[0:PAD, :] = jnp.zeros((PAD, pad.shape[1]), SINGLE)
    pad[PAD + ROWS : PAD + ROWS + PAD, :] = jnp.zeros((PAD, pad.shape[1]), SINGLE)


def parity(k):
    return (1, -1) if k == 0 else ((0, 0) if k == 1 else (1, 0))


def k_conv_two(inv_ref, total_ref, tab_ref, mask_ref, edge_ref, a_ref, w0, w1, w2, out_ref, col_ref, sum_ref, pad):
    step = pl.program_id(0)
    weights = (w0, w1, w2)
    gain, bias = tab_ref[0:1, :], tab_ref[1:2, :]
    for s in range(3):

        @pl.when(step == s)
        def _(s=s):
            if s < 2:
                for k in range(2):
                    plane = 2 * s + k
                    clear_pad(pad.at[plane])
                    for m in range(2):
                        xhat, _unused = normed(a_ref[k, part(m), :], total_ref, inv_ref, m, 0.25)
                        h = silu(xhat * gain + bias) * mask_ref[part(m), :]
                        pad[plane, PAD + m * HALF : PAD + (m + 1) * HALF, :] = h.astype(BFLOAT).astype(SINGLE)
            row_plane, di = parity((s + 1) % 3)
            for kx in range(3):
                col_plane, dj = parity(kx)
                tap = shifted(pad.at[2 * row_plane + col_plane], edge_ref, di, dj)
                col_ref[kx] = tap
                term = dot(tap, weights[kx][...])
                if s == 0 and kx == 0:
                    out_ref[...] = term
                else:
                    out_ref[...] += term
            if s == 2:
                a = out_ref[...]
                masked = a * mask_ref[...]
                put_sums(sum_ref, [masked, masked * a], True)


def k_conv_one(inv_ref, total_ref, tab_ref, mask_ref, edge_ref, a_ref, w0, w1, w2, out_ref, col_ref, sum_ref, pad):
    step = pl.program_id(0)
    weights = (w0, w1, w2)
    gain, bias = tab_ref[0:1, :], tab_ref[1:2, :]
    for s in range(3):

        @pl.when(step == s)
        def _(s=s):
            if s == 0:
                clear_pad(pad)
                for m in range(2):
                    xhat, _unused = normed(a_ref[part(m), :], total_ref, inv_ref, m)
                    h = silu(xhat * gain + bias) * mask_ref[part(m), :]
                    pad[PAD + m * HALF : PAD + (m + 1) * HALF, :] = h.astype(BFLOAT).astype(SINGLE)
            for kx in range(3):
                tap = shifted(pad, edge_ref, s - 1, kx - 1)
                col_ref[kx] = tap
                term = dot(tap, weights[kx][...])
                if s == 0 and kx == 0:
                    out_ref[...] = term
                else:
                    out_ref[...] += term
            if s == 2:
                a = out_ref[...]
                masked = a * mask_ref[...]
                put_sums(sum_ref, [masked, masked * a], True)


def k_expand(inv_ref, total_ref, tab_ref, mask_ref, a_ref, w_ref, h_ref, out_ref, sum_ref):
    @pl.when(pl.program_id(0) == 0)
    def _():
        gain, bias = tab_ref[0:1, :], tab_ref[1:2, :]
        for m in range(2):
            xhat, _unused = normed(a_ref[part(m), :], total_ref, inv_ref, m)
            h_ref[part(m), :] = (silu(xhat * gain + bias) * mask_ref[part(m), :]).astype(BFLOAT)

    a = dot(h_ref[...], w_ref[...])
    out_ref[...] = a
    put_sums(sum_ref, [a, a * a], True)


def k_short(x_ref, w0, w1, out_ref, sum_ref):
    a = dot(x_ref[0, :, :TILE], w0[...]) + dot(x_ref[0, :, TILE:], w1[...])
    out_ref[...] = a
    put_sums(sum_ref, [a, a * a], True)


def k_join(inv_ref, t3_ref, ts_ref, tab3_ref, tabs_ref, mask_ref, a3_ref, as_ref, w_ref, y_ref, out_ref, sum_ref):
    step = pl.program_id(0)
    for m in range(2):
        x3, _unused = normed(a3_ref[part(m), :], t3_ref, inv_ref, m)
        xs, _unused = normed(as_ref[part(m), :], ts_ref, inv_ref, m)
        joined = (x3 * tab3_ref[0:1, :] + tab3_ref[1:2, :]) + (xs * tabs_ref[0:1, :] + tabs_ref[1:2, :])
        y_ref[part(m), :] = (silu(joined) * mask_ref[part(m), :]).astype(BFLOAT)
    term = dot(y_ref[...], w_ref[...])

    @pl.when(step == 0)
    def _():
        out_ref[...] = term

    @pl.when(step > 0)
    def _():
        out_ref[...] += term

    @pl.when(step == pl.num_programs(0) - 1)
    def _():
        a = out_ref[...]
        put_sums(sum_ref, [a, a * a], True)


def k_head(slot_ref, inv_ref, total_ref, tab_ref, mask_ref, a_ref, y_ref, c0, c1, c2, c3, blk_ref, gz_ref, sum_ref):
    cots = (c0, c1, c2, c3)
    gain, bias = tab_ref[0:1, :], tab_ref[1:2, :]
    for m in range(2):
        mask = mask_ref[part(m), :]
        xhat, _unused = normed(a_ref[part(m), :], total_ref, inv_ref, m)
        z = (xhat * gain + bias) + y_ref[part(m), :].astype(SINGLE)
        gate = jax.nn.sigmoid(z)
        blk_ref[0, part(m), :] = (z * gate * mask).astype(BFLOAT)
        cot = jnp.concatenate([cots[2 * m][0], cots[2 * m + 1][0]], axis=0).astype(SINGLE)
        gz = cot * mask * (gate * (1.0 + z * (1.0 - gate)))
        gz_ref[part(m), :] = gz
        sum_ref[m : m + 1, :] = jnp.sum(gz, axis=0, keepdims=True)
        sum_ref[2 + m : 3 + m, :] = jnp.sum(gz * xhat, axis=0, keepdims=True)


def finish_back(gz_ref, sum_ref, grad, a_ref, total_ref, tab_ref, inv_ref, mask_ref):
    gain, bias = tab_ref[0:1, :], tab_ref[1:2, :]
    for m in range(2):
        xhat, _unused = normed(a_ref[part(m), :], total_ref, inv_ref, m)
        gz = grad[part(m)] * mask_ref[part(m), :] * slope(xhat * gain + bias)
        gz_ref[part(m), :] = gz
        sum_ref[m : m + 1, :] = jnp.sum(gz, axis=0, keepdims=True)
        sum_ref[2 + m : 3 + m, :] = jnp.sum(gz * xhat, axis=0, keepdims=True)


def k_back_six(inv_ref, gz_ref, a_ref, total_ref, s_ref, tab_ref, mask_ref, w_ref, low_ref, low_total, low_tab, ga_ref, out_ref, sum_ref, acc):
    step = pl.program_id(0)
    for m in range(2):
        xhat, rstd = normed(a_ref[part(m), :], total_ref, inv_ref, m)
        ga_ref[part(m), :] = conv_grad(
            gz_ref[part(m), :], xhat, rstd, tab_ref[0:1, :], mask_ref[part(m), :], s_ref, inv_ref, m
        )
    term = dot_back(ga_ref[...], w_ref[...])

    @pl.when(step == 0)
    def _():
        acc[...] = term

    @pl.when(step > 0)
    def _():
        acc[...] += term

    @pl.when(step == pl.num_programs(0) - 1)
    def _():
        finish_back(out_ref, sum_ref, acc[...], low_ref, low_total, low_tab, inv_ref, mask_ref)


def k_back_conv_one(inv_ref, gz_ref, a_ref, total_ref, s_ref, tab_ref, mask_ref, edge_ref, w0, w1, w2, low_ref, low_total, low_tab, ga_ref, out_ref, sum_ref, pad, acc):
    step = pl.program_id(0)
    weights = (w0, w1, w2)
    for s in range(3):

        @pl.when(step == s)
        def _(s=s):
            if s == 0:
                clear_pad(pad)
                for m in range(2):
                    xhat, rstd = normed(a_ref[part(m), :], total_ref, inv_ref, m)
                    ga = conv_grad(
                        gz_ref[part(m), :], xhat, rstd, tab_ref[0:1, :], mask_ref[part(m), :], s_ref, inv_ref, m
                    )
                    ga_ref[part(m), :] = ga
                    pad[PAD + m * HALF : PAD + (m + 1) * HALF, :] = ga.astype(SINGLE)
            for kx in range(3):
                term = dot_back(shifted(pad, edge_ref, 1 - s, 1 - kx), weights[kx][...])
                if s == 0 and kx == 0:
                    acc[...] = term
                else:
                    acc[...] += term
            if s == 2:
                finish_back(out_ref, sum_ref, acc[...], low_ref, low_total, low_tab, inv_ref, mask_ref)


def k_back_four(inv_ref, gz_ref, a_ref, total_ref, s_ref, tab_ref, mask_ref, w_ref, up_ref, a3_ref, as_ref, t3_ref, ts_ref, tab3_ref, tabs_ref, ga_ref, gj_ref, sum_ref):
    @pl.when(pl.program_id(0) == 0)
    def _():
        for m in range(2):
            xhat, rstd = normed(a_ref[part(m), :], total_ref, inv_ref, m)
            ga_ref[part(m), :] = conv_grad(
                gz_ref[part(m), :], xhat, rstd, tab_ref[0:1, :], mask_ref[part(m), :], s_ref, inv_ref, m
            )

    grad = dot_back(ga_ref[...], w_ref[...]) + up_ref[...]
    for m in range(2):
        x3, _unused = normed(a3_ref[part(m), :], t3_ref, inv_ref, m)
        xs, _unused = normed(as_ref[part(m), :], ts_ref, inv_ref, m)
        joined = (x3 * tab3_ref[0:1, :] + tab3_ref[1:2, :]) + (xs * tabs_ref[0:1, :] + tabs_ref[1:2, :])
        gj = grad[part(m)].astype(BFLOAT).astype(SINGLE) * mask_ref[part(m), :] * slope(joined)
        gj_ref[part(m), :] = gj
        for k, value in enumerate((gj, gj * x3, gj * xs)):
            row = 2 * k + m
            sum_ref[row : row + 1, :] = jnp.sum(value, axis=0, keepdims=True)


def k_back_three(inv_ref, gj_ref, a3_ref, as_ref, t3_ref, ts_ref, s_ref, tab3_ref, tabs_ref, mask_ref, w_ref, low_ref, low_total, low_tab, g3_ref, gs_ref, out_ref, sum_ref, acc):
    step = pl.program_id(0)
    for m in range(2):
        mask = mask_ref[part(m), :]
        gj = gj_ref[part(m), :]
        x3, r3 = normed(a3_ref[part(m), :], t3_ref, inv_ref, m)
        g3_ref[part(m), :] = conv_grad(gj, x3, r3, tab3_ref[0:1, :], mask, s_ref, inv_ref, m)
        xs, rs = normed(as_ref[part(m), :], ts_ref, inv_ref, m)
        gs_ref[part(m), :] = conv_grad(gj, xs, rs, tabs_ref[0:1, :], mask, s_ref, inv_ref, m, second=4)
    term = dot_back(g3_ref[...], w_ref[...])

    @pl.when(step == 0)
    def _():
        acc[...] = term

    @pl.when(step > 0)
    def _():
        acc[...] += term

    @pl.when(step == pl.num_programs(0) - 1)
    def _():
        finish_back(out_ref, sum_ref, acc[...], low_ref, low_total, low_tab, inv_ref, mask_ref)


def k_back_conv_two(inv_ref, gz_ref, a_ref, total_ref, s_ref, tab_ref, mask_ref, edge_ref, w0, w1, w2, low_ref, low_total, low_tab, ga_ref, out_ref, sum_ref, pad, acc):
    step = pl.program_id(0)
    weights = (w0, w1, w2)
    gain, bias = low_tab[0:1, :], low_tab[1:2, :]
    for s in range(3):

        @pl.when(step == s)
        def _(s=s):
            if s == 0:
                clear_pad(pad)
                for m in range(2):
                    xhat, rstd = normed(a_ref[part(m), :], total_ref, inv_ref, m)
                    ga = conv_grad(
                        gz_ref[part(m), :], xhat, rstd, tab_ref[0:1, :], mask_ref[part(m), :], s_ref, inv_ref, m
                    )
                    ga_ref[part(m), :] = ga
                    pad[PAD + m * HALF : PAD + (m + 1) * HALF, :] = ga.astype(SINGLE)
                sum_ref[...] = jnp.zeros_like(sum_ref)
            row_plane, di = parity((s + 1) % 3)
            for kx in (1, 0, 2):
                col_plane, dj = parity(kx)
                term = dot_back(shifted(pad, edge_ref, -di, -dj), weights[kx][...])
                if s == 2 or kx == 2:
                    acc[col_plane] += term
                else:
                    acc[col_plane] = term
            if s != 1:
                for k in range(2):
                    for m in range(2):
                        xhat, _unused = normed(low_ref[k, part(m), :], low_total, inv_ref, m, 0.25)
                        gz = acc[k, part(m), :] * mask_ref[part(m), :] * slope(xhat * gain + bias)
                        out_ref[k, part(m), :] = gz
                        for q, value in enumerate((gz, gz * xhat)):
                            row = 2 * q + m
                            sum_ref[row : row + 1, :] += jnp.sum(value, axis=0, keepdims=True)


def k_wide_back(g_ref, w_ref, out_ref):
    out_ref[...] = dot_back(g_ref[...], w_ref[...])


def k_last(slot_ref, inv_ref, gz_ref, a_ref, total_ref, s_ref, tab_ref, mask_ref, w_ref, short_ref, perm_ref, ga_ref, out_ref):
    m = pl.program_id(0) // 2
    inv = inv_ref[m] * 0.25
    mean = total_ref[pl.ds(m, 1), :] * inv
    var = total_ref[pl.ds(2 + m, 1), :] * inv - mean * mean
    rstd = lax.rsqrt(var + EPS)
    first_row = s_ref[pl.ds(m, 1), :] * inv
    second_row = s_ref[pl.ds(2 + m, 1), :] * inv
    mask = mask_ref[...]
    parts = []
    for k in range(4):
        xhat = (a_ref[k] - mean) * rstd
        ga = (mask * ((rstd * tab_ref[0:1, :]) * (gz_ref[k] - first_row - xhat * second_row))).astype(BFLOAT)
        ga_ref[k] = ga
        grad = dot_back(ga, w_ref[...])
        if k == 0:
            grad = grad + short_ref[...]
        parts.append((grad * mask).astype(BFLOAT))
    planes = jnp.concatenate(parts, axis=0)
    image = lax.dot_general(perm_ref[...], planes, (((0,), (0,)), ((), ())), preferred_element_type=SINGLE).astype(BFLOAT)
    core = slot_ref[SLOTS]
    out_ref[core, 0] = image[:, : C_IN // 2]
    out_ref[1 - core, 0] = image[:, C_IN // 2 :]


def k_place(slot_ref, own_ref, got_ref, out_ref):
    step = pl.program_id(0)

    @pl.when(step < SLOTS)
    def _():
        out_ref[0] = own_ref[0, 0]

    @pl.when(step >= SLOTS)
    def _():
        out_ref[0] = got_ref[0]


def k_grad(slot_ref, feature_ref, grad_ref, *refs):
    keep_ref, send_ref = refs[-2:]
    feature, grad = feature_ref[...], grad_ref[...]
    feature = feature.reshape(-1, feature.shape[-1])
    grad = grad.reshape(-1, grad.shape[-1])
    tile = lax.dot_general(feature, grad, (((0,), (0,)), ((), ())), preferred_element_type=SINGLE).astype(BFLOAT)
    half = tile.shape[1] // 2

    @pl.when(slot_ref[SLOTS] == 0)
    def _():
        keep_ref[...] = tile[:, :half]
        send_ref[...] = tile[:, half:]

    @pl.when(slot_ref[SLOTS] == 1)
    def _():
        keep_ref[...] = tile[:, half:]
        send_ref[...] = tile[:, :half]


def k_split(me_ref, *refs):
    own, got, outs = refs[:4], refs[4:8], refs[8:]
    for own_ref, got_ref, out_ref in zip(own, got, outs):
        out_ref[0] = (own_ref[...].astype(SINGLE) + got_ref[...].astype(SINGLE)).astype(BFLOAT)


def full(shape):
    zeros = (0,) * len(shape)
    return pl.BlockSpec(tuple(shape), lambda *_: zeros)


SCALARS = pl.BlockSpec(memory_space=pltpu.SMEM)


def spec(shape, index):
    return pl.BlockSpec(tuple(shape), index)


def call(kernel, name, grid, in_specs, out_specs, out_shape, scratch, args, prefetch=0):
    return pl.pallas_call(
        kernel,
        out_shape=out_shape,
        grid_spec=pltpu.PrefetchScalarGridSpec(
            num_scalar_prefetch=prefetch,
            grid=grid,
            in_specs=in_specs,
            out_specs=out_specs,
            scratch_shapes=scratch,
        ),
        compiler_params=pltpu.CompilerParams(vmem_limit_bytes=VMEM_LIMIT),
        name=name,
    )(*args)


def shape_of(shape, dtype=SINGLE):
    return jax.ShapeDtypeStruct(tuple(shape), dtype)


def permutation():
    table = np.zeros((4 * PIX, 4 * PIX), np.float32)
    for pi in range(2):
        for pj in range(2):
            for i in range(HB):
                for j in range(WB):
                    table[((2 * pi + pj) * WB + j) * HB + i, (2 * i + pi) * 2 * WB + 2 * j + pj] = 1.0
    return jnp.asarray(table, BFLOAT)


def edges():
    rows = np.arange(ROWS)
    i, j = rows % HB, (rows // HB) % WB
    return jnp.asarray(np.stack([i > 0, i < HB - 1, j > 0, j < WB - 1]).astype(np.float32)[..., None])


def group_table(start_index, rows_local, bounds):
    global_rows = start_index * rows_local + jnp.arange(rows_local, dtype=jnp.int32)
    group_ids = jnp.zeros((rows_local,), jnp.int32)
    for boundary in bounds:
        group_ids = group_ids + (global_rows >= boundary).astype(jnp.int32)
    return (group_ids[:, None] == jnp.arange(len(bounds) + 1, dtype=jnp.int32)[None, :]).astype(SINGLE)


def rounded(value):
    return lax.reduce_precision(value, 8, 7)


def split_group(name, keep, got, rows, index):
    cols = keep.shape[1]

    def block(which, sent):
        def at(q, me):
            other, low, high = (q >> 2) & 1, (q >> 1) & 1, q & 1
            pair = other * 2 + sent if which == 0 else sent * 2 + other
            return (index(which, me[0] ^ (high * 8 + low * 4 + pair)), 0)

        return spec((rows, cols), at)

    blocks = [block(which, sent) for which in range(2) for sent in range(2)]
    return call(
        k_split, name, (8,), blocks + blocks,
        [spec((1, rows, cols), lambda q, me: (q, 0, 0))] * 4,
        [shape_of((8, rows, cols), BFLOAT)] * 4, [],
        (lax.axis_index("dp")[None].astype(jnp.int32),) + (keep,) * 4 + (got,) * 4, prefetch=1,
    )


def halve(keep, send, bits):
    size = lax.axis_size("dp")
    for bit in bits:
        got = lax.ppermute(send, "dp", [(i, i ^ bit) for i in range(size)])
        total = keep.astype(SINGLE) + got.astype(SINGLE)
        half = total.shape[0] // 2
        if half:
            keep, send = total[:half].astype(BFLOAT), total[half:].astype(BFLOAT)
    return total[0]


def scatter_group(name, keep, send, block, by_rows):
    got = swap_pipe(send)
    size = lax.axis_size("dp")
    if size == 16:
        rows = block // 2 if by_rows else block
        index = (lambda which, m: 2 * m + which) if by_rows else (lambda which, m: 16 * which + m)
        keep0, send0, keep1, send1 = split_group("split_" + name, keep, got, rows, index)
        return halve(keep0, send0, (1, 2, 4, 8)), halve(keep1, send1, (2, 1, 4, 8))
    total = (keep.astype(SINGLE) + got.astype(SINGLE)).astype(BFLOAT)
    if by_rows:
        own = lax.psum_scatter(total, "dp", scatter_dimension=0, tiled=True).astype(SINGLE)
        return own[: block // 2], own[block // 2 :]
    middle = total.shape[0] // 2
    return tuple(lax.psum_scatter(p, "dp", scatter_dimension=0, tiled=True).astype(SINGLE) for p in (total[:middle], total[middle:]))


def on_device(images, cotangent, heights, widths, assign, w_narrow, w_wide, bn_mid, bn_wide, mom_narrow, mom_wide, mom_bn_mid, mom_bn_wide):
    core = lax.axis_index("pipe")
    shard = lax.axis_index(("pipe", "dp"))
    hot_narrow = group_table(shard, w_narrow.shape[0], (C_IN, C_IN + 9 * C_MID, C_IN + 9 * C_MID + C_OUT))
    hot_wide = group_table(shard, w_wide.shape[0], (C_MID, C_MID + C_IN))

    narrow = lax.all_gather(w_narrow.astype(BFLOAT), ("pipe", "dp"), axis=0, tiled=True)
    wide = lax.all_gather(w_wide.astype(BFLOAT), ("pipe", "dp"), axis=0, tiled=True)

    order = assign[0].reshape(2, SLOTS)
    own_slots = lax.dynamic_index_in_dim(order, core, 0, keepdims=False)
    other_slots = lax.dynamic_index_in_dim(order, 1 - core, 0, keepdims=False)
    slots = jnp.concatenate([own_slots, core[None].astype(jnp.int32), other_slots])

    counts = jnp.sum((heights * widths)[assign[0]].reshape(4, 2), axis=1).astype(SINGLE)
    mid_cols, wide_cols = bn_mid.shape[1], bn_wide.shape[1]
    tables = jnp.concatenate(
        [
            lax.dynamic_update_slice(jnp.zeros((8, C_MID), SINGLE), rounded(bn_mid), (0, shard * mid_cols)),
            lax.dynamic_update_slice(jnp.zeros((6, C_OUT), SINGLE), rounded(bn_wide), (0, shard * wide_cols)).reshape(24, C_MID),
        ]
    )
    tables = tables + swap_pipe(tables)
    count_rows = jnp.zeros((8, C_MID), SINGLE).at[0, :4].set(counts)
    gathered = dp_sum(jnp.concatenate([tables, count_rows]))
    mid, table = gathered[:8], gathered[8:32].reshape(6, C_OUT)
    inv = lax.dynamic_slice(1.0 / gathered[32, :4], (2 * core,), (2,))

    heights_own, widths_own = heights[own_slots], widths[own_slots]
    inside = (jnp.arange(HB)[None, None, :] < heights_own[:, None, None]) & (jnp.arange(WB)[None, :, None] < widths_own[:, None, None])
    mask = inside.astype(SINGLE).reshape(ROWS, 1)
    edge = edges()
    perm = permutation()

    mid1, mid2, mid4, mid5 = (mid[2 * k : 2 * k + 2] for k in range(4))
    tab3, tabs, tab6 = (table[2 * k : 2 * k + 2] for k in range(3))

    def weight_grad(name, feature, feature_spec, grad, tiles, shape, rows, base, bufs):
        out_spec = spec((rows, shape[1]), lambda t, slot: (base + t, 0))
        return pl.pallas_call(
            k_grad,
            out_shape=[shape_of(shape, BFLOAT)] * 2,
            grid_spec=pltpu.PrefetchScalarGridSpec(
                num_scalar_prefetch=1,
                grid=(tiles,),
                in_specs=[feature_spec, full(grad.shape)] + [pl.BlockSpec(memory_space=pl.ANY)] * (2 if bufs else 0),
                out_specs=[out_spec] * 2,
            ),
            input_output_aliases={3: 0, 4: 1} if bufs else {},
            compiler_params=pltpu.CompilerParams(vmem_limit_bytes=VMEM_LIMIT),
            name=name,
        )(slots, feature, grad, *(bufs or ()))

    wide_tile = spec((ROWS, 256), lambda t, slot: (0, t))
    tap_tile = spec((1, ROWS, C_MID), lambda t, slot: (t, 0, 0))
    full_row = full((4, C_MID))
    full_tab = full((2, C_MID))
    full_mask = full((ROWS, 1))
    full_edge = full((4, ROWS, 1))
    full_mid = full((ROWS, C_MID))

    def narrow_block(index):
        return spec((TILE, TILE), index)

    chunk = spec((ROWS, TILE), lambda k, *_: (0, k))
    chunk_sum = spec((4, TILE), lambda k, *_: (0, k))
    chunk_tab = spec((2, TILE), lambda k, *_: (0, k))

    x = call(
        k_prep, "prep", (SLOTS,),
        [spec((1, 4 * PIX, C_IN), lambda s, slot: (slot[s], 0, 0)), full((4 * PIX, 4 * PIX)), spec((PIX, 1), lambda s, slot: (s, 0))],
        spec((4, PIX, C_IN), lambda s, slot: (0, s, 0)),
        shape_of((4, ROWS, C_IN), BFLOAT), [],
        (slots, images.reshape(IMG_DEV, 4 * PIX, C_IN), perm, mask), prefetch=1,
    )

    a1, part1 = call(
        k_first, "a1", (4,),
        [spec((1, ROWS, C_IN), lambda k: (k, 0, 0)), full((C_IN, C_MID))],
        [spec((1, ROWS, C_MID), lambda k: (k, 0, 0)), full_row],
        [shape_of((4, ROWS, C_MID)), shape_of((4, C_MID))], [],
        (x, narrow),
    )
    a_s, part_s = call(
        k_short, "as", (4,),
        [spec((1, ROWS, C_IN), lambda k: (0, 0, 0)), spec((TILE, TILE), lambda k: (1, k)), spec((TILE, TILE), lambda k: (2, k))],
        [chunk, chunk_sum],
        [shape_of((ROWS, C_OUT)), shape_of((4, C_OUT))], [],
        (x, wide, wide),
    )
    total1 = dp_sum(part1)

    def conv_weights(first, order_of):
        return [narrow_block(lambda s, kx=kx: (first + 3 * order_of(s) + kx, 0)) for kx in range(3)]

    turned = lambda s: lax.rem(s + 1, 3)
    straight = lambda s: s

    a2, col1, part2 = call(
        k_conv_two, "a2", (3,),
        [SCALARS, full_row, full_tab, full_mask, full_edge, spec((2, ROWS, C_MID), lambda s: (jnp.minimum(s, 1), 0, 0))] + conv_weights(2, turned),
        [full_mid, spec((3, ROWS, C_MID), lambda s: (turned(s), 0, 0)), full_row],
        [shape_of((ROWS, C_MID)), shape_of((9, ROWS, C_MID), BFLOAT), shape_of((4, C_MID))],
        [pltpu.VMEM((4, PAD + ROWS + PAD, C_MID), SINGLE)],
        (inv, total1, mid1, mask, edge, a1, narrow, narrow, narrow),
    )
    total2 = dp_sum(part2)

    def expand(name, a, total, tab, row):
        return call(
            k_expand, name, (4,),
            [SCALARS, full_row, full_tab, full_mask, full_mid, spec((TILE, TILE), lambda k: (row, k))],
            [full_mid, chunk, chunk_sum],
            [shape_of((ROWS, C_MID), BFLOAT), shape_of((ROWS, C_OUT)), shape_of((4, C_OUT))], [],
            (inv, total, tab, mask, a, wide),
        )

    h2, a3, part3 = expand("a3", a2, total2, mid2, 0)
    total3s = dp_sum(jnp.concatenate([part3, part_s]))
    total3, total_s = total3s[:4], total3s[4:]

    y, a4, part4 = call(
        k_join, "a4", (4,),
        [SCALARS, chunk_sum, chunk_sum, chunk_tab, chunk_tab, full_mask, chunk, chunk, narrow_block(lambda k: (11 + k, 0))],
        [chunk, full_mid, full_row],
        [shape_of((ROWS, C_OUT), BFLOAT), shape_of((ROWS, C_MID)), shape_of((4, C_MID))], [],
        (inv, total3, total_s, tab3, tabs, mask, a3, a_s, narrow),
    )
    total4 = dp_sum(part4)

    a5, col4, part5 = call(
        k_conv_one, "a5", (3,),
        [SCALARS, full_row, full_tab, full_mask, full_edge, full_mid] + conv_weights(15, straight),
        [full_mid, spec((3, ROWS, C_MID), lambda s: (s, 0, 0)), full_row],
        [shape_of((ROWS, C_MID)), shape_of((9, ROWS, C_MID), BFLOAT), shape_of((4, C_MID))],
        [pltpu.VMEM((PAD + ROWS + PAD, C_MID), SINGLE)],
        (inv, total4, mid4, mask, edge, a4, narrow, narrow, narrow),
    )
    total5 = dp_sum(part5)
    h5, a6, part6 = expand("a6", a5, total5, mid5, 3)
    total6 = dp_sum(part6)

    cot = cotangent.transpose(0, 2, 1, 3).reshape(IMG_DEV, PIX, C_OUT)
    blk, gz6, s6 = call(
        k_head, "head", (4,),
        [SCALARS, chunk_sum, chunk_tab, full_mask, chunk, chunk]
        + [spec((1, PIX, TILE), lambda k, slot, s=s: (slot[s], 0, k)) for s in range(SLOTS)],
        [
            spec((1, ROWS, TILE), lambda k, slot: ((k // 2) ^ slot[SLOTS], 0, lax.rem(k, 2))),
            chunk,
            chunk_sum,
        ],
        [shape_of((2, ROWS, C_OUT // 2), BFLOAT), shape_of((ROWS, C_OUT)), shape_of((4, C_OUT))], [],
        (slots, inv, total6, tab6, mask, a6, y, cot, cot, cot, cot), prefetch=1,
    )
    sum6 = dp_sum(s6)

    ga6, gz5, s5 = call(
        k_back_six, "g5", (4,),
        [SCALARS, chunk, chunk, chunk_sum, chunk_sum, chunk_tab, full_mask, spec((TILE, TILE), lambda k: (3, k)), full_mid, full_row, full_tab],
        [chunk, full_mid, full_row],
        [shape_of((ROWS, C_OUT), BFLOAT), shape_of((ROWS, C_MID)), shape_of((4, C_MID))],
        [pltpu.VMEM((ROWS, C_MID), SINGLE)],
        (inv, gz6, a6, total6, sum6, tab6, mask, wide, a5, total5, mid5),
    )
    sum5 = dp_sum(s5)
    bufs_w = weight_grad("dw6", h5, wide_tile, ga6, 2, (2048, 1024), 256, 6, None)

    ga5, gz4, s4 = call(
        k_back_conv_one, "g4", (3,),
        [SCALARS, full_mid, full_mid, full_row, full_row, full_tab, full_mask, full_edge] + conv_weights(15, straight) + [full_mid, full_row, full_tab],
        [full_mid, full_mid, full_row],
        [shape_of((ROWS, C_MID), BFLOAT), shape_of((ROWS, C_MID)), shape_of((4, C_MID))],
        [pltpu.VMEM((PAD + ROWS + PAD, C_MID), SINGLE), pltpu.VMEM((ROWS, C_MID), SINGLE)],
        (inv, gz5, a5, total5, sum5, mid5, mask, edge, narrow, narrow, narrow, a4, total4, mid4),
    )
    sum4 = dp_sum(s4)
    bufs_b = weight_grad("dw5", col4, tap_tile, ga5, 9, (6144, 256), TILE, 3, None)

    ga4, gj, s3 = call(
        k_back_four, "gy", (4,),
        [SCALARS, full_mid, full_mid, full_row, full_row, full_tab, full_mask, narrow_block(lambda k: (11 + k, 0)),
         chunk, chunk, chunk, chunk_sum, chunk_sum, chunk_tab, chunk_tab],
        [full_mid, chunk, spec((6, TILE), lambda k: (0, k))],
        [shape_of((ROWS, C_MID), BFLOAT), shape_of((ROWS, C_OUT)), shape_of((6, C_OUT))], [],
        (inv, gz4, a4, total4, sum4, mid4, mask, narrow, gz6, a3, a_s, total3, total_s, tab3, tabs),
    )
    sum3 = dp_sum(s3)
    bufs_b = weight_grad("dw4b", y, spec((ROWS, TILE), lambda t, slot: (0, 1 + t)), ga4, 3, (6144, 256), TILE, 0, bufs_b)
    bufs_a = weight_grad("dw4a", y, spec((ROWS, TILE), lambda t, slot: (0, t)), ga4, 1, (6144, 256), TILE, 11, None)

    ga3, gas, gz2, s2 = call(
        k_back_three, "g2", (4,),
        [SCALARS, chunk, chunk, chunk, chunk_sum, chunk_sum, spec((6, TILE), lambda k: (0, k)), chunk_tab, chunk_tab, full_mask,
         spec((TILE, TILE), lambda k: (0, k)), full_mid, full_row, full_tab],
        [chunk, chunk, full_mid, full_row],
        [shape_of((ROWS, C_OUT), BFLOAT), shape_of((ROWS, C_OUT), BFLOAT), shape_of((ROWS, C_MID)), shape_of((4, C_MID))],
        [pltpu.VMEM((ROWS, C_MID), SINGLE)],
        (inv, gj, a3, a_s, total3, total_s, sum3, tab3, tabs, mask, wide, a2, total2, mid2),
    )
    sum2 = dp_sum(s2)
    bufs_w = weight_grad("dw3", h2, wide_tile, ga3, 2, (2048, 1024), 256, 0, bufs_w)
    bufs_w = weight_grad("dws", x, spec((1, ROWS, 256), lambda t, slot: (0, 0, t)), gas, 4, (2048, 1024), 256, 2, bufs_w)
    dxs = call(
        k_wide_back, "dxs", (2,),
        [full((ROWS, C_OUT)), spec((TILE, C_OUT), lambda k: (1 + k, 0))],
        spec((ROWS, TILE), lambda k: (0, k)),
        shape_of((ROWS, C_IN)), [],
        (gas, wide),
    )

    ga2, gz1, s1 = call(
        k_back_conv_two, "g1", (3,),
        [SCALARS, full_mid, full_mid, full_row, full_row, full_tab, full_mask, full_edge] + conv_weights(2, turned)
        + [spec((2, ROWS, C_MID), lambda s: (jnp.minimum(s, 1), 0, 0)), full_row, full_tab],
        [full_mid, spec((2, ROWS, C_MID), lambda s: (jnp.minimum(s, 1), 0, 0)), full_row],
        [shape_of((ROWS, C_MID), BFLOAT), shape_of((4, ROWS, C_MID)), shape_of((4, C_MID))],
        [pltpu.VMEM((PAD + ROWS + PAD, C_MID), SINGLE), pltpu.VMEM((2, ROWS, C_MID), SINGLE)],
        (inv, gz2, a2, total2, sum2, mid2, mask, edge, narrow, narrow, narrow, a1, total1, mid1),
    )
    sum1 = dp_sum(s1)
    bufs_a = weight_grad("dw2", col1, tap_tile, ga2, 9, (6144, 256), TILE, 2, bufs_a)

    image_part = spec((4, PIX, C_MID), lambda s, slot: (0, s, 0))
    ga1, image_grad = call(
        k_last, "gx", (SLOTS,),
        [SCALARS, image_part, image_part, full_row, full_row, full_tab, spec((PIX, 1), lambda s, slot: (s, 0)),
         full((C_IN, C_MID)), spec((PIX, C_IN), lambda s, slot: (s, 0)), full((4 * PIX, 4 * PIX))],
        [image_part, spec((2, 1, 4 * PIX, C_IN // 2), lambda s, slot: (0, s, 0, 0))],
        [shape_of((4, ROWS, C_MID), BFLOAT), shape_of((2, SLOTS, 4 * PIX, C_IN // 2), BFLOAT)], [],
        (slots, inv, gz1, a1, total1, sum1, mid1, mask, narrow, dxs, perm), prefetch=1,
    )
    bufs_a = weight_grad("dw1", x, spec((4, ROWS, TILE), lambda t, slot: (0, 0, t)), ga1, 2, (6144, 256), TILE, 0, bufs_a)

    def place(name, pair):
        got = swap_pipe(pair[1])
        block = (1,) + pair.shape[2:]
        return call(
            k_place, name, (IMG_DEV,),
            [
                spec((1,) + block, lambda t, slot: (0, jnp.minimum(t, SLOTS - 1), 0, 0)),
                spec(block, lambda t, slot: (jnp.maximum(t - SLOTS, 0), 0, 0)),
            ],
            spec(block, lambda t, slot: (slot[t + (t >= SLOTS)], 0, 0)),
            shape_of((IMG_DEV,) + pair.shape[2:], BFLOAT), [],
            (slots, pair, got), prefetch=1,
        )

    block_local = place("place_out", blk.reshape(2, SLOTS, PIX, C_OUT // 2)).reshape(IMG_DEV, WB, HB, C_OUT // 2).transpose(0, 2, 1, 3)
    grad_local = place("place_grad", image_grad).reshape(IMG_DEV, 2 * HB, 2 * WB, C_IN // 2)

    half_a0, half_a1 = scatter_group("a", *bufs_a, w_narrow.shape[0], True)
    half_w0, half_w1 = scatter_group("w", *bufs_w, w_wide.shape[0], False)
    sum_b = (bufs_b[0].astype(SINGLE) + swap_pipe(bufs_b[1]).astype(SINGLE)).astype(BFLOAT)
    half_b = lax.psum_scatter(sum_b, "dp", scatter_dimension=0, tiled=True).astype(SINGLE)
    half_a = jnp.concatenate([half_a0, half_a1], axis=0)

    def join_halves(first, second):
        mine = jnp.where(core == 0, first, second)
        got = swap_pipe(jnp.where(core == 0, second, first))
        return jnp.where(core == 0, jnp.concatenate([mine, got], axis=1), jnp.concatenate([got, mine], axis=1))

    grad_narrow = join_halves(half_a, half_b)
    grad_wide = join_halves(half_w0, half_w1)

    def pair_sum(rows):
        return rows[0] + rows[1]

    mid_rows = jnp.stack([pair_sum(v) for t in (sum1, sum2, sum4, sum5) for v in (t[2:4], t[0:2])])
    wide_rows = jnp.stack([pair_sum(v) for v in (sum3[2:4], sum3[0:2], sum3[4:6], sum3[0:2], sum6[2:4], sum6[0:2])])
    mid_rows = mid_rows + swap_pipe(mid_rows)
    wide_rows = wide_rows + swap_pipe(wide_rows)
    grad_mid = lax.dynamic_slice(mid_rows, (0, shard * mid_cols), (8, mid_cols))
    grad_table = lax.dynamic_slice(wide_rows, (0, shard * wide_cols), (6, wide_cols))

    def square_vector(narrow_rows, wide_rows, mid_part, table_part):
        return jnp.concatenate(
            [
                jnp.dot(jnp.sum(narrow_rows * narrow_rows, axis=1), hot_narrow, precision=PRECISE),
                jnp.dot(jnp.sum(wide_rows * wide_rows, axis=1), hot_wide, precision=PRECISE),
                jnp.sum(mid_part * mid_part, axis=1),
                jnp.sum(table_part * table_part, axis=1),
            ]
        )

    squares = jnp.stack([square_vector(w_narrow, w_wide, bn_mid, bn_wide), square_vector(grad_narrow, grad_wide, grad_mid, grad_table)])
    squares = dp_sum(squares + swap_pipe(squares))
    norms = jnp.sqrt(squares)
    weight_norms, grad_norms = norms[0], norms[1]
    ratios = TRUST * weight_norms / (grad_norms + DECAY * weight_norms)
    ratio_narrow = jnp.dot(hot_narrow, ratios[:4], precision=PRECISE)
    ratio_wide = jnp.dot(hot_wide, ratios[4:7], precision=PRECISE)

    def lars_step(weight, gradient, moment, ratio_rows):
        new_moment = MOMENTUM * moment + RATE * ratio_rows[:, None] * (gradient + DECAY * weight)
        return (weight - new_moment, new_moment)

    new_narrow, new_mom_narrow = lars_step(w_narrow, grad_narrow, mom_narrow, ratio_narrow)
    new_wide, new_mom_wide = lars_step(w_wide, grad_wide, mom_wide, ratio_wide)
    new_mid, new_mom_mid = lars_step(bn_mid, grad_mid, mom_bn_mid, ratios[7:15])
    new_table, new_mom_table = lars_step(bn_wide, grad_table, mom_bn_wide, ratios[15:21])
    return (
        block_local, grad_local, grad_narrow, grad_wide, grad_mid, grad_table,
        new_mom_narrow, new_mom_wide, new_mom_mid, new_mom_table,
        new_narrow, new_wide, new_mid, new_table,
    )


def solution(mesh):
    rows = P(("pipe", "dp"), None)
    columns = P(None, ("pipe", "dp"))
    feature = P("dp", None, None, None)
    return jax.shard_map(
        on_device,
        mesh=mesh,
        in_specs=(feature, feature, P("dp"), P("dp"), P("dp", None), rows, rows, columns, columns, rows, rows, columns, columns),
        out_specs=(P("dp", None, None, "pipe"), P("dp", None, None, "pipe"), rows, rows, columns, columns, rows, rows, columns, columns, rows, rows, columns, columns),
        check_vma=False,
    )
```

time: 3340 us -> 706 us (0.21); the launches traced: 3280 us -> 696 us
  local copies, waits for them, and re-layouts: 1030 us -> 16.4 us
  blocking collectives: 768 us -> 0 us
  waiting for transfers between devices: 851 us -> 309 us
  matrix products: 269 us -> 2.63 us
  other arithmetic: 307 us -> 49.2 us
  Pallas kernels: 0 us -> 196 us
  starting transfers between devices: 23 us -> 108 us
    psum x9 -> x0, blocking collectives: 632 us -> none  [the longest x4 295 us: norm_back(): first_total, second_total = lax.psum((first_rows, second_rows), 'dp')]
    slice x101 -> x19, local copies, waits for them, and re-layouts: 514 us -> 6.12 us  [the longest x1 2.06 us: place(): got = swap_pipe(pair[1])]
    reduce_scatter x2 -> x1, waiting for transfers between devices: 452 us -> 7.47 us  [on_device(): lax.psum_scatter(sum_b, 'dp', scatter_dimension=0, tiled=True)]
    psum x4 -> x0, waiting for transfers between devices: 399 us -> none  [the longest x2 212 us: norm_back(): first_total, second_total = lax.psum((first_rows, second_rows), 'dp')]
    dot_general x88 -> x4, matrix products: 269 us -> 2.08 us  [the longest x2 1.11 us: square_vector(): jnp.dot(jnp.sum(narrow_rows * narrow_rows, axis=1), hot_narrow, precision...]
    ppermute x13 -> x83, waiting for transfers between devices: 0.03 us -> 201 us  [the longest x56 124 us: dp_sum(): lax.ppermute(value, 'dp', [(i, i ^ step) for i in range(size)])]
    unnamed x1182 -> x77, local copies, waits for them, and re-layouts: 204 us -> 3.51 us
    pallas_call x0 -> x28, Pallas kernels: none -> 196 us  [the longest x20 145 us: call(): pl.pallas_call(kernel, out_shape=out_shape, grid_spec=pltpu.PrefetchScala...]
  transfers between devices with their start and end apart: 23 -> 86, of which waited for: 6 -> 65; matrix products, arithmetic and copies ran while one was open for 26% -> 7% of each run, Pallas kernels for 0% -> 19%
where the time goes in v1:
time: 706 us; the launch traced here: 696 us
  waiting for transfers between devices  309 us (44%)
  Pallas kernels  196 us (28%)
  starting transfers between devices  108 us (15%)
  other arithmetic  49.2 us (7%)
  local copies, waits for them, and re-layouts  16.4 us (2%)
  between operations  15.1 us (2%)
    pallas_call x20, Pallas kernels, call(): pl.pallas_call(kernel, out_shape=out_shape, grid_spec=pltpu.PrefetchScala...  145 us
    ppermute x56, waiting for transfers between devices, dp_sum(): lax.ppermute(value, 'dp', [(i, i ^ step) for i in range(size)])  124 us
    ppermute x56, starting transfers between devices, dp_sum(): lax.ppermute(value, 'dp', [(i, i ^ step) for i in range(size)])  88.1 us
    ppermute x16, waiting for transfers between devices, halve(): got = lax.ppermute(send, 'dp', [(i, i ^ bit) for i in range(size)])  77 us
    all_gather x1, waiting for transfers between devices, on_device(): lax.all_gather(w_narrow.astype(BFLOAT), ('pipe', 'dp'), axis=0, tiled=True)  65.1 us
    pallas_call x8, Pallas kernels, weight_grad(): pl.pallas_call(k_grad, out_shape=[shape_of(shape, BFLOAT)] * 2, grid_spec...  50.8 us
    all_gather x1, waiting for transfers between devices, on_device(): lax.all_gather(w_wide.astype(BFLOAT), ('pipe', 'dp'), axis=0, tiled=True)  34.6 us
    ppermute x16, starting transfers between devices, halve(): got = lax.ppermute(send, 'dp', [(i, i ^ bit) for i in range(size)])  17.7 us
  transfers between devices with their start and end apart: 86, of which 65 were waited for; matrix products, arithmetic and copies ran while one was open for 7% of the time, Pallas kernels for 19%

profile of v1, /device:TPU:0, one launch (start us, length us, event | category | flops | bytes accessed | tf_op | source)
XLA Modules:
  0.0 695.7 jit_solution(6290897219314179456)
XLA Ops:
  40.7 6.0 prep.1.x_ref.feature_ref
  46.8 65.1 %all-gather.3.cloned.1.call-done.w_ref.w0.w1.w2 = bf16[12288,512]{1,0:T(8,128)(2,1)} async-done(((bf16[384,512]{1,0:T(8,128)(2,1)}), bf16[12288,512]{1,0:T(8,128)(2,1)}) %all-gather.3.cloned.1.call-update) | async-done | bytes 12582928 | tf_op jit(solution)/shard_map/all_gather | solution.py:579
  111.8 5.7 a1.1
  134.6 8.2 %a2.1 = (f32[384,512]{1,0:T(8,128)}, bf16[9,384,512]{2,1,0:T(8,128)(2,1)}, f32[4,512]{1,0:T(4,128)}) custom-call(f32[2]{0:T(128)} %fusion.11.inv_ref, f32[4,512]{1,0:T(4,128)} %add.418.total_ref.low_total, f32[2,512]{1,0:T(2,128)} %get-tuple-element.184.tab_ref.low_tab, f32[384,1]{1,0:T(8,128)} %reshape.313.mask_ref, f32[4,384,1]{2,1,0:T(8,128)} %constant.103.clone.edge_ref, ...), custom_call_target="tpu_custom_call" | custom-call | tf_op jit(solution)/shard_map/a2/pallas_call | solution.py:479
  156.4 34.6 %all-gather.5.cloned.1.call-done.w_ref.w0.w1 = bf16[2048,2048]{1,0:T(8,128)(2,1)} async-done(((bf16[64,2048]{1,0:T(8,128)(2,1)}), bf16[2048,2048]{1,0:T(8,128)(2,1)}) %all-gather.5.cloned.1.call-update) | async-done | bytes 8388624 | tf_op jit(solution)/shard_map/all_gather | solution.py:580
  191.0 5.8 as.1
  223.2 7.1 %a4.1 = (bf16[384,2048]{1,0:T(8,128)(2,1)}, f32[384,512]{1,0:T(8,128)}, f32[4,512]{1,0:T(4,128)}) custom-call(f32[2]{0:T(128)} %fusion.11.inv_ref, f32[4,2048]{1,0:T(4,128)} %get-tuple-element.189.t3_ref, f32[4,2048]{1,0:T(4,128)} %get-tuple-element.188.ts_ref, f32[2,2048]{1,0:T(2,128)} %slice.319.tab3_ref, f32[2,2048]{1,0:T(2,128)} %slice.321.tabs_ref, ...), custom_call_target="tpu_custom_call" | custom-call | tf_op jit(solution)/shard_map/a4/pallas_call | solution.py:479
  247.4 8.1 %a5.1 = (f32[384,512]{1,0:T(8,128)}, bf16[9,384,512]{2,1,0:T(8,128)(2,1)}, f32[4,512]{1,0:T(4,128)}) custom-call(f32[2]{0:T(128)} %fusion.11.inv_ref, f32[4,512]{1,0:T(4,128)} %add.430.total_ref.low_total, f32[2,512]{1,0:T(2,128)} %get-tuple-element.182.tab_ref.low_tab, f32[384,1]{1,0:T(8,128)} %reshape.313.mask_ref, f32[4,384,1]{2,1,0:T(8,128)} %constant.103.clone.edge_ref, ...), custom_call_target="tpu_custom_call" | custom-call | tf_op jit(solution)/shard_map/a5/pallas_call | solution.py:479
  272.5 5.4 a6.1
  296.4 7.5 %head.1 = (bf16[2,384,1024]{2,1,0:T(8,128)(2,1)}, f32[384,2048]{1,0:T(8,128)}, f32[4,2048]{1,0:T(4,128)}) custom-call(s32[9]{0:T(128)} %pad_add_fusion.slot_ref, f32[2]{0:T(128)} %fusion.11.inv_ref, f32[4,2048]{1,0:T(4,128)} %add.438.total_ref, f32[2,2048]{1,0:T(2,128)} %slice.325.tab_ref, f32[384,1]{1,0:T(8,128)} %reshape.313.mask_ref, ...), custom_call_target="tpu_custom_call" | custom-call | tf_op jit(solution)/shard_map/head/pallas_call | solution.py:479
  322.4 7.4 %g5.1 = (bf16[384,2048]{1,0:T(8,128)(2,1)}, f32[384,512]{1,0:T(8,128)}, f32[4,512]{1,0:T(4,128)}) custom-call(f32[2]{0:T(128)} %fusion.11.inv_ref, f32[384,2048]{1,0:T(8,128)} %get-tuple-element.106.gz_ref.up_ref, f32[384,2048]{1,0:T(8,128)} %get-tuple-element.103.a_ref, f32[4,2048]{1,0:T(4,128)} %add.438.total_ref, f32[4,2048]{1,0:T(4,128)} %add.442.s_ref, ...), custom_call_target="tpu_custom_call" | custom-call | tf_op jit(solution)/shard_map/g5/pallas_call | solution.py:479
  346.9 7.3 %g4.1 = (bf16[384,512]{1,0:T(8,128)(2,1)}, f32[384,512]{1,0:T(8,128)}, f32[4,512]{1,0:T(4,128)}) custom-call(f32[2]{0:T(128)} %fusion.11.inv_ref, f32[384,512]{1,0:T(8,128)} %get-tuple-element.108.gz_ref, f32[384,512]{1,0:T(8,128)} %get-tuple-element.101.a_ref.low_ref, f32[4,512]{1,0:T(4,128)} %add.434.total_ref.low_total, f32[4,512]{1,0:T(4,128)} %add.446.s_ref, ...), custom_call_target="tpu_custom_call" | custom-call | tf_op jit(solution)/shard_map/g4/pallas_call | solution.py:479
  368.0 10.0 %dw5.1 = (bf16[6144,256]{1,0:T(8,128)(2,1)}, bf16[6144,256]{1,0:T(8,128)(2,1)}) custom-call(s32[9]{0:T(128)} %pad_add_fusion.slot_ref, bf16[9,384,512]{2,1,0:T(8,128)(2,1)} %get-tuple-element.134.feature_ref, bf16[384,512]{1,0:T(8,128)(2,1)} %get-tuple-element.135.grad_ref), custom_call_target="tpu_custom_call" | custom-call | tf_op jit(solution)/shard_map/dw5/pallas_call | solution.py:612
  378.6 9.2 %gy.1 = (bf16[384,512]{1,0:T(8,128)(2,1)}, f32[384,2048]{1,0:T(8,128)}, f32[6,2048]{1,0:T(8,128)}) custom-call(f32[2]{0:T(128)} %fusion.11.inv_ref, f32[384,512]{1,0:T(8,128)} %get-tuple-element.110.gz_ref, f32[384,512]{1,0:T(8,128)} %get-tuple-element.99.a_ref.low_ref, f32[4,512]{1,0:T(4,128)} %add.430.total_ref.low_total, f32[4,512]{1,0:T(4,128)} %add.450.s_ref, ...), custom_call_target="tpu_custom_call" | custom-call | tf_op jit(solution)/shard_map/gy/pallas_call | solution.py:479
  412.9 8.9 %g2.1 = (bf16[384,2048]{1,0:T(8,128)(2,1)}, bf16[384,2048]{1,0:T(8,128)(2,1)}, f32[384,512]{1,0:T(8,128)}, f32[4,512]{1,0:T(4,128)}) custom-call(f32[2]{0:T(128)} %fusion.11.inv_ref, f32[384,2048]{1,0:T(8,128)} %get-tuple-element.112.gj_ref, f32[384,2048]{1,0:T(8,128)} %get-tuple-element.96.a3_ref, f32[384,2048]{1,0:T(8,128)} %get-tuple-element.97.as_ref, ...), custom_call_target="tpu_custom_call" | custom-call | tf_op jit(solution)/shard_map/g2/pallas_call | solution.py:479
  426.7 7.2 %dws.1 = (bf16[2048,1024]{1,0:T(8,128)(2,1)}, bf16[2048,1024]{1,0:T(8,128)(2,1)}) custom-call(s32[9]{0:T(128)} %pad_add_fusion.slot_ref, bf16[4,384,1024]{2,1,0:T(8,128)(2,1)} %prep.1.x_ref.feature_ref, bf16[384,2048]{1,0:T(8,128)(2,1)} %get-tuple-element.118.g_ref.grad_ref, ...), custom_call_target="tpu_custom_call", output_to_operand_aliasing={{0}: (3, {}), {1}: (4, {})} | custom-call | tf_op jit(solution)/shard_map/dws/pallas_call | solution.py:612
  450.0 9.2 %g1.1 = (bf16[384,512]{1,0:T(8,128)(2,1)}, f32[4,384,512]{2,1,0:T(8,128)}, f32[4,512]{1,0:T(4,128)}) custom-call(f32[2]{0:T(128)} %fusion.11.inv_ref, f32[384,512]{1,0:T(8,128)} %get-tuple-element.114.gz_ref, f32[384,512]{1,0:T(8,128)} %get-tuple-element.93.a_ref.low_ref, f32[4,512]{1,0:T(4,128)} %add.422.total_ref.low_total, f32[4,512]{1,0:T(4,128)} %add.458.s_ref, ...), custom_call_target="tpu_custom_call" | custom-call | tf_op jit(solution)/shard_map/g1/pallas_call | solution.py:479
  481.4 10.0 %dw2.1 = (bf16[6144,256]{1,0:T(8,128)(2,1)}, bf16[6144,256]{1,0:T(8,128)(2,1)}) custom-call(s32[9]{0:T(128)} %pad_add_fusion.slot_ref, bf16[9,384,512]{2,1,0:T(8,128)(2,1)} %get-tuple-element.121.feature_ref, bf16[384,512]{1,0:T(8,128)(2,1)} %get-tuple-element.122.grad_ref, ...), custom_call_target="tpu_custom_call", output_to_operand_aliasing={{0}: (3, {}), {1}: (4, {})} | custom-call | tf_op jit(solution)/shard_map/dw2/pallas_call | solution.py:612
  492.0 11.3 %gx.1 = (bf16[4,384,512]{2,1,0:T(8,128)(2,1)}, bf16[2,4,384,512]{3,2,1,0:T(8,128)(2,1)}) custom-call(s32[9]{0:T(128)} %pad_add_fusion.slot_ref, f32[2]{0:T(128)} %fusion.11.inv_ref, f32[4,384,512]{2,1,0:T(8,128)} %get-tuple-element.116.gz_ref, f32[4,384,512]{2,1,0:T(8,128)} %get-tuple-element.91.a_ref.low_ref, f32[4,512]{1,0:T(4,128)} %add.418.total_ref.low_total, ...), custom_call_target="tpu_custom_call" | custom-call | tf_op jit(solution)/shard_map/gx/pallas_call | solution.py:479
  503.3 5.5 dw1.1
  521.3 6.8 split_a.1
  533.0 7.7 %split_w.1 = (bf16[8,64,1024]{2,1,0:T(8,128)(2,1)}, bf16[8,64,1024]{2,1,0:T(8,128)(2,1)}, bf16[8,64,1024]{2,1,0:T(8,128)(2,1)}, bf16[8,64,1024]{2,1,0:T(8,128)(2,1)}) custom-call(s32[1]{0:T(128)} %bitcast.18.me_ref, bf16[2048,1024]{1,0:T(8,128)(2,1)} %get-tuple-element.148.refs_0_.refs_1_.refs_2_.refs_3_, ...), custom_call_target="tpu_custom_call" | custom-call | tf_op jit(solution)/shard_map/split_w/pallas_call | solution.py:479
  542.3 9.3 %collective-permute-done.56 = bf16[8,192,256]{2,1,0:T(8,128)(2,1)S(1)} collective-permute-done((bf16[8,192,256]{2,1,0:T(8,128)(2,1)}, bf16[8,192,256]{2,1,0:T(8,128)(2,1)S(1)}, u32[]{:S(2)}, u32[]{:S(2)}) %collective-permute-start.56) | collective-permute-done | bytes 786464 | tf_op jit(solution)/shard_map/ppermute | solution.py:549
  557.7 7.7 %collective-permute-done.57 = bf16[4,192,256]{2,1,0:T(8,128)(2,1)} collective-permute-done((bf16[4,192,256]{2,1,0:T(8,128)(2,1)S(1)}, bf16[4,192,256]{2,1,0:T(8,128)(2,1)}, u32[]{:S(2)}, u32[]{:S(2)}) %collective-permute-start.57) | collective-permute-done | bytes 393248 | tf_op jit(solution)/shard_map/ppermute | solution.py:549
  566.6 20.0 %collective-permute-done.61 = bf16[4,192,256]{2,1,0:T(8,128)(2,1)} collective-permute-done((bf16[4,192,256]{2,1,0:T(8,128)(2,1)}, bf16[4,192,256]{2,1,0:T(8,128)(2,1)}, u32[]{:S(2)}, u32[]{:S(2)}) %collective-permute-start.61) | collective-permute-done | bytes 393248 | tf_op jit(solution)/shard_map/ppermute | solution.py:549
  596.9 7.9 %collective-permute-done.68 = bf16[4,64,1024]{2,1,0:T(8,128)(2,1)S(1)} collective-permute-done((bf16[4,64,1024]{2,1,0:T(8,128)(2,1)S(1)}, bf16[4,64,1024]{2,1,0:T(8,128)(2,1)S(1)}, u32[]{:S(2)}, u32[]{:S(2)}) %collective-permute-start.68) | collective-permute-done | bytes 524320 | tf_op jit(solution)/shard_map/ppermute | solution.py:549
  612.5 10.9 %collective-permute-done.69 = bf16[2,64,1024]{2,1,0:T(8,128)(2,1)S(1)} collective-permute-done((bf16[2,64,1024]{2,1,0:T(8,128)(2,1)S(1)}, bf16[2,64,1024]{2,1,0:T(8,128)(2,1)S(1)}, u32[]{:S(2)}, u32[]{:S(2)}) %collective-permute-start.69) | collective-permute-done | bytes 262176 | tf_op jit(solution)/shard_map/ppermute | solution.py:549
  624.1 7.0 %collective-permute-done.73 = bf16[2,64,1024]{2,1,0:T(8,128)(2,1)S(1)} collective-permute-done((bf16[2,64,1024]{2,1,0:T(8,128)(2,1)S(1)}, bf16[2,64,1024]{2,1,0:T(8,128)(2,1)S(1)}, u32[]{:S(2)}, u32[]{:S(2)}) %collective-permute-start.73) | collective-permute-done | bytes 262176 | tf_op jit(solution)/shard_map/ppermute | solution.py:549
  634.9 5.4 collective-permute-done.70
  644.6 7.5 %reduce-scatter.2.cloned.1.call-done = bf16[384,256]{1,0:T(8,128)(2,1)} async-done(((bf16[6144,256]{1,0:T(8,128)(2,1)}), bf16[384,256]{1,0:T(8,128)(2,1)}) %reduce-scatter.2.cloned.1.call-update) | async-done | bytes 196624 | tf_op jit(solution)/shard_map/reduce_scatter | solution.py:827
  669.5 6.3 place_out.1
  676.9 7.0 %place_grad.1 = bf16[8,384,512]{2,1,0:T(8,128)(2,1)} custom-call(s32[9]{0:T(128)} %pad_add_fusion.slot_ref, bf16[2,4,384,512]{3,2,1,0:T(8,128)(2,1)} %get-tuple-element.119.own_ref, bf16[4,384,512]{2,1,0:T(8,128)(2,1)} %copy-done.7), custom_call_target="tpu_custom_call" | custom-call | tf_op jit(solution)/shard_map/place_grad/pallas_call | solution.py:479
  (408 shorter events, 337.7 us)
Async XLA Ops:
  7.2 104.6 %all-gather.3.cloned.1.call-start = ((), (), s32[]{:S(2)}) async-start(), calls=%async_computation.1 | async-start | bytes 12976128 | tf_op jit(solution)/shard_map/all_gather | solution.py:579
  9.6 181.4 %all-gather.5.cloned.1.call-start = ((), (), s32[]{:S(2)}) async-start(), calls=%async_computation.2 | async-start | bytes 8650752 | tf_op jit(solution)/shard_map/all_gather | solution.py:580
  11.8 640.3 %reduce-scatter.2.cloned.1.call-start = ((), (), s32[]{:S(2)}) async-start(), calls=%async_computation.3 | async-start | bytes 3342336 | tf_op jit(solution)/shard_map/reduce_scatter | solution.py:827
  20.3 6.7 collective-permute-start.1
  38.0 80.9 %collective-permute-start.4 = (f32[40,512]{1,0:T(8,128)S(1)}, f32[40,512]{1,0:T(8,128)S(1)}, u32[]{:S(2)}, u32[]{:S(2)}) collective-permute-start(f32[40,512]{1,0:T(8,128)S(1)} %add.411), channel_id=1, source_target_pairs={{0,8},{1,9},{2,10},{3,11},{4,12},{5,13},{6,14},{7,15},{8,0},{9,1},... | collective-permute-start | bytes 245768 | tf_op jit(solution)/shard_map/ppermute | solution.py:37
  155.0 41.7 %collective-permute-start.12 = (f32[4,512]{1,0:T(4,128)S(1)}, f32[4,512]{1,0:T(4,128)S(1)}, u32[]{:S(2)}, u32[]{:S(2)}) collective-permute-start(f32[4,512]{1,0:T(4,128)S(1)} %add.421), channel_id=1, source_target_pairs={{0,8},{1,9},{2,10},{3,11},{4,12},{5,13},{6,14},{7,15},{8,0},{9,1},... | collective-permute-start | bytes 24584 | tf_op jit(solution)/shard_map/ppermute | solution.py:37
  366.1 11.9 %collective-permute-start.41 = (f32[4,512]{1,0:T(4,128)S(1)}, f32[4,512]{1,0:T(4,128)S(1)}, u32[]{:S(2)}, u32[]{:S(2)}) collective-permute-start(f32[4,512]{1,0:T(4,128)S(1)} %add.449), channel_id=1, source_target_pairs={{0,8},{1,9},{2,10},{3,11},{4,12},{5,13},{6,14},{7,15},{8,0},{9,1},... | collective-permute-start | bytes 24584 | tf_op jit(solution)/shard_map/ppermute | solution.py:37
  393.0 115.8 %collective-permute-start.64 = (bf16[6144,256]{1,0:T(8,128)(2,1)}, bf16[6144,256]{1,0:T(8,128)(2,1)}, u32[]{:S(2)}, u32[]{:S(2)}) collective-permute-start(bf16[6144,256]{1,0:T(8,128)(2,1)} %get-tuple-element.139), channel_id=1, source_target_pairs={{0,16},{16,0},{1,17},{17,1},{2,18},{18,2},{3,19},{19,3},{4,20},{20... | collective-permute-start | bytes 9437192 | tf_op jit(solution)/shard_map/ppermute | solution.py:43
  433.8 99.2 %collective-permute-start.66 = (bf16[2048,1024]{1,0:T(8,128)(2,1)}, bf16[2048,1024]{1,0:T(8,128)(2,1)}, u32[]{:S(2)}, u32[]{:S(2)}) collective-permute-start(bf16[2048,1024]{1,0:T(8,128)(2,1)} %get-tuple-element.149), channel_id=1, source_target_pairs={{0,16},{16,0},{1,17},{17,1},{2,18},{18,2},{3,19},{19,3},{4,20},{20... | collective-permute-start | bytes 12582920 | tf_op jit(solution)/shard_map/ppermute | solution.py:43
  471.2 20.2 %collective-permute-start.53 = (f32[4,512]{1,0:T(4,128)S(1)}, f32[4,512]{1,0:T(4,128)S(1)}, u32[]{:S(2)}, u32[]{:S(2)}) collective-permute-start(f32[4,512]{1,0:T(4,128)S(1)} %add.461), channel_id=1, source_target_pairs={{0,8},{1,9},{2,10},{3,11},{4,12},{5,13},{6,14},{7,15},{8,0},{9,1},... | collective-permute-start | bytes 24584 | tf_op jit(solution)/shard_map/ppermute | solution.py:37
  508.8 10.8 %collective-permute-start.55 = (bf16[6144,256]{1,0:T(8,128)(2,1)}, bf16[6144,256]{1,0:T(8,128)(2,1)S(1)}, u32[]{:S(2)}, u32[]{:S(2)}) collective-permute-start(bf16[6144,256]{1,0:T(8,128)(2,1)} %get-tuple-element.129), channel_id=1, source_target_pairs={{0,16},{16,0},{1,17},{17,1},{2,18},{18,2},{3,19},{19,3},{4,20},{20... | collective-permute-start | bytes 9437192 | tf_op jit(solution)/shard_map/ppermute | solution.py:43
  517.9 151.5 %collective-permute-start.29 = (bf16[4,96,1024]{2,1,0:T(8,128)(2,1)}, bf16[4,96,1024]{2,1,0:T(8,128)(2,1)}, u32[]{:S(2)}, u32[]{:S(2)}) collective-permute-start(bf16[4,96,1024]{2,1,0:T(8,128)(2,1)} %bitcast.13), channel_id=1, source_target_pairs={{0,16},{16,0},{1,17},{17,1},{2,18},{18,2},{3,19},{19,3},{4,20},{20... | collective-permute-start | bytes 2359304 | tf_op jit(solution)/shard_map/ppermute | solution.py:43
  528.1 23.5 %collective-permute-start.56 = (bf16[8,192,256]{2,1,0:T(8,128)(2,1)}, bf16[8,192,256]{2,1,0:T(8,128)(2,1)S(1)}, u32[]{:S(2)}, u32[]{:S(2)}) collective-permute-start(bf16[8,192,256]{2,1,0:T(8,128)(2,1)} %get-tuple-element.131), channel_id=1, source_target_pairs={{0,1},{1,0},{2,3},{3,2},{4,5},{5,4},{6,7},{7,6},{8,9},{9,8},{10,11... | collective-permute-start | bytes 2359304 | tf_op jit(solution)/shard_map/ppermute | solution.py:549
  530.3 23.6 %collective-permute-start.60 = (bf16[8,192,256]{2,1,0:T(8,128)(2,1)}, bf16[8,192,256]{2,1,0:T(8,128)(2,1)S(1)}, u32[]{:S(2)}, u32[]{:S(2)}) collective-permute-start(bf16[8,192,256]{2,1,0:T(8,128)(2,1)} %get-tuple-element.133), channel_id=1, source_target_pairs={{0,2},{1,3},{2,0},{3,1},{4,6},{5,7},{6,4},{7,5},{8,10},{9,11},{10,... | collective-permute-start | bytes 2359304 | tf_op jit(solution)/shard_map/ppermute | solution.py:549
  540.7 47.6 %collective-permute-start.67 = (bf16[8,64,1024]{2,1,0:T(8,128)(2,1)}, bf16[8,64,1024]{2,1,0:T(8,128)(2,1)}, u32[]{:S(2)}, u32[]{:S(2)}) collective-permute-start(bf16[8,64,1024]{2,1,0:T(8,128)(2,1)} %get-tuple-element.151), channel_id=1, source_target_pairs={{0,1},{1,0},{2,3},{3,2},{4,5},{5,4},{6,7},{7,6},{8,9},{9,8},{10,11... | collective-permute-start | bytes 3145736 | tf_op jit(solution)/shard_map/ppermute | solution.py:549
  551.8 13.6 %collective-permute-start.57 = (bf16[4,192,256]{2,1,0:T(8,128)(2,1)S(1)}, bf16[4,192,256]{2,1,0:T(8,128)(2,1)}, u32[]{:S(2)}, u32[]{:S(2)}) collective-permute-start(bf16[4,192,256]{2,1,0:T(8,128)(2,1)S(1)} %slice.403), channel_id=1, source_target_pairs={{0,2},{1,3},{2,0},{3,1},{4,6},{5,7},{6,4},{7,5},{8,10},{9,11},{10,... | collective-permute-start | bytes 1179656 | tf_op jit(solution)/shard_map/ppermute | solution.py:549
  553.4 38.1 %collective-permute-start.71 = (bf16[8,64,1024]{2,1,0:T(8,128)(2,1)}, bf16[8,64,1024]{2,1,0:T(8,128)(2,1)}, u32[]{:S(2)}, u32[]{:S(2)}) collective-permute-start(bf16[8,64,1024]{2,1,0:T(8,128)(2,1)} %get-tuple-element.153), channel_id=1, source_target_pairs={{0,2},{1,3},{2,0},{3,1},{4,6},{5,7},{6,4},{7,5},{8,10},{9,11},{10,... | collective-permute-start | bytes 3145736 | tf_op jit(solution)/shard_map/ppermute | solution.py:549
  554.9 31.7 %collective-permute-start.61 = (bf16[4,192,256]{2,1,0:T(8,128)(2,1)}, bf16[4,192,256]{2,1,0:T(8,128)(2,1)}, u32[]{:S(2)}, u32[]{:S(2)}) collective-permute-start(bf16[4,192,256]{2,1,0:T(8,128)(2,1)} %slice.409), channel_id=1, source_target_pairs={{0,1},{1,0},{2,3},{3,2},{4,5},{5,4},{6,7},{7,6},{8,9},{9,8},{10,11... | collective-permute-start | bytes 1179656 | tf_op jit(solution)/shard_map/ppermute | solution.py:549
  565.4 87.8 %collective-permute-start.77 = (f32[6,2048]{1,0:T(8,128)}, f32[6,2048]{1,0:T(8,128)S(1)}, u32[]{:S(2)}, u32[]{:S(2)}) collective-permute-start(f32[6,2048]{1,0:T(8,128)} %stack.11), channel_id=1, source_target_pairs={{0,16},{16,0},{1,17},{17,1},{2,18},{18,2},{3,19},{19,3},{4,20},{20... | collective-permute-start | bytes 147464 | tf_op jit(solution)/shard_map/ppermute | solution.py:43
  586.6 8.2 %collective-permute-start.58 = (bf16[2,192,256]{2,1,0:T(8,128)(2,1)S(1)}, bf16[2,192,256]{2,1,0:T(8,128)(2,1)S(1)}, u32[]{:S(2)}, u32[]{:S(2)}) collective-permute-start(bf16[2,192,256]{2,1,0:T(8,128)(2,1)S(1)} %slice.405), channel_id=1, source_target_pairs={{0,4},{1,5},{2,6},{3,7},{4,0},{5,1},{6,2},{7,3},{8,12},{9,13},{10,... | collective-permute-start | bytes 589832 | tf_op jit(solution)/shard_map/ppermute | solution.py:549
  588.3 8.5 %collective-permute-start.62 = (bf16[2,192,256]{2,1,0:T(8,128)(2,1)S(1)}, bf16[2,192,256]{2,1,0:T(8,128)(2,1)S(1)}, u32[]{:S(2)}, u32[]{:S(2)}) collective-permute-start(bf16[2,192,256]{2,1,0:T(8,128)(2,1)S(1)} %slice.411), channel_id=1, source_target_pairs={{0,4},{1,5},{2,6},{3,7},{4,0},{5,1},{6,2},{7,3},{8,12},{9,13},{10,... | collective-permute-start | bytes 589832 | tf_op jit(solution)/shard_map/ppermute | solution.py:549
  591.5 13.2 %collective-permute-start.68 = (bf16[4,64,1024]{2,1,0:T(8,128)(2,1)S(1)}, bf16[4,64,1024]{2,1,0:T(8,128)(2,1)S(1)}, u32[]{:S(2)}, u32[]{:S(2)}) collective-permute-start(bf16[4,64,1024]{2,1,0:T(8,128)(2,1)S(1)} %slice.415), channel_id=1, source_target_pairs={{0,2},{1,3},{2,0},{3,1},{4,6},{5,7},{6,4},{7,5},{8,10},{9,11},{10,... | collective-permute-start | bytes 1572872 | tf_op jit(solution)/shard_map/ppermute | solution.py:549
  594.7 13.0 %collective-permute-start.72 = (bf16[4,64,1024]{2,1,0:T(8,128)(2,1)S(1)}, bf16[4,64,1024]{2,1,0:T(8,128)(2,1)S(1)}, u32[]{:S(2)}, u32[]{:S(2)}) collective-permute-start(bf16[4,64,1024]{2,1,0:T(8,128)(2,1)S(1)} %slice.421), channel_id=1, source_target_pairs={{0,1},{1,0},{2,3},{3,2},{4,5},{5,4},{6,7},{7,6},{8,9},{9,8},{10,11... | collective-permute-start | bytes 1572872 | tf_op jit(solution)/shard_map/ppermute | solution.py:549
  596.8 57.5 %collective-permute-start.76 = (f32[8,512]{1,0:T(8,128)S(1)}, f32[8,512]{1,0:T(8,128)S(1)}, u32[]{:S(2)}, u32[]{:S(2)}) collective-permute-start(f32[8,512]{1,0:T(8,128)S(1)} %stack.10), channel_id=1, source_target_pairs={{0,16},{16,0},{1,17},{17,1},{2,18},{18,2},{3,19},{19,3},{4,20},{20... | collective-permute-start | bytes 49160 | tf_op jit(solution)/shard_map/ppermute | solution.py:43
  607.7 15.7 %collective-permute-start.69 = (bf16[2,64,1024]{2,1,0:T(8,128)(2,1)S(1)}, bf16[2,64,1024]{2,1,0:T(8,128)(2,1)S(1)}, u32[]{:S(2)}, u32[]{:S(2)}) collective-permute-start(bf16[2,64,1024]{2,1,0:T(8,128)(2,1)S(1)} %slice.417), channel_id=1, source_target_pairs={{0,4},{1,5},{2,6},{3,7},{4,0},{5,1},{6,2},{7,3},{8,12},{9,13},{10,... | collective-permute-start | bytes 786440 | tf_op jit(solution)/shard_map/ppermute | solution.py:549
  611.3 19.8 %collective-permute-start.73 = (bf16[2,64,1024]{2,1,0:T(8,128)(2,1)S(1)}, bf16[2,64,1024]{2,1,0:T(8,128)(2,1)S(1)}, u32[]{:S(2)}, u32[]{:S(2)}) collective-permute-start(bf16[2,64,1024]{2,1,0:T(8,128)(2,1)S(1)} %slice.423), channel_id=1, source_target_pairs={{0,4},{1,5},{2,6},{3,7},{4,0},{5,1},{6,2},{7,3},{8,12},{9,13},{10,... | collective-permute-start | bytes 786440 | tf_op jit(solution)/shard_map/ppermute | solution.py:549
  623.4 7.9 %collective-permute-start.63 = (bf16[1,192,256]{2,1,0:T(8,128)(2,1)S(1)}, bf16[1,192,256]{2,1,0:T(8,128)(2,1)S(1)}, u32[]{:S(2)}, u32[]{:S(2)}) collective-permute-start(bf16[1,192,256]{2,1,0:T(8,128)(2,1)S(1)} %slice.413), channel_id=1, source_target_pairs={{0,8},{1,9},{2,10},{3,11},{4,12},{5,13},{6,14},{7,15},{8,0},{9,1},... | collective-permute-start | bytes 294920 | tf_op jit(solution)/shard_map/ppermute | solution.py:549
  631.1 9.2 %collective-permute-start.70 = (bf16[1,64,1024]{2,1,0:T(8,128)(2,1)S(1)}, bf16[1,64,1024]{2,1,0:T(8,128)(2,1)S(1)}, u32[]{:S(2)}, u32[]{:S(2)}) collective-permute-start(bf16[1,64,1024]{2,1,0:T(8,128)(2,1)S(1)} %slice.419), channel_id=1, source_target_pairs={{0,8},{1,9},{2,10},{3,11},{4,12},{5,13},{6,14},{7,15},{8,0},{9,1},... | collective-permute-start | bytes 393224 | tf_op jit(solution)/shard_map/ppermute | solution.py:549
  631.3 12.6 %collective-permute-start.74 = (bf16[1,64,1024]{2,1,0:T(8,128)(2,1)S(1)}, bf16[1,64,1024]{2,1,0:T(8,128)(2,1)S(1)}, u32[]{:S(2)}, u32[]{:S(2)}) collective-permute-start(bf16[1,64,1024]{2,1,0:T(8,128)(2,1)S(1)} %slice.425), channel_id=1, source_target_pairs={{0,8},{1,9},{2,10},{3,11},{4,12},{5,13},{6,14},{7,15},{8,0},{9,1},... | collective-permute-start | bytes 393224 | tf_op jit(solution)/shard_map/ppermute | solution.py:549
  640.3 35.5 %collective-permute-start.54 = (bf16[4,384,512]{2,1,0:T(8,128)(2,1)S(1)}, bf16[4,384,512]{2,1,0:T(8,128)(2,1)S(1)}, u32[]{:S(2)}, u32[]{:S(2)}) collective-permute-start(bf16[4,384,512]{2,1,0:T(8,128)(2,1)S(1)} %slice_bitcast_fusion), channel_id=1, source_target_pairs={{0,16},{16,0},{1,17},{17,1},{2,18},{18,2},{3,19},{19,3},{4,20},{20... | collective-permute-start | bytes 4718600 | tf_op jit(solution)/shard_map/ppermute | solution.py:43
  644.6 9.8 %collective-permute-start.75 = (f32[64,1024]{1,0:T(8,128)}, f32[64,1024]{1,0:T(8,128)}, u32[]{:S(2)}, u32[]{:S(2)}) collective-permute-start(f32[64,1024]{1,0:T(8,128)} %get-tuple-element.172), channel_id=1, source_target_pairs={{0,16},{16,0},{1,17},{17,1},{2,18},{18,2},{3,19},{19,3},{4,20},{20... | collective-permute-start | bytes 786440 | tf_op jit(solution)/shard_map/ppermute | solution.py:43
  668.7 15.3 %collective-permute-start.82 = (f32[2,21]{1,0:T(2,128)S(1)}, f32[2,21]{1,0:T(2,128)S(1)}, u32[]{:S(2)}, u32[]{:S(2)}) collective-permute-start(f32[2,21]{1,0:T(2,128)S(1)} %add.505), channel_id=1, source_target_pairs={{0,8},{1,9},{2,10},{3,11},{4,12},{5,13},{6,14},{7,15},{8,0},{9,1},... | collective-permute-start | bytes 512 | tf_op jit(solution)/shard_map/ppermute | solution.py:37
  (92 other events, 807.5 us)
Sparse Core Ops, SparseCore 0:
  11.5 100.2 all-gather.2
  115.3 75.6 all-gather.4
  514.3 137.7 reduce-scatter.1

commit v2 on v1

v2 whole, which is shorter than its diff:
```python
import jax
import jax.numpy as jnp
import numpy as np
from jax import lax
from jax.experimental import pallas as pl
from jax.experimental.pallas import tpu as pltpu
from jax.sharding import PartitionSpec as P

C_IN = 1024
C_MID = 512
C_OUT = 2048
R_N = 12288
R_W = 2048
HB = 8
WB = 12
IMG_DEV = 8
SLOTS = 4
PIX = HB * WB
ROWS = SLOTS * PIX
HALF = ROWS // 2
PAD = 16
TILE = 512

EPS = 1e-05
MOMENTUM = 0.9
DECAY = 5e-05
TRUST = 0.001
RATE = 29.0
PRECISE = lax.Precision.HIGHEST
BFLOAT = jnp.bfloat16
SINGLE = jnp.float32
MIB = 1024 * 1024
BYTES_PER_US = 1200000
MICROSECONDS = {
    "prep": 5, "a1": 3, "a2": 5, "as": 4.5, "a3": 4, "a4": 4.7, "a5": 4, "a6": 3.7, "head": 5.3, "g5": 5.2, "g4": 5.4, "gy": 7,
    "g2": 7.3, "g1": 8, "g0": 3, "gx": 6.4, "dxs": 5, "dw1": 3.4, "dw2": 2.1, "dw3": 2.9, "dws": 2.9, "dw4a": 1.7, "dw4b": 1.9,
    "dw5": 1.5, "dw6": 2.8, "place_out": 3.4, "place_grad": 5, "wa": 3, "wb": 3, "turn": 1.7, "keep": 1.7,
}


def pairs(bit):
    return [(i, i ^ bit) for i in range(lax.axis_size("dp"))]


def exchange(value, bit):
    return lax.ppermute(value, "dp", pairs(bit))


def pin(value, after):
    return lax.optimization_barrier((value, after))[0]


def dp_sum(value, fillers=()):
    size = lax.axis_size("dp")
    results = []
    step = 1
    while step < size:
        got = exchange(value, step)
        if len(results) < len(fillers):
            result = fillers[len(results)](value)
            got, result = lax.optimization_barrier((got, result))
            results.append(result)
        value = value + got
        step *= 2
    for filler in fillers[len(results) :]:
        results.append(filler(value))
    return value, results


def swap_pipe(value):
    return lax.ppermute(value, "pipe", [(0, 1), (1, 0)])


def dot(left, right):
    return jnp.dot(left, right, preferred_element_type=SINGLE)


def dot_back(left, right):
    return lax.dot_general(left, right, (((1,), (1,)), ((), ())), preferred_element_type=SINGLE)


def silu(value):
    return value * jax.nn.sigmoid(value)


def slope(value):
    gate = jax.nn.sigmoid(value)
    return gate * (1.0 + value * (1.0 - gate))


def put_sums(ref, values, first):
    for k, value in enumerate(values):
        for m in range(2):
            total = jnp.sum(value[m * HALF : (m + 1) * HALF], axis=0, keepdims=True)
            row = 2 * k + m
            ref[row : row + 1, :] = total if first else ref[row : row + 1, :] + total


def both(function):
    return jnp.concatenate([function(0), function(1)], axis=0)


def part(m):
    return slice(m * HALF, (m + 1) * HALF)


def moments(total_ref, inv_ref, m, scale=1.0):
    inv = inv_ref[m] * scale
    mean = total_ref[m : m + 1, :] * inv
    var = total_ref[2 + m : 3 + m, :] * inv - mean * mean
    return mean, lax.rsqrt(var + EPS)


def normed(a, total_ref, inv_ref, m, scale=1.0):
    mean, rstd = moments(total_ref, inv_ref, m, scale)
    return (a - mean) * rstd, rstd


def conv_grad(gz, xhat, rstd, gain, mask, sum_ref, inv_ref, m, scale=1.0, second=2):
    inv = inv_ref[m] * scale
    first_row = sum_ref[m : m + 1, :] * inv
    second_row = sum_ref[second + m : second + m + 1, :] * inv
    return (mask * ((rstd * gain) * (gz - first_row - xhat * second_row))).astype(BFLOAT)


def k_prep(slot_ref, img_ref, perm_ref, mask_ref, out_ref):
    planes = dot(perm_ref[...], img_ref[0])
    mask = mask_ref[...]
    for k in range(4):
        out_ref[k] = (planes[k * PIX : (k + 1) * PIX] * mask).astype(BFLOAT)


def k_first(x_ref, w_ref, a_ref, sum_ref):
    a = dot(x_ref[0], w_ref[...])
    a_ref[0] = a

    @pl.when(pl.program_id(0) == 0)
    def _():
        sum_ref[...] = jnp.zeros_like(sum_ref)

    put_sums(sum_ref, [a, a * a], False)


def shift_mask(di, dj):
    if not di and not dj:
        return None
    pixel = lax.broadcasted_iota(jnp.int32, (SLOTS, PIX, 1), 1)
    inside = None
    if di:
        row = pixel & (HB - 1)
        inside = row >= -di if di < 0 else row < HB - di
    if dj:
        column = pixel >= -dj * HB if dj < 0 else pixel < PIX - dj * HB
        inside = column if inside is None else inside & column
    return jnp.where(inside, 1.0, 0.0).astype(SINGLE).reshape(ROWS, 1)


def rows_at(pad, di, dj):
    start = PAD + HB * dj + di
    rows = pad[start : start + ROWS, :]
    mask = shift_mask(di, dj)
    return rows if mask is None else rows * mask


def clear_pad(pad):
    pad[0:PAD, :] = jnp.zeros((PAD, pad.shape[1]), SINGLE)
    pad[PAD + ROWS : PAD + ROWS + PAD, :] = jnp.zeros((PAD, pad.shape[1]), SINGLE)


def body(pad, m):
    return pad.at[PAD + m * HALF : PAD + (m + 1) * HALF, :]


def carried(ref, fresh):
    return jnp.where(fresh, 0.0, ref[...])


def k_conv_two(inv_ref, total_ref, tab_ref, mask_ref, a_ref, w0, w1, w2, out_ref, h_ref, sum_ref, pad, moved):
    step = pl.program_id(0)
    gain, bias = tab_ref[0:1, :], tab_ref[1:2, :]

    @pl.when(step < 2)
    def _():
        for k in range(2):
            clear_pad(pad.at[k])
            clear_pad(moved.at[k])
            for m in range(2):
                xhat, _unused = normed(a_ref[k, part(m), :], total_ref, inv_ref, m, 0.25)
                h = (silu(xhat * gain + bias) * mask_ref[part(m), :]).astype(BFLOAT)
                h_ref[k, part(m), :] = h
                body(pad.at[k], m)[...] = h.astype(SINGLE)
                body(moved.at[k], m)[...] = h.astype(SINGLE)

    @pl.when(step == 2)
    def _():
        for k in range(2):
            moved[k, PAD : PAD + ROWS, :] = rows_at(pad.at[k], -1, 0)

    term = dot(rows_at(moved.at[0], 0, 0).astype(BFLOAT), w1[...])
    term += dot(rows_at(moved.at[1], 0, -1).astype(BFLOAT), w0[...])
    term += dot(rows_at(moved.at[1], 0, 0).astype(BFLOAT), w2[...])
    out_ref[...] = carried(out_ref, step == 0) + term

    @pl.when(step == 2)
    def _():
        a = out_ref[...]
        masked = a * mask_ref[...]
        put_sums(sum_ref, [masked, masked * a], True)


def k_conv_one(inv_ref, total_ref, tab_ref, mask_ref, a_ref, w0, w1, w2, out_ref, h_ref, sum_ref, pad, moved):
    step = pl.program_id(0)
    gain, bias = tab_ref[0:1, :], tab_ref[1:2, :]

    @pl.when(step == 0)
    def _():
        clear_pad(pad)
        clear_pad(moved)
        for m in range(2):
            xhat, _unused = normed(a_ref[part(m), :], total_ref, inv_ref, m)
            h = (silu(xhat * gain + bias) * mask_ref[part(m), :]).astype(BFLOAT)
            h_ref[part(m), :] = h
            body(pad, m)[...] = h.astype(SINGLE)

    for s in range(3):

        @pl.when(step == s)
        def _(s=s):
            moved[PAD : PAD + ROWS, :] = rows_at(pad, s - 1, 0)

    term = dot(rows_at(moved, 0, -1).astype(BFLOAT), w0[...])
    term += dot(rows_at(moved, 0, 0).astype(BFLOAT), w1[...])
    term += dot(rows_at(moved, 0, 1).astype(BFLOAT), w2[...])
    out_ref[...] = carried(out_ref, step == 0) + term

    @pl.when(step == 2)
    def _():
        a = out_ref[...]
        masked = a * mask_ref[...]
        put_sums(sum_ref, [masked, masked * a], True)


def k_expand(inv_ref, total_ref, tab_ref, mask_ref, a_ref, w_ref, h_ref, out_ref, sum_ref):
    @pl.when(pl.program_id(0) == 0)
    def _():
        gain, bias = tab_ref[0:1, :], tab_ref[1:2, :]
        for m in range(2):
            xhat, _unused = normed(a_ref[part(m), :], total_ref, inv_ref, m)
            h_ref[part(m), :] = (silu(xhat * gain + bias) * mask_ref[part(m), :]).astype(BFLOAT)

    a = dot(h_ref[...], w_ref[...])
    out_ref[...] = a
    put_sums(sum_ref, [a, a * a], True)


def k_short(x_ref, w0, w1, out_ref, sum_ref):
    a = dot(x_ref[0, :, :TILE], w0[...]) + dot(x_ref[0, :, TILE:], w1[...])
    out_ref[...] = a
    put_sums(sum_ref, [a, a * a], True)


def k_meet(inv_ref, t3_ref, ts_ref, tab3_ref, tabs_ref, mask_ref, a3_ref, as_ref, wa_ref, wb_ref, y_ref, out_ref, sum_ref):
    step = pl.program_id(0)
    for m in range(2):
        x3, _unused = normed(a3_ref[part(m), :], t3_ref, inv_ref, m)
        xs, _unused = normed(as_ref[part(m), :], ts_ref, inv_ref, m)
        joined = (x3 * tab3_ref[0:1, :] + tab3_ref[1:2, :]) + (xs * tabs_ref[0:1, :] + tabs_ref[1:2, :])
        y_ref[part(m), :] = (silu(joined) * mask_ref[part(m), :]).astype(BFLOAT)

    @pl.when(step == 0)
    def _():
        out_ref[...] = dot(y_ref[...], wa_ref[...])

    @pl.when(step > 0)
    def _():
        out_ref[...] += dot(y_ref[...], wb_ref[...])

    @pl.when(step == pl.num_programs(0) - 1)
    def _():
        a = out_ref[...]
        put_sums(sum_ref, [a, a * a], True)


def k_head(slot_ref, inv_ref, total_ref, tab_ref, mask_ref, a_ref, y_ref, c0, c1, c2, c3, blk_ref, gz_ref, sum_ref):
    cots = (c0, c1, c2, c3)
    gain, bias = tab_ref[0:1, :], tab_ref[1:2, :]
    for m in range(2):
        mask = mask_ref[part(m), :]
        xhat, _unused = normed(a_ref[part(m), :], total_ref, inv_ref, m)
        z = (xhat * gain + bias) + y_ref[part(m), :].astype(SINGLE)
        gate = jax.nn.sigmoid(z)
        blk_ref[0, part(m), :] = (z * gate * mask).astype(BFLOAT)
        cot = jnp.concatenate([cots[2 * m][0], cots[2 * m + 1][0]], axis=0).astype(SINGLE)
        gz = cot * mask * (gate * (1.0 + z * (1.0 - gate)))
        gz_ref[part(m), :] = gz
        sum_ref[m : m + 1, :] = jnp.sum(gz, axis=0, keepdims=True)
        sum_ref[2 + m : 3 + m, :] = jnp.sum(gz * xhat, axis=0, keepdims=True)


def finish_back(gz_ref, sum_ref, grad, a_ref, total_ref, tab_ref, inv_ref, mask_ref):
    gain, bias = tab_ref[0:1, :], tab_ref[1:2, :]
    for m in range(2):
        xhat, _unused = normed(a_ref[part(m), :], total_ref, inv_ref, m)
        gz = grad[part(m)] * mask_ref[part(m), :] * slope(xhat * gain + bias)
        gz_ref[part(m), :] = gz
        sum_ref[m : m + 1, :] = jnp.sum(gz, axis=0, keepdims=True)
        sum_ref[2 + m : 3 + m, :] = jnp.sum(gz * xhat, axis=0, keepdims=True)


def k_back_six(inv_ref, gz_ref, a_ref, total_ref, s_ref, tab_ref, mask_ref, w_ref, low_ref, low_total, low_tab, ga_ref, out_ref, sum_ref, acc):
    step = pl.program_id(0)
    for m in range(2):
        xhat, rstd = normed(a_ref[part(m), :], total_ref, inv_ref, m)
        ga_ref[part(m), :] = conv_grad(
            gz_ref[part(m), :], xhat, rstd, tab_ref[0:1, :], mask_ref[part(m), :], s_ref, inv_ref, m
        )
    term = dot_back(ga_ref[...], w_ref[...])

    @pl.when(step == 0)
    def _():
        acc[...] = term

    @pl.when(step > 0)
    def _():
        acc[...] += term

    @pl.when(step == pl.num_programs(0) - 1)
    def _():
        finish_back(out_ref, sum_ref, acc[...], low_ref, low_total, low_tab, inv_ref, mask_ref)


def k_back_conv_one(inv_ref, gz_ref, a_ref, total_ref, s_ref, tab_ref, mask_ref, w0, w1, w2, low_ref, low_total, low_tab, col_ref, out_ref, sum_ref, pad, moved, acc):
    step = pl.program_id(0)

    @pl.when(step == 0)
    def _():
        clear_pad(pad)
        clear_pad(moved)
        for m in range(2):
            xhat, rstd = normed(a_ref[part(m), :], total_ref, inv_ref, m)
            ga = conv_grad(gz_ref[part(m), :], xhat, rstd, tab_ref[0:1, :], mask_ref[part(m), :], s_ref, inv_ref, m)
            body(pad, m)[...] = ga.astype(SINGLE)

    for s in range(3):

        @pl.when(step == s)
        def _(s=s):
            moved[PAD : PAD + ROWS, :] = rows_at(pad, 1 - s, 0)

    term = None
    for kx, weight in enumerate((w0, w1, w2)):
        tap = rows_at(moved, 0, 1 - kx).astype(BFLOAT)
        col_ref[kx] = tap
        product = dot_back(tap, weight[...])
        term = product if term is None else term + product
    acc[...] = carried(acc, step == 0) + term

    @pl.when(step == 2)
    def _():
        finish_back(out_ref, sum_ref, acc[...], low_ref, low_total, low_tab, inv_ref, mask_ref)


def k_back_four(inv_ref, gz_ref, a_ref, total_ref, s_ref, tab_ref, mask_ref, wa_ref, wb_ref, up_ref, a3_ref, as_ref, t3_ref, ts_ref, tab3_ref, tabs_ref, ga_ref, gj_ref, sum_ref):
    @pl.when(pl.program_id(0) == 0)
    def _():
        for m in range(2):
            xhat, rstd = normed(a_ref[part(m), :], total_ref, inv_ref, m)
            ga_ref[part(m), :] = conv_grad(
                gz_ref[part(m), :], xhat, rstd, tab_ref[0:1, :], mask_ref[part(m), :], s_ref, inv_ref, m
            )

    weight = jnp.where(pl.program_id(0) == 0, wa_ref[...], wb_ref[...])
    grad = dot_back(ga_ref[...], weight) + up_ref[...]
    for m in range(2):
        x3, _unused = normed(a3_ref[part(m), :], t3_ref, inv_ref, m)
        xs, _unused = normed(as_ref[part(m), :], ts_ref, inv_ref, m)
        joined = (x3 * tab3_ref[0:1, :] + tab3_ref[1:2, :]) + (xs * tabs_ref[0:1, :] + tabs_ref[1:2, :])
        gj = grad[part(m)].astype(BFLOAT).astype(SINGLE) * mask_ref[part(m), :] * slope(joined)
        gj_ref[part(m), :] = gj
        for k, value in enumerate((gj, gj * x3, gj * xs)):
            row = 2 * k + m
            sum_ref[row : row + 1, :] = jnp.sum(value, axis=0, keepdims=True)


def k_back_three(inv_ref, gj_ref, a3_ref, as_ref, t3_ref, ts_ref, s_ref, tab3_ref, tabs_ref, mask_ref, w_ref, low_ref, low_total, low_tab, g3_ref, gs_ref, out_ref, sum_ref, acc):
    step = pl.program_id(0)
    for m in range(2):
        mask = mask_ref[part(m), :]
        gj = gj_ref[part(m), :]
        x3, r3 = normed(a3_ref[part(m), :], t3_ref, inv_ref, m)
        g3_ref[part(m), :] = conv_grad(gj, x3, r3, tab3_ref[0:1, :], mask, s_ref, inv_ref, m)
        xs, rs = normed(as_ref[part(m), :], ts_ref, inv_ref, m)
        gs_ref[part(m), :] = conv_grad(gj, xs, rs, tabs_ref[0:1, :], mask, s_ref, inv_ref, m, second=4)
    term = dot_back(g3_ref[...], w_ref[...])

    @pl.when(step == 0)
    def _():
        acc[...] = term

    @pl.when(step > 0)
    def _():
        acc[...] += term

    @pl.when(step == pl.num_programs(0) - 1)
    def _():
        finish_back(out_ref, sum_ref, acc[...], low_ref, low_total, low_tab, inv_ref, mask_ref)


def k_back_conv_two(inv_ref, gz_ref, a_ref, total_ref, s_ref, tab_ref, mask_ref, w0, w1, w2, low_ref, low_total, low_tab, col_ref, out_ref, sum_ref, pad, moved, acc):
    step = pl.program_id(0)
    gain, bias = low_tab[0:1, :], low_tab[1:2, :]

    @pl.when(step == 0)
    def _():
        clear_pad(pad)
        clear_pad(moved)
        for m in range(2):
            xhat, rstd = normed(a_ref[part(m), :], total_ref, inv_ref, m)
            ga = conv_grad(gz_ref[part(m), :], xhat, rstd, tab_ref[0:1, :], mask_ref[part(m), :], s_ref, inv_ref, m)
            body(pad, m)[...] = ga.astype(SINGLE)
            body(moved, m)[...] = ga.astype(SINGLE)
        sum_ref[...] = jnp.zeros_like(sum_ref)

    @pl.when(step == 2)
    def _():
        moved[PAD : PAD + ROWS, :] = rows_at(pad, 1, 0)

    plain = rows_at(moved, 0, 0).astype(BFLOAT)
    aside = rows_at(moved, 0, 1).astype(BFLOAT)
    col_ref[0], col_ref[1], col_ref[2] = aside, plain, plain
    acc[0] = carried(acc.at[0], step < 2) + dot_back(plain, w1[...])
    acc[1] = carried(acc.at[1], step < 2) + (dot_back(aside, w0[...]) + dot_back(plain, w2[...]))

    @pl.when(step != 1)
    def _():
        for k in range(2):
            for m in range(2):
                xhat, _unused = normed(low_ref[k, part(m), :], low_total, inv_ref, m, 0.25)
                gz = acc[k, part(m), :] * mask_ref[part(m), :] * slope(xhat * gain + bias)
                out_ref[k, part(m), :] = gz
                for q, value in enumerate((gz, gz * xhat)):
                    row = 2 * q + m
                    sum_ref[row : row + 1, :] += jnp.sum(value, axis=0, keepdims=True)


def k_wide_back(g_ref, w_ref, *refs):
    refs[-1][...] = dot_back(g_ref[...], w_ref[...])


def k_first_grad(inv_ref, gz_ref, a_ref, total_ref, s_ref, tab_ref, mask_ref, ga_ref):
    for m in range(2):
        xhat, rstd = normed(a_ref[0, part(m), :], total_ref, inv_ref, m, 0.25)
        ga_ref[0, part(m), :] = conv_grad(
            gz_ref[0, part(m), :], xhat, rstd, tab_ref[0:1, :], mask_ref[part(m), :], s_ref, inv_ref, m, 0.25
        )


def k_image_grad(slot_ref, ga_ref, mask_ref, w_ref, short_ref, perm_ref, *refs):
    out_ref = refs[-1]
    grads = dot_back(ga_ref[...].reshape(4 * PIX, C_MID), w_ref[...])
    mask = mask_ref[...]
    parts = []
    for k in range(4):
        grad = grads[k * PIX : (k + 1) * PIX]
        if k == 0:
            grad = grad + short_ref[...]
        parts.append((grad * mask).astype(BFLOAT))
    planes = jnp.concatenate(parts, axis=0)
    image = lax.dot_general(perm_ref[...], planes, (((0,), (0,)), ((), ())), preferred_element_type=SINGLE).astype(BFLOAT)
    core = slot_ref[SLOTS]
    out_ref[core, 0] = image[:, : C_IN // 2]
    out_ref[1 - core, 0] = image[:, C_IN // 2 :]


def k_place(slot_ref, own_ref, got_ref, *refs):
    out_ref = refs[-1]
    step = pl.program_id(0)

    @pl.when(step < SLOTS)
    def _():
        out_ref[0] = own_ref[0, 0]

    @pl.when(step >= SLOTS)
    def _():
        out_ref[0] = got_ref[0]


def k_turn(in_ref, *refs):
    refs[-1][...] = in_ref[...].reshape(in_ref.shape[-2:]).T


def k_grad(slot_ref, feature_ref, grad_ref, *refs):
    keep_ref, send_ref = refs[-2:]
    core = slot_ref[SLOTS]
    rows, half = feature_ref.shape[-2], grad_ref.shape[-1] // 2
    for k in range(grad_ref.shape[0]):
        feature = feature_ref[k % feature_ref.shape[0]]
        for ref, side in ((keep_ref, core), (send_ref, 1 - core)):
            columns = pl.ds(pl.multiple_of(side * half, half), half)
            ref[k * rows : (k + 1) * rows] = dot(feature, grad_ref[k, :, columns]).astype(BFLOAT)


def k_keep(in_ref, *refs):
    out_ref, sem = refs[-2:]
    copy = pltpu.make_async_copy(in_ref, out_ref, sem)
    copy.start()
    copy.wait()


def k_join(*refs):
    ins, outs, sems = refs[:4], refs[-3:-1], refs[-1]
    copies = []
    for which in range(2):
        for side in range(2):
            source = ins[2 * which + side]
            size = source.shape[0]
            copies.append(pltpu.make_async_copy(source, outs[which].at[pl.ds(side * size, size)], sems.at[len(copies)]))
    for copy in copies:
        copy.start()
    for copy in copies:
        copy.wait()


def k_gather(me_ref, *refs):
    ins, out_ref, sems = refs[:8], refs[8], refs[9]
    rows, cols = ins[0].shape[1:]
    copies = []
    for other in range(2):
        column = pl.multiple_of((1 - me_ref[1] if other else me_ref[1]) * cols, cols)
        for which in range(2):
            for came in range(2):
                source = ins[4 * other + 2 * which + came]
                for q in range(8):
                    third, low, high = q >> 2, (q >> 1) & 1, q & 1
                    pair = 2 * third + came if which == 0 else 2 * came + third
                    block = me_ref[0] ^ (8 * high + 4 * low + pair)
                    row = pl.multiple_of((2 * block + which) * rows, rows)
                    target = out_ref.at[pl.ds(row, rows), pl.ds(column, cols)]
                    copies.append(pltpu.make_async_copy(source.at[q], target, sems.at[len(copies)]))
    for copy in copies:
        copy.start()
    for copy in copies:
        copy.wait()


def k_split(me_ref, *refs):
    own, got, outs = refs[:4], refs[4:8], refs[8:]
    for own_ref, got_ref, out_ref in zip(own, got, outs):
        out_ref[0] = (own_ref[...].astype(SINGLE) + got_ref[...].astype(SINGLE)).astype(BFLOAT)


def full(shape):
    zeros = (0,) * len(shape)
    return pl.BlockSpec(tuple(shape), lambda *_: zeros)


SCALARS = pl.BlockSpec(memory_space=pltpu.SMEM)
ANYWHERE = pl.BlockSpec(memory_space=pl.ANY)


def spec(shape, index):
    return pl.BlockSpec(tuple(shape), index)


def call(kernel, name, grid, in_specs, out_specs, out_shape, scratch, args, prefetch=0, vmem=8, aliases=None):
    return pl.pallas_call(
        kernel,
        out_shape=out_shape,
        grid_spec=pltpu.PrefetchScalarGridSpec(
            num_scalar_prefetch=prefetch,
            grid=grid,
            in_specs=in_specs,
            out_specs=out_specs,
            scratch_shapes=scratch,
        ),
        input_output_aliases=aliases or {},
        compiler_params=pltpu.CompilerParams(vmem_limit_bytes=vmem * MIB),
        cost_estimate=pl.CostEstimate(flops=0, bytes_accessed=int(MICROSECONDS.get(name, 1) * BYTES_PER_US), transcendentals=0),
        name=name,
    )(*args)


def shape_of(shape, dtype=SINGLE):
    return jax.ShapeDtypeStruct(tuple(shape), dtype)


def vmem_of(shape, dtype=SINGLE):
    return pltpu.VMEM(tuple(shape), dtype)


def hbm_of(shape, dtype=SINGLE):
    return pltpu.HBM(tuple(shape), dtype)


def in_vmem(value):
    return pltpu.with_memory_space_constraint(value, pltpu.VMEM)


def in_hbm(value):
    return pltpu.with_memory_space_constraint(value, pltpu.HBM)


def permutation():
    table = np.zeros((4 * PIX, 4 * PIX), np.float32)
    for pi in range(2):
        for pj in range(2):
            for i in range(HB):
                for j in range(WB):
                    table[((2 * pi + pj) * WB + j) * HB + i, (2 * i + pi) * 2 * WB + 2 * j + pj] = 1.0
    return jnp.asarray(table, BFLOAT)


def group_table(start_index, rows_local, bounds):
    global_rows = start_index * rows_local + jnp.arange(rows_local, dtype=jnp.int32)
    group_ids = jnp.zeros((rows_local,), jnp.int32)
    for boundary in bounds:
        group_ids = group_ids + (global_rows >= boundary).astype(jnp.int32)
    return (group_ids[:, None] == jnp.arange(len(bounds) + 1, dtype=jnp.int32)[None, :]).astype(SINGLE)


def rounded(value):
    return lax.reduce_precision(value, 8, 7)


def split_group(name, keep, got, rows, index):
    cols = keep.shape[1]

    def block(which, sent):
        def at(q, me):
            other, low, high = (q >> 2) & 1, (q >> 1) & 1, q & 1
            pair = other * 2 + sent if which == 0 else sent * 2 + other
            return (index(which, me[0] ^ (high * 8 + low * 4 + pair)), 0)

        return spec((rows, cols), at)

    blocks = [block(which, sent) for which in range(2) for sent in range(2)]
    return call(
        k_split, name, (8,), blocks + blocks,
        [spec((1, rows, cols), lambda q, me: (q, 0, 0))] * 4,
        [shape_of((8, rows, cols), BFLOAT)] * 4, [],
        (lax.axis_index("dp")[None].astype(jnp.int32),) + (keep,) * 4 + (got,) * 4, prefetch=1,
    )


def halved(keep, got):
    total = keep.astype(SINGLE) + got.astype(SINGLE)
    half = total.shape[0] // 2
    return total[:half].astype(BFLOAT), total[half:].astype(BFLOAT)


def added(keep, got):
    return keep[0].astype(SINGLE) + got[0].astype(SINGLE)


def halve(keep, send, bits, came=None):
    for bit in bits:
        got, came = exchange(send, bit) if came is None else came, None
        if keep.shape[0] > 1:
            keep, send = halved(keep, got)
    return added(keep, got)


def scatter_plain(keep, got, block, by_rows):
    total = (keep.astype(SINGLE) + got.astype(SINGLE)).astype(BFLOAT)
    if by_rows:
        own = lax.psum_scatter(total, "dp", scatter_dimension=0, tiled=True).astype(SINGLE)
        return own[: block // 2], own[block // 2 :]
    middle = total.shape[0] // 2
    return tuple(lax.psum_scatter(p, "dp", scatter_dimension=0, tiled=True).astype(SINGLE) for p in (total[:middle], total[middle:]))


def joined(value, got):
    return jnp.concatenate([value, got], axis=0)


def gather_blocks(name, core, parts, others, out_shape):
    scalars = jnp.stack([lax.axis_index("dp"), core]).astype(jnp.int32)
    pieces = [a for pair in list(parts) + list(others) for a in pair]
    return call(
        k_gather, name, (), [ANYWHERE] * 8, ANYWHERE, vmem_of(out_shape, BFLOAT),
        [pltpu.SemaphoreType.DMA((64,))], (scalars, *pieces), prefetch=1, vmem=2,
    )


def swap_all(parts):
    return [tuple(swap_pipe(a) for a in pair) for pair in parts]


def join_two(stayed, came, token):
    pieces = (stayed[0], came[0], stayed[1], came[1])
    shape = (2 * stayed[0].shape[0],) + stayed[0].shape[1:]
    return call(
        k_join, "join", (), [ANYWHERE] * 5, [ANYWHERE] * 2, [vmem_of(shape, BFLOAT)] * 2,
        [pltpu.SemaphoreType.DMA((4,))], pieces + (token,), vmem=2,
    )


def keep_in_hbm(value):
    def filler(token):
        return call(
            k_keep, "keep", (), [ANYWHERE] * 2, ANYWHERE, hbm_of(value.shape, value.dtype),
            [pltpu.SemaphoreType.DMA], (in_vmem(value), token), vmem=2,
        )

    return filler


def nothing(token):
    return token


def both_of(*fillers):
    return lambda token: tuple(filler(token) for filler in fillers)


def on_device(images, cotangent, heights, widths, assign, w_narrow, w_wide, bn_mid, bn_wide, mom_narrow, mom_wide, mom_bn_mid, mom_bn_wide):
    core = lax.axis_index("pipe")
    shard = lax.axis_index(("pipe", "dp"))
    fast = lax.axis_size("dp") == 16

    own_narrow = w_narrow.astype(BFLOAT)
    own_wide = w_wide.astype(BFLOAT)
    rows_n, half_n = w_narrow.shape[0], C_MID // 2
    part_n = rows_n // 2
    whole_n = (R_N // 2, C_MID)
    if fast:
        sent = swap_pipe(jnp.where(core == 0, own_narrow[:, half_n:], own_narrow[:, :half_n]))
        kept = jnp.where(core == 0, own_narrow[:, :half_n], own_narrow[:, half_n:])
        mine_a, mine_b = jnp.where(core == 0, kept, sent), jnp.where(core == 0, sent, kept)
        a0, a1 = mine_a[None, :part_n], mine_a[None, part_n:]
        b0, b1 = mine_b[None, :part_n], mine_b[None, part_n:]
        got = lax.optimization_barrier((exchange(a0, 8), exchange(a1, 8)))
        a0, a1 = join_two((a0, a1), got, got[1])
        got = lax.optimization_barrier((exchange(a0, 4), exchange(a1, 4)))
        a0, a1 = join_two((a0, a1), got, got[1])
        got = lax.optimization_barrier((exchange(a0, 2), exchange(a1, 1)))
        a0, a1 = join_two((a0, a1), got, got[1])
        third_done = a1
        last0, last1 = exchange(a0, 1), exchange(a1, 2)
        stay_a = swap_all([(a0,), (a1,)])
        b0, b1 = pin((b0, b1), third_done)
        got = exchange(b0, 8), exchange(b1, 8)
        own_wide = pin(own_wide, third_done)
    else:
        narrow = lax.all_gather(own_narrow, ("pipe", "dp"), axis=0, tiled=True)
        narrow_a, narrow_b = narrow[: R_N // 2], narrow[R_N // 2 :]
        third_done = narrow
    wide = lax.all_gather(own_wide, ("pipe", "dp"), axis=0, tiled=True)

    own_heights, own_widths, own_assign = pin((heights, widths, assign), third_done)
    order = own_assign[0].reshape(2, SLOTS)
    own_slots = lax.dynamic_index_in_dim(order, core, 0, keepdims=False)
    other_slots = lax.dynamic_index_in_dim(order, 1 - core, 0, keepdims=False)
    slots = jnp.concatenate([own_slots, core[None].astype(jnp.int32), other_slots])
    heights_own, widths_own = own_heights[own_slots], own_widths[own_slots]
    inside = (jnp.arange(HB)[None, None, :] < heights_own[:, None, None]) & (jnp.arange(WB)[None, :, None] < widths_own[:, None, None])
    mask = in_vmem(inside.astype(SINGLE).reshape(ROWS, 1))
    perm = permutation()
    x = call(
        k_prep, "prep", (SLOTS,),
        [spec((1, 4 * PIX, C_IN), lambda s, slot: (slot[s], 0, 0)), full((4 * PIX, 4 * PIX)), spec((PIX, 1), lambda s, slot: (s, 0))],
        spec((4, PIX, C_IN), lambda s, slot: (0, s, 0)),
        vmem_of((4, ROWS, C_IN), BFLOAT), [],
        (slots, in_hbm(images.reshape(IMG_DEV, 4 * PIX, C_IN)), in_hbm(perm), mask), prefetch=1, vmem=10,
    )
    counts = jnp.sum((own_heights * own_widths)[own_assign[0]].reshape(4, 2), axis=1).astype(SINGLE)
    mid_cols, wide_cols = bn_mid.shape[1], bn_wide.shape[1]
    tables = jnp.concatenate(
        [
            lax.dynamic_update_slice(jnp.zeros((8, C_MID), SINGLE), rounded(bn_mid), (0, shard * mid_cols)),
            lax.dynamic_update_slice(jnp.zeros((6, C_OUT), SINGLE), rounded(bn_wide), (0, shard * wide_cols)).reshape(24, C_MID),
        ]
    )
    tables = pin(tables, third_done)
    tables = tables + swap_pipe(tables)
    tables = jnp.concatenate([tables, jnp.zeros((4, C_MID), SINGLE).at[0, :4].set(counts)])

    held = {}
    if fast:
        last0, last1, got, x, tables = lax.optimization_barrier((last0, last1, got, x, tables))
        came_a = swap_all([(last0,), (last1,)])
        own_b = join_two((b0, b1), got, got[1])
        held["got"] = exchange(own_b[0], 4), exchange(own_b[1], 4)
        narrow_a = gather_blocks("wa", core, [(a0, last0), (a1, last1)], [u + v for u, v in zip(stay_a, came_a)], whole_n)

    def turn(feature, feature_spec, grid, shape, index):
        def filler(token):
            return call(
                k_turn, "turn", grid, [feature_spec, ANYWHERE],
                spec((C_MID, ROWS), index), hbm_of(shape, BFLOAT), [], (feature, token),
            )

        return filler

    def weight_grad(name, feature, feature_spec, grad, grad_spec, tiles, shape, rows, base, bufs, token, space):
        out_spec = spec((rows, shape[1]), lambda t, slot: (base + t, 0))
        hold = in_vmem if space is vmem_of else in_hbm
        extra = tuple(hold(b) for b in bufs or ()) + (() if token is None else (token,))
        return call(
            k_grad, name, (tiles,), [feature_spec, grad_spec] + [ANYWHERE] * len(extra),
            [out_spec] * 2, [space(shape, BFLOAT)] * 2, [], (slots, feature, grad) + extra,
            prefetch=1, vmem=9, aliases={3: 0, 4: 1} if bufs else {},
        )

    full_row = full((4, C_MID))
    full_tab = full((2, C_MID))
    full_mask = full((ROWS, 1))
    full_mid = full((ROWS, C_MID))
    plane_pair = spec((2, ROWS, C_MID), lambda s: (jnp.minimum(s, 1), 0, 0))

    def narrow_block(index):
        return spec((TILE, TILE), index)

    chunk = spec((ROWS, TILE), lambda k, *_: (0, k))
    chunk_sum = spec((4, TILE), lambda k, *_: (0, k))
    chunk_tab = spec((2, TILE), lambda k, *_: (0, k))
    four_a = narrow_block(lambda k: (11, 0))
    four_b = narrow_block(lambda k: (jnp.maximum(k - 1, 0), 0))

    a1, part1 = call(
        k_first, "a1", (4,),
        [spec((1, ROWS, C_IN), lambda k: (k, 0, 0)), full((C_IN, C_MID))],
        [spec((1, ROWS, C_MID), lambda k: (k, 0, 0)), full_row],
        [hbm_of((4, ROWS, C_MID)), shape_of((4, C_MID))], [],
        (in_vmem(x), in_vmem(narrow_a)), vmem=8,
    )

    def third_b(token):
        if not fast:
            return token
        big = join_two(own_b, pin(held["got"], token), token)
        held["got"] = exchange(big[0], 2), exchange(big[1], 1)
        return big

    a1 = in_hbm(a1)
    first_sum, (a_kept, x_kept, big_b) = dp_sum(jnp.concatenate([part1, tables]), [keep_in_hbm(narrow_a), keep_in_hbm(x), third_b])
    x_kept, a_kept = in_hbm(x_kept), in_hbm(a_kept)
    total1, tables = first_sum[:4], first_sum[4:]
    mid, table = tables[:8], tables[8:32].reshape(6, C_OUT)
    inv = lax.dynamic_slice(1.0 / tables[32, :4], (2 * core,), (2,))
    mid1, mid2, mid4, mid5 = (mid[2 * k : 2 * k + 2] for k in range(4))
    tab3, tabs, tab6 = (table[2 * k : 2 * k + 2] for k in range(3))

    a_s, part_s = call(
        k_short, "as", (4,),
        [spec((1, ROWS, C_IN), lambda k: (0, 0, 0)), spec((TILE, TILE), lambda k: (1, k)), spec((TILE, TILE), lambda k: (2, k))],
        [chunk, chunk_sum],
        [vmem_of((ROWS, C_OUT)), shape_of((4, C_OUT))], [],
        (in_vmem(x), in_hbm(wide), in_hbm(wide)), vmem=8,
    )

    def conv_weights(first, order_of):
        return [narrow_block(lambda s, kx=kx: (first + 3 * order_of(s) + kx, 0)) for kx in range(3)]

    turned = lambda s: lax.rem(s + 1, 3)
    straight = lambda s: s

    a2, h1, part2 = call(
        k_conv_two, "a2", (3,),
        [SCALARS, full_row, full_tab, full_mask, plane_pair] + conv_weights(2, turned),
        [full_mid, plane_pair, full_row],
        [vmem_of((ROWS, C_MID)), vmem_of((4, ROWS, C_MID), BFLOAT), shape_of((4, C_MID))],
        [pltpu.VMEM((2, PAD + ROWS + PAD, C_MID), SINGLE)] * 2,
        (inv, total1, mid1, mask, a1) + (a_kept,) * 3, vmem=15,
    )
    a2 = in_vmem(a2)

    def fourth_b(token):
        if not fast:
            return token
        big = join_two(big_b, pin(held["got"], token), token)
        held["got"] = exchange(big[0], 1), exchange(big[1], 2)
        return big

    turn_h1 = turn(h1, spec((1, ROWS, C_MID), lambda k: (k, 0, 0)), (4,), (4 * C_MID, ROWS), lambda k: (k, 0))
    total2, (h1_t, _unused, whole_b) = dp_sum(part2, [turn_h1, nothing, fourth_b])

    def expand(name, a, total, tab, row):
        return call(
            k_expand, name, (4,),
            [SCALARS, full_row, full_tab, full_mask, full_mid, spec((TILE, TILE), lambda k: (row, k))],
            [full_mid, chunk, chunk_sum],
            [vmem_of((ROWS, C_MID), BFLOAT), vmem_of((ROWS, C_OUT)), shape_of((4, C_OUT))], [],
            (inv, total, tab, mask, a, in_hbm(wide)), vmem=8,
        )

    h2, a3, part3 = expand("a3", a2, total2, mid2, 0)
    whole = spec((ROWS, C_MID), lambda k: (0, 0))

    def swap_b(token):
        if not fast:
            return token
        ready = pin(whole_b + held["got"], token)
        return [(ready[0], ready[2]), (ready[1], ready[3])]

    def gather_b(token):
        if not fast:
            return narrow_b
        others = pin(held["others"], token)
        return gather_blocks("wb", core, held["parts"], others, whole_n)

    def start_swap_b(token):
        if fast:
            held["parts"] = swap_b(token)
            held["others"] = swap_all(held["parts"])
        return token

    total3s, ((h2_t, as_kept), (_unused, a3_kept), _unused, narrow_b) = dp_sum(
        jnp.concatenate([part3, part_s]),
        [
            both_of(turn(h2, whole, (1,), (C_MID, ROWS), lambda k: (0, 0)), keep_in_hbm(a_s)),
            both_of(start_swap_b, keep_in_hbm(a3)),
            nothing,
            gather_b,
        ],
    )
    as_kept, a3_kept = in_hbm(as_kept), in_hbm(a3_kept)
    total3, total_s = total3s[:4], total3s[4:]

    y, a4, part4 = call(
        k_meet, "a4", (4,),
        [SCALARS, chunk_sum, chunk_sum, chunk_tab, chunk_tab, full_mask, chunk, chunk, four_a, four_b],
        [chunk, full_mid, full_row],
        [vmem_of((ROWS, C_OUT), BFLOAT), vmem_of((ROWS, C_MID)), shape_of((4, C_MID))], [],
        (inv, total3, total_s, tab3, tabs, mask, in_vmem(a3), in_vmem(a_s), a_kept, in_vmem(narrow_b)), vmem=10,
    )
    a4 = in_vmem(a4)
    def turn_x(q, start, into):
        def filler(token):
            extra = () if into is None else (in_hbm(into[-1]),)
            held["x_t"] = call(
                k_turn, "turn", (2,), [spec((1, ROWS, C_MID), lambda k: (start + k, 0, q))] + [ANYWHERE] * (1 + len(extra)),
                spec((C_MID, ROWS), lambda k: (q, start + k)), hbm_of((C_IN, 4 * ROWS), BFLOAT), [], (x_kept, *extra, token),
                aliases={1: 0} if extra else {},
            )
            return held["x_t"]

        return filler

    total4, (y_t, y_kept, x_t0, x_t1) = dp_sum(
        part4,
        [
            turn(in_vmem(y), spec((ROWS, C_MID), lambda k: (0, k)), (4,), (4 * C_MID, ROWS), lambda k: (k, 0)),
            keep_in_hbm(y),
            turn_x(0, 0, None),
            lambda token: turn_x(0, 2, [held["x_t"]])(token),
        ],
    )
    del x_t0

    a5, h4, part5 = call(
        k_conv_one, "a5", (3,),
        [SCALARS, full_row, full_tab, full_mask, full_mid] + conv_weights(3, straight),
        [full_mid, full_mid, full_row],
        [vmem_of((ROWS, C_MID)), vmem_of((ROWS, C_MID), BFLOAT), shape_of((4, C_MID))],
        [pltpu.VMEM((PAD + ROWS + PAD, C_MID), SINGLE)] * 2,
        (inv, total4, mid4, mask, a4) + (in_vmem(narrow_b),) * 3, vmem=9,
    )
    a5 = in_vmem(a5)
    total5, (h4_t, b_kept, _unused, x_t) = dp_sum(
        part5,
        [
            turn(h4, whole, (1,), (C_MID, ROWS), lambda k: (0, 0)),
            keep_in_hbm(narrow_b),
            turn_x(1, 0, [x_t1]),
            lambda token: turn_x(1, 2, [held["x_t"]])(token),
        ],
    )
    b_kept = in_hbm(b_kept)
    h5, a6, part6 = expand("a6", a5, total5, mid5, 3)
    total6, (h5_t, a6_kept) = dp_sum(part6, [turn(h5, whole, (1,), (C_MID, ROWS), lambda k: (0, 0)), keep_in_hbm(a6)])
    a6_kept = in_hbm(a6_kept)

    cot = in_hbm(cotangent.transpose(0, 2, 1, 3).reshape(IMG_DEV, PIX, C_OUT))
    blk, gz6, s6 = call(
        k_head, "head", (4,),
        [SCALARS, chunk_sum, chunk_tab, full_mask, chunk, chunk]
        + [spec((1, PIX, TILE), lambda k, slot, s=s: (slot[s], 0, k)) for s in range(SLOTS)],
        [
            spec((1, ROWS, TILE), lambda k, slot: ((k // 2) ^ slot[SLOTS], 0, lax.rem(k, 2))),
            chunk,
            chunk_sum,
        ],
        [shape_of((2, ROWS, C_OUT // 2), BFLOAT), vmem_of((ROWS, C_OUT)), shape_of((4, C_OUT))], [],
        (slots, inv, total6, tab6, mask, in_vmem(a6), in_hbm(y_kept), cot, cot, cot, cot), prefetch=1, vmem=10,
    )
    gz6 = in_vmem(gz6)

    def place(name, pair, got, token):
        block = (1,) + pair.shape[2:]
        return call(
            k_place, name, (IMG_DEV,),
            [
                spec((1,) + block, lambda t, slot: (0, jnp.minimum(t, SLOTS - 1), 0, 0)),
                spec(block, lambda t, slot: (jnp.maximum(t - SLOTS, 0), 0, 0)),
                ANYWHERE,
            ],
            spec(block, lambda t, slot: (slot[t + (t >= SLOTS)], 0, 0)),
            shape_of((IMG_DEV,) + pair.shape[2:], BFLOAT), [],
            (slots, pair, got, token), prefetch=1, vmem=4,
        )

    blk = blk.reshape(2, SLOTS, PIX, C_OUT // 2)
    sum6, (got_blk, _unused, _unused, block_local) = dp_sum(
        s6,
        [
            lambda token: swap_pipe(pin(blk[1], token)),
            lambda token: token,
            lambda token: token,
            lambda token: token,
        ],
    )

    ga6, gz5, s5 = call(
        k_back_six, "g5", (4,),
        [SCALARS, chunk, chunk, chunk_sum, chunk_sum, chunk_tab, full_mask, spec((TILE, TILE), lambda k: (3, k)), full_mid, full_row, full_tab],
        [chunk, full_mid, full_row],
        [vmem_of((ROWS, C_OUT), BFLOAT), vmem_of((ROWS, C_MID)), shape_of((4, C_MID))],
        [pltpu.VMEM((ROWS, C_MID), SINGLE)],
        (inv, gz6, a6_kept, total6, sum6, tab6, mask, in_hbm(wide), a5, total5, mid5), vmem=11,
    )
    gz5 = in_vmem(gz5)

    def wide_rows(k):
        return spec((1, 256, ROWS), lambda t, slot: (0, t + k, 0))

    def whole_wide(grad):
        return grad.reshape((1,) + grad.shape), full((1,) + grad.shape)

    wide_shape, narrow_shape = (R_W, C_OUT // 2), (R_N // 2, C_MID // 2)
    sum5, (bufs_w, block_local) = dp_sum(
        s5,
        [
            lambda token: weight_grad("dw6", h5_t[None], wide_rows(0), *whole_wide(ga6), 2, wide_shape, 256, 6, None, token, hbm_of),
            lambda token: place("place_out", blk, got_blk, token),
        ],
    )
    block_local = block_local.reshape(IMG_DEV, WB, HB, C_OUT // 2).transpose(0, 2, 1, 3)

    col5, gz4, s4 = call(
        k_back_conv_one, "g4", (3,),
        [SCALARS, full_mid, full_mid, full_row, full_row, full_tab, full_mask] + conv_weights(3, straight) + [full_mid, full_row, full_tab],
        [spec((3, ROWS, C_MID), lambda s: (s, 0, 0)), full_mid, full_row],
        [vmem_of((9, ROWS, C_MID), BFLOAT), vmem_of((ROWS, C_MID)), shape_of((4, C_MID))],
        [pltpu.VMEM((PAD + ROWS + PAD, C_MID), SINGLE)] * 2 + [pltpu.VMEM((ROWS, C_MID), SINGLE)],
        (inv, gz5, a5, total5, sum5, mid5, mask, b_kept, b_kept, b_kept, a4, total4, mid4), vmem=13,
    )
    gz4 = in_vmem(gz4)
    one_turned = spec((1, C_MID, ROWS), lambda t, slot: (0, 0, 0))
    held_b = []

    def grad_five(k):
        def filler(token):
            grad_spec = spec((3, ROWS, C_MID), lambda t, slot: (k, 0, 0))
            held_b[:] = weight_grad("dw5", h4_t[None], one_turned, in_vmem(col5), grad_spec, 1, narrow_shape, 3 * TILE, 1 + k, list(held_b), token, vmem_of)
            return tuple(held_b)

        return filler

    sum4, results4 = dp_sum(s4, [grad_five(k) for k in range(3)])
    bufs_b = results4[2]

    ga4, gj, s3 = call(
        k_back_four, "gy", (4,),
        [SCALARS, full_mid, full_mid, full_row, full_row, full_tab, full_mask, four_a, four_b,
         chunk, chunk, chunk, chunk_sum, chunk_sum, chunk_tab, chunk_tab],
        [full_mid, chunk, spec((6, TILE), lambda k: (0, k))],
        [vmem_of((ROWS, C_MID), BFLOAT), vmem_of((ROWS, C_OUT)), shape_of((6, C_OUT))], [],
        (inv, gz4, a4, total4, sum4, mid4, mask, a_kept, b_kept, gz6, a3_kept, as_kept, total3, total_s, tab3, tabs), vmem=15,
    )
    gj = in_vmem(gj)

    by_rows = lambda which, m: 2 * m + which

    def grad_four(token):
        y_tiles = y_t.reshape(4, C_MID, ROWS)
        one = full((1, ROWS, C_MID))
        grad = in_vmem(ga4.reshape(1, ROWS, C_MID))
        held["grad_b"] = weight_grad("dw4b", y_tiles, spec((1, C_MID, ROWS), lambda t, slot: (1 + t, 0, 0)), grad, one, 3, narrow_shape, TILE, 0, bufs_b, token, vmem_of)
        return held["grad_b"]

    def grad_four_first(token):
        return weight_grad(
            "dw4a", y_t.reshape(4, C_MID, ROWS), spec((1, C_MID, ROWS), lambda t, slot: (0, 0, 0)), in_vmem(ga4.reshape(1, ROWS, C_MID)),
            full((1, ROWS, C_MID)), 1, narrow_shape, TILE, 11, None, token, vmem_of,
        )

    def swap_grad_b(token):
        held["got_b"] = swap_pipe(pin(held["grad_b"][1], token))
        return token

    def split_b(token):
        if not fast:
            return token
        keep, got = pin((held["grad_b"][0], held["got_b"]), token)
        state = split_group("split_b", in_vmem(keep), got, part_n, by_rows)
        held["came_b"] = exchange(state[1], 1), exchange(state[3], 2)
        return state

    sum3, results3 = dp_sum(s3, [grad_four, both_of(swap_grad_b, grad_four_first), split_b])
    bufs_b, bufs_a = results3[0], results3[1][1]
    held["b"] = results3[2]

    ga3, gas, gz2, s2 = call(
        k_back_three, "g2", (4,),
        [SCALARS, chunk, chunk, chunk, chunk_sum, chunk_sum, spec((6, TILE), lambda k: (0, k)), chunk_tab, chunk_tab, full_mask,
         spec((TILE, TILE), lambda k: (0, k)), full_mid, full_row, full_tab],
        [chunk, chunk, full_mid, full_row],
        [hbm_of((ROWS, C_OUT), BFLOAT), hbm_of((ROWS, C_OUT), BFLOAT), vmem_of((ROWS, C_MID)), shape_of((4, C_MID))],
        [pltpu.VMEM((ROWS, C_MID), SINGLE)],
        (inv, gj, a3_kept, as_kept, total3, total_s, sum3, tab3, tabs, mask, in_hbm(wide), a2, total2, mid2), vmem=14,
    )
    gz2 = in_vmem(gz2)

    def step_b(bits):
        def filler(token):
            if not fast:
                return token
            keep0, _sent, keep1, _sent = held["b"]
            came0, came1 = pin(held["came_b"], token)
            stay0, sent0 = halved(keep0, came0)
            stay1, sent1 = halved(keep1, came1)
            held["came_b"] = exchange(sent0, bits[0]), exchange(sent1, bits[1])
            return stay0, sent0, stay1, sent1

        return filler

    def grad_three(token):
        held["w"] = weight_grad("dw3", h2_t[None], wide_rows(0), *whole_wide(ga3), 2, wide_shape, 256, 0, bufs_w, token, hbm_of)
        return held["w"]

    def grad_short(q):
        def filler(token):
            held["w"] = weight_grad("dws", x_t[None], wide_rows(2 * q), *whole_wide(gas), 2, wide_shape, 256, 2 + 2 * q, held["w"], token, hbm_of)
            return held["w"]

        return filler

    sum2, results2 = dp_sum(s2, [grad_three, grad_short(0), step_b((2, 1)), grad_short(1)])
    held["b"], bufs_w = results2[2:]
    got_w = swap_pipe(bufs_w[1])

    col2, gz1, s1 = call(
        k_back_conv_two, "g1", (3,),
        [SCALARS, full_mid, full_mid, full_row, full_row, full_tab, full_mask] + conv_weights(2, turned)
        + [plane_pair, full_row, full_tab],
        [spec((3, ROWS, C_MID), lambda s: (turned(s), 0, 0)), plane_pair, full_row],
        [vmem_of((9, ROWS, C_MID), BFLOAT), vmem_of((4, ROWS, C_MID)), shape_of((4, C_MID))],
        [pltpu.VMEM((PAD + ROWS + PAD, C_MID), SINGLE)] * 2 + [pltpu.VMEM((2, ROWS, C_MID), SINGLE)],
        (inv, gz2, a2, total2, sum2, mid2, mask, a_kept, a_kept, a_kept, a1, total1, mid1), vmem=16,
    )
    gz1 = in_vmem(gz1)
    h1_planes = h1_t.reshape(4, C_MID, ROWS)

    def grad_two(row):
        def filler(token):
            first = 2 * (1 - (row & 1))
            held["a"] = weight_grad(
                "dw2", h1_planes, spec((1, C_MID, ROWS), lambda t, slot: (first + (1 - (t & 1)), 0, 0)), in_vmem(col2),
                spec((1, ROWS, C_MID), lambda t, slot: (3 * row + t, 0, 0)), 3, narrow_shape, TILE, 2 + 3 * row, held["a"], token, vmem_of,
            )
            return held["a"]

        return filler

    def wide_back(token):
        return call(
            k_wide_back, "dxs", (2,),
            [full((ROWS, C_OUT)), spec((TILE, C_OUT), lambda k: (1 + k, 0)), ANYWHERE],
            spec((ROWS, TILE), lambda k: (0, k)),
            hbm_of((ROWS, C_IN)), [],
            (in_hbm(gas), in_hbm(wide), token), vmem=11,
        )

    def split_w(token):
        if fast:
            keep, got = pin((bufs_w[0], got_w), token)
            held["split"] = split_group("split_w", keep, got, w_wide.shape[0], lambda which, m: 16 * which + m)
            return held["split"]
        return token

    def send_w(token):
        if fast:
            sent0, sent1 = pin((held["split"][1], held["split"][3]), token)
            held["came"] = exchange(sent0, 1), exchange(sent1, 2)
        return token

    held["a"] = bufs_a
    sum1, results1 = dp_sum(s1, [both_of(step_b((4, 4)), split_w), grad_two(0), both_of(send_w, grad_two(1)), grad_two(2)])
    held["b"], held["split"] = results1[0]
    bufs_a = results1[3]
    sum1, held["b"] = lax.optimization_barrier((sum1, step_b((8, 8))(sum1)))

    plane = spec((1, ROWS, C_MID), lambda k: (k, 0, 0))
    ga1 = call(
        k_first_grad, "g0", (4,), [SCALARS, plane, plane, full_row, full_row, full_tab, full_mask], plane,
        vmem_of((4, ROWS, C_MID), BFLOAT), [], (inv, gz1, a1, total1, sum1, mid1, mask),
    )
    if fast:
        came_w = held["came"]
        state_w = halved(held["split"][0], came_w[0]) + halved(held["split"][2], came_w[1])
        ga1, state_w = lax.optimization_barrier((ga1, state_w))
    flat_ga1 = in_vmem(ga1.reshape(1, 4 * ROWS, C_MID))
    bufs_a = weight_grad(
        "dw1", x_t.reshape(2, C_MID, 4 * ROWS), spec((1, C_MID, 4 * ROWS), lambda t, slot: (t, 0, 0)), flat_ga1, full((1, 4 * ROWS, C_MID)),
        2, narrow_shape, TILE, 0, bufs_a, None, vmem_of,
    )
    got_a = swap_pipe(bufs_a[1])
    dxs = wide_back(ga1)

    def image_grads(token):
        pair = call(
            k_image_grad, "gx", (SLOTS,),
            [spec((4, PIX, C_MID), lambda s, slot: (0, s, 0)), spec((PIX, 1), lambda s, slot: (s, 0)), full((C_IN, C_MID)),
             spec((PIX, C_IN), lambda s, slot: (s, 0)), full((4 * PIX, 4 * PIX)), ANYWHERE],
            spec((2, 1, 4 * PIX, C_IN // 2), lambda s, slot: (0, s, 0, 0)),
            shape_of((2, SLOTS, 4 * PIX, C_IN // 2), BFLOAT), [],
            (slots, in_vmem(ga1), mask, a_kept, in_hbm(dxs), in_hbm(perm), token), prefetch=1, vmem=10,
        )
        return pair, swap_pipe(pair[1])

    pair, got_pair = image_grads(ga1)
    grad_local = place("place_grad", pair, got_pair, ga1)
    if fast:
        state_a = split_group("split_a", in_vmem(bufs_a[0]), got_a, part_n, by_rows)
        half_b = jnp.concatenate([added(held["b"][k], held["came_b"][k // 2]) for k in (0, 2)], axis=0)
        half_w0 = halve(state_w[0], state_w[1], (2, 4, 8))
        half_w1 = halve(state_w[2], state_w[3], (1, 4, 8))
        half_a = jnp.concatenate([halve(state_a[0], state_a[1], (1, 2, 4, 8)), halve(state_a[2], state_a[3], (2, 1, 4, 8))], axis=0)
    else:
        half_a = jnp.concatenate(scatter_plain(bufs_a[0], got_a, rows_n, True), axis=0)
        half_w0, half_w1 = scatter_plain(bufs_w[0], got_w, w_wide.shape[0], False)
        half_b = jnp.concatenate(scatter_plain(bufs_b[0], held["got_b"], rows_n, True), axis=0)
    grad_local = grad_local.reshape(IMG_DEV, 2 * HB, 2 * WB, C_IN // 2)

    def join_halves(first, second):
        mine = jnp.where(core == 0, first, second)
        got = swap_pipe(jnp.where(core == 0, second, first))
        return jnp.where(core == 0, jnp.concatenate([mine, got], axis=1), jnp.concatenate([got, mine], axis=1))

    grad_narrow = join_halves(half_a, half_b)
    grad_wide = join_halves(half_w0, half_w1)

    hot_narrow = group_table(shard, w_narrow.shape[0], (C_IN, C_IN + 9 * C_MID, C_IN + 9 * C_MID + C_OUT))
    hot_wide = group_table(shard, w_wide.shape[0], (C_MID, C_MID + C_IN))

    def pair_sum(rows):
        return rows[0] + rows[1]

    mid_rows = jnp.stack([pair_sum(v) for t in (sum1, sum2, sum4, sum5) for v in (t[2:4], t[0:2])])
    wide_rows = jnp.stack([pair_sum(v) for v in (sum3[2:4], sum3[0:2], sum3[4:6], sum3[0:2], sum6[2:4], sum6[0:2])])
    mid_rows = mid_rows + swap_pipe(mid_rows)
    wide_rows = wide_rows + swap_pipe(wide_rows)
    grad_mid = lax.dynamic_slice(mid_rows, (0, shard * mid_cols), (8, mid_cols))
    grad_table = lax.dynamic_slice(wide_rows, (0, shard * wide_cols), (6, wide_cols))

    def square_vector(narrow_rows, wide_rows, mid_part, table_part):
        return jnp.concatenate(
            [
                jnp.dot(jnp.sum(narrow_rows * narrow_rows, axis=1), hot_narrow, precision=PRECISE),
                jnp.dot(jnp.sum(wide_rows * wide_rows, axis=1), hot_wide, precision=PRECISE),
                jnp.sum(mid_part * mid_part, axis=1),
                jnp.sum(table_part * table_part, axis=1),
            ]
        )

    squares = jnp.stack([square_vector(w_narrow, w_wide, bn_mid, bn_wide), square_vector(grad_narrow, grad_wide, grad_mid, grad_table)])
    squares, _unused = dp_sum(squares + swap_pipe(squares))
    norms = jnp.sqrt(squares)
    weight_norms, grad_norms = norms[0], norms[1]
    ratios = TRUST * weight_norms / (grad_norms + DECAY * weight_norms)
    ratio_narrow = jnp.dot(hot_narrow, ratios[:4], precision=PRECISE)
    ratio_wide = jnp.dot(hot_wide, ratios[4:7], precision=PRECISE)

    def lars_step(weight, gradient, moment, ratio_rows):
        new_moment = MOMENTUM * moment + RATE * ratio_rows[:, None] * (gradient + DECAY * weight)
        return (weight - new_moment, new_moment)

    new_narrow, new_mom_narrow = lars_step(w_narrow, grad_narrow, mom_narrow, ratio_narrow)
    new_wide, new_mom_wide = lars_step(w_wide, grad_wide, mom_wide, ratio_wide)
    new_mid, new_mom_mid = lars_step(bn_mid, grad_mid, mom_bn_mid, ratios[7:15])
    new_table, new_mom_table = lars_step(bn_wide, grad_table, mom_bn_wide, ratios[15:21])
    return (
        block_local, grad_local, grad_narrow, grad_wide, grad_mid, grad_table,
        new_mom_narrow, new_mom_wide, new_mom_mid, new_mom_table,
        new_narrow, new_wide, new_mid, new_table,
    )


def solution(mesh):
    rows = P(("pipe", "dp"), None)
    columns = P(None, ("pipe", "dp"))
    feature = P("dp", None, None, None)
    return jax.shard_map(
        on_device,
        mesh=mesh,
        in_specs=(feature, feature, P("dp"), P("dp"), P("dp", None), rows, rows, columns, columns, rows, rows, columns, columns),
        out_specs=(P("dp", None, None, "pipe"), P("dp", None, None, "pipe"), rows, rows, columns, columns, rows, rows, columns, columns, rows, rows, columns, columns),
        check_vma=False,
    )
```

time: 706 us -> 559 us (0.79)
  waiting for transfers between devices: 309 us -> 204 us
  other arithmetic: 49.2 us -> 22.6 us
  Pallas kernels: 196 us -> 176 us
  local copies, waits for them, and re-layouts: 16.4 us -> 24.2 us
    all_gather x2 -> x1, waiting for transfers between devices: 99.7 us -> 0.01 us  [on_device(): wide = lax.all_gather(own_wide, ('pipe', 'dp'), axis=0, tiled=True)]
    pallas_call x8 -> x0, Pallas kernels: 50.8 us -> none  [weight_grad(): pl.pallas_call(k_grad, out_shape=[shape_of(shape, BFLOAT)] * 2, grid_spec...]
    pallas_call x20 -> x59, Pallas kernels: 145 us -> 176 us  [call(): pl.pallas_call(kernel, out_shape=out_shape, grid_spec=pltpu.PrefetchScala...]
    add x56, other arithmetic: 14.1 us -> 3.19 us  [the longest x4 1.98 us: added(): return keep[0].astype(SINGLE) + got[0].astype(SINGLE)]
    unnamed x77 -> x176, local copies, waits for them, and re-layouts: 3.51 us -> 12.9 us
    reduce_scatter x1 -> x0, waiting for transfers between devices: 7.47 us -> none  [on_device(): lax.psum_scatter(sum_b, 'dp', scatter_dimension=0, tiled=True)]
    ppermute x72 -> x92, starting transfers between devices: 106 us -> 102 us  [exchange(): return lax.ppermute(value, 'dp', pairs(bit))]
    ppermute x72 -> x92, waiting for transfers between devices: 201 us -> 198 us  [exchange(): return lax.ppermute(value, 'dp', pairs(bit))]
  transfers between devices with their start and end apart: 86 -> 113, of which waited for: 65 -> 73; matrix products, arithmetic and copies ran while one was open for 7% -> 5% of each run, Pallas kernels for 19% -> 24%
where the time goes in v2:
time: 559 us; the launch traced here: 549 us
  waiting for transfers between devices  204 us (36%)
  Pallas kernels  176 us (31%)
  starting transfers between devices  105 us (19%)
  local copies, waits for them, and re-layouts  24.2 us (4%)
  other arithmetic  22.6 us (4%)
  between operations  16.4 us (3%)
    ppermute x92, waiting for transfers between devices, exchange(): return lax.ppermute(value, 'dp', pairs(bit))  198 us
    pallas_call x59, Pallas kernels, call(): pl.pallas_call(kernel, out_shape=out_shape, grid_spec=pltpu.PrefetchScala...  176 us
    ppermute x92, starting transfers between devices, exchange(): return lax.ppermute(value, 'dp', pairs(bit))  102 us
    unnamed x176, local copies, waits for them, and re-layouts  12.9 us
  transfers between devices with their start and end apart: 113, of which 73 were waited for; matrix products, arithmetic and copies ran while one was open for 5% of the time, Pallas kernels for 24%

profile of v2, /device:TPU:0, one launch (start us, length us, event | category | flops | bytes accessed | tf_op | source)
XLA Modules:
  0.0 549.4 jit_solution(7340953356388269433)
XLA Ops:
  11.1 4.0 collective-permute-start.2
  15.2 7.7 %collective-permute-done.2.refs_3_.refs_4_ = bf16[1,192,256]{2,1,0:T(8,128)(2,1)S(1)} collective-permute-done((bf16[1,192,256]{2,1,0:T(8,128)(2,1)S(1)}, bf16[1,192,256]{2,1,0:T(8,128)(2,1)S(1)}, u32[]{:S(2)}, u32[]{:S(2)}) %collective-permute-start.2) | collective-permute-done | bytes 98336 | tf_op jit(solution)/shard_map/ppermute | solution.py:46
  27.2 5.8 %collective-permute-done.3.refs_1_ = bf16[2,192,256]{2,1,0:T(8,128)(2,1)S(1)} collective-permute-done((bf16[2,192,256]{2,1,0:T(8,128)(2,1)S(1)}, bf16[2,192,256]{2,1,0:T(8,128)(2,1)S(1)}, u32[]{:S(2)}, u32[]{:S(2)}) %collective-permute-start.3) | collective-permute-done | bytes 196640 | tf_op jit(solution)/shard_map/ppermute | solution.py:46
  41.1 5.6 %collective-permute-done.5.refs_1_ = bf16[4,192,256]{2,1,0:T(8,128)(2,1)S(1)} collective-permute-done((bf16[4,192,256]{2,1,0:T(8,128)(2,1)S(1)}, bf16[4,192,256]{2,1,0:T(8,128)(2,1)S(1)}, u32[]{:S(2)}, u32[]{:S(2)}) %collective-permute-start.5) | collective-permute-done | bytes 393248 | tf_op jit(solution)/shard_map/ppermute | solution.py:46
  56.5 4.2 collective-permute-start.9
  61.2 4.8 prep.1.x_ref.in_ref
  69.6 6.6 %collective-permute-done.10.refs_3_.refs_4_ = bf16[1,192,256]{2,1,0:T(8,128)(2,1)S(1)} collective-permute-done((bf16[1,192,256]{2,1,0:T(8,128)(2,1)S(1)}, bf16[1,192,256]{2,1,0:T(8,128)(2,1)S(1)}, u32[]{:S(2)}, u32[]{:S(2)}) %collective-permute-start.10) | collective-permute-done | bytes 98336 | tf_op jit(solution)/shard_map/ppermute | solution.py:46
  101.6 4.2 collective-permute-done.20.refs_3_
  112.6 7.2 %collective-permute-done.21 = f32[40,512]{1,0:T(8,128)S(1)} collective-permute-done((f32[40,512]{1,0:T(8,128)S(1)}, f32[40,512]{1,0:T(8,128)S(1)}, u32[]{:S(2)}, u32[]{:S(2)}) %collective-permute-start.21) | collective-permute-done | bytes 81952 | tf_op jit(solution)/shard_map/ppermute | solution.py:46
  120.4 5.9 %a2.1 = (f32[384,512]{1,0:T(8,128)S(1)}, bf16[4,384,512]{2,1,0:T(8,128)(2,1)S(1)}, f32[4,512]{1,0:T(4,128)S(1)}) custom-call(f32[2]{0:T(128)S(1)} %fusion.13.inv_ref, f32[4,512]{1,0:T(4,128)S(1)} %slice.493.total_ref.low_total, f32[2,512]{1,0:T(2,128)S(1)} %get-tuple-element.518.tab_ref.low_tab, f32[384,1]{1,0:T(8,128)S(1)} %reshape.366.mask_ref, ...), custom_call_target="tpu_custom_call" | custom-call | bytes 6000000 | tf_op jit(solution)/shard_map/a2/pallas_call | solution.py:566
  146.9 4.5 as.1
  151.5 4.2 a3.1
  171.9 4.3 wb.1.wb_ref.w0.w1.w2.in_ref
  177.1 4.7 a4.1
  238.2 5.4 head.1
  260.7 5.2 g5.1
  282.9 5.4 g4.1
  303.9 7.0 %gy.1 = (bf16[384,512]{1,0:T(8,128)(2,1)S(1)}, f32[384,2048]{1,0:T(8,128)S(1)}, f32[6,2048]{1,0:T(8,128)S(1)}) custom-call(f32[2]{0:T(128)S(1)} %fusion.13.inv_ref, f32[384,512]{1,0:T(8,128)S(1)} %get-tuple-element.357.gz_ref, f32[384,512]{1,0:T(8,128)S(1)} %copy-done.16, f32[4,512]{1,0:T(4,128)S(1)} %add.447.total_ref.low_total, f32[4,512]{1,0:T(4,128)S(1)} %add.467.s_ref, ...), custom_call_target="tpu_custom_call" | custom-call | bytes 8400000 | tf_op jit(solution)/shard_map/gy/pallas_call | solution.py:566
  333.3 7.3 %g2.1 = (bf16[384,2048]{1,0:T(8,128)(2,1)}, bf16[384,2048]{1,0:T(8,128)(2,1)}, f32[384,512]{1,0:T(8,128)S(1)}, f32[4,512]{1,0:T(4,128)S(1)}) custom-call(f32[2]{0:T(128)S(1)} %fusion.13.inv_ref, f32[384,2048]{1,0:T(8,128)S(1)} %get-tuple-element.372.gj_ref, f32[384,2048]{1,0:T(8,128)} %keep.10.a3_ref, f32[384,2048]{1,0:T(8,128)} %keep.9.as_ref, ...), custom_call_target="tpu_custom_call" | custom-call | bytes 8760000 | tf_op jit(solution)/shard_map/g2/pallas_call | solution.py:566
  360.2 7.2 %g1.1 = (bf16[9,384,512]{2,1,0:T(8,128)(2,1)S(1)}, f32[4,384,512]{2,1,0:T(8,128)S(1)}, f32[4,512]{1,0:T(4,128)S(1)}) custom-call(f32[2]{0:T(128)S(1)} %fusion.13.inv_ref, f32[384,512]{1,0:T(8,128)S(1)} %get-tuple-element.392.gz_ref, f32[384,512]{1,0:T(8,128)S(1)} %copy-done.19, f32[4,512]{1,0:T(4,128)S(1)} %copy-done.37, f32[4,512]{1,0:T(4,128)S(1)} %add.477.s_ref, ...), custom_call_target="tpu_custom_call" | custom-call | bytes 9600000 | tf_op jit(solution)/shard_map/g1/pallas_call | solution.py:566
  403.5 10.1 %collective-permute-done.83 = bf16[8,64,1024]{2,1,0:T(8,128)(2,1)S(1)} collective-permute-done((bf16[8,64,1024]{2,1,0:T(8,128)(2,1)S(1)}, bf16[8,64,1024]{2,1,0:T(8,128)(2,1)S(1)}, u32[]{:S(2)}, u32[]{:S(2)}) %collective-permute-start.83) | collective-permute-done | bytes 1048608 | tf_op jit(solution)/shard_map/ppermute | solution.py:46
  427.1 5.6 %collective-permute-done.95 = bf16[1,192,256]{2,1,0:T(8,128)(2,1)S(1)} collective-permute-done((bf16[1,192,256]{2,1,0:T(8,128)(2,1)}, bf16[1,192,256]{2,1,0:T(8,128)(2,1)S(1)}, u32[]{:S(2)}, u32[]{:S(2)}) %collective-permute-start.95) | collective-permute-done | bytes 98336 | tf_op jit(solution)/shard_map/ppermute | solution.py:46
  437.4 5.1 dxs.1.short_ref
  442.5 6.4 %gx.1.own_ref = bf16[2,4,384,512]{3,2,1,0:T(8,128)(2,1)S(1)} custom-call(s32[9]{0:T(128)S(1)} %pad_add_fusion.slot_ref, bf16[4,384,512]{2,1,0:T(8,128)(2,1)S(1)} %copy-done.5, f32[384,1]{1,0:T(8,128)S(1)} %reshape.366.mask_ref, bf16[6144,512]{1,0:T(8,128)(2,1)} %keep.7.w0.w1.w2.wa_ref.w_ref, f32[384,1024]{1,0:T(8,128)} %dxs.1.short_ref, ...), custom_call_target="tpu_custom_call" | custom-call | bytes 7680000 | tf_op jit(solution)/shard_map/gx/pallas_call | solution.py:566
  452.6 4.9 split_a.1
  463.8 12.3 %collective-permute-done.87 = bf16[8,192,256]{2,1,0:T(8,128)(2,1)S(1)} collective-permute-done((bf16[8,192,256]{2,1,0:T(8,128)(2,1)S(1)}, bf16[8,192,256]{2,1,0:T(8,128)(2,1)S(1)}, u32[]{:S(2)}, u32[]{:S(2)}) %collective-permute-start.87) | collective-permute-done | bytes 786464 | tf_op jit(solution)/shard_map/ppermute | solution.py:46
  478.2 5.2 collective-permute-done.103
  485.7 7.4 %collective-permute-done.92 = bf16[4,192,256]{2,1,0:T(8,128)(2,1)S(1)} collective-permute-done((bf16[4,192,256]{2,1,0:T(8,128)(2,1)S(1)}, bf16[4,192,256]{2,1,0:T(8,128)(2,1)S(1)}, u32[]{:S(2)}, u32[]{:S(2)}) %collective-permute-start.92) | collective-permute-done | bytes 393248 | tf_op jit(solution)/shard_map/ppermute | solution.py:46
  493.3 6.2 %collective-permute-done.89 = bf16[2,192,256]{2,1,0:T(8,128)(2,1)S(1)} collective-permute-done((bf16[2,192,256]{2,1,0:T(8,128)(2,1)S(1)}, bf16[2,192,256]{2,1,0:T(8,128)(2,1)S(1)}, u32[]{:S(2)}, u32[]{:S(2)}) %collective-permute-start.89) | collective-permute-done | bytes 196640 | tf_op jit(solution)/shard_map/ppermute | solution.py:46
  499.6 5.9 %collective-permute-done.93 = bf16[2,192,256]{2,1,0:T(8,128)(2,1)S(1)} collective-permute-done((bf16[2,192,256]{2,1,0:T(8,128)(2,1)S(1)}, bf16[2,192,256]{2,1,0:T(8,128)(2,1)S(1)}, u32[]{:S(2)}, u32[]{:S(2)}) %collective-permute-start.93) | collective-permute-done | bytes 196640 | tf_op jit(solution)/shard_map/ppermute | solution.py:46
  505.5 7.3 %collective-permute-done.90 = bf16[1,192,256]{2,1,0:T(8,128)(2,1)S(1)} collective-permute-done((bf16[1,192,256]{2,1,0:T(8,128)(2,1)S(1)}, bf16[1,192,256]{2,1,0:T(8,128)(2,1)S(1)}, u32[]{:S(2)}, u32[]{:S(2)}) %collective-permute-start.90) | collective-permute-done | bytes 98336 | tf_op jit(solution)/shard_map/ppermute | solution.py:46
  512.9 5.5 collective-permute-done.94
  (607 shorter events, 340.0 us)
Async XLA Ops:
  7.2 139.7 %all-gather.2.cloned.1.call-start = ((), (), s32[]{:S(2)}) async-start(), calls=%async_computation | async-start | bytes 8650752 | tf_op jit(solution)/shard_map/all_gather | solution.py:748
  11.1 11.8 %collective-permute-start.2 = (bf16[1,192,256]{2,1,0:T(8,128)(2,1)S(1)}, bf16[1,192,256]{2,1,0:T(8,128)(2,1)S(1)}, u32[]{:S(2)}, u32[]{:S(2)}) collective-permute-start(bf16[1,192,256]{2,1,0:T(8,128)(2,1)S(1)} %get-tuple-element.510.refs_2_), channel_id=1, source_target_pairs={{0,8},{1,9},{2,10},{3,11},{4,12},{5,13},{6,14},{7,15},{8,0},{9,1},... | collective-permute-start | bytes 294920 | tf_op jit(solution)/shard_map/ppermute | solution.py:46
  53.4 24.1 %collective-permute-start.12 = (bf16[8,192,256]{2,1,0:T(8,128)(2,1)}, bf16[8,192,256]{2,1,0:T(8,128)(2,1)}, u32[]{:S(2)}, u32[]{:S(2)}) collective-permute-start(bf16[8,192,256]{2,1,0:T(8,128)(2,1)} %get-tuple-element.256.refs_0_), channel_id=1, source_target_pairs={{0,16},{16,0},{1,17},{17,1},{2,18},{18,2},{3,19},{19,3},{4,20},{20... | collective-permute-start | bytes 2359304 | tf_op jit(solution)/shard_map/ppermute | solution.py:71
  53.4 22.8 %collective-permute-start.7 = (bf16[8,192,256]{2,1,0:T(8,128)(2,1)}, bf16[8,192,256]{2,1,0:T(8,128)(2,1)}, u32[]{:S(2)}, u32[]{:S(2)}) collective-permute-start(bf16[8,192,256]{2,1,0:T(8,128)(2,1)} %get-tuple-element.256.refs_0_), channel_id=1, source_target_pairs={{0,1},{1,0},{2,3},{3,2},{4,5},{5,4},{6,7},{7,6},{8,9},{9,8},{10,11... | collective-permute-start | bytes 2359304 | tf_op jit(solution)/shard_map/ppermute | solution.py:46
  55.1 21.8 %collective-permute-start.8 = (bf16[8,192,256]{2,1,0:T(8,128)(2,1)}, bf16[8,192,256]{2,1,0:T(8,128)(2,1)}, u32[]{:S(2)}, u32[]{:S(2)}) collective-permute-start(bf16[8,192,256]{2,1,0:T(8,128)(2,1)} %get-tuple-element.257.refs_2_), channel_id=1, source_target_pairs={{0,2},{1,3},{2,0},{3,1},{4,6},{5,7},{6,4},{7,5},{8,10},{9,11},{10,... | collective-permute-start | bytes 2359304 | tf_op jit(solution)/shard_map/ppermute | solution.py:46
  56.5 13.1 %collective-permute-start.9 = (bf16[1,192,256]{2,1,0:T(8,128)(2,1)S(1)}, bf16[1,192,256]{2,1,0:T(8,128)(2,1)}, u32[]{:S(2)}, u32[]{:S(2)}) collective-permute-start(bf16[1,192,256]{2,1,0:T(8,128)(2,1)S(1)} %get-tuple-element.258.refs_0_), channel_id=1, source_target_pairs={{0,8},{1,9},{2,10},{3,11},{4,12},{5,13},{6,14},{7,15},{8,0},{9,1},... | collective-permute-start | bytes 294920 | tf_op jit(solution)/shard_map/ppermute | solution.py:46
  89.0 12.7 %collective-permute-start.19 = (bf16[2,192,256]{2,1,0:T(8,128)(2,1)S(1)}, bf16[2,192,256]{2,1,0:T(8,128)(2,1)S(1)}, u32[]{:S(2)}, u32[]{:S(2)}) collective-permute-start(bf16[2,192,256]{2,1,0:T(8,128)(2,1)S(1)} %get-tuple-element.273.refs_0_), channel_id=1, source_target_pairs={{0,4},{1,5},{2,6},{3,7},{4,0},{5,1},{6,2},{7,3},{8,12},{9,13},{10,... | collective-permute-start | bytes 589832 | tf_op jit(solution)/shard_map/ppermute | solution.py:46
  91.5 14.4 %collective-permute-start.20 = (bf16[2,192,256]{2,1,0:T(8,128)(2,1)S(1)}, bf16[2,192,256]{2,1,0:T(8,128)(2,1)S(1)}, u32[]{:S(2)}, u32[]{:S(2)}) collective-permute-start(bf16[2,192,256]{2,1,0:T(8,128)(2,1)S(1)} %get-tuple-element.274.refs_2_), channel_id=1, source_target_pairs={{0,4},{1,5},{2,6},{3,7},{4,0},{5,1},{6,2},{7,3},{8,12},{9,13},{10,... | collective-permute-start | bytes 589832 | tf_op jit(solution)/shard_map/ppermute | solution.py:46
  107.8 12.0 %collective-permute-start.21 = (f32[40,512]{1,0:T(8,128)S(1)}, f32[40,512]{1,0:T(8,128)S(1)}, u32[]{:S(2)}, u32[]{:S(2)}) collective-permute-start(f32[40,512]{1,0:T(8,128)S(1)} %add.433), channel_id=1, source_target_pairs={{0,8},{1,9},{2,10},{3,11},{4,12},{5,13},{6,14},{7,15},{8,0},{9,1},... | collective-permute-start | bytes 245768 | tf_op jit(solution)/shard_map/ppermute | solution.py:46
  110.5 24.9 %collective-permute-start.25 = (bf16[4,192,256]{2,1,0:T(8,128)(2,1)}, bf16[4,192,256]{2,1,0:T(8,128)(2,1)S(1)}, u32[]{:S(2)}, u32[]{:S(2)}) collective-permute-start(bf16[4,192,256]{2,1,0:T(8,128)(2,1)} %copy-done.32), channel_id=1, source_target_pairs={{0,2},{1,3},{2,0},{3,1},{4,6},{5,7},{6,4},{7,5},{8,10},{9,11},{10,... | collective-permute-start | bytes 1179656 | tf_op jit(solution)/shard_map/ppermute | solution.py:46
  111.7 23.7 %collective-permute-start.26 = (bf16[4,192,256]{2,1,0:T(8,128)(2,1)}, bf16[4,192,256]{2,1,0:T(8,128)(2,1)S(1)}, u32[]{:S(2)}, u32[]{:S(2)}) collective-permute-start(bf16[4,192,256]{2,1,0:T(8,128)(2,1)} %copy-done.34), channel_id=1, source_target_pairs={{0,1},{1,0},{2,3},{3,2},{4,5},{5,4},{6,7},{7,6},{8,9},{9,8},{10,11... | collective-permute-start | bytes 1179656 | tf_op jit(solution)/shard_map/ppermute | solution.py:46
  136.6 23.5 %collective-permute-start.32 = (bf16[8,192,256]{2,1,0:T(8,128)(2,1)}, bf16[8,192,256]{2,1,0:T(8,128)(2,1)}, u32[]{:S(2)}, u32[]{:S(2)}) collective-permute-start(bf16[8,192,256]{2,1,0:T(8,128)(2,1)} %get-tuple-element.305.refs_0_), channel_id=1, source_target_pairs={{0,1},{1,0},{2,3},{3,2},{4,5},{5,4},{6,7},{7,6},{8,9},{9,8},{10,11... | collective-permute-start | bytes 2359304 | tf_op jit(solution)/shard_map/ppermute | solution.py:46
  137.6 22.4 %collective-permute-start.33 = (bf16[8,192,256]{2,1,0:T(8,128)(2,1)}, bf16[8,192,256]{2,1,0:T(8,128)(2,1)}, u32[]{:S(2)}, u32[]{:S(2)}) collective-permute-start(bf16[8,192,256]{2,1,0:T(8,128)(2,1)} %get-tuple-element.307.refs_2_), channel_id=1, source_target_pairs={{0,2},{1,3},{2,0},{3,1},{4,6},{5,7},{6,4},{7,5},{8,10},{9,11},{10,... | collective-permute-start | bytes 2359304 | tf_op jit(solution)/shard_map/ppermute | solution.py:46
  160.1 11.8 %collective-permute-start.34 = (bf16[8,192,256]{2,1,0:T(8,128)(2,1)}, bf16[8,192,256]{2,1,0:T(8,128)(2,1)}, u32[]{:S(2)}, u32[]{:S(2)}) collective-permute-start(bf16[8,192,256]{2,1,0:T(8,128)(2,1)} %get-tuple-element.305.refs_0_), channel_id=1, source_target_pairs={{0,16},{16,0},{1,17},{17,1},{2,18},{18,2},{3,19},{19,3},{4,20},{20... | collective-permute-start | bytes 2359304 | tf_op jit(solution)/shard_map/ppermute | solution.py:71
  321.8 29.8 %collective-permute-start.71 = (bf16[8,192,256]{2,1,0:T(8,128)(2,1)S(1)}, bf16[8,192,256]{2,1,0:T(8,128)(2,1)S(1)}, u32[]{:S(2)}, u32[]{:S(2)}) collective-permute-start(bf16[8,192,256]{2,1,0:T(8,128)(2,1)S(1)} %get-tuple-element.388), channel_id=1, source_target_pairs={{0,1},{1,0},{2,3},{3,2},{4,5},{5,4},{6,7},{7,6},{8,9},{9,8},{10,11... | collective-permute-start | bytes 2359304 | tf_op jit(solution)/shard_map/ppermute | solution.py:46
  322.7 28.9 %collective-permute-start.72 = (bf16[8,192,256]{2,1,0:T(8,128)(2,1)S(1)}, bf16[8,192,256]{2,1,0:T(8,128)(2,1)S(1)}, u32[]{:S(2)}, u32[]{:S(2)}) collective-permute-start(bf16[8,192,256]{2,1,0:T(8,128)(2,1)S(1)} %get-tuple-element.390), channel_id=1, source_target_pairs={{0,2},{1,3},{2,0},{3,1},{4,6},{5,7},{6,4},{7,5},{8,10},{9,11},{10,... | collective-permute-start | bytes 2359304 | tf_op jit(solution)/shard_map/ppermute | solution.py:46
  358.4 17.1 %collective-permute-start.77 = (bf16[2048,1024]{1,0:T(8,128)(2,1)}, bf16[2048,1024]{1,0:T(8,128)(2,1)S(1)}, u32[]{:S(2)}, u32[]{:S(2)}) collective-permute-start(bf16[2048,1024]{1,0:T(8,128)(2,1)} %get-tuple-element.421), channel_id=1, source_target_pairs={{0,16},{16,0},{1,17},{17,1},{2,18},{18,2},{3,19},{19,3},{4,20},{20... | collective-permute-start | bytes 12582920 | tf_op jit(solution)/shard_map/ppermute | solution.py:71
  371.4 25.2 %collective-permute-start.81 = (bf16[2,192,256]{2,1,0:T(8,128)(2,1)}, bf16[2,192,256]{2,1,0:T(8,128)(2,1)}, u32[]{:S(2)}, u32[]{:S(2)}) collective-permute-start(bf16[2,192,256]{2,1,0:T(8,128)(2,1)} %get-tuple-element.502), channel_id=1, source_target_pairs={{0,4},{1,5},{2,6},{3,7},{4,0},{5,1},{6,2},{7,3},{8,12},{9,13},{10,... | collective-permute-start | bytes 589832 | tf_op jit(solution)/shard_map/ppermute | solution.py:46
  373.8 22.8 %collective-permute-start.82 = (bf16[2,192,256]{2,1,0:T(8,128)(2,1)}, bf16[2,192,256]{2,1,0:T(8,128)(2,1)}, u32[]{:S(2)}, u32[]{:S(2)}) collective-permute-start(bf16[2,192,256]{2,1,0:T(8,128)(2,1)} %get-tuple-element.500), channel_id=1, source_target_pairs={{0,4},{1,5},{2,6},{3,7},{4,0},{5,1},{6,2},{7,3},{8,12},{9,13},{10,... | collective-permute-start | bytes 589832 | tf_op jit(solution)/shard_map/ppermute | solution.py:46
  390.3 23.2 %collective-permute-start.83 = (bf16[8,64,1024]{2,1,0:T(8,128)(2,1)S(1)}, bf16[8,64,1024]{2,1,0:T(8,128)(2,1)S(1)}, u32[]{:S(2)}, u32[]{:S(2)}) collective-permute-start(bf16[8,64,1024]{2,1,0:T(8,128)(2,1)S(1)} %copy-done.55), channel_id=1, source_target_pairs={{0,1},{1,0},{2,3},{3,2},{4,5},{5,4},{6,7},{7,6},{8,9},{9,8},{10,11... | collective-permute-start | bytes 3145736 | tf_op jit(solution)/shard_map/ppermute | solution.py:46
  392.7 22.8 %collective-permute-start.84 = (bf16[8,64,1024]{2,1,0:T(8,128)(2,1)S(1)}, bf16[8,64,1024]{2,1,0:T(8,128)(2,1)S(1)}, u32[]{:S(2)}, u32[]{:S(2)}) collective-permute-start(bf16[8,64,1024]{2,1,0:T(8,128)(2,1)S(1)} %copy-done.53), channel_id=1, source_target_pairs={{0,2},{1,3},{2,0},{3,1},{4,6},{5,7},{6,4},{7,5},{8,10},{9,11},{10,... | collective-permute-start | bytes 3145736 | tf_op jit(solution)/shard_map/ppermute | solution.py:46
  420.3 32.2 %collective-permute-start.86 = (bf16[6144,256]{1,0:T(8,128)(2,1)}, bf16[6144,256]{1,0:T(8,128)(2,1)}, u32[]{:S(2)}, u32[]{:S(2)}) collective-permute-start(bf16[6144,256]{1,0:T(8,128)(2,1)} %get-tuple-element.455), channel_id=1, source_target_pairs={{0,16},{16,0},{1,17},{17,1},{2,18},{18,2},{3,19},{19,3},{4,20},{20... | collective-permute-start | bytes 9437192 | tf_op jit(solution)/shard_map/ppermute | solution.py:71
  421.8 96.8 %collective-permute-start.106 = (f32[6,2048]{1,0:T(8,128)}, f32[6,2048]{1,0:T(8,128)}, u32[]{:S(2)}, u32[]{:S(2)}) collective-permute-start(f32[6,2048]{1,0:T(8,128)} %stack.17), channel_id=1, source_target_pairs={{0,16},{16,0},{1,17},{17,1},{2,18},{18,2},{3,19},{19,3},{4,20},{20... | collective-permute-start | bytes 147464 | tf_op jit(solution)/shard_map/ppermute | solution.py:71
  423.9 25.0 %collective-permute-start.98 = (bf16[4,64,1024]{2,1,0:T(8,128)(2,1)}, bf16[4,64,1024]{2,1,0:T(8,128)(2,1)}, u32[]{:S(2)}, u32[]{:S(2)}) collective-permute-start(bf16[4,64,1024]{2,1,0:T(8,128)(2,1)} %get-tuple-element.463), channel_id=1, source_target_pairs={{0,2},{1,3},{2,0},{3,1},{4,6},{5,7},{6,4},{7,5},{8,10},{9,11},{10,... | collective-permute-start | bytes 1572872 | tf_op jit(solution)/shard_map/ppermute | solution.py:46
  433.4 16.9 %collective-permute-start.101 = (bf16[4,64,1024]{2,1,0:T(8,128)(2,1)}, bf16[4,64,1024]{2,1,0:T(8,128)(2,1)S(1)}, u32[]{:S(2)}, u32[]{:S(2)}) collective-permute-start(bf16[4,64,1024]{2,1,0:T(8,128)(2,1)} %get-tuple-element.465), channel_id=1, source_target_pairs={{0,1},{1,0},{2,3},{3,2},{4,5},{5,4},{6,7},{7,6},{8,9},{9,8},{10,11... | collective-permute-start | bytes 1572872 | tf_op jit(solution)/shard_map/ppermute | solution.py:46
  450.5 13.2 %collective-permute-start.102 = (bf16[2,64,1024]{2,1,0:T(8,128)(2,1)S(1)}, bf16[2,64,1024]{2,1,0:T(8,128)(2,1)S(1)}, u32[]{:S(2)}, u32[]{:S(2)}) collective-permute-start(bf16[2,64,1024]{2,1,0:T(8,128)(2,1)S(1)} %slice.537), channel_id=1, source_target_pairs={{0,4},{1,5},{2,6},{3,7},{4,0},{5,1},{6,2},{7,3},{8,12},{9,13},{10,... | collective-permute-start | bytes 786440 | tf_op jit(solution)/shard_map/ppermute | solution.py:46
  457.5 18.6 %collective-permute-start.87 = (bf16[8,192,256]{2,1,0:T(8,128)(2,1)S(1)}, bf16[8,192,256]{2,1,0:T(8,128)(2,1)S(1)}, u32[]{:S(2)}, u32[]{:S(2)}) collective-permute-start(bf16[8,192,256]{2,1,0:T(8,128)(2,1)S(1)} %get-tuple-element.457), channel_id=1, source_target_pairs={{0,1},{1,0},{2,3},{3,2},{4,5},{5,4},{6,7},{7,6},{8,9},{9,8},{10,11... | collective-permute-start | bytes 2359304 | tf_op jit(solution)/shard_map/ppermute | solution.py:46
  458.9 17.8 %collective-permute-start.91 = (bf16[8,192,256]{2,1,0:T(8,128)(2,1)S(1)}, bf16[8,192,256]{2,1,0:T(8,128)(2,1)S(1)}, u32[]{:S(2)}, u32[]{:S(2)}) collective-permute-start(bf16[8,192,256]{2,1,0:T(8,128)(2,1)S(1)} %get-tuple-element.459), channel_id=1, source_target_pairs={{0,2},{1,3},{2,0},{3,1},{4,6},{5,7},{6,4},{7,5},{8,10},{9,11},{10,... | collective-permute-start | bytes 2359304 | tf_op jit(solution)/shard_map/ppermute | solution.py:46
  460.1 59.3 %collective-permute-start.105 = (f32[8,512]{1,0:T(8,128)S(1)}, f32[8,512]{1,0:T(8,128)S(1)}, u32[]{:S(2)}, u32[]{:S(2)}) collective-permute-start(f32[8,512]{1,0:T(8,128)S(1)} %copy-done.72), channel_id=1, source_target_pairs={{0,16},{16,0},{1,17},{17,1},{2,18},{18,2},{3,19},{19,3},{4,20},{20... | collective-permute-start | bytes 49160 | tf_op jit(solution)/shard_map/ppermute | solution.py:71
  463.7 14.3 %collective-permute-start.100 = (bf16[1,64,1024]{2,1,0:T(8,128)(2,1)S(1)}, bf16[1,64,1024]{2,1,0:T(8,128)(2,1)S(1)}, u32[]{:S(2)}, u32[]{:S(2)}) collective-permute-start(bf16[1,64,1024]{2,1,0:T(8,128)(2,1)S(1)} %slice.535), channel_id=1, source_target_pairs={{0,8},{1,9},{2,10},{3,11},{4,12},{5,13},{6,14},{7,15},{8,0},{9,1},... | collective-permute-start | bytes 393224 | tf_op jit(solution)/shard_map/ppermute | solution.py:46
  478.1 55.0 %collective-permute-start.85 = (bf16[4,384,512]{2,1,0:T(8,128)(2,1)S(1)}, bf16[4,384,512]{2,1,0:T(8,128)(2,1)S(1)}, u32[]{:S(2)}, u32[]{:S(2)}) collective-permute-start(bf16[4,384,512]{2,1,0:T(8,128)(2,1)S(1)} %slice_bitcast_fusion), channel_id=1, source_target_pairs={{0,16},{16,0},{1,17},{17,1},{2,18},{18,2},{3,19},{19,3},{4,20},{20... | collective-permute-start | bytes 4718600 | tf_op jit(solution)/shard_map/ppermute | solution.py:71
  485.6 34.1 %collective-permute-start.104 = (f32[64,1024]{1,0:T(8,128)S(1)}, f32[64,1024]{1,0:T(8,128)S(1)}, u32[]{:S(2)}, u32[]{:S(2)}) collective-permute-start(f32[64,1024]{1,0:T(8,128)S(1)} %get-tuple-element.488), channel_id=1, source_target_pairs={{0,16},{16,0},{1,17},{17,1},{2,18},{18,2},{3,19},{19,3},{4,20},{20... | collective-permute-start | bytes 786440 | tf_op jit(solution)/shard_map/ppermute | solution.py:71
  (169 other events, 1519.5 us)
Sparse Core Ops, SparseCore 0:
  48.6 96.7 all-gather.1

commit v3 on v2

--- a/solution.py
+++ b/solution.py
@@ -1,3 +1,5 @@
+import functools
+
 import jax
 import jax.numpy as jnp
 import numpy as np
@@ -26,7 +28,8 @@
 DECAY = 5e-05
 TRUST = 0.001
 RATE = 29.0
-PRECISE = lax.Precision.HIGHEST
+NARROW_BOUNDS = (C_IN, C_IN + 9 * C_MID, C_IN + 9 * C_MID + C_OUT)
+WIDE_BOUNDS = (C_MID, C_MID + C_IN)
 BFLOAT = jnp.bfloat16
 SINGLE = jnp.float32
 MIB = 1024 * 1024
@@ -34,7 +37,7 @@
 MICROSECONDS = {
     "prep": 5, "a1": 3, "a2": 5, "as": 4.5, "a3": 4, "a4": 4.7, "a5": 4, "a6": 3.7, "head": 5.3, "g5": 5.2, "g4": 5.4, "gy": 7,
     "g2": 7.3, "g1": 8, "g0": 3, "gx": 6.4, "dxs": 5, "dw1": 3.4, "dw2": 2.1, "dw3": 2.9, "dws": 2.9, "dw4a": 1.7, "dw4b": 1.9,
-    "dw5": 1.5, "dw6": 2.8, "place_out": 3.4, "place_grad": 5, "wa": 3, "wb": 3, "turn": 1.7, "keep": 1.7,
+    "dw5": 1.5, "dw6": 2.8, "place_out": 3.4, "place_grad": 5, "wa": 3, "wb": 3, "turn": 1.7, "keep": 1.7, "halve": 1, "squares": 2, "update": 3,
 }
 
 
@@ -50,18 +53,20 @@
     return lax.optimization_barrier((value, after))[0]
 
 
-def dp_sum(value, fillers=()):
+def dp_sum(value, fillers=(), first=None):
     size = lax.axis_size("dp")
+    bits = [1 << k for k in range(size.bit_length() - 1)]
+    if first in bits:
+        at = bits.index(first)
+        bits = bits[at:] + bits[:at]
     results = []
-    step = 1
-    while step < size:
-        got = exchange(value, step)
+    for bit in bits:
+        got = exchange(value, bit)
         if len(results) < len(fillers):
             result = fillers[len(results)](value)
             got, result = lax.optimization_barrier((got, result))
             results.append(result)
         value = value + got
-        step *= 2
     for filler in fillers[len(results) :]:
         results.append(filler(value))
     return value, results
@@ -123,11 +128,23 @@
     return (mask * ((rstd * gain) * (gz - first_row - xhat * second_row))).astype(BFLOAT)
 
 
-def k_prep(slot_ref, img_ref, perm_ref, mask_ref, out_ref):
+def k_prep(core_ref, assign_ref, height_ref, width_ref, img_ref, perm_ref, out_ref, mask_ref, count_ref):
+    slot = pl.program_id(0)
+    image = assign_ref[core_ref[0] * SLOTS + slot]
+    pixel = lax.broadcasted_iota(jnp.int32, (PIX, 1), 0)
+    inside = ((pixel & (HB - 1)) < height_ref[image]) & (pixel < width_ref[image] * HB)
+    mask = jnp.where(inside, 1.0, 0.0).astype(SINGLE)
+    mask_ref[...] = mask
     planes = dot(perm_ref[...], img_ref[0])
-    mask = mask_ref[...]
     for k in range(4):
         out_ref[k] = (planes[k * PIX : (k + 1) * PIX] * mask).astype(BFLOAT)
+    column = lax.broadcasted_iota(jnp.int32, count_ref.shape, 1)
+    counts = jnp.zeros(count_ref.shape, jnp.int32)
+    for m in range(4):
+        pair = (assign_ref[2 * m], assign_ref[2 * m + 1])
+        total = sum(height_ref[k] * width_ref[k] for k in pair)
+        counts = jnp.where(column == m, total, counts)
+    count_ref[...] = counts.astype(SINGLE)
 
 
 def k_first(x_ref, w_ref, a_ref, sum_ref):
@@ -507,18 +524,37 @@
     copy.wait()
 
 
-def k_join(*refs):
-    ins, outs, sems = refs[:4], refs[-3:-1], refs[-1]
+def k_join(n_in, n_out, *refs):
+    stayed, came = refs[:n_in], refs[n_in : 2 * n_in]
+    outs, sems = refs[-1 - n_out : -1], refs[-1]
     copies = []
     for which in range(2):
-        for side in range(2):
-            source = ins[2 * which + side]
+        target = outs[0].at[which] if n_out == 1 else outs[which]
+        for side, sources in enumerate((stayed, came)):
+            source = sources[0].at[which] if n_in == 1 else sources[which]
             size = source.shape[0]
-            copies.append(pltpu.make_async_copy(source, outs[which].at[pl.ds(side * size, size)], sems.at[len(copies)]))
+            copies.append(pltpu.make_async_copy(source, target.at[pl.ds(side * size, size)], sems.at[len(copies)]))
     for copy in copies:
         copy.start()
     for copy in copies:
         copy.wait()
+
+
+def k_halve(*refs):
+    for which in range(2):
+        keep0, keep1, came0, came1 = refs[4 * which : 4 * which + 4]
+        stay = (keep0[0].astype(SINGLE) + came0[0].astype(SINGLE)).astype(BFLOAT)
+        sent = (keep1[0].astype(SINGLE) + came1[0].astype(SINGLE)).astype(BFLOAT)
+        if len(refs) == 10:
+            refs[8][which, 0], refs[9][which, 0] = stay, sent
+        else:
+            refs[8 + 2 * which][0], refs[9 + 2 * which][0] = stay, sent
+
+
+def k_halve_both(keep_ref, came_ref, stay_ref, sent_ref):
+    total = (keep_ref[...].astype(SINGLE) + came_ref[...].astype(SINGLE)).astype(BFLOAT)
+    half = total.shape[1] // 2
+    stay_ref[...], sent_ref[...] = total[:, :half], total[:, half:]
 
 
 def k_gather(me_ref, *refs):
@@ -549,9 +585,57 @@
         out_ref[0] = (own_ref[...].astype(SINGLE) + got_ref[...].astype(SINGLE)).astype(BFLOAT)
 
 
+def group_of(rows, start, bounds):
+    index = lax.broadcasted_iota(jnp.int32, (rows, 1), 0) + start
+    return sum((index >= bound).astype(jnp.int32) for bound in bounds)
+
+
+def k_squares(start_ref, *refs):
+    out_ref = refs[-1]
+    lane = lax.broadcasted_iota(jnp.int32, (1, 128), 1)
+    out_ref[...] = jnp.zeros_like(out_ref)
+    for k in range(2):
+        squares = [jnp.sum(ref[...] * ref[...], axis=1, keepdims=True) for ref in refs[4 * k : 4 * k + 4]]
+        total = jnp.zeros((1, 128), SINGLE)
+        for which, bounds in enumerate((NARROW_BOUNDS, WIDE_BOUNDS)):
+            group = group_of(squares[which].shape[0], start_ref[which], bounds)
+            for g in range(len(bounds) + 1):
+                part_sum = jnp.sum(jnp.where(group == g, squares[which], 0.0))
+                total = total + jnp.where(lane == 4 * which + g, part_sum, 0.0)
+        for rows, first in ((squares[2], 7), (squares[3], 15)):
+            row = lax.broadcasted_iota(jnp.int32, (rows.shape[0], 128), 0)
+            column = lax.broadcasted_iota(jnp.int32, (rows.shape[0], 128), 1)
+            total = total + jnp.sum(jnp.where(column == row + first, rows, 0.0), axis=0, keepdims=True)
+        out_ref[k : k + 1, :] = total
+
+
+def k_update(start_ref, square_ref, *refs):
+    step = pl.program_id(0)
+    norms = jnp.sqrt(square_ref[...])
+    weight_norm, grad_norm = norms[0:1], norms[1:2]
+    ratio = TRUST * weight_norm / (grad_norm + DECAY * weight_norm)
+    lane = lax.broadcasted_iota(jnp.int32, (1, 128), 1)
+    for k in range(4):
+        weight, grad = refs[k][...], refs[4 + k][...]
+        rows = weight.shape[0]
+        if k < 2:
+            bounds = (NARROW_BOUNDS, WIDE_BOUNDS)[k]
+            group = group_of(rows, start_ref[k] + step * rows, bounds)
+            scale = jnp.zeros((rows, 1), SINGLE)
+            for g in range(len(bounds) + 1):
+                scale = jnp.where(group == g, jnp.sum(jnp.where(lane == 4 * k + g, ratio, 0.0)), scale)
+        else:
+            row = lax.broadcasted_iota(jnp.int32, (rows, 128), 0)
+            column = lax.broadcasted_iota(jnp.int32, (rows, 128), 1)
+            scale = jnp.sum(jnp.where(column == row + (7, 15)[k - 2], ratio, 0.0), axis=1, keepdims=True)
+        moment = MOMENTUM * refs[8 + k][...] + RATE * scale * (grad + DECAY * weight)
+        refs[12 + k][...] = moment
+        refs[16 + k][...] = weight - moment
+
+
 def full(shape):
     zeros = (0,) * len(shape)
-    return pl.BlockSpec(tuple(shape), lambda *_: zeros)
+    return pl.BlockSpec(tuple(shape), lambda *_: zeros, pipeline_mode=pl.Buffered(1))
 
 
 SCALARS = pl.BlockSpec(memory_space=pltpu.SMEM)
@@ -610,14 +694,6 @@
     return jnp.asarray(table, BFLOAT)
 
 
-def group_table(start_index, rows_local, bounds):
-    global_rows = start_index * rows_local + jnp.arange(rows_local, dtype=jnp.int32)
-    group_ids = jnp.zeros((rows_local,), jnp.int32)
-    for boundary in bounds:
-        group_ids = group_ids + (global_rows >= boundary).astype(jnp.int32)
-    return (group_ids[:, None] == jnp.arange(len(bounds) + 1, dtype=jnp.int32)[None, :]).astype(SINGLE)
-
-
 def rounded(value):
     return lax.reduce_precision(value, 8, 7)
 
@@ -642,22 +718,30 @@
     )
 
 
-def halved(keep, got):
-    total = keep.astype(SINGLE) + got.astype(SINGLE)
-    half = total.shape[0] // 2
-    return total[:half].astype(BFLOAT), total[half:].astype(BFLOAT)
-
-
-def added(keep, got):
-    return keep[0].astype(SINGLE) + got[0].astype(SINGLE)
-
-
-def halve(keep, send, bits, came=None):
-    for bit in bits:
-        got, came = exchange(send, bit) if came is None else came, None
-        if keep.shape[0] > 1:
-            keep, send = halved(keep, got)
-    return added(keep, got)
+def halved(state, came, merge):
+    (keep0, _sent, keep1, _sent), (came0, came1) = state, came
+    count, block = keep0.shape[0] // 2, keep0.shape[1:]
+    low, high = (spec((1,) + block, lambda q, at=at: (q + at, 0, 0)) for at in (0, count))
+    if merge:
+        outs, out_spec = [vmem_of((2, count) + block, BFLOAT)] * 2, [spec((2, 1) + block, lambda q: (0, q, 0, 0))] * 2
+    else:
+        outs, out_spec = [vmem_of((count,) + block, BFLOAT)] * 4, [low] * 4
+    return tuple(call(
+        k_halve, "halve", (count,), [low, high] * 4, out_spec, outs, [], (keep0, keep0, came0, came0, keep1, keep1, came1, came1), vmem=4,
+    ))
+
+
+def halved_both(state, came):
+    shape = state[0].shape
+    half = (2, shape[1] // 2) + shape[2:]
+    return tuple(call(
+        k_halve_both, "halve", (1,), [full(shape)] * 2, [full(half)] * 2, [vmem_of(half, BFLOAT)] * 2, [], (state[0], came), vmem=4,
+    ))
+
+
+def added(state, came):
+    total = state[0].astype(SINGLE) + came.astype(SINGLE)
+    return total[0, 0], total[1, 0]
 
 
 def scatter_plain(keep, got, block, by_rows):
@@ -686,12 +770,14 @@
     return [tuple(swap_pipe(a) for a in pair) for pair in parts]
 
 
-def join_two(stayed, came, token):
-    pieces = (stayed[0], came[0], stayed[1], came[1])
-    shape = (2 * stayed[0].shape[0],) + stayed[0].shape[1:]
+def join_parts(stayed, came, token, n_out):
+    n_in = len(stayed)
+    shape = stayed[0].shape[-3:]
+    shape = (2 * shape[0],) + shape[1:]
+    outs = [vmem_of(shape, BFLOAT)] * 2 if n_out == 2 else [vmem_of((2,) + shape, BFLOAT)]
     return call(
-        k_join, "join", (), [ANYWHERE] * 5, [ANYWHERE] * 2, [vmem_of(shape, BFLOAT)] * 2,
-        [pltpu.SemaphoreType.DMA((4,))], pieces + (token,), vmem=2,
+        functools.partial(k_join, n_in, n_out), "join", (), [ANYWHERE] * (2 * n_in + 1), [ANYWHERE] * n_out, outs,
+        [pltpu.SemaphoreType.DMA((4,))], tuple(stayed) + tuple(came) + (token,), vmem=2,
     )
 
 
@@ -727,43 +813,36 @@
         sent = swap_pipe(jnp.where(core == 0, own_narrow[:, half_n:], own_narrow[:, :half_n]))
         kept = jnp.where(core == 0, own_narrow[:, :half_n], own_narrow[:, half_n:])
         mine_a, mine_b = jnp.where(core == 0, kept, sent), jnp.where(core == 0, sent, kept)
-        a0, a1 = mine_a[None, :part_n], mine_a[None, part_n:]
-        b0, b1 = mine_b[None, :part_n], mine_b[None, part_n:]
-        got = lax.optimization_barrier((exchange(a0, 8), exchange(a1, 8)))
-        a0, a1 = join_two((a0, a1), got, got[1])
-        got = lax.optimization_barrier((exchange(a0, 4), exchange(a1, 4)))
-        a0, a1 = join_two((a0, a1), got, got[1])
-        got = lax.optimization_barrier((exchange(a0, 2), exchange(a1, 1)))
-        a0, a1 = join_two((a0, a1), got, got[1])
-        third_done = a1
-        last0, last1 = exchange(a0, 1), exchange(a1, 2)
+        a, b = (mine.reshape(2, 1, part_n, half_n) for mine in (mine_a, mine_b))
+        (a,) = join_parts((a,), (exchange(a, 8),), a, 1)
+        a0, a1 = join_parts((a,), (exchange(a, 4),), a, 2)
+        b = pin(b, a1)
+        got, got_b = lax.optimization_barrier(((exchange(a0, 2), exchange(a1, 1)), exchange(b, 8)))
+        a0, a1 = join_parts((a0, a1), got, got[1], 2)
+        (b,) = join_parts((b,), (got_b,), got_b, 1)
         stay_a = swap_all([(a0,), (a1,)])
-        b0, b1 = pin((b0, b1), third_done)
-        got = exchange(b0, 8), exchange(b1, 8)
-        own_wide = pin(own_wide, third_done)
+        own_wide = pin(own_wide, a1)
+        wide = lax.all_gather(own_wide, ("pipe", "dp"), axis=0, tiled=True)
     else:
         narrow = lax.all_gather(own_narrow, ("pipe", "dp"), axis=0, tiled=True)
         narrow_a, narrow_b = narrow[: R_N // 2], narrow[R_N // 2 :]
-        third_done = narrow
-    wide = lax.all_gather(own_wide, ("pipe", "dp"), axis=0, tiled=True)
-
-    own_heights, own_widths, own_assign = pin((heights, widths, assign), third_done)
-    order = own_assign[0].reshape(2, SLOTS)
+        wide = lax.all_gather(own_wide, ("pipe", "dp"), axis=0, tiled=True)
+
+    perm = permutation()
+    core_row = core[None].astype(jnp.int32)
+    x, mask, count_rows = call(
+        k_prep, "prep", (SLOTS,),
+        [spec((1, 4 * PIX, C_IN), lambda s, core, order, *_: (order[core[0] * SLOTS + s], 0, 0)), full((4 * PIX, 4 * PIX))],
+        [spec((4, PIX, C_IN), lambda s, *_: (0, s, 0)), spec((PIX, 1), lambda s, *_: (s, 0)), full((4, C_MID))],
+        [vmem_of((4, ROWS, C_IN), BFLOAT), vmem_of((ROWS, 1)), shape_of((4, C_MID))], [],
+        (core_row, assign[0], heights, widths, in_hbm(images.reshape(IMG_DEV, 4 * PIX, C_IN)), in_hbm(perm)), prefetch=4, vmem=7,
+    )
+    mask = in_vmem(mask)
+    order = assign[0].reshape(2, SLOTS)
     own_slots = lax.dynamic_index_in_dim(order, core, 0, keepdims=False)
     other_slots = lax.dynamic_index_in_dim(order, 1 - core, 0, keepdims=False)
-    slots = jnp.concatenate([own_slots, core[None].astype(jnp.int32), other_slots])
-    heights_own, widths_own = own_heights[own_slots], own_widths[own_slots]
-    inside = (jnp.arange(HB)[None, None, :] < heights_own[:, None, None]) & (jnp.arange(WB)[None, :, None] < widths_own[:, None, None])
-    mask = in_vmem(inside.astype(SINGLE).reshape(ROWS, 1))
-    perm = permutation()
-    x = call(
-        k_prep, "prep", (SLOTS,),
-        [spec((1, 4 * PIX, C_IN), lambda s, slot: (slot[s], 0, 0)), full((4 * PIX, 4 * PIX)), spec((PIX, 1), lambda s, slot: (s, 0))],
-        spec((4, PIX, C_IN), lambda s, slot: (0, s, 0)),
-        vmem_of((4, ROWS, C_IN), BFLOAT), [],
-        (slots, in_hbm(images.reshape(IMG_DEV, 4 * PIX, C_IN)), in_hbm(perm), mask), prefetch=1, vmem=10,
-    )
-    counts = jnp.sum((own_heights * own_widths)[own_assign[0]].reshape(4, 2), axis=1).astype(SINGLE)
+    slots = jnp.concatenate([own_slots, core_row, other_slots])
+
     mid_cols, wide_cols = bn_mid.shape[1], bn_wide.shape[1]
     tables = jnp.concatenate(
         [
@@ -771,16 +850,14 @@
             lax.dynamic_update_slice(jnp.zeros((6, C_OUT), SINGLE), rounded(bn_wide), (0, shard * wide_cols)).reshape(24, C_MID),
         ]
     )
-    tables = pin(tables, third_done)
     tables = tables + swap_pipe(tables)
-    tables = jnp.concatenate([tables, jnp.zeros((4, C_MID), SINGLE).at[0, :4].set(counts)])
+    tables = jnp.concatenate([tables, count_rows])
 
     held = {}
     if fast:
-        last0, last1, got, x, tables = lax.optimization_barrier((last0, last1, got, x, tables))
+        last0, last1, got_b, x, tables = lax.optimization_barrier((exchange(a0, 1), exchange(a1, 2), exchange(b, 4), x, tables))
         came_a = swap_all([(last0,), (last1,)])
-        own_b = join_two((b0, b1), got, got[1])
-        held["got"] = exchange(own_b[0], 4), exchange(own_b[1], 4)
+        part_b = join_parts((b,), (got_b,), got_b, 2)
         narrow_a = gather_blocks("wa", core, [(a0, last0), (a1, last1)], [u + v for u, v in zip(stay_a, came_a)], whole_n)
 
     def turn(feature, feature_spec, grid, shape, index):
@@ -799,7 +876,7 @@
         return call(
             k_grad, name, (tiles,), [feature_spec, grad_spec] + [ANYWHERE] * len(extra),
             [out_spec] * 2, [space(shape, BFLOAT)] * 2, [], (slots, feature, grad) + extra,
-            prefetch=1, vmem=9, aliases={3: 0, 4: 1} if bufs else {},
+            prefetch=1, vmem=7, aliases={3: 0, 4: 1} if bufs else {},
         )
 
     full_row = full((4, C_MID))
@@ -822,18 +899,18 @@
         [spec((1, ROWS, C_IN), lambda k: (k, 0, 0)), full((C_IN, C_MID))],
         [spec((1, ROWS, C_MID), lambda k: (k, 0, 0)), full_row],
         [hbm_of((4, ROWS, C_MID)), shape_of((4, C_MID))], [],
-        (in_vmem(x), in_vmem(narrow_a)), vmem=8,
-    )
-
-    def third_b(token):
+        (in_vmem(x), in_vmem(narrow_a)), vmem=6,
+    )
+
+    a1 = in_hbm(a1)
+    def second_part_b(token):
         if not fast:
             return token
-        big = join_two(own_b, pin(held["got"], token), token)
-        held["got"] = exchange(big[0], 2), exchange(big[1], 1)
-        return big
-
-    a1 = in_hbm(a1)
-    first_sum, (a_kept, x_kept, big_b) = dp_sum(jnp.concatenate([part1, tables]), [keep_in_hbm(narrow_a), keep_in_hbm(x), third_b])
+        part = pin(part_b, token)
+        held["got"] = exchange(part[0], 2), exchange(part[1], 1)
+        return token
+
+    first_sum, (a_kept, (x_kept, first_b), _unused) = dp_sum(jnp.concatenate([part1, tables]), [keep_in_hbm(narrow_a), lambda token: (keep_in_hbm(x)(token), part_b if fast else token), second_part_b])
     x_kept, a_kept = in_hbm(x_kept), in_hbm(a_kept)
     total1, tables = first_sum[:4], first_sum[4:]
     mid, table = tables[:8], tables[8:32].reshape(6, C_OUT)
@@ -846,7 +923,7 @@
         [spec((1, ROWS, C_IN), lambda k: (0, 0, 0)), spec((TILE, TILE), lambda k: (1, k)), spec((TILE, TILE), lambda k: (2, k))],
         [chunk, chunk_sum],
         [vmem_of((ROWS, C_OUT)), shape_of((4, C_OUT))], [],
-        (in_vmem(x), in_hbm(wide), in_hbm(wide)), vmem=8,
+        (in_vmem(x), in_hbm(wide), in_hbm(wide)), vmem=6,
     )
 
     def conv_weights(first, order_of):
@@ -861,19 +938,24 @@
         [full_mid, plane_pair, full_row],
         [vmem_of((ROWS, C_MID)), vmem_of((4, ROWS, C_MID), BFLOAT), shape_of((4, C_MID))],
         [pltpu.VMEM((2, PAD + ROWS + PAD, C_MID), SINGLE)] * 2,
-        (inv, total1, mid1, mask, a1) + (a_kept,) * 3, vmem=15,
+        (inv, total1, mid1, mask, a1) + (a_kept,) * 3, vmem=11,
     )
     a2 = in_vmem(a2)
 
-    def fourth_b(token):
+    def third_part_b(token):
         if not fast:
             return token
-        big = join_two(big_b, pin(held["got"], token), token)
-        held["got"] = exchange(big[0], 1), exchange(big[1], 2)
-        return big
+        held["big_b"] = join_parts(first_b, pin(held["got"], token), token, 2)
+        return held["big_b"]
+
+    def fourth_b(token):
+        if fast:
+            big = pin(held["big_b"], token)
+            held["got"] = exchange(big[0], 1), exchange(big[1], 2)
+        return token
 
     turn_h1 = turn(h1, spec((1, ROWS, C_MID), lambda k: (k, 0, 0)), (4,), (4 * C_MID, ROWS), lambda k: (k, 0))
-    total2, (h1_t, _unused, whole_b) = dp_sum(part2, [turn_h1, nothing, fourth_b])
+    total2, (h1_t, big_b, _unused) = dp_sum(part2, [turn_h1, third_part_b, fourth_b])
 
     def expand(name, a, total, tab, row):
         return call(
@@ -881,7 +963,7 @@
             [SCALARS, full_row, full_tab, full_mask, full_mid, spec((TILE, TILE), lambda k: (row, k))],
             [full_mid, chunk, chunk_sum],
             [vmem_of((ROWS, C_MID), BFLOAT), vmem_of((ROWS, C_OUT)), shape_of((4, C_OUT))], [],
-            (inv, total, tab, mask, a, in_hbm(wide)), vmem=8,
+            (inv, total, tab, mask, a, in_hbm(wide)), vmem=6,
         )
 
     h2, a3, part3 = expand("a3", a2, total2, mid2, 0)
@@ -890,7 +972,7 @@
     def swap_b(token):
         if not fast:
             return token
-        ready = pin(whole_b + held["got"], token)
+        ready = pin(tuple(big_b) + held["got"], token)
         return [(ready[0], ready[2]), (ready[1], ready[3])]
 
     def gather_b(token):
@@ -922,7 +1004,7 @@
         [SCALARS, chunk_sum, chunk_sum, chunk_tab, chunk_tab, full_mask, chunk, chunk, four_a, four_b],
         [chunk, full_mid, full_row],
         [vmem_of((ROWS, C_OUT), BFLOAT), vmem_of((ROWS, C_MID)), shape_of((4, C_MID))], [],
-        (inv, total3, total_s, tab3, tabs, mask, in_vmem(a3), in_vmem(a_s), a_kept, in_vmem(narrow_b)), vmem=10,
+        (inv, total3, total_s, tab3, tabs, mask, in_vmem(a3), in_vmem(a_s), a_kept, in_vmem(narrow_b)), vmem=8,
     )
     a4 = in_vmem(a4)
     def turn_x(q, start, into):
@@ -954,7 +1036,7 @@
         [full_mid, full_mid, full_row],
         [vmem_of((ROWS, C_MID)), vmem_of((ROWS, C_MID), BFLOAT), shape_of((4, C_MID))],
         [pltpu.VMEM((PAD + ROWS + PAD, C_MID), SINGLE)] * 2,
-        (inv, total4, mid4, mask, a4) + (in_vmem(narrow_b),) * 3, vmem=9,
+        (inv, total4, mid4, mask, a4) + (in_vmem(narrow_b),) * 3, vmem=8,
     )
     a5 = in_vmem(a5)
     total5, (h4_t, b_kept, _unused, x_t) = dp_sum(
@@ -982,7 +1064,7 @@
             chunk_sum,
         ],
         [shape_of((2, ROWS, C_OUT // 2), BFLOAT), vmem_of((ROWS, C_OUT)), shape_of((4, C_OUT))], [],
-        (slots, inv, total6, tab6, mask, in_vmem(a6), in_hbm(y_kept), cot, cot, cot, cot), prefetch=1, vmem=10,
+        (slots, inv, total6, tab6, mask, in_vmem(a6), in_hbm(y_kept), cot, cot, cot, cot), prefetch=1, vmem=9,
     )
     gz6 = in_vmem(gz6)
 
@@ -997,7 +1079,7 @@
             ],
             spec(block, lambda t, slot: (slot[t + (t >= SLOTS)], 0, 0)),
             shape_of((IMG_DEV,) + pair.shape[2:], BFLOAT), [],
-            (slots, pair, got, token), prefetch=1, vmem=4,
+            (slots, pair, got, token), prefetch=1, vmem=9,
         )
 
     blk = blk.reshape(2, SLOTS, PIX, C_OUT // 2)
@@ -1017,7 +1099,7 @@
         [chunk, full_mid, full_row],
         [vmem_of((ROWS, C_OUT), BFLOAT), vmem_of((ROWS, C_MID)), shape_of((4, C_MID))],
         [pltpu.VMEM((ROWS, C_MID), SINGLE)],
-        (inv, gz6, a6_kept, total6, sum6, tab6, mask, in_hbm(wide), a5, total5, mid5), vmem=11,
+        (inv, gz6, a6_kept, total6, sum6, tab6, mask, in_hbm(wide), a5, total5, mid5), vmem=9,
     )
     gz5 = in_vmem(gz5)
 
@@ -1043,7 +1125,7 @@
         [spec((3, ROWS, C_MID), lambda s: (s, 0, 0)), full_mid, full_row],
         [vmem_of((9, ROWS, C_MID), BFLOAT), vmem_of((ROWS, C_MID)), shape_of((4, C_MID))],
         [pltpu.VMEM((PAD + ROWS + PAD, C_MID), SINGLE)] * 2 + [pltpu.VMEM((ROWS, C_MID), SINGLE)],
-        (inv, gz5, a5, total5, sum5, mid5, mask, b_kept, b_kept, b_kept, a4, total4, mid4), vmem=13,
+        (inv, gz5, a5, total5, sum5, mid5, mask, b_kept, b_kept, b_kept, a4, total4, mid4), vmem=10,
     )
     gz4 = in_vmem(gz4)
     one_turned = spec((1, C_MID, ROWS), lambda t, slot: (0, 0, 0))
@@ -1066,7 +1148,7 @@
          chunk, chunk, chunk, chunk_sum, chunk_sum, chunk_tab, chunk_tab],
         [full_mid, chunk, spec((6, TILE), lambda k: (0, k))],
         [vmem_of((ROWS, C_MID), BFLOAT), vmem_of((ROWS, C_OUT)), shape_of((6, C_OUT))], [],
-        (inv, gz4, a4, total4, sum4, mid4, mask, a_kept, b_kept, gz6, a3_kept, as_kept, total3, total_s, tab3, tabs), vmem=15,
+        (inv, gz4, a4, total4, sum4, mid4, mask, a_kept, b_kept, gz6, a3_kept, as_kept, total3, total_s, tab3, tabs), vmem=12,
     )
     gj = in_vmem(gj)
 
@@ -1108,22 +1190,30 @@
         [chunk, chunk, full_mid, full_row],
         [hbm_of((ROWS, C_OUT), BFLOAT), hbm_of((ROWS, C_OUT), BFLOAT), vmem_of((ROWS, C_MID)), shape_of((4, C_MID))],
         [pltpu.VMEM((ROWS, C_MID), SINGLE)],
-        (inv, gj, a3_kept, as_kept, total3, total_s, sum3, tab3, tabs, mask, in_hbm(wide), a2, total2, mid2), vmem=14,
+        (inv, gj, a3_kept, as_kept, total3, total_s, sum3, tab3, tabs, mask, in_hbm(wide), a2, total2, mid2), vmem=11,
     )
     gz2 = in_vmem(gz2)
 
-    def step_b(bits):
-        def filler(token):
-            if not fast:
-                return token
-            keep0, _sent, keep1, _sent = held["b"]
-            came0, came1 = pin(held["came_b"], token)
-            stay0, sent0 = halved(keep0, came0)
-            stay1, sent1 = halved(keep1, came1)
-            held["came_b"] = exchange(sent0, bits[0]), exchange(sent1, bits[1])
-            return stay0, sent0, stay1, sent1
-
-        return filler
+    def second_b(token):
+        if not fast:
+            return token
+        state = halved(held["b"], pin(held["came_b"], token), False)
+        held["came_b"] = exchange(state[1], 2), exchange(state[3], 1)
+        return state
+
+    def third_exchange_b(token):
+        if not fast:
+            return token
+        state = halved(held["b"], pin(held["came_b"], token), True)
+        held["came_b"] = exchange(state[1], 4)
+        return state
+
+    def fourth_exchange_b(token):
+        if not fast:
+            return token
+        state = halved_both(held["b"], pin(held["came_b"], token))
+        held["came_b"] = exchange(state[1], 8)
+        return state
 
     def grad_three(token):
         held["w"] = weight_grad("dw3", h2_t[None], wide_rows(0), *whole_wide(ga3), 2, wide_shape, 256, 0, bufs_w, token, hbm_of)
@@ -1136,9 +1226,21 @@
 
         return filler
 
-    sum2, results2 = dp_sum(s2, [grad_three, grad_short(0), step_b((2, 1)), grad_short(1)])
-    held["b"], bufs_w = results2[2:]
-    got_w = swap_pipe(bufs_w[1])
+    def start_swap_w(token):
+        held["got_w"] = swap_pipe(pin(held["w"][1], token))
+        return token
+
+    def two_grads(token):
+        grad_three(token)
+        return grad_short(0)(token)
+
+    sum2, results2 = dp_sum(s2, [two_grads, both_of(second_b, grad_short(1)), start_swap_w])
+    held["b"], bufs_w = results2[1]
+    got_w = held["got_w"]
+    if fast:
+        split = split_group("split_w", bufs_w[0], pin(got_w, sum2), w_wide.shape[0], lambda which, m: 16 * which + m)
+        sum2, split, held["b"] = lax.optimization_barrier((sum2, split, third_exchange_b(sum2)))
+        held["came"] = exchange(split[1], 1), exchange(split[3], 2)
 
     col2, gz1, s1 = call(
         k_back_conv_two, "g1", (3,),
@@ -1147,7 +1249,7 @@
         [spec((3, ROWS, C_MID), lambda s: (turned(s), 0, 0)), plane_pair, full_row],
         [vmem_of((9, ROWS, C_MID), BFLOAT), vmem_of((4, ROWS, C_MID)), shape_of((4, C_MID))],
         [pltpu.VMEM((PAD + ROWS + PAD, C_MID), SINGLE)] * 2 + [pltpu.VMEM((2, ROWS, C_MID), SINGLE)],
-        (inv, gz2, a2, total2, sum2, mid2, mask, a_kept, a_kept, a_kept, a1, total1, mid1), vmem=16,
+        (inv, gz2, a2, total2, sum2, mid2, mask, a_kept, a_kept, a_kept, a1, total1, mid1), vmem=12,
     )
     gz1 = in_vmem(gz1)
     h1_planes = h1_t.reshape(4, C_MID, ROWS)
@@ -1169,44 +1271,32 @@
             [full((ROWS, C_OUT)), spec((TILE, C_OUT), lambda k: (1 + k, 0)), ANYWHERE],
             spec((ROWS, TILE), lambda k: (0, k)),
             hbm_of((ROWS, C_IN)), [],
-            (in_hbm(gas), in_hbm(wide), token), vmem=11,
+            (in_hbm(gas), in_hbm(wide), token), vmem=8,
         )
 
-    def split_w(token):
-        if fast:
-            keep, got = pin((bufs_w[0], got_w), token)
-            held["split"] = split_group("split_w", keep, got, w_wide.shape[0], lambda which, m: 16 * which + m)
-            return held["split"]
-        return token
-
-    def send_w(token):
-        if fast:
-            sent0, sent1 = pin((held["split"][1], held["split"][3]), token)
-            held["came"] = exchange(sent0, 1), exchange(sent1, 2)
-        return token
+    def first_w(token):
+        if not fast:
+            return token
+        came = pin(held["came"], token)
+        return halved(split, came, False)
 
     held["a"] = bufs_a
-    sum1, results1 = dp_sum(s1, [both_of(step_b((4, 4)), split_w), grad_two(0), both_of(send_w, grad_two(1)), grad_two(2)])
-    held["b"], held["split"] = results1[0]
-    bufs_a = results1[3]
-    sum1, held["b"] = lax.optimization_barrier((sum1, step_b((8, 8))(sum1)))
-
+    sum1, results1 = dp_sum(s1, [grad_two(0), grad_two(1), both_of(fourth_exchange_b, grad_two(2)), first_w], 4)
+    held["b"], bufs_a = results1[2]
+    state_w = results1[3]
+    state_b = held["b"]
     plane = spec((1, ROWS, C_MID), lambda k: (k, 0, 0))
     ga1 = call(
         k_first_grad, "g0", (4,), [SCALARS, plane, plane, full_row, full_row, full_tab, full_mask], plane,
         vmem_of((4, ROWS, C_MID), BFLOAT), [], (inv, gz1, a1, total1, sum1, mid1, mask),
     )
-    if fast:
-        came_w = held["came"]
-        state_w = halved(held["split"][0], came_w[0]) + halved(held["split"][2], came_w[1])
-        ga1, state_w = lax.optimization_barrier((ga1, state_w))
     flat_ga1 = in_vmem(ga1.reshape(1, 4 * ROWS, C_MID))
     bufs_a = weight_grad(
         "dw1", x_t.reshape(2, C_MID, 4 * ROWS), spec((1, C_MID, 4 * ROWS), lambda t, slot: (t, 0, 0)), flat_ga1, full((1, 4 * ROWS, C_MID)),
         2, narrow_shape, TILE, 0, bufs_a, None, vmem_of,
     )
     got_a = swap_pipe(bufs_a[1])
-    dxs = wide_back(ga1)
+    dxs = wide_back(bufs_a[0])
 
     def image_grads(token):
         pair = call(
@@ -1215,22 +1305,39 @@
              spec((PIX, C_IN), lambda s, slot: (s, 0)), full((4 * PIX, 4 * PIX)), ANYWHERE],
             spec((2, 1, 4 * PIX, C_IN // 2), lambda s, slot: (0, s, 0, 0)),
             shape_of((2, SLOTS, 4 * PIX, C_IN // 2), BFLOAT), [],
-            (slots, in_vmem(ga1), mask, a_kept, in_hbm(dxs), in_hbm(perm), token), prefetch=1, vmem=10,
+            (slots, in_vmem(ga1), mask, a_kept, in_hbm(dxs), in_hbm(perm), token), prefetch=1, vmem=9,
         )
         return pair, swap_pipe(pair[1])
 
-    pair, got_pair = image_grads(ga1)
-    grad_local = place("place_grad", pair, got_pair, ga1)
     if fast:
+        state_w = halved(state_w, (exchange(state_w[1], 2), exchange(state_w[3], 1)), True)
+        got_a, dxs, state_w, came_b = lax.optimization_barrier((got_a, dxs, state_w, held["came_b"]))
+        came_w = exchange(state_w[1], 4)
         state_a = split_group("split_a", in_vmem(bufs_a[0]), got_a, part_n, by_rows)
-        half_b = jnp.concatenate([added(held["b"][k], held["came_b"][k // 2]) for k in (0, 2)], axis=0)
-        half_w0 = halve(state_w[0], state_w[1], (2, 4, 8))
-        half_w1 = halve(state_w[2], state_w[3], (1, 4, 8))
-        half_a = jnp.concatenate([halve(state_a[0], state_a[1], (1, 2, 4, 8)), halve(state_a[2], state_a[3], (2, 1, 4, 8))], axis=0)
+        came_a = exchange(state_a[1], 1), exchange(state_a[3], 2)
+        pair, got_pair = image_grads(state_a[0])
+        state_w = halved_both(state_w, came_w)
+        came_a, state_w, pair = lax.optimization_barrier((came_a, state_w, pair))
+        came_w = exchange(state_w[1], 8)
+        state_a = halved(state_a, came_a, False)
+        came_a = exchange(state_a[1], 2), exchange(state_a[3], 1)
+        half_w0, half_w1 = added(state_w, came_w)
+        half_b = jnp.concatenate(added(state_b, came_b), axis=0)
+        came_a, half_w0, half_w1, half_b = lax.optimization_barrier((came_a, half_w0, half_w1, half_b))
+        state_a = halved(state_a, came_a, True)
+        came_a = exchange(state_a[1], 4)
+        grad_local = place("place_grad", pair, got_pair, state_a[0])
+        came_a, grad_local = lax.optimization_barrier((came_a, grad_local))
+        state_a = halved_both(state_a, came_a)
+        came_a = exchange(state_a[1], 8)
+        sum1, sum2, sum3, sum4, sum5, sum6 = pin((sum1, sum2, sum3, sum4, sum5, sum6), state_a[0])
+        half_a = jnp.concatenate(added(state_a, came_a), axis=0)
     else:
         half_a = jnp.concatenate(scatter_plain(bufs_a[0], got_a, rows_n, True), axis=0)
         half_w0, half_w1 = scatter_plain(bufs_w[0], got_w, w_wide.shape[0], False)
         half_b = jnp.concatenate(scatter_plain(bufs_b[0], held["got_b"], rows_n, True), axis=0)
+        pair, got_pair = image_grads(ga1)
+        grad_local = place("place_grad", pair, got_pair, ga1)
     grad_local = grad_local.reshape(IMG_DEV, 2 * HB, 2 * WB, C_IN // 2)
 
     def join_halves(first, second):
@@ -1240,9 +1347,6 @@
 
     grad_narrow = join_halves(half_a, half_b)
     grad_wide = join_halves(half_w0, half_w1)
-
-    hot_narrow = group_table(shard, w_narrow.shape[0], (C_IN, C_IN + 9 * C_MID, C_IN + 9 * C_MID + C_OUT))
-    hot_wide = group_table(shard, w_wide.shape[0], (C_MID, C_MID + C_IN))
 
     def pair_sum(rows):
         return rows[0] + rows[1]
@@ -1254,32 +1358,20 @@
     grad_mid = lax.dynamic_slice(mid_rows, (0, shard * mid_cols), (8, mid_cols))
     grad_table = lax.dynamic_slice(wide_rows, (0, shard * wide_cols), (6, wide_cols))
 
-    def square_vector(narrow_rows, wide_rows, mid_part, table_part):
-        return jnp.concatenate(
-            [
-                jnp.dot(jnp.sum(narrow_rows * narrow_rows, axis=1), hot_narrow, precision=PRECISE),
-                jnp.dot(jnp.sum(wide_rows * wide_rows, axis=1), hot_wide, precision=PRECISE),
-                jnp.sum(mid_part * mid_part, axis=1),
-                jnp.sum(table_part * table_part, axis=1),
-            ]
-        )
-
-    squares = jnp.stack([square_vector(w_narrow, w_wide, bn_mid, bn_wide), square_vector(grad_narrow, grad_wide, grad_mid, grad_table)])
+    starts = (shard * jnp.array([rows_n, w_wide.shape[0]])).astype(jnp.int32)
+    weights, grads = (w_narrow, w_wide, bn_mid, bn_wide), (grad_narrow, grad_wide, grad_mid, grad_table)
+    whole_specs = [full(v.shape) for v in weights]
+    squares = call(
+        k_squares, "squares", (1,), whole_specs * 2, full((8, 128)), shape_of((8, 128)), [], (starts, *weights, *grads), prefetch=1, vmem=10,
+    )
     squares, _unused = dp_sum(squares + swap_pipe(squares))
-    norms = jnp.sqrt(squares)
-    weight_norms, grad_norms = norms[0], norms[1]
-    ratios = TRUST * weight_norms / (grad_norms + DECAY * weight_norms)
-    ratio_narrow = jnp.dot(hot_narrow, ratios[:4], precision=PRECISE)
-    ratio_wide = jnp.dot(hot_wide, ratios[4:7], precision=PRECISE)
-
-    def lars_step(weight, gradient, moment, ratio_rows):
-        new_moment = MOMENTUM * moment + RATE * ratio_rows[:, None] * (gradient + DECAY * weight)
-        return (weight - new_moment, new_moment)
-
-    new_narrow, new_mom_narrow = lars_step(w_narrow, grad_narrow, mom_narrow, ratio_narrow)
-    new_wide, new_mom_wide = lars_step(w_wide, grad_wide, mom_wide, ratio_wide)
-    new_mid, new_mom_mid = lars_step(bn_mid, grad_mid, mom_bn_mid, ratios[7:15])
-    new_table, new_mom_table = lars_step(bn_wide, grad_table, mom_bn_wide, ratios[15:21])
+    parts = 4 if rows_n % 64 == 0 and w_wide.shape[0] % 64 == 0 else 1
+    specs = [spec((v.shape[0] // parts, v.shape[1]), lambda k, *_: (k, 0)) for v in weights[:2]] + whole_specs[2:]
+    updated = call(
+        k_update, "update", (parts,), [full((8, 128))] + specs * 3, specs * 2, [shape_of(v.shape) for v in weights] * 2, [],
+        (starts, squares, *weights, *grads, mom_narrow, mom_wide, mom_bn_mid, mom_bn_wide), prefetch=1, vmem=12,
+    )
+    new_mom_narrow, new_mom_wide, new_mom_mid, new_mom_table, new_narrow, new_wide, new_mid, new_table = updated
     return (
         block_local, grad_local, grad_narrow, grad_wide, grad_mid, grad_table,
         new_mom_narrow, new_mom_wide, new_mom_mid, new_mom_table,

time: 559 us -> 516 us (0.923)
  local copies, waits for them, and re-layouts: 24.2 us -> 7.37 us
  other arithmetic: 22.6 us -> 11 us
  starting transfers between devices: 105 us -> 98.4 us
    ppermute x92 -> x82, waiting for transfers between devices: 198 us -> 185 us  [exchange(): return lax.ppermute(value, 'dp', pairs(bit))]
    unnamed x176 -> x91, local copies, waits for them, and re-layouts: 12.9 us -> 4.88 us
    ppermute x92 -> x82, starting transfers between devices: 102 us -> 94.4 us  [exchange(): return lax.ppermute(value, 'dp', pairs(bit))]
    all_gather x1, waiting for transfers between devices: 0.01 us -> 7.34 us  [on_device(): wide = lax.all_gather(own_wide, ('pipe', 'dp'), axis=0, tiled=True)]
    reduce_sum x9 -> x0, other arithmetic: 6.42 us -> none  [the longest x2 2.32 us: square_vector(): jnp.sum(narrow_rows * narrow_rows, axis=1)]
    another operation x20 -> x0, other arithmetic: 5.98 us -> none
    pallas_call x59 -> x70, Pallas kernels: 176 us -> 173 us  [call(): pl.pallas_call(kernel, out_shape=out_shape, grid_spec=pltpu.PrefetchScala...]
  transfers between devices with their start and end apart: 113 -> 103, of which waited for: 73 -> 70; matrix products, arithmetic and copies ran while one was open for 5% -> 2% of each run, Pallas kernels for 24% -> 24%
where the time goes in v3:
time: 516 us; the launch traced here: 506 us
  waiting for transfers between devices  201 us (39%)
  Pallas kernels  173 us (34%)
  starting transfers between devices  98.4 us (19%)
  between operations  15.9 us (3%)
  other arithmetic  11 us (2%)
  local copies, waits for them, and re-layouts  7.37 us (1%)
    ppermute x82, waiting for transfers between devices, exchange(): return lax.ppermute(value, 'dp', pairs(bit))  185 us
    pallas_call x70, Pallas kernels, call(): pl.pallas_call(kernel, out_shape=out_shape, grid_spec=pltpu.PrefetchScala...  173 us
    ppermute x82, starting transfers between devices, exchange(): return lax.ppermute(value, 'dp', pairs(bit))  94.4 us
  transfers between devices with their start and end apart: 103, of which 70 were waited for; matrix products, arithmetic and copies ran while one was open for 2% of the time, Pallas kernels for 24%

profile of v3, /device:TPU:0, one launch (start us, length us, event | category | flops | bytes accessed | tf_op | source)
XLA Modules:
  0.0 506.0 jit_solution(502981794049305104)
XLA Ops:
  10.2 4.0 collective-permute-start.1
  14.2 9.4 %collective-permute-done.1.refs_1_ = bf16[2,1,192,256]{3,2,1,0:T(8,128)(2,1)S(1)} collective-permute-done((bf16[2,1,192,256]{3,2,1,0:T(8,128)(2,1)S(1)}, bf16[2,1,192,256]{3,2,1,0:T(8,128)(2,1)S(1)}, u32[]{:S(2)}, u32[]{:S(2)}) %collective-permute-start.1) | collective-permute-done | bytes 196640 | tf_op jit(solution)/shard_map/ppermute | solution.py:49
  24.9 9.9 %collective-permute-done.2.refs_1_ = bf16[2,2,192,256]{3,2,1,0:T(8,128)(2,1)S(1)} collective-permute-done((bf16[2,2,192,256]{3,2,1,0:T(8,128)(2,1)S(1)}, bf16[2,2,192,256]{3,2,1,0:T(8,128)(2,1)S(1)}, u32[]{:S(2)}, u32[]{:S(2)}) %collective-permute-start.2) | collective-permute-done | bytes 393248 | tf_op jit(solution)/shard_map/ppermute | solution.py:49
  42.5 7.5 %collective-permute-done.5.refs_1_.refs_2_ = bf16[2,1,192,256]{3,2,1,0:T(8,128)(2,1)S(1)} collective-permute-done((bf16[2,1,192,256]{3,2,1,0:T(8,128)(2,1)S(1)}, bf16[2,1,192,256]{3,2,1,0:T(8,128)(2,1)S(1)}, u32[]{:S(2)}, u32[]{:S(2)}) %collective-permute-start.5) | collective-permute-done | bytes 196640 | tf_op jit(solution)/shard_map/ppermute | solution.py:49
  54.4 4.9 prep.1
  59.9 7.4 %collective-permute-done.8.refs_1_.refs_2_ = bf16[2,2,192,256]{3,2,1,0:T(8,128)(2,1)S(1)} collective-permute-done((bf16[2,2,192,256]{3,2,1,0:T(8,128)(2,1)S(1)}, bf16[2,2,192,256]{3,2,1,0:T(8,128)(2,1)S(1)}, u32[]{:S(2)}, u32[]{:S(2)}) %collective-permute-start.8) | collective-permute-done | bytes 393248 | tf_op jit(solution)/shard_map/ppermute | solution.py:49
  67.3 4.7 collective-permute-done.6.refs_1_
  105.6 5.9 %a2.1 = (f32[384,512]{1,0:T(8,128)S(1)}, bf16[4,384,512]{2,1,0:T(8,128)(2,1)S(1)}, f32[4,512]{1,0:T(4,128)S(1)}) custom-call(f32[2]{0:T(128)S(1)} %fusion.2.inv_ref, f32[4,512]{1,0:T(4,128)S(1)} %slice.261.total_ref.low_total, f32[2,512]{1,0:T(2,128)S(1)} %get-tuple-element.558.tab_ref.low_tab, f32[384,1]{1,0:T(8,128)S(1)} %get-tuple-element.298.mask_ref, ...), custom_call_target="tpu_custom_call" | custom-call | bytes 6000000 | tf_op jit(solution)/shard_map/a2/pallas_call | solution.py:650
  114.9 7.2 %collective-permute-done.18 = f32[4,512]{1,0:T(4,128)S(1)} collective-permute-done((f32[4,512]{1,0:T(4,128)S(1)}, f32[4,512]{1,0:T(4,128)S(1)}, u32[]{:S(2)}, u32[]{:S(2)}) %collective-permute-start.18) | collective-permute-done | bytes 8224 | tf_op jit(solution)/shard_map/ppermute | solution.py:49
  135.1 7.3 %all-gather.2.cloned.1.call-done.w_ref.w0.w1 = bf16[2048,2048]{1,0:T(8,128)(2,1)} async-done(((bf16[64,2048]{1,0:T(8,128)(2,1)}), bf16[2048,2048]{1,0:T(8,128)(2,1)}) %all-gather.2.cloned.1.call-update) | async-done | bytes 8388624 | tf_op jit(solution)/shard_map/all_gather | solution.py:825
  142.4 4.5 as.1
  146.9 4.2 a3.1
  160.9 4.3 collective-permute-done.26
  167.5 4.3 wb.1.wb_ref.w0.w1.w2.in_ref
  171.8 4.7 a4.1
  192.7 4.0 a5.1
  212.3 3.8 a6.1
  235.6 5.4 %head.1 = (bf16[2,384,1024]{2,1,0:T(8,128)(2,1)S(1)}, f32[384,2048]{1,0:T(8,128)S(1)}, f32[4,2048]{1,0:T(4,128)S(1)}) custom-call(s32[9]{0:T(128)S(1)} %pad_add_fusion.1.slot_ref, f32[2]{0:T(128)S(1)} %fusion.2.inv_ref, f32[4,2048]{1,0:T(4,128)S(1)} %add.282.total_ref, f32[2,2048]{1,0:T(2,128)S(1)} %slice.223.tab_ref, ...), custom_call_target="tpu_custom_call" | custom-call | bytes 6360000 | tf_op jit(solution)/shard_map/head/pallas_call | solution.py:650
  258.0 5.2 %g5.1 = (bf16[384,2048]{1,0:T(8,128)(2,1)S(1)}, f32[384,512]{1,0:T(8,128)S(1)}, f32[4,512]{1,0:T(4,128)S(1)}) custom-call(f32[2]{0:T(128)S(1)} %fusion.2.inv_ref, f32[384,2048]{1,0:T(8,128)S(1)} %get-tuple-element.360.gz_ref.up_ref, f32[384,2048]{1,0:T(8,128)} %keep.13.a_ref, f32[4,2048]{1,0:T(4,128)S(1)} %add.282.total_ref, f32[4,2048]{1,0:T(4,128)S(1)} %add.286.s_ref, ...), custom_call_target="tpu_custom_call" | custom-call | bytes 6240000 | tf_op jit(solution)/shard_map/g5/pallas_call | solution.py:650
  279.7 5.4 %g4.1 = (bf16[9,384,512]{2,1,0:T(8,128)(2,1)S(1)}, f32[384,512]{1,0:T(8,128)S(1)}, f32[4,512]{1,0:T(4,128)S(1)}) custom-call(f32[2]{0:T(128)S(1)} %fusion.2.inv_ref, f32[384,512]{1,0:T(8,128)S(1)} %get-tuple-element.378.gz_ref, f32[384,512]{1,0:T(8,128)S(1)} %copy-done.13, f32[4,512]{1,0:T(4,128)S(1)} %add.278.total_ref.low_total, f32[4,512]{1,0:T(4,128)S(1)} %add.290.s_ref, ...), custom_call_target="tpu_custom_call" | custom-call | bytes 6480000 | tf_op jit(solution)/shard_map/g4/pallas_call | solution.py:650
  300.7 6.7 %gy.1 = (bf16[384,512]{1,0:T(8,128)(2,1)S(1)}, f32[384,2048]{1,0:T(8,128)S(1)}, f32[6,2048]{1,0:T(8,128)S(1)}) custom-call(f32[2]{0:T(128)S(1)} %fusion.2.inv_ref, f32[384,512]{1,0:T(8,128)S(1)} %get-tuple-element.381.gz_ref, f32[384,512]{1,0:T(8,128)S(1)} %copy-done.8, f32[4,512]{1,0:T(4,128)S(1)} %add.274.total_ref.low_total, f32[4,512]{1,0:T(4,128)S(1)} %add.294.s_ref, ...), custom_call_target="tpu_custom_call" | custom-call | bytes 8400000 | tf_op jit(solution)/shard_map/gy/pallas_call | solution.py:650
  330.4 7.3 %g2.1 = (bf16[384,2048]{1,0:T(8,128)(2,1)}, bf16[384,2048]{1,0:T(8,128)(2,1)}, f32[384,512]{1,0:T(8,128)S(1)}, f32[4,512]{1,0:T(4,128)S(1)}) custom-call(f32[2]{0:T(128)S(1)} %fusion.2.inv_ref, f32[384,2048]{1,0:T(8,128)S(1)} %get-tuple-element.396.gj_ref, f32[384,2048]{1,0:T(8,128)} %keep.10.a3_ref, f32[384,2048]{1,0:T(8,128)} %keep.9.as_ref, ...), custom_call_target="tpu_custom_call" | custom-call | bytes 8760000 | tf_op jit(solution)/shard_map/g2/pallas_call | solution.py:650
  369.4 7.2 %g1.1 = (bf16[9,384,512]{2,1,0:T(8,128)(2,1)S(1)}, f32[4,384,512]{2,1,0:T(8,128)S(1)}, f32[4,512]{1,0:T(4,128)S(1)}) custom-call(f32[2]{0:T(128)S(1)} %fusion.2.inv_ref, f32[384,512]{1,0:T(8,128)S(1)} %get-tuple-element.416.gz_ref, f32[384,512]{1,0:T(8,128)S(1)} %copy-done.11, f32[4,512]{1,0:T(4,128)S(1)} %add.266.total_ref.low_total, ...), custom_call_target="tpu_custom_call" | custom-call | bytes 9600000 | tf_op jit(solution)/shard_map/g1/pallas_call | solution.py:650
  403.6 5.0 dxs.1.short_ref
  408.6 5.3 %collective-permute-done.81.refs_2_.refs_3_ = bf16[4,64,1024]{2,1,0:T(8,128)(2,1)S(1)} collective-permute-done((bf16[4,64,1024]{2,1,0:T(8,128)(2,1)S(1)}, bf16[4,64,1024]{2,1,0:T(8,128)(2,1)S(1)}, u32[]{:S(2)}, u32[]{:S(2)}) %collective-permute-start.81) | collective-permute-done | bytes 524320 | tf_op jit(solution)/shard_map/ppermute | solution.py:49
  419.8 6.6 %gx.1.own_ref = bf16[2,4,384,512]{3,2,1,0:T(8,128)(2,1)S(1)} custom-call(s32[9]{0:T(128)S(1)} %pad_add_fusion.1.slot_ref, bf16[4,384,512]{2,1,0:T(8,128)(2,1)S(1)} %g0.1.ga_ref, f32[384,1]{1,0:T(8,128)S(1)} %get-tuple-element.298.mask_ref, bf16[6144,512]{1,0:T(8,128)(2,1)} %keep.7.w0.w1.w2.wa_ref.w_ref, f32[384,1024]{1,0:T(8,128)} %dxs.1.short_ref, ...), custom_call_target="tpu_custom_call" | custom-call | bytes 7680000 | tf_op jit(solution)/shard_map/gx/pallas_call | solution.py:650
  426.7 4.2 collective-permute-done.86.came_ref
  440.5 8.1 %collective-permute-done.89 = bf16[2,1,64,1024]{3,2,1,0:T(8,128)(2,1)S(1)} collective-permute-done((bf16[2,1,64,1024]{3,2,1,0:T(8,128)(2,1)S(1)}, bf16[2,1,64,1024]{3,2,1,0:T(8,128)(2,1)S(1)}, u32[]{:S(2)}, u32[]{:S(2)}) %collective-permute-start.89) | collective-permute-done | bytes 262176 | tf_op jit(solution)/shard_map/ppermute | solution.py:49
  450.5 3.8 place_grad.1
  454.3 6.4 %collective-permute-done.90.came_ref = bf16[2,2,192,256]{3,2,1,0:T(8,128)(2,1)S(1)} collective-permute-done((bf16[2,2,192,256]{3,2,1,0:T(8,128)(2,1)S(1)}, bf16[2,2,192,256]{3,2,1,0:T(8,128)(2,1)S(1)}, u32[]{:S(2)}, u32[]{:S(2)}) %collective-permute-start.90) | collective-permute-done | bytes 393248 | tf_op jit(solution)/shard_map/ppermute | solution.py:49
  461.9 10.4 %collective-permute-done.92 = bf16[2,1,192,256]{3,2,1,0:T(8,128)(2,1)S(1)} collective-permute-done((bf16[2,1,192,256]{3,2,1,0:T(8,128)(2,1)S(1)}, bf16[2,1,192,256]{3,2,1,0:T(8,128)(2,1)S(1)}, u32[]{:S(2)}, u32[]{:S(2)}) %collective-permute-start.92) | collective-permute-done | bytes 196640 | tf_op jit(solution)/shard_map/ppermute | solution.py:49
  491.7 4.1 collective-permute-done.101
  (440 shorter events, 301.0 us)
Async XLA Ops:
  7.2 135.2 %all-gather.2.cloned.1.call-start = ((), (), s32[]{:S(2)}) async-start(), calls=%async_computation | async-start | bytes 8650752 | tf_op jit(solution)/shard_map/all_gather | solution.py:825
  10.2 13.4 %collective-permute-start.1 = (bf16[2,1,192,256]{3,2,1,0:T(8,128)(2,1)S(1)}, bf16[2,1,192,256]{3,2,1,0:T(8,128)(2,1)S(1)}, u32[]{:S(2)}, u32[]{:S(2)}) collective-permute-start(bf16[2,1,192,256]{3,2,1,0:T(8,128)(2,1)S(1)} %bitcast.65), channel_id=1, source_target_pairs={{0,8},{1,9},{2,10},{3,11},{4,12},{5,13},{6,14},{7,15},{8,0},{9,1},... | collective-permute-start | bytes 589832 | tf_op jit(solution)/shard_map/ppermute | solution.py:49
  35.9 14.1 %collective-permute-start.3 = (bf16[4,192,256]{2,1,0:T(8,128)(2,1)S(1)}, bf16[4,192,256]{2,1,0:T(8,128)(2,1)S(1)}, u32[]{:S(2)}, u32[]{:S(2)}) collective-permute-start(bf16[4,192,256]{2,1,0:T(8,128)(2,1)S(1)} %get-tuple-element.277.refs_0_), channel_id=1, source_target_pairs={{0,2},{1,3},{2,0},{3,1},{4,6},{5,7},{6,4},{7,5},{8,10},{9,11},{10,... | collective-permute-start | bytes 1179656 | tf_op jit(solution)/shard_map/ppermute | solution.py:49
  37.2 12.8 %collective-permute-start.4 = (bf16[4,192,256]{2,1,0:T(8,128)(2,1)S(1)}, bf16[4,192,256]{2,1,0:T(8,128)(2,1)S(1)}, u32[]{:S(2)}, u32[]{:S(2)}) collective-permute-start(bf16[4,192,256]{2,1,0:T(8,128)(2,1)S(1)} %get-tuple-element.278.refs_1_), channel_id=1, source_target_pairs={{0,1},{1,0},{2,3},{3,2},{4,5},{5,4},{6,7},{7,6},{8,9},{9,8},{10,11... | collective-permute-start | bytes 1179656 | tf_op jit(solution)/shard_map/ppermute | solution.py:49
  51.2 20.8 %collective-permute-start.6 = (bf16[8,192,256]{2,1,0:T(8,128)(2,1)}, bf16[8,192,256]{2,1,0:T(8,128)(2,1)}, u32[]{:S(2)}, u32[]{:S(2)}) collective-permute-start(bf16[8,192,256]{2,1,0:T(8,128)(2,1)} %get-tuple-element.282.refs_0_), channel_id=1, source_target_pairs={{0,1},{1,0},{2,3},{3,2},{4,5},{5,4},{6,7},{7,6},{8,9},{9,8},{10,11... | collective-permute-start | bytes 2359304 | tf_op jit(solution)/shard_map/ppermute | solution.py:49
  51.8 20.4 %collective-permute-start.7 = (bf16[8,192,256]{2,1,0:T(8,128)(2,1)}, bf16[8,192,256]{2,1,0:T(8,128)(2,1)}, u32[]{:S(2)}, u32[]{:S(2)}) collective-permute-start(bf16[8,192,256]{2,1,0:T(8,128)(2,1)} %get-tuple-element.283.refs_2_), channel_id=1, source_target_pairs={{0,2},{1,3},{2,0},{3,1},{4,6},{5,7},{6,4},{7,5},{8,10},{9,11},{10,... | collective-permute-start | bytes 2359304 | tf_op jit(solution)/shard_map/ppermute | solution.py:49
  53.5 13.8 %collective-permute-start.8 = (bf16[2,2,192,256]{3,2,1,0:T(8,128)(2,1)S(1)}, bf16[2,2,192,256]{3,2,1,0:T(8,128)(2,1)S(1)}, u32[]{:S(2)}, u32[]{:S(2)}) collective-permute-start(bf16[2,2,192,256]{3,2,1,0:T(8,128)(2,1)S(1)} %join.9.refs_0_), channel_id=1, source_target_pairs={{0,4},{1,5},{2,6},{3,7},{4,0},{5,1},{6,2},{7,3},{8,12},{9,13},{10,... | collective-permute-start | bytes 1179656 | tf_op jit(solution)/shard_map/ppermute | solution.py:49
  59.3 13.5 %collective-permute-start.10 = (bf16[8,192,256]{2,1,0:T(8,128)(2,1)}, bf16[8,192,256]{2,1,0:T(8,128)(2,1)S(1)}, u32[]{:S(2)}, u32[]{:S(2)}) collective-permute-start(bf16[8,192,256]{2,1,0:T(8,128)(2,1)} %get-tuple-element.282.refs_0_), channel_id=1, source_target_pairs={{0,16},{16,0},{1,17},{17,1},{2,18},{18,2},{3,19},{19,3},{4,20},{20... | collective-permute-start | bytes 2359304 | tf_op jit(solution)/shard_map/ppermute | solution.py:76
  59.5 13.3 %collective-permute-start.12 = (bf16[8,192,256]{2,1,0:T(8,128)(2,1)}, bf16[8,192,256]{2,1,0:T(8,128)(2,1)S(1)}, u32[]{:S(2)}, u32[]{:S(2)}) collective-permute-start(bf16[8,192,256]{2,1,0:T(8,128)(2,1)} %get-tuple-element.283.refs_2_), channel_id=1, source_target_pairs={{0,16},{16,0},{1,17},{17,1},{2,18},{18,2},{3,19},{19,3},{4,20},{20... | collective-permute-start | bytes 2359304 | tf_op jit(solution)/shard_map/ppermute | solution.py:76
  101.2 20.9 %collective-permute-start.20 = (bf16[4,192,256]{2,1,0:T(8,128)(2,1)}, bf16[4,192,256]{2,1,0:T(8,128)(2,1)S(1)}, u32[]{:S(2)}, u32[]{:S(2)}) collective-permute-start(bf16[4,192,256]{2,1,0:T(8,128)(2,1)} %copy-done.25), channel_id=1, source_target_pairs={{0,2},{1,3},{2,0},{3,1},{4,6},{5,7},{6,4},{7,5},{8,10},{9,11},{10,... | collective-permute-start | bytes 1179656 | tf_op jit(solution)/shard_map/ppermute | solution.py:49
  102.3 19.8 %collective-permute-start.21 = (bf16[4,192,256]{2,1,0:T(8,128)(2,1)}, bf16[4,192,256]{2,1,0:T(8,128)(2,1)S(1)}, u32[]{:S(2)}, u32[]{:S(2)}) collective-permute-start(bf16[4,192,256]{2,1,0:T(8,128)(2,1)} %copy-done.27), channel_id=1, source_target_pairs={{0,1},{1,0},{2,3},{3,2},{4,5},{5,4},{6,7},{7,6},{8,9},{9,8},{10,11... | collective-permute-start | bytes 1179656 | tf_op jit(solution)/shard_map/ppermute | solution.py:49
  126.0 29.5 %collective-permute-start.28 = (bf16[8,192,256]{2,1,0:T(8,128)(2,1)}, bf16[8,192,256]{2,1,0:T(8,128)(2,1)}, u32[]{:S(2)}, u32[]{:S(2)}) collective-permute-start(bf16[8,192,256]{2,1,0:T(8,128)(2,1)} %get-tuple-element.328.refs_0_), channel_id=1, source_target_pairs={{0,1},{1,0},{2,3},{3,2},{4,5},{5,4},{6,7},{7,6},{8,9},{9,8},{10,11... | collective-permute-start | bytes 2359304 | tf_op jit(solution)/shard_map/ppermute | solution.py:49
  126.6 28.9 %collective-permute-start.29 = (bf16[8,192,256]{2,1,0:T(8,128)(2,1)}, bf16[8,192,256]{2,1,0:T(8,128)(2,1)}, u32[]{:S(2)}, u32[]{:S(2)}) collective-permute-start(bf16[8,192,256]{2,1,0:T(8,128)(2,1)} %get-tuple-element.330.refs_2_), channel_id=1, source_target_pairs={{0,2},{1,3},{2,0},{3,1},{4,6},{5,7},{6,4},{7,5},{8,10},{9,11},{10,... | collective-permute-start | bytes 2359304 | tf_op jit(solution)/shard_map/ppermute | solution.py:49
  155.5 12.0 %collective-permute-start.30 = (bf16[8,192,256]{2,1,0:T(8,128)(2,1)}, bf16[8,192,256]{2,1,0:T(8,128)(2,1)}, u32[]{:S(2)}, u32[]{:S(2)}) collective-permute-start(bf16[8,192,256]{2,1,0:T(8,128)(2,1)} %get-tuple-element.328.refs_0_), channel_id=1, source_target_pairs={{0,16},{16,0},{1,17},{17,1},{2,18},{18,2},{3,19},{19,3},{4,20},{20... | collective-permute-start | bytes 2359304 | tf_op jit(solution)/shard_map/ppermute | solution.py:76
  155.6 11.9 %collective-permute-start.31 = (bf16[8,192,256]{2,1,0:T(8,128)(2,1)}, bf16[8,192,256]{2,1,0:T(8,128)(2,1)}, u32[]{:S(2)}, u32[]{:S(2)}) collective-permute-start(bf16[8,192,256]{2,1,0:T(8,128)(2,1)} %collective-permute-done.28.refs_1_), channel_id=1, source_target_pairs={{0,16},{16,0},{1,17},{17,1},{2,18},{18,2},{3,19},{19,3},{4,20},{20... | collective-permute-start | bytes 2359304 | tf_op jit(solution)/shard_map/ppermute | solution.py:76
  318.5 31.1 %collective-permute-start.66 = (bf16[8,192,256]{2,1,0:T(8,128)(2,1)S(1)}, bf16[8,192,256]{2,1,0:T(8,128)(2,1)S(1)}, u32[]{:S(2)}, u32[]{:S(2)}) collective-permute-start(bf16[8,192,256]{2,1,0:T(8,128)(2,1)S(1)} %get-tuple-element.412), channel_id=1, source_target_pairs={{0,1},{1,0},{2,3},{3,2},{4,5},{5,4},{6,7},{7,6},{8,9},{9,8},{10,11... | collective-permute-start | bytes 2359304 | tf_op jit(solution)/shard_map/ppermute | solution.py:49
  319.9 29.7 %collective-permute-start.67 = (bf16[8,192,256]{2,1,0:T(8,128)(2,1)S(1)}, bf16[8,192,256]{2,1,0:T(8,128)(2,1)S(1)}, u32[]{:S(2)}, u32[]{:S(2)}) collective-permute-start(bf16[8,192,256]{2,1,0:T(8,128)(2,1)S(1)} %get-tuple-element.414), channel_id=1, source_target_pairs={{0,2},{1,3},{2,0},{3,1},{4,6},{5,7},{6,4},{7,5},{8,10},{9,11},{10,... | collective-permute-start | bytes 2359304 | tf_op jit(solution)/shard_map/ppermute | solution.py:49
  351.8 12.5 %collective-permute-start.70 = (bf16[2048,1024]{1,0:T(8,128)(2,1)S(1)}, bf16[2048,1024]{1,0:T(8,128)(2,1)S(1)}, u32[]{:S(2)}, u32[]{:S(2)}) collective-permute-start(bf16[2048,1024]{1,0:T(8,128)(2,1)S(1)} %copy-done.40), channel_id=1, source_target_pairs={{0,16},{16,0},{1,17},{17,1},{2,18},{18,2},{3,19},{19,3},{4,20},{20... | collective-permute-start | bytes 12582920 | tf_op jit(solution)/shard_map/ppermute | solution.py:76
  365.5 25.7 %collective-permute-start.78 = (bf16[8,64,1024]{2,1,0:T(8,128)(2,1)S(1)}, bf16[8,64,1024]{2,1,0:T(8,128)(2,1)S(1)}, u32[]{:S(2)}, u32[]{:S(2)}) collective-permute-start(bf16[8,64,1024]{2,1,0:T(8,128)(2,1)S(1)} %get-tuple-element.474), channel_id=1, source_target_pairs={{0,1},{1,0},{2,3},{3,2},{4,5},{5,4},{6,7},{7,6},{8,9},{9,8},{10,11... | collective-permute-start | bytes 3145736 | tf_op jit(solution)/shard_map/ppermute | solution.py:49
  366.8 24.4 %collective-permute-start.79 = (bf16[8,64,1024]{2,1,0:T(8,128)(2,1)S(1)}, bf16[8,64,1024]{2,1,0:T(8,128)(2,1)S(1)}, u32[]{:S(2)}, u32[]{:S(2)}) collective-permute-start(bf16[8,64,1024]{2,1,0:T(8,128)(2,1)S(1)} %get-tuple-element.475), channel_id=1, source_target_pairs={{0,2},{1,3},{2,0},{3,1},{4,6},{5,7},{6,4},{7,5},{8,10},{9,11},{10,... | collective-permute-start | bytes 3145736 | tf_op jit(solution)/shard_map/ppermute | solution.py:49
  367.8 19.7 %collective-permute-start.76 = (bf16[2,2,192,256]{3,2,1,0:T(8,128)(2,1)S(1)}, bf16[2,2,192,256]{3,2,1,0:T(8,128)(2,1)S(1)}, u32[]{:S(2)}, u32[]{:S(2)}) collective-permute-start(bf16[2,2,192,256]{3,2,1,0:T(8,128)(2,1)S(1)} %get-tuple-element.452), channel_id=1, source_target_pairs={{0,4},{1,5},{2,6},{3,7},{4,0},{5,1},{6,2},{7,3},{8,12},{9,13},{10,... | collective-permute-start | bytes 1179656 | tf_op jit(solution)/shard_map/ppermute | solution.py:49
  399.5 15.5 %collective-permute-start.80 = (bf16[6144,256]{1,0:T(8,128)(2,1)S(1)}, bf16[6144,256]{1,0:T(8,128)(2,1)S(1)}, u32[]{:S(2)}, u32[]{:S(2)}) collective-permute-start(bf16[6144,256]{1,0:T(8,128)(2,1)S(1)} %get-tuple-element.487), channel_id=1, source_target_pairs={{0,16},{16,0},{1,17},{17,1},{2,18},{18,2},{3,19},{19,3},{4,20},{20... | collective-permute-start | bytes 9437192 | tf_op jit(solution)/shard_map/ppermute | solution.py:76
  399.6 14.3 %collective-permute-start.81 = (bf16[4,64,1024]{2,1,0:T(8,128)(2,1)S(1)}, bf16[4,64,1024]{2,1,0:T(8,128)(2,1)S(1)}, u32[]{:S(2)}, u32[]{:S(2)}) collective-permute-start(bf16[4,64,1024]{2,1,0:T(8,128)(2,1)S(1)} %get-tuple-element.489), channel_id=1, source_target_pairs={{0,2},{1,3},{2,0},{3,1},{4,6},{5,7},{6,4},{7,5},{8,10},{9,11},{10,... | collective-permute-start | bytes 1572872 | tf_op jit(solution)/shard_map/ppermute | solution.py:49
  400.7 14.0 %collective-permute-start.82 = (bf16[4,64,1024]{2,1,0:T(8,128)(2,1)S(1)}, bf16[4,64,1024]{2,1,0:T(8,128)(2,1)S(1)}, u32[]{:S(2)}, u32[]{:S(2)}) collective-permute-start(bf16[4,64,1024]{2,1,0:T(8,128)(2,1)S(1)} %get-tuple-element.491), channel_id=1, source_target_pairs={{0,1},{1,0},{2,3},{3,2},{4,5},{5,4},{6,7},{7,6},{8,9},{9,8},{10,11... | collective-permute-start | bytes 1572872 | tf_op jit(solution)/shard_map/ppermute | solution.py:49
  401.9 13.1 %collective-permute-start.83 = (bf16[2,1,192,256]{3,2,1,0:T(8,128)(2,1)S(1)}, bf16[2,1,192,256]{3,2,1,0:T(8,128)(2,1)S(1)}, u32[]{:S(2)}, u32[]{:S(2)}) collective-permute-start(bf16[2,1,192,256]{3,2,1,0:T(8,128)(2,1)S(1)} %get-tuple-element.469), channel_id=1, source_target_pairs={{0,8},{1,9},{2,10},{3,11},{4,12},{5,13},{6,14},{7,15},{8,0},{9,1},... | collective-permute-start | bytes 589832 | tf_op jit(solution)/shard_map/ppermute | solution.py:49
  415.9 18.8 %collective-permute-start.84 = (bf16[8,192,256]{2,1,0:T(8,128)(2,1)S(1)}, bf16[8,192,256]{2,1,0:T(8,128)(2,1)S(1)}, u32[]{:S(2)}, u32[]{:S(2)}) collective-permute-start(bf16[8,192,256]{2,1,0:T(8,128)(2,1)S(1)} %get-tuple-element.496), channel_id=1, source_target_pairs={{0,1},{1,0},{2,3},{3,2},{4,5},{5,4},{6,7},{7,6},{8,9},{9,8},{10,11... | collective-permute-start | bytes 2359304 | tf_op jit(solution)/shard_map/ppermute | solution.py:49
  417.2 18.5 %collective-permute-start.85 = (bf16[8,192,256]{2,1,0:T(8,128)(2,1)S(1)}, bf16[8,192,256]{2,1,0:T(8,128)(2,1)S(1)}, u32[]{:S(2)}, u32[]{:S(2)}) collective-permute-start(bf16[8,192,256]{2,1,0:T(8,128)(2,1)S(1)} %get-tuple-element.497), channel_id=1, source_target_pairs={{0,2},{1,3},{2,0},{3,1},{4,6},{5,7},{6,4},{7,5},{8,10},{9,11},{10,... | collective-permute-start | bytes 2359304 | tf_op jit(solution)/shard_map/ppermute | solution.py:49
  418.3 12.6 %collective-permute-start.86 = (bf16[2,2,64,1024]{3,2,1,0:T(8,128)(2,1)S(1)}, bf16[2,2,64,1024]{3,2,1,0:T(8,128)(2,1)S(1)}, u32[]{:S(2)}, u32[]{:S(2)}) collective-permute-start(bf16[2,2,64,1024]{3,2,1,0:T(8,128)(2,1)S(1)} %get-tuple-element.499), channel_id=1, source_target_pairs={{0,4},{1,5},{2,6},{3,7},{4,0},{5,1},{6,2},{7,3},{8,12},{9,13},{10,... | collective-permute-start | bytes 1572872 | tf_op jit(solution)/shard_map/ppermute | solution.py:49
  426.5 23.9 %collective-permute-start.91 = (bf16[4,384,512]{2,1,0:T(8,128)(2,1)S(1)}, bf16[4,384,512]{2,1,0:T(8,128)(2,1)S(1)}, u32[]{:S(2)}, u32[]{:S(2)}) collective-permute-start(bf16[4,384,512]{2,1,0:T(8,128)(2,1)S(1)} %slice_bitcast_fusion), channel_id=1, source_target_pairs={{0,16},{16,0},{1,17},{17,1},{2,18},{18,2},{3,19},{19,3},{4,20},{20... | collective-permute-start | bytes 4718600 | tf_op jit(solution)/shard_map/ppermute | solution.py:76
  435.7 12.9 %collective-permute-start.89 = (bf16[2,1,64,1024]{3,2,1,0:T(8,128)(2,1)S(1)}, bf16[2,1,64,1024]{3,2,1,0:T(8,128)(2,1)S(1)}, u32[]{:S(2)}, u32[]{:S(2)}) collective-permute-start(bf16[2,1,64,1024]{3,2,1,0:T(8,128)(2,1)S(1)} %get-tuple-element.510), channel_id=1, source_target_pairs={{0,8},{1,9},{2,10},{3,11},{4,12},{5,13},{6,14},{7,15},{8,0},{9,1},... | collective-permute-start | bytes 786440 | tf_op jit(solution)/shard_map/ppermute | solution.py:49
  449.2 11.6 %collective-permute-start.90 = (bf16[2,2,192,256]{3,2,1,0:T(8,128)(2,1)S(1)}, bf16[2,2,192,256]{3,2,1,0:T(8,128)(2,1)S(1)}, u32[]{:S(2)}, u32[]{:S(2)}) collective-permute-start(bf16[2,2,192,256]{3,2,1,0:T(8,128)(2,1)S(1)} %get-tuple-element.516), channel_id=1, source_target_pairs={{0,4},{1,5},{2,6},{3,7},{4,0},{5,1},{6,2},{7,3},{8,12},{9,13},{10,... | collective-permute-start | bytes 1179656 | tf_op jit(solution)/shard_map/ppermute | solution.py:49
  461.8 13.4 %collective-permute-start.95 = (f32[8,512]{1,0:T(8,128)S(1)}, f32[8,512]{1,0:T(8,128)S(1)}, u32[]{:S(2)}, u32[]{:S(2)}) collective-permute-start(f32[8,512]{1,0:T(8,128)S(1)} %stack.10), channel_id=1, source_target_pairs={{0,16},{16,0},{1,17},{17,1},{2,18},{18,2},{3,19},{19,3},{4,20},{20... | collective-permute-start | bytes 49160 | tf_op jit(solution)/shard_map/ppermute | solution.py:76
  (116 other events, 1132.4 us)
Sparse Core Ops, SparseCore 0:
  51.3 91.0 all-gather.1

commit v4 on v3

--- a/solution.py
+++ b/solution.py
@@ -33,7 +33,7 @@
 BFLOAT = jnp.bfloat16
 SINGLE = jnp.float32
 MIB = 1024 * 1024
-BYTES_PER_US = 1200000
+BYTES_PER_US = 600000
 MICROSECONDS = {
     "prep": 5, "a1": 3, "a2": 5, "as": 4.5, "a3": 4, "a4": 4.7, "a5": 4, "a6": 3.7, "head": 5.3, "g5": 5.2, "g4": 5.4, "gy": 7,
     "g2": 7.3, "g1": 8, "g0": 3, "gx": 6.4, "dxs": 5, "dw1": 3.4, "dw2": 2.1, "dw3": 2.9, "dws": 2.9, "dw4a": 1.7, "dw4b": 1.9,
@@ -51,6 +51,15 @@
 
 def pin(value, after):
     return lax.optimization_barrier((value, after))[0]
+
+
+class Total:
+    def __init__(self, *parts):
+        self.parts = parts
+
+    @property
+    def sum(self):
+        return self.parts[0] + self.parts[1]
 
 
 def dp_sum(value, fillers=(), first=None):
@@ -66,10 +75,12 @@
             result = fillers[len(results)](value)
             got, result = lax.optimization_barrier((got, result))
             results.append(result)
+        if bit == bits[-1]:
+            break
         value = value + got
     for filler in fillers[len(results) :]:
-        results.append(filler(value))
-    return value, results
+        results.append(filler(got))
+    return Total(value, got), results
 
 
 def swap_pipe(value):
@@ -128,9 +139,70 @@
     return (mask * ((rstd * gain) * (gz - first_row - xhat * second_row))).astype(BFLOAT)
 
 
+class Both:
+    def __init__(self, refs, start=0):
+        self.refs, self.start = refs, start
+
+    def __getitem__(self, index):
+        rows, columns = index
+        rows = slice(rows.start + self.start, rows.stop + self.start)
+        return sum(ref[rows, columns] for ref in self.refs)
+
+
+class Chunk:
+    def __init__(self, refs, which, step):
+        self.refs, self.first = refs, WIDE_ROW + 8 * which + step
+
+    def __getitem__(self, index):
+        rows, columns = index
+        return sum(ref[pl.ds(self.first + 4 * rows.start, 1), columns] for ref in self.refs)
+
+
+class Inverse:
+    def __init__(self, refs, core):
+        self.refs, self.core = refs, core
+
+    def __getitem__(self, m):
+        row = sum(ref[COUNT_ROW : COUNT_ROW + 1, 0:128] for ref in self.refs)
+        lane = lax.broadcasted_iota(jnp.int32, (1, 128), 1)
+        return 1.0 / jnp.sum(jnp.where(lane == 2 * self.core + m, row, 0.0), axis=1, keepdims=True)
+
+
+ONE = (0,)
+MID_ROW, WIDE_ROW, COUNT_ROW, TABLE_ROWS = 4, 12, 36, 40
+
+
+def paired(kernel, views, tabs=None, inv=None, tables=1, lead=0):
+    def run(*refs):
+        fixed, refs = {}, list(refs)
+        if inv is not None:
+            core = refs.pop(0)[0]
+            table, refs[lead : lead + tables] = refs[lead : lead + tables], []
+            step = pl.program_id(0)
+            fixed[inv] = Inverse(table, core)
+            for at, (kind, which) in (tabs or {}).items():
+                if kind == "wide":
+                    fixed[at] = Chunk(table, which, step)
+                else:
+                    fixed[at] = Both(table, MID_ROW + 2 * which if kind == "mid" else 0)
+        given, at = [], 0
+        while at < len(refs) or len(given) in fixed:
+            if len(given) in fixed:
+                given.append(fixed[len(given)])
+            elif len(given) in views:
+                given.extend([Both(refs[at : at + 2], start) for start in views[len(given)]])
+                at += 2
+            else:
+                given.append(refs[at])
+                at += 1
+        return kernel(*given)
+
+    return run
+
+
 def k_prep(core_ref, assign_ref, height_ref, width_ref, img_ref, perm_ref, out_ref, mask_ref, count_ref):
     slot = pl.program_id(0)
-    image = assign_ref[core_ref[0] * SLOTS + slot]
+    image = assign_ref[0, core_ref[0] * SLOTS + slot]
     pixel = lax.broadcasted_iota(jnp.int32, (PIX, 1), 0)
     inside = ((pixel & (HB - 1)) < height_ref[image]) & (pixel < width_ref[image] * HB)
     mask = jnp.where(inside, 1.0, 0.0).astype(SINGLE)
@@ -141,7 +213,7 @@
     column = lax.broadcasted_iota(jnp.int32, count_ref.shape, 1)
     counts = jnp.zeros(count_ref.shape, jnp.int32)
     for m in range(4):
-        pair = (assign_ref[2 * m], assign_ref[2 * m + 1])
+        pair = (assign_ref[0, 2 * m], assign_ref[0, 2 * m + 1])
         total = sum(height_ref[k] * width_ref[k] for k in pair)
         counts = jnp.where(column == m, total, counts)
     count_ref[...] = counts.astype(SINGLE)
@@ -298,7 +370,7 @@
         put_sums(sum_ref, [a, a * a], True)
 
 
-def k_head(slot_ref, inv_ref, total_ref, tab_ref, mask_ref, a_ref, y_ref, c0, c1, c2, c3, blk_ref, gz_ref, sum_ref):
+def k_head(order_ref, inv_ref, total_ref, tab_ref, mask_ref, a_ref, y_ref, c0, c1, c2, c3, blk_ref, gz_ref, sum_ref):
     cots = (c0, c1, c2, c3)
     gain, bias = tab_ref[0:1, :], tab_ref[1:2, :]
     for m in range(2):
@@ -472,7 +544,7 @@
         )
 
 
-def k_image_grad(slot_ref, ga_ref, mask_ref, w_ref, short_ref, perm_ref, *refs):
+def k_image_grad(core_ref, ga_ref, mask_ref, w_ref, short_ref, perm_ref, *refs):
     out_ref = refs[-1]
     grads = dot_back(ga_ref[...].reshape(4 * PIX, C_MID), w_ref[...])
     mask = mask_ref[...]
@@ -484,12 +556,12 @@
         parts.append((grad * mask).astype(BFLOAT))
     planes = jnp.concatenate(parts, axis=0)
     image = lax.dot_general(perm_ref[...], planes, (((0,), (0,)), ((), ())), preferred_element_type=SINGLE).astype(BFLOAT)
-    core = slot_ref[SLOTS]
+    core = core_ref[0]
     out_ref[core, 0] = image[:, : C_IN // 2]
     out_ref[1 - core, 0] = image[:, C_IN // 2 :]
 
 
-def k_place(slot_ref, own_ref, got_ref, *refs):
+def k_place(core_ref, order_ref, own_ref, got_ref, *refs):
     out_ref = refs[-1]
     step = pl.program_id(0)
 
@@ -506,9 +578,9 @@
     refs[-1][...] = in_ref[...].reshape(in_ref.shape[-2:]).T
 
 
-def k_grad(slot_ref, feature_ref, grad_ref, *refs):
+def k_grad(core_ref, feature_ref, grad_ref, *refs):
     keep_ref, send_ref = refs[-2:]
-    core = slot_ref[SLOTS]
+    core = core_ref[0]
     rows, half = feature_ref.shape[-2], grad_ref.shape[-1] // 2
     for k in range(grad_ref.shape[0]):
         feature = feature_ref[k % feature_ref.shape[0]]
@@ -611,7 +683,7 @@
 
 def k_update(start_ref, square_ref, *refs):
     step = pl.program_id(0)
-    norms = jnp.sqrt(square_ref[...])
+    norms = jnp.sqrt(square_ref[0:8, :])
     weight_norm, grad_norm = norms[0:1], norms[1:2]
     ratio = TRUST * weight_norm / (grad_norm + DECAY * weight_norm)
     lane = lax.broadcasted_iota(jnp.int32, (1, 128), 1)
@@ -832,17 +904,12 @@
     core_row = core[None].astype(jnp.int32)
     x, mask, count_rows = call(
         k_prep, "prep", (SLOTS,),
-        [spec((1, 4 * PIX, C_IN), lambda s, core, order, *_: (order[core[0] * SLOTS + s], 0, 0)), full((4 * PIX, 4 * PIX))],
+        [spec((1, 4 * PIX, C_IN), lambda s, core, order, *_: (order[0, core[0] * SLOTS + s], 0, 0)), full((4 * PIX, 4 * PIX))],
         [spec((4, PIX, C_IN), lambda s, *_: (0, s, 0)), spec((PIX, 1), lambda s, *_: (s, 0)), full((4, C_MID))],
         [vmem_of((4, ROWS, C_IN), BFLOAT), vmem_of((ROWS, 1)), shape_of((4, C_MID))], [],
-        (core_row, assign[0], heights, widths, in_hbm(images.reshape(IMG_DEV, 4 * PIX, C_IN)), in_hbm(perm)), prefetch=4, vmem=7,
+        (core_row, assign, heights, widths, in_hbm(images.reshape(IMG_DEV, 4 * PIX, C_IN)), in_hbm(perm)), prefetch=4, vmem=7,
     )
     mask = in_vmem(mask)
-    order = assign[0].reshape(2, SLOTS)
-    own_slots = lax.dynamic_index_in_dim(order, core, 0, keepdims=False)
-    other_slots = lax.dynamic_index_in_dim(order, 1 - core, 0, keepdims=False)
-    slots = jnp.concatenate([own_slots, core_row, other_slots])
-
     mid_cols, wide_cols = bn_mid.shape[1], bn_wide.shape[1]
     tables = jnp.concatenate(
         [
@@ -875,12 +942,12 @@
         extra = tuple(hold(b) for b in bufs or ()) + (() if token is None else (token,))
         return call(
             k_grad, name, (tiles,), [feature_spec, grad_spec] + [ANYWHERE] * len(extra),
-            [out_spec] * 2, [space(shape, BFLOAT)] * 2, [], (slots, feature, grad) + extra,
+            [out_spec] * 2, [space(shape, BFLOAT)] * 2, [], (core_row, feature, grad) + extra,
             prefetch=1, vmem=7, aliases={3: 0, 4: 1} if bufs else {},
         )
 
     full_row = full((4, C_MID))
-    full_tab = full((2, C_MID))
+    full_table = full((TABLE_ROWS, C_MID))
     full_mask = full((ROWS, 1))
     full_mid = full((ROWS, C_MID))
     plane_pair = spec((2, ROWS, C_MID), lambda s: (jnp.minimum(s, 1), 0, 0))
@@ -890,7 +957,7 @@
 
     chunk = spec((ROWS, TILE), lambda k, *_: (0, k))
     chunk_sum = spec((4, TILE), lambda k, *_: (0, k))
-    chunk_tab = spec((2, TILE), lambda k, *_: (0, k))
+    chunk_eight = spec((8, TILE), lambda k, *_: (0, k))
     four_a = narrow_block(lambda k: (11, 0))
     four_b = narrow_block(lambda k: (jnp.maximum(k - 1, 0), 0))
 
@@ -912,11 +979,7 @@
 
     first_sum, (a_kept, (x_kept, first_b), _unused) = dp_sum(jnp.concatenate([part1, tables]), [keep_in_hbm(narrow_a), lambda token: (keep_in_hbm(x)(token), part_b if fast else token), second_part_b])
     x_kept, a_kept = in_hbm(x_kept), in_hbm(a_kept)
-    total1, tables = first_sum[:4], first_sum[4:]
-    mid, table = tables[:8], tables[8:32].reshape(6, C_OUT)
-    inv = lax.dynamic_slice(1.0 / tables[32, :4], (2 * core,), (2,))
-    mid1, mid2, mid4, mid5 = (mid[2 * k : 2 * k + 2] for k in range(4))
-    tab3, tabs, tab6 = (table[2 * k : 2 * k + 2] for k in range(3))
+    base = in_vmem(first_sum.sum)
 
     a_s, part_s = call(
         k_short, "as", (4,),
@@ -933,12 +996,12 @@
     straight = lambda s: s
 
     a2, h1, part2 = call(
-        k_conv_two, "a2", (3,),
-        [SCALARS, full_row, full_tab, full_mask, plane_pair] + conv_weights(2, turned),
+        paired(k_conv_two, {}, {1: ("base", 0), 2: ("mid", 0)}, 0, 2), "a2", (3,),
+        [SCALARS, full_table, full_table, full_mask, plane_pair] + conv_weights(2, turned),
         [full_mid, plane_pair, full_row],
         [vmem_of((ROWS, C_MID)), vmem_of((4, ROWS, C_MID), BFLOAT), shape_of((4, C_MID))],
         [pltpu.VMEM((2, PAD + ROWS + PAD, C_MID), SINGLE)] * 2,
-        (inv, total1, mid1, mask, a1) + (a_kept,) * 3, vmem=11,
+        (core_row, *first_sum.parts, mask, a1) + (a_kept,) * 3, vmem=11,
     )
     a2 = in_vmem(a2)
 
@@ -957,16 +1020,16 @@
     turn_h1 = turn(h1, spec((1, ROWS, C_MID), lambda k: (k, 0, 0)), (4,), (4 * C_MID, ROWS), lambda k: (k, 0))
     total2, (h1_t, big_b, _unused) = dp_sum(part2, [turn_h1, third_part_b, fourth_b])
 
-    def expand(name, a, total, tab, row):
+    def expand(name, a, total, which, row):
         return call(
-            k_expand, name, (4,),
-            [SCALARS, full_row, full_tab, full_mask, full_mid, spec((TILE, TILE), lambda k: (row, k))],
+            paired(k_expand, {1: ONE}, {2: ("mid", which)}, 0), name, (4,),
+            [SCALARS, full_table, full_row, full_row, full_mask, full_mid, spec((TILE, TILE), lambda k: (row, k))],
             [full_mid, chunk, chunk_sum],
             [vmem_of((ROWS, C_MID), BFLOAT), vmem_of((ROWS, C_OUT)), shape_of((4, C_OUT))], [],
-            (inv, total, tab, mask, a, in_hbm(wide)), vmem=6,
+            (core_row, base, *total.parts, mask, a, in_hbm(wide)), vmem=6,
         )
 
-    h2, a3, part3 = expand("a3", a2, total2, mid2, 0)
+    h2, a3, part3 = expand("a3", a2, total2, 1, 0)
     whole = spec((ROWS, C_MID), lambda k: (0, 0))
 
     def swap_b(token):
@@ -997,14 +1060,13 @@
         ],
     )
     as_kept, a3_kept = in_hbm(as_kept), in_hbm(a3_kept)
-    total3, total_s = total3s[:4], total3s[4:]
 
     y, a4, part4 = call(
-        k_meet, "a4", (4,),
-        [SCALARS, chunk_sum, chunk_sum, chunk_tab, chunk_tab, full_mask, chunk, chunk, four_a, four_b],
+        paired(k_meet, {1: (0, 4)}, {3: ("wide", 0), 4: ("wide", 1)}, 0), "a4", (4,),
+        [SCALARS, full_table, chunk_eight, chunk_eight, full_mask, chunk, chunk, four_a, four_b],
         [chunk, full_mid, full_row],
         [vmem_of((ROWS, C_OUT), BFLOAT), vmem_of((ROWS, C_MID)), shape_of((4, C_MID))], [],
-        (inv, total3, total_s, tab3, tabs, mask, in_vmem(a3), in_vmem(a_s), a_kept, in_vmem(narrow_b)), vmem=8,
+        (core_row, base, *total3s.parts, mask, in_vmem(a3), in_vmem(a_s), a_kept, in_vmem(narrow_b)), vmem=8,
     )
     a4 = in_vmem(a4)
     def turn_x(q, start, into):
@@ -1031,12 +1093,12 @@
     del x_t0
 
     a5, h4, part5 = call(
-        k_conv_one, "a5", (3,),
-        [SCALARS, full_row, full_tab, full_mask, full_mid] + conv_weights(3, straight),
+        paired(k_conv_one, {1: ONE}, {2: ("mid", 2)}, 0), "a5", (3,),
+        [SCALARS, full_table, full_row, full_row, full_mask, full_mid] + conv_weights(3, straight),
         [full_mid, full_mid, full_row],
         [vmem_of((ROWS, C_MID)), vmem_of((ROWS, C_MID), BFLOAT), shape_of((4, C_MID))],
         [pltpu.VMEM((PAD + ROWS + PAD, C_MID), SINGLE)] * 2,
-        (inv, total4, mid4, mask, a4) + (in_vmem(narrow_b),) * 3, vmem=8,
+        (core_row, base, *total4.parts, mask, a4) + (in_vmem(narrow_b),) * 3, vmem=8,
     )
     a5 = in_vmem(a5)
     total5, (h4_t, b_kept, _unused, x_t) = dp_sum(
@@ -1049,22 +1111,22 @@
         ],
     )
     b_kept = in_hbm(b_kept)
-    h5, a6, part6 = expand("a6", a5, total5, mid5, 3)
+    h5, a6, part6 = expand("a6", a5, total5, 3, 3)
     total6, (h5_t, a6_kept) = dp_sum(part6, [turn(h5, whole, (1,), (C_MID, ROWS), lambda k: (0, 0)), keep_in_hbm(a6)])
     a6_kept = in_hbm(a6_kept)
 
     cot = in_hbm(cotangent.transpose(0, 2, 1, 3).reshape(IMG_DEV, PIX, C_OUT))
     blk, gz6, s6 = call(
-        k_head, "head", (4,),
-        [SCALARS, chunk_sum, chunk_tab, full_mask, chunk, chunk]
-        + [spec((1, PIX, TILE), lambda k, slot, s=s: (slot[s], 0, k)) for s in range(SLOTS)],
+        paired(k_head, {2: ONE}, {3: ("wide", 2)}, 1, lead=1), "head", (4,),
+        [full_table, chunk_sum, chunk_sum, full_mask, chunk, chunk]
+        + [spec((1, PIX, TILE), lambda k, core, order, s=s: (order[0, core[0] * SLOTS + s], 0, k)) for s in range(SLOTS)],
         [
-            spec((1, ROWS, TILE), lambda k, slot: ((k // 2) ^ slot[SLOTS], 0, lax.rem(k, 2))),
+            spec((1, ROWS, TILE), lambda k, core, _order: ((k // 2) ^ core[0], 0, lax.rem(k, 2))),
             chunk,
             chunk_sum,
         ],
         [shape_of((2, ROWS, C_OUT // 2), BFLOAT), vmem_of((ROWS, C_OUT)), shape_of((4, C_OUT))], [],
-        (slots, inv, total6, tab6, mask, in_vmem(a6), in_hbm(y_kept), cot, cot, cot, cot), prefetch=1, vmem=9,
+        (core_row, assign, base, *total6.parts, mask, in_vmem(a6), in_hbm(y_kept), cot, cot, cot, cot), prefetch=2, vmem=9,
     )
     gz6 = in_vmem(gz6)
 
@@ -1073,13 +1135,13 @@
         return call(
             k_place, name, (IMG_DEV,),
             [
-                spec((1,) + block, lambda t, slot: (0, jnp.minimum(t, SLOTS - 1), 0, 0)),
-                spec(block, lambda t, slot: (jnp.maximum(t - SLOTS, 0), 0, 0)),
+                spec((1,) + block, lambda t, *_: (0, jnp.minimum(t, SLOTS - 1), 0, 0)),
+                spec(block, lambda t, *_: (jnp.maximum(t - SLOTS, 0), 0, 0)),
                 ANYWHERE,
             ],
-            spec(block, lambda t, slot: (slot[t + (t >= SLOTS)], 0, 0)),
+            spec(block, lambda t, core, order: (order[0, (core[0] * SLOTS + t) & (IMG_DEV - 1)], 0, 0)),
             shape_of((IMG_DEV,) + pair.shape[2:], BFLOAT), [],
-            (slots, pair, got, token), prefetch=1, vmem=9,
+            (core_row, assign, pair, got, token), prefetch=2, vmem=9,
         )
 
     blk = blk.reshape(2, SLOTS, PIX, C_OUT // 2)
@@ -1094,12 +1156,13 @@
     )
 
     ga6, gz5, s5 = call(
-        k_back_six, "g5", (4,),
-        [SCALARS, chunk, chunk, chunk_sum, chunk_sum, chunk_tab, full_mask, spec((TILE, TILE), lambda k: (3, k)), full_mid, full_row, full_tab],
+        paired(k_back_six, {3: ONE, 4: ONE, 9: ONE}, {5: ("wide", 2), 10: ("mid", 3)}, 0), "g5", (4,),
+        [SCALARS, full_table, chunk, chunk, chunk_sum, chunk_sum, chunk_sum, chunk_sum, full_mask, spec((TILE, TILE), lambda k: (3, k)), full_mid,
+         full_row, full_row],
         [chunk, full_mid, full_row],
         [vmem_of((ROWS, C_OUT), BFLOAT), vmem_of((ROWS, C_MID)), shape_of((4, C_MID))],
         [pltpu.VMEM((ROWS, C_MID), SINGLE)],
-        (inv, gz6, a6_kept, total6, sum6, tab6, mask, in_hbm(wide), a5, total5, mid5), vmem=9,
+        (core_row, base, gz6, a6_kept, *total6.parts, *sum6.parts, mask, in_hbm(wide), a5, *total5.parts), vmem=9,
     )
     gz5 = in_vmem(gz5)
 
@@ -1113,19 +1176,20 @@
     sum5, (bufs_w, block_local) = dp_sum(
         s5,
         [
-            lambda token: weight_grad("dw6", h5_t[None], wide_rows(0), *whole_wide(ga6), 2, wide_shape, 256, 6, None, token, hbm_of),
+            lambda token: weight_grad("dw6", h5_t[None], wide_rows(0), *whole_wide(ga6), 2, wide_shape, 256, 6, None, token, vmem_of),
             lambda token: place("place_out", blk, got_blk, token),
         ],
     )
     block_local = block_local.reshape(IMG_DEV, WB, HB, C_OUT // 2).transpose(0, 2, 1, 3)
 
     col5, gz4, s4 = call(
-        k_back_conv_one, "g4", (3,),
-        [SCALARS, full_mid, full_mid, full_row, full_row, full_tab, full_mask] + conv_weights(3, straight) + [full_mid, full_row, full_tab],
+        paired(k_back_conv_one, {3: ONE, 4: ONE, 11: ONE}, {5: ("mid", 3), 12: ("mid", 2)}, 0), "g4", (3,),
+        [SCALARS, full_table, full_mid, full_mid, full_row, full_row, full_row, full_row, full_mask] + conv_weights(3, straight)
+        + [full_mid, full_row, full_row],
         [spec((3, ROWS, C_MID), lambda s: (s, 0, 0)), full_mid, full_row],
         [vmem_of((9, ROWS, C_MID), BFLOAT), vmem_of((ROWS, C_MID)), shape_of((4, C_MID))],
         [pltpu.VMEM((PAD + ROWS + PAD, C_MID), SINGLE)] * 2 + [pltpu.VMEM((ROWS, C_MID), SINGLE)],
-        (inv, gz5, a5, total5, sum5, mid5, mask, b_kept, b_kept, b_kept, a4, total4, mid4), vmem=10,
+        (core_row, base, gz5, a5, *total5.parts, *sum5.parts, mask, b_kept, b_kept, b_kept, a4, *total4.parts), vmem=10,
     )
     gz4 = in_vmem(gz4)
     one_turned = spec((1, C_MID, ROWS), lambda t, slot: (0, 0, 0))
@@ -1143,12 +1207,12 @@
     bufs_b = results4[2]
 
     ga4, gj, s3 = call(
-        k_back_four, "gy", (4,),
-        [SCALARS, full_mid, full_mid, full_row, full_row, full_tab, full_mask, four_a, four_b,
-         chunk, chunk, chunk, chunk_sum, chunk_sum, chunk_tab, chunk_tab],
+        paired(k_back_four, {3: ONE, 4: ONE, 12: (0, 4)}, {5: ("mid", 2), 14: ("wide", 0), 15: ("wide", 1)}, 0), "gy", (4,),
+        [SCALARS, full_table, full_mid, full_mid, full_row, full_row, full_row, full_row, full_mask, four_a, four_b,
+         chunk, chunk, chunk, chunk_eight, chunk_eight],
         [full_mid, chunk, spec((6, TILE), lambda k: (0, k))],
         [vmem_of((ROWS, C_MID), BFLOAT), vmem_of((ROWS, C_OUT)), shape_of((6, C_OUT))], [],
-        (inv, gz4, a4, total4, sum4, mid4, mask, a_kept, b_kept, gz6, a3_kept, as_kept, total3, total_s, tab3, tabs), vmem=12,
+        (core_row, base, gz4, a4, *total4.parts, *sum4.parts, mask, a_kept, b_kept, gz6, a3_kept, as_kept, *total3s.parts), vmem=12,
     )
     gj = in_vmem(gj)
 
@@ -1184,13 +1248,13 @@
     held["b"] = results3[2]
 
     ga3, gas, gz2, s2 = call(
-        k_back_three, "g2", (4,),
-        [SCALARS, chunk, chunk, chunk, chunk_sum, chunk_sum, spec((6, TILE), lambda k: (0, k)), chunk_tab, chunk_tab, full_mask,
-         spec((TILE, TILE), lambda k: (0, k)), full_mid, full_row, full_tab],
+        paired(k_back_three, {4: (0, 4), 6: ONE, 12: ONE}, {7: ("wide", 0), 8: ("wide", 1), 13: ("mid", 1)}, 0), "g2", (4,),
+        [SCALARS, full_table, chunk, chunk, chunk, chunk_eight, chunk_eight, spec((6, TILE), lambda k: (0, k)), spec((6, TILE), lambda k: (0, k)), full_mask,
+         spec((TILE, TILE), lambda k: (0, k)), full_mid, full_row, full_row],
         [chunk, chunk, full_mid, full_row],
         [hbm_of((ROWS, C_OUT), BFLOAT), hbm_of((ROWS, C_OUT), BFLOAT), vmem_of((ROWS, C_MID)), shape_of((4, C_MID))],
         [pltpu.VMEM((ROWS, C_MID), SINGLE)],
-        (inv, gj, a3_kept, as_kept, total3, total_s, sum3, tab3, tabs, mask, in_hbm(wide), a2, total2, mid2), vmem=11,
+        (core_row, base, gj, a3_kept, as_kept, *total3s.parts, *sum3.parts, mask, in_hbm(wide), a2, *total2.parts), vmem=11,
     )
     gz2 = in_vmem(gz2)
 
@@ -1216,12 +1280,12 @@
         return state
 
     def grad_three(token):
-        held["w"] = weight_grad("dw3", h2_t[None], wide_rows(0), *whole_wide(ga3), 2, wide_shape, 256, 0, bufs_w, token, hbm_of)
+        held["w"] = weight_grad("dw3", h2_t[None], wide_rows(0), *whole_wide(ga3), 2, wide_shape, 256, 0, bufs_w, token, vmem_of)
         return held["w"]
 
     def grad_short(q):
         def filler(token):
-            held["w"] = weight_grad("dws", x_t[None], wide_rows(2 * q), *whole_wide(gas), 2, wide_shape, 256, 2 + 2 * q, held["w"], token, hbm_of)
+            held["w"] = weight_grad("dws", x_t[None], wide_rows(2 * q), *whole_wide(gas), 2, wide_shape, 256, 2 + 2 * q, held["w"], token, vmem_of)
             return held["w"]
 
         return filler
@@ -1238,18 +1302,19 @@
     held["b"], bufs_w = results2[1]
     got_w = held["got_w"]
     if fast:
-        split = split_group("split_w", bufs_w[0], pin(got_w, sum2), w_wide.shape[0], lambda which, m: 16 * which + m)
-        sum2, split, held["b"] = lax.optimization_barrier((sum2, split, third_exchange_b(sum2)))
+        split = split_group("split_w", bufs_w[0], pin(got_w, sum2.parts[1]), w_wide.shape[0], lambda which, m: 16 * which + m)
+        last, split, held["b"] = lax.optimization_barrier((sum2.parts[1], split, third_exchange_b(sum2.parts[1])))
+        sum2 = Total(sum2.parts[0], last)
         held["came"] = exchange(split[1], 1), exchange(split[3], 2)
 
     col2, gz1, s1 = call(
-        k_back_conv_two, "g1", (3,),
-        [SCALARS, full_mid, full_mid, full_row, full_row, full_tab, full_mask] + conv_weights(2, turned)
-        + [plane_pair, full_row, full_tab],
+        paired(k_back_conv_two, {3: ONE, 4: ONE}, {5: ("mid", 1), 11: ("base", 0), 12: ("mid", 0)}, 0), "g1", (3,),
+        [SCALARS, full_table, full_mid, full_mid, full_row, full_row, full_row, full_row, full_mask] + conv_weights(2, turned)
+        + [plane_pair],
         [spec((3, ROWS, C_MID), lambda s: (turned(s), 0, 0)), plane_pair, full_row],
         [vmem_of((9, ROWS, C_MID), BFLOAT), vmem_of((4, ROWS, C_MID)), shape_of((4, C_MID))],
         [pltpu.VMEM((PAD + ROWS + PAD, C_MID), SINGLE)] * 2 + [pltpu.VMEM((2, ROWS, C_MID), SINGLE)],
-        (inv, gz2, a2, total2, sum2, mid2, mask, a_kept, a_kept, a_kept, a1, total1, mid1), vmem=12,
+        (core_row, base, gz2, a2, *total2.parts, *sum2.parts, mask, a_kept, a_kept, a_kept, a1), vmem=12,
     )
     gz1 = in_vmem(gz1)
     h1_planes = h1_t.reshape(4, C_MID, ROWS)
@@ -1287,8 +1352,9 @@
     state_b = held["b"]
     plane = spec((1, ROWS, C_MID), lambda k: (k, 0, 0))
     ga1 = call(
-        k_first_grad, "g0", (4,), [SCALARS, plane, plane, full_row, full_row, full_tab, full_mask], plane,
-        vmem_of((4, ROWS, C_MID), BFLOAT), [], (inv, gz1, a1, total1, sum1, mid1, mask),
+        paired(k_first_grad, {4: ONE}, {3: ("base", 0), 5: ("mid", 0)}, 0), "g0", (4,),
+        [SCALARS, full_table, plane, plane, full_row, full_row, full_mask], plane,
+        vmem_of((4, ROWS, C_MID), BFLOAT), [], (core_row, base, gz1, a1, *sum1.parts, mask),
     )
     flat_ga1 = in_vmem(ga1.reshape(1, 4 * ROWS, C_MID))
     bufs_a = weight_grad(
@@ -1296,27 +1362,28 @@
         2, narrow_shape, TILE, 0, bufs_a, None, vmem_of,
     )
     got_a = swap_pipe(bufs_a[1])
-    dxs = wide_back(bufs_a[0])
-
-    def image_grads(token):
+    sums = [sum1, sum2, sum3, sum4, sum5, sum6]
+
+    def image_grads(token, dxs):
         pair = call(
             k_image_grad, "gx", (SLOTS,),
             [spec((4, PIX, C_MID), lambda s, slot: (0, s, 0)), spec((PIX, 1), lambda s, slot: (s, 0)), full((C_IN, C_MID)),
              spec((PIX, C_IN), lambda s, slot: (s, 0)), full((4 * PIX, 4 * PIX)), ANYWHERE],
             spec((2, 1, 4 * PIX, C_IN // 2), lambda s, slot: (0, s, 0, 0)),
             shape_of((2, SLOTS, 4 * PIX, C_IN // 2), BFLOAT), [],
-            (slots, in_vmem(ga1), mask, a_kept, in_hbm(dxs), in_hbm(perm), token), prefetch=1, vmem=9,
+            (core_row, in_vmem(ga1), mask, a_kept, in_hbm(dxs), in_hbm(perm), token), prefetch=1, vmem=9,
         )
         return pair, swap_pipe(pair[1])
 
     if fast:
         state_w = halved(state_w, (exchange(state_w[1], 2), exchange(state_w[3], 1)), True)
-        got_a, dxs, state_w, came_b = lax.optimization_barrier((got_a, dxs, state_w, held["came_b"]))
+        got_a, state_w, came_b = lax.optimization_barrier((got_a, state_w, held["came_b"]))
         came_w = exchange(state_w[1], 4)
         state_a = split_group("split_a", in_vmem(bufs_a[0]), got_a, part_n, by_rows)
         came_a = exchange(state_a[1], 1), exchange(state_a[3], 2)
-        pair, got_pair = image_grads(state_a[0])
+        dxs = wide_back(state_a[0])
         state_w = halved_both(state_w, came_w)
+        pair, got_pair = image_grads(state_w[0], dxs)
         came_a, state_w, pair = lax.optimization_barrier((came_a, state_w, pair))
         came_w = exchange(state_w[1], 8)
         state_a = halved(state_a, came_a, False)
@@ -1330,13 +1397,14 @@
         came_a, grad_local = lax.optimization_barrier((came_a, grad_local))
         state_a = halved_both(state_a, came_a)
         came_a = exchange(state_a[1], 8)
-        sum1, sum2, sum3, sum4, sum5, sum6 = pin((sum1, sum2, sum3, sum4, sum5, sum6), state_a[0])
+        sums = pin(tuple(t.parts for t in sums), state_a[0])
+        sums = [Total(*parts) for parts in sums]
         half_a = jnp.concatenate(added(state_a, came_a), axis=0)
     else:
         half_a = jnp.concatenate(scatter_plain(bufs_a[0], got_a, rows_n, True), axis=0)
         half_w0, half_w1 = scatter_plain(bufs_w[0], got_w, w_wide.shape[0], False)
         half_b = jnp.concatenate(scatter_plain(bufs_b[0], held["got_b"], rows_n, True), axis=0)
-        pair, got_pair = image_grads(ga1)
+        pair, got_pair = image_grads(ga1, wide_back(ga1))
         grad_local = place("place_grad", pair, got_pair, ga1)
     grad_local = grad_local.reshape(IMG_DEV, 2 * HB, 2 * WB, C_IN // 2)
 
@@ -1347,6 +1415,8 @@
 
     grad_narrow = join_halves(half_a, half_b)
     grad_wide = join_halves(half_w0, half_w1)
+
+    sum1, sum2, sum3, sum4, sum5, sum6 = (t.sum for t in sums)
 
     def pair_sum(rows):
         return rows[0] + rows[1]
@@ -1368,8 +1438,8 @@
     parts = 4 if rows_n % 64 == 0 and w_wide.shape[0] % 64 == 0 else 1
     specs = [spec((v.shape[0] // parts, v.shape[1]), lambda k, *_: (k, 0)) for v in weights[:2]] + whole_specs[2:]
     updated = call(
-        k_update, "update", (parts,), [full((8, 128))] + specs * 3, specs * 2, [shape_of(v.shape) for v in weights] * 2, [],
-        (starts, squares, *weights, *grads, mom_narrow, mom_wide, mom_bn_mid, mom_bn_wide), prefetch=1, vmem=12,
+        paired(k_update, {1: ONE}), "update", (parts,), [full((8, 128))] * 2 + specs * 3, specs * 2, [shape_of(v.shape) for v in weights] * 2, [],
+        (starts, *squares.parts, *weights, *grads, mom_narrow, mom_wide, mom_bn_mid, mom_bn_wide), prefetch=1, vmem=12,
     )
     new_mom_narrow, new_mom_wide, new_mom_mid, new_mom_table, new_narrow, new_wide, new_mid, new_table = updated
     return (

time: 516 us -> 501 us (0.971)
  starting transfers between devices: 98.4 us -> 115 us
  waiting for transfers between devices: 201 us -> 186 us
  Pallas kernels: 173 us -> 162 us
    ppermute x82, starting transfers between devices: 94.4 us -> 111 us  [exchange(): return lax.ppermute(value, 'dp', pairs(bit))]
    pallas_call x70, Pallas kernels: 173 us -> 162 us  [call(): pl.pallas_call(kernel, out_shape=out_shape, grid_spec=pltpu.PrefetchScala...]
    all_gather x1, waiting for transfers between devices: 7.34 us -> 0.02 us  [on_device(): wide = lax.all_gather(own_wide, ('pipe', 'dp'), axis=0, tiled=True)]
    ppermute x82, waiting for transfers between devices: 185 us -> 179 us  [exchange(): return lax.ppermute(value, 'dp', pairs(bit))]
  transfers between devices with their start and end apart: 103 -> 103, of which waited for: 70 -> 69; matrix products, arithmetic and copies ran while one was open for 2% -> 1% of each run, Pallas kernels for 24% -> 23%
where the time goes in v4:
time: 501 us; the launch traced here: 491 us
  waiting for transfers between devices  186 us (37%)
  Pallas kernels  162 us (32%)
  starting transfers between devices  115 us (23%)
  between operations  15.6 us (3%)
  other arithmetic  7.95 us (2%)
    ppermute x82, waiting for transfers between devices, exchange(): return lax.ppermute(value, 'dp', pairs(bit))  179 us
    pallas_call x70, Pallas kernels, call(): pl.pallas_call(kernel, out_shape=out_shape, grid_spec=pltpu.PrefetchScala...  162 us
    ppermute x82, starting transfers between devices, exchange(): return lax.ppermute(value, 'dp', pairs(bit))  111 us
  transfers between devices with their start and end apart: 103, of which 69 were waited for; matrix products, arithmetic and copies ran while one was open for 1% of the time, Pallas kernels for 23%

profile of v4, /device:TPU:0, one launch (start us, length us, event | category | flops | bytes accessed | tf_op | source)
XLA Modules:
  0.0 490.8 jit_solution(12853897883011152581)
XLA Ops:
  10.2 4.0 collective-permute-start.1
  14.2 9.4 %collective-permute-done.1.refs_1_ = bf16[2,1,192,256]{3,2,1,0:T(8,128)(2,1)S(1)} collective-permute-done((bf16[2,1,192,256]{3,2,1,0:T(8,128)(2,1)S(1)}, bf16[2,1,192,256]{3,2,1,0:T(8,128)(2,1)S(1)}, u32[]{:S(2)}, u32[]{:S(2)}) %collective-permute-start.1) | collective-permute-done | bytes 196640 | tf_op jit(solution)/shard_map/ppermute | solution.py:49
  25.0 9.9 %collective-permute-done.2.refs_1_ = bf16[2,2,192,256]{3,2,1,0:T(8,128)(2,1)S(1)} collective-permute-done((bf16[2,2,192,256]{3,2,1,0:T(8,128)(2,1)S(1)}, bf16[2,2,192,256]{3,2,1,0:T(8,128)(2,1)S(1)}, u32[]{:S(2)}, u32[]{:S(2)}) %collective-permute-start.2) | collective-permute-done | bytes 393248 | tf_op jit(solution)/shard_map/ppermute | solution.py:49
  42.5 7.5 %collective-permute-done.5.refs_1_.refs_2_ = bf16[2,1,192,256]{3,2,1,0:T(8,128)(2,1)S(1)} collective-permute-done((bf16[2,1,192,256]{3,2,1,0:T(8,128)(2,1)S(1)}, bf16[2,1,192,256]{3,2,1,0:T(8,128)(2,1)S(1)}, u32[]{:S(2)}, u32[]{:S(2)}) %collective-permute-start.5) | collective-permute-done | bytes 196640 | tf_op jit(solution)/shard_map/ppermute | solution.py:49
  54.4 4.9 prep.1
  59.9 7.5 %collective-permute-done.8.refs_1_.refs_2_ = bf16[2,2,192,256]{3,2,1,0:T(8,128)(2,1)S(1)} collective-permute-done((bf16[2,2,192,256]{3,2,1,0:T(8,128)(2,1)S(1)}, bf16[2,2,192,256]{3,2,1,0:T(8,128)(2,1)S(1)}, u32[]{:S(2)}, u32[]{:S(2)}) %collective-permute-start.8) | collective-permute-done | bytes 393248 | tf_op jit(solution)/shard_map/ppermute | solution.py:49
  67.4 4.6 collective-permute-done.6.refs_1_
  79.0 3.6 a1.1
  103.2 7.2 %collective-permute-done.17.refs_2_ = f32[40,512]{1,0:T(8,128)S(1)} collective-permute-done((f32[40,512]{1,0:T(8,128)S(1)}, f32[40,512]{1,0:T(8,128)S(1)}, u32[]{:S(2)}, u32[]{:S(2)}) %collective-permute-start.17) | collective-permute-done | bytes 81952 | tf_op jit(solution)/shard_map/ppermute | solution.py:49
  110.4 6.0 %a2.1 = (f32[384,512]{1,0:T(8,128)S(1)}, bf16[4,384,512]{2,1,0:T(8,128)(2,1)S(1)}, f32[4,512]{1,0:T(4,128)S(1)}) custom-call(s32[1]{0:T(128)} %bitcast.core_ref.refs_0_, f32[40,512]{1,0:T(8,128)S(1)} %add.229.refs_1_, f32[40,512]{1,0:T(8,128)S(1)} %collective-permute-done.17.refs_2_, ...), custom_call_target="tpu_custom_call" | custom-call | bytes 3000000 | tf_op jit(solution)/shard_map/a2/pallas_call | solution.py:722
  129.4 3.6 collective-permute-start.23
  133.1 4.5 as.1
  137.6 3.8 a3.1
  161.2 5.1 %a4.1 = (bf16[384,2048]{1,0:T(8,128)(2,1)S(1)}, f32[384,512]{1,0:T(8,128)S(1)}, f32[4,512]{1,0:T(4,128)S(1)}) custom-call(s32[1]{0:T(128)} %bitcast.core_ref.refs_0_, f32[40,512]{1,0:T(8,128)S(1)} %add.230.refs_1_.refs_2_, f32[8,2048]{1,0:T(8,128)S(1)} %add.236.refs_2_.refs_14_.refs_5_, f32[8,2048]{1,0:T(8,128)S(1)} %collective-permute-done.27.refs_3_.refs_15_.refs_6_, ...), custom_call_target="tpu_custom_call" | custom-call | bytes 2820000 | tf_op jit(solution)/shard_map/a4/pallas_call | solution.py:722
  181.9 3.6 a5.1
  201.7 3.8 a6.1
  222.4 5.6 %head.1 = (bf16[2,384,1024]{2,1,0:T(8,128)(2,1)S(1)}, f32[384,2048]{1,0:T(8,128)S(1)}, f32[4,2048]{1,0:T(4,128)S(1)}) custom-call(s32[1]{0:T(128)} %bitcast.core_ref.refs_0_, s32[1,8]{1,0:T(1,128)S(1)} %copy-done.27, f32[40,512]{1,0:T(8,128)S(1)} %add.230.refs_1_.refs_2_, f32[4,2048]{1,0:T(4,128)S(1)} %add.245.refs_3_.refs_4_, ...), custom_call_target="tpu_custom_call" | custom-call | bytes 3180000 | tf_op jit(solution)/shard_map/head/pallas_call | solution.py:722
  244.9 5.5 %g5.1 = (bf16[384,2048]{1,0:T(8,128)(2,1)S(1)}, f32[384,512]{1,0:T(8,128)S(1)}, f32[4,512]{1,0:T(4,128)S(1)}) custom-call(s32[1]{0:T(128)} %bitcast.core_ref.refs_0_, f32[40,512]{1,0:T(8,128)S(1)} %add.230.refs_1_.refs_2_, f32[384,2048]{1,0:T(8,128)S(1)} %get-tuple-element.365.refs_2_.refs_11_, f32[384,2048]{1,0:T(8,128)} %keep.13.refs_3_, ...), custom_call_target="tpu_custom_call" | custom-call | bytes 3120000 | tf_op jit(solution)/shard_map/g5/pallas_call | solution.py:722
  266.8 5.5 %g4.1 = (bf16[9,384,512]{2,1,0:T(8,128)(2,1)S(1)}, f32[384,512]{1,0:T(8,128)S(1)}, f32[4,512]{1,0:T(4,128)S(1)}) custom-call(s32[1]{0:T(128)} %bitcast.core_ref.refs_0_, f32[40,512]{1,0:T(8,128)S(1)} %add.230.refs_1_.refs_2_, f32[384,512]{1,0:T(8,128)S(1)} %get-tuple-element.383.refs_2_, f32[384,512]{1,0:T(8,128)S(1)} %get-tuple-element.358.refs_5_.refs_10_.refs_3_, ...), custom_call_target="tpu_custom_call" | custom-call | bytes 3240000 | tf_op jit(solution)/shard_map/g4/pallas_call | solution.py:722
  287.9 6.8 %gy.1 = (bf16[384,512]{1,0:T(8,128)(2,1)S(1)}, f32[384,2048]{1,0:T(8,128)S(1)}, f32[6,2048]{1,0:T(8,128)S(1)}) custom-call(s32[1]{0:T(128)} %bitcast.core_ref.refs_0_, f32[40,512]{1,0:T(8,128)S(1)} %add.230.refs_1_.refs_2_, f32[384,512]{1,0:T(8,128)S(1)} %get-tuple-element.386.refs_2_, f32[384,512]{1,0:T(8,128)S(1)} %get-tuple-element.350.refs_5_.refs_12_.refs_3_, ...), custom_call_target="tpu_custom_call" | custom-call | bytes 4200000 | tf_op jit(solution)/shard_map/gy/pallas_call | solution.py:722
  314.2 3.9 collective-permute-done.63.refs_8_
  318.1 8.1 %g2.1 = (bf16[384,2048]{1,0:T(8,128)(2,1)}, bf16[384,2048]{1,0:T(8,128)(2,1)}, f32[384,512]{1,0:T(8,128)S(1)}, f32[4,512]{1,0:T(4,128)S(1)}) custom-call(s32[1]{0:T(128)} %bitcast.core_ref.refs_0_, f32[40,512]{1,0:T(8,128)S(1)} %add.230.refs_1_.refs_2_, f32[384,2048]{1,0:T(8,128)S(1)} %get-tuple-element.401.refs_2_, f32[384,2048]{1,0:T(8,128)} %keep.10.refs_12_.refs_3_, ...), custom_call_target="tpu_custom_call" | custom-call | bytes 4380000 | tf_op jit(solution)/shard_map/g2/pallas_call | solution.py:722
  353.6 7.4 %g1.1 = (bf16[9,384,512]{2,1,0:T(8,128)(2,1)S(1)}, f32[4,384,512]{2,1,0:T(8,128)S(1)}, f32[4,512]{1,0:T(4,128)S(1)}) custom-call(s32[1]{0:T(128)} %bitcast.core_ref.refs_0_, f32[40,512]{1,0:T(8,128)S(1)} %add.230.refs_1_.refs_2_, f32[384,512]{1,0:T(8,128)S(1)} %get-tuple-element.421.refs_2_, f32[384,512]{1,0:T(8,128)S(1)} %copy-done.5, ...), custom_call_target="tpu_custom_call" | custom-call | bytes 4800000 | tf_op jit(solution)/shard_map/g1/pallas_call | solution.py:722
  387.0 10.3 %collective-permute-done.81.refs_2_.refs_3_ = bf16[4,64,1024]{2,1,0:T(8,128)(2,1)S(1)} collective-permute-done((bf16[4,64,1024]{2,1,0:T(8,128)(2,1)S(1)}, bf16[4,64,1024]{2,1,0:T(8,128)(2,1)S(1)}, u32[]{:S(2)}, u32[]{:S(2)}) %collective-permute-start.81) | collective-permute-done | bytes 524320 | tf_op jit(solution)/shard_map/ppermute | solution.py:49
  403.6 5.0 %dxs.1.short_ref = f32[384,1024]{1,0:T(8,128)} custom-call(bf16[384,2048]{1,0:T(8,128)(2,1)} %get-tuple-element.423.g_ref, bf16[2048,2048]{1,0:T(8,128)(2,1)} %all-gather.2.cloned.1.call-done.refs_6_.w0.w1.refs_9_.refs_10_.w_ref, bf16[8,192,256]{2,1,0:T(8,128)(2,1)S(1)} %get-tuple-element.500.refs_0_.refs_1_), custom_call_target="tpu_custom_call" | custom-call | bytes 3000000 | tf_op jit(solution)/shard_map/dxs/pallas_call | solution.py:722
  411.9 6.1 %gx.1.own_ref = bf16[2,4,384,512]{3,2,1,0:T(8,128)(2,1)S(1)} custom-call(s32[1]{0:T(128)} %bitcast.core_ref.refs_0_, bf16[4,384,512]{2,1,0:T(8,128)(2,1)S(1)} %g0.1.ga_ref, f32[384,1]{1,0:T(8,128)S(1)} %get-tuple-element.303.refs_3_.refs_4_.refs_5_.refs_8_.refs_9_.refs_6_.mask_ref, ...), custom_call_target="tpu_custom_call" | custom-call | bytes 3840000 | tf_op jit(solution)/shard_map/gx/pallas_call | solution.py:722
  425.1 8.4 %collective-permute-done.89 = bf16[2,1,64,1024]{3,2,1,0:T(8,128)(2,1)S(1)} collective-permute-done((bf16[2,1,64,1024]{3,2,1,0:T(8,128)(2,1)S(1)}, bf16[2,1,64,1024]{3,2,1,0:T(8,128)(2,1)S(1)}, u32[]{:S(2)}, u32[]{:S(2)}) %collective-permute-start.89) | collective-permute-done | bytes 262176 | tf_op jit(solution)/shard_map/ppermute | solution.py:49
  435.3 3.8 place_grad.1
  439.2 6.4 %collective-permute-done.90.came_ref = bf16[2,2,192,256]{3,2,1,0:T(8,128)(2,1)S(1)} collective-permute-done((bf16[2,2,192,256]{3,2,1,0:T(8,128)(2,1)S(1)}, bf16[2,2,192,256]{3,2,1,0:T(8,128)(2,1)S(1)}, u32[]{:S(2)}, u32[]{:S(2)}) %collective-permute-start.90) | collective-permute-done | bytes 393248 | tf_op jit(solution)/shard_map/ppermute | solution.py:49
  447.8 9.5 %collective-permute-done.92 = bf16[2,1,192,256]{3,2,1,0:T(8,128)(2,1)S(1)} collective-permute-done((bf16[2,1,192,256]{3,2,1,0:T(8,128)(2,1)S(1)}, bf16[2,1,192,256]{3,2,1,0:T(8,128)(2,1)S(1)}, u32[]{:S(2)}, u32[]{:S(2)}) %collective-permute-start.92) | collective-permute-done | bytes 196640 | tf_op jit(solution)/shard_map/ppermute | solution.py:49
  472.7 3.6 collective-permute-done.100
  477.3 3.5 collective-permute-done.101.refs_2_
  (396 shorter events, 286.7 us)
Async XLA Ops:
  7.2 125.9 %all-gather.2.cloned.1.call-start = ((), (), s32[]{:S(2)}) async-start(), calls=%async_computation | async-start | bytes 8650752 | tf_op jit(solution)/shard_map/all_gather | solution.py:897
  10.2 13.4 %collective-permute-start.1 = (bf16[2,1,192,256]{3,2,1,0:T(8,128)(2,1)S(1)}, bf16[2,1,192,256]{3,2,1,0:T(8,128)(2,1)S(1)}, u32[]{:S(2)}, u32[]{:S(2)}) collective-permute-start(bf16[2,1,192,256]{3,2,1,0:T(8,128)(2,1)S(1)} %bitcast.58), channel_id=1, source_target_pairs={{0,8},{1,9},{2,10},{3,11},{4,12},{5,13},{6,14},{7,15},{8,0},{9,1},... | collective-permute-start | bytes 589832 | tf_op jit(solution)/shard_map/ppermute | solution.py:49
  35.9 14.1 %collective-permute-start.3 = (bf16[4,192,256]{2,1,0:T(8,128)(2,1)S(1)}, bf16[4,192,256]{2,1,0:T(8,128)(2,1)S(1)}, u32[]{:S(2)}, u32[]{:S(2)}) collective-permute-start(bf16[4,192,256]{2,1,0:T(8,128)(2,1)S(1)} %get-tuple-element.282.refs_0_), channel_id=1, source_target_pairs={{0,2},{1,3},{2,0},{3,1},{4,6},{5,7},{6,4},{7,5},{8,10},{9,11},{10,... | collective-permute-start | bytes 1179656 | tf_op jit(solution)/shard_map/ppermute | solution.py:49
  37.2 12.8 %collective-permute-start.4 = (bf16[4,192,256]{2,1,0:T(8,128)(2,1)S(1)}, bf16[4,192,256]{2,1,0:T(8,128)(2,1)S(1)}, u32[]{:S(2)}, u32[]{:S(2)}) collective-permute-start(bf16[4,192,256]{2,1,0:T(8,128)(2,1)S(1)} %get-tuple-element.283.refs_1_), channel_id=1, source_target_pairs={{0,1},{1,0},{2,3},{3,2},{4,5},{5,4},{6,7},{7,6},{8,9},{9,8},{10,11... | collective-permute-start | bytes 1179656 | tf_op jit(solution)/shard_map/ppermute | solution.py:49
  51.2 20.8 %collective-permute-start.6 = (bf16[8,192,256]{2,1,0:T(8,128)(2,1)}, bf16[8,192,256]{2,1,0:T(8,128)(2,1)}, u32[]{:S(2)}, u32[]{:S(2)}) collective-permute-start(bf16[8,192,256]{2,1,0:T(8,128)(2,1)} %get-tuple-element.287.refs_0_), channel_id=1, source_target_pairs={{0,1},{1,0},{2,3},{3,2},{4,5},{5,4},{6,7},{7,6},{8,9},{9,8},{10,11... | collective-permute-start | bytes 2359304 | tf_op jit(solution)/shard_map/ppermute | solution.py:49
  51.8 20.4 %collective-permute-start.7 = (bf16[8,192,256]{2,1,0:T(8,128)(2,1)}, bf16[8,192,256]{2,1,0:T(8,128)(2,1)}, u32[]{:S(2)}, u32[]{:S(2)}) collective-permute-start(bf16[8,192,256]{2,1,0:T(8,128)(2,1)} %get-tuple-element.288.refs_2_), channel_id=1, source_target_pairs={{0,2},{1,3},{2,0},{3,1},{4,6},{5,7},{6,4},{7,5},{8,10},{9,11},{10,... | collective-permute-start | bytes 2359304 | tf_op jit(solution)/shard_map/ppermute | solution.py:49
  53.5 13.9 %collective-permute-start.8 = (bf16[2,2,192,256]{3,2,1,0:T(8,128)(2,1)S(1)}, bf16[2,2,192,256]{3,2,1,0:T(8,128)(2,1)S(1)}, u32[]{:S(2)}, u32[]{:S(2)}) collective-permute-start(bf16[2,2,192,256]{3,2,1,0:T(8,128)(2,1)S(1)} %join.9.refs_0_), channel_id=1, source_target_pairs={{0,4},{1,5},{2,6},{3,7},{4,0},{5,1},{6,2},{7,3},{8,12},{9,13},{10,... | collective-permute-start | bytes 1179656 | tf_op jit(solution)/shard_map/ppermute | solution.py:49
  59.3 13.5 %collective-permute-start.10 = (bf16[8,192,256]{2,1,0:T(8,128)(2,1)}, bf16[8,192,256]{2,1,0:T(8,128)(2,1)S(1)}, u32[]{:S(2)}, u32[]{:S(2)}) collective-permute-start(bf16[8,192,256]{2,1,0:T(8,128)(2,1)} %get-tuple-element.287.refs_0_), channel_id=1, source_target_pairs={{0,16},{16,0},{1,17},{17,1},{2,18},{18,2},{3,19},{19,3},{4,20},{20... | collective-permute-start | bytes 2359304 | tf_op jit(solution)/shard_map/ppermute | solution.py:87
  59.5 13.3 %collective-permute-start.12 = (bf16[8,192,256]{2,1,0:T(8,128)(2,1)}, bf16[8,192,256]{2,1,0:T(8,128)(2,1)S(1)}, u32[]{:S(2)}, u32[]{:S(2)}) collective-permute-start(bf16[8,192,256]{2,1,0:T(8,128)(2,1)} %get-tuple-element.288.refs_2_), channel_id=1, source_target_pairs={{0,16},{16,0},{1,17},{17,1},{2,18},{18,2},{3,19},{19,3},{4,20},{20... | collective-permute-start | bytes 2359304 | tf_op jit(solution)/shard_map/ppermute | solution.py:87
  94.0 27.5 %collective-permute-start.20 = (bf16[4,192,256]{2,1,0:T(8,128)(2,1)S(1)}, bf16[4,192,256]{2,1,0:T(8,128)(2,1)S(1)}, u32[]{:S(2)}, u32[]{:S(2)}) collective-permute-start(bf16[4,192,256]{2,1,0:T(8,128)(2,1)S(1)} %get-tuple-element.311.refs_0_), channel_id=1, source_target_pairs={{0,2},{1,3},{2,0},{3,1},{4,6},{5,7},{6,4},{7,5},{8,10},{9,11},{10,... | collective-permute-start | bytes 1179656 | tf_op jit(solution)/shard_map/ppermute | solution.py:49
  94.6 26.9 %collective-permute-start.21 = (bf16[4,192,256]{2,1,0:T(8,128)(2,1)S(1)}, bf16[4,192,256]{2,1,0:T(8,128)(2,1)S(1)}, u32[]{:S(2)}, u32[]{:S(2)}) collective-permute-start(bf16[4,192,256]{2,1,0:T(8,128)(2,1)S(1)} %get-tuple-element.312.refs_1_), channel_id=1, source_target_pairs={{0,1},{1,0},{2,3},{3,2},{4,5},{5,4},{6,7},{7,6},{8,9},{9,8},{10,11... | collective-permute-start | bytes 1179656 | tf_op jit(solution)/shard_map/ppermute | solution.py:49
  124.1 21.7 %collective-permute-start.28 = (bf16[8,192,256]{2,1,0:T(8,128)(2,1)}, bf16[8,192,256]{2,1,0:T(8,128)(2,1)}, u32[]{:S(2)}, u32[]{:S(2)}) collective-permute-start(bf16[8,192,256]{2,1,0:T(8,128)(2,1)} %get-tuple-element.333.refs_0_), channel_id=1, source_target_pairs={{0,1},{1,0},{2,3},{3,2},{4,5},{5,4},{6,7},{7,6},{8,9},{9,8},{10,11... | collective-permute-start | bytes 2359304 | tf_op jit(solution)/shard_map/ppermute | solution.py:49
  124.4 21.4 %collective-permute-start.29 = (bf16[8,192,256]{2,1,0:T(8,128)(2,1)}, bf16[8,192,256]{2,1,0:T(8,128)(2,1)}, u32[]{:S(2)}, u32[]{:S(2)}) collective-permute-start(bf16[8,192,256]{2,1,0:T(8,128)(2,1)} %get-tuple-element.335.refs_2_), channel_id=1, source_target_pairs={{0,2},{1,3},{2,0},{3,1},{4,6},{5,7},{6,4},{7,5},{8,10},{9,11},{10,... | collective-permute-start | bytes 2359304 | tf_op jit(solution)/shard_map/ppermute | solution.py:49
  145.8 12.2 %collective-permute-start.30 = (bf16[8,192,256]{2,1,0:T(8,128)(2,1)}, bf16[8,192,256]{2,1,0:T(8,128)(2,1)S(1)}, u32[]{:S(2)}, u32[]{:S(2)}) collective-permute-start(bf16[8,192,256]{2,1,0:T(8,128)(2,1)} %get-tuple-element.333.refs_0_), channel_id=1, source_target_pairs={{0,16},{16,0},{1,17},{17,1},{2,18},{18,2},{3,19},{19,3},{4,20},{20... | collective-permute-start | bytes 2359304 | tf_op jit(solution)/shard_map/ppermute | solution.py:87
  145.9 12.1 %collective-permute-start.31 = (bf16[8,192,256]{2,1,0:T(8,128)(2,1)}, bf16[8,192,256]{2,1,0:T(8,128)(2,1)S(1)}, u32[]{:S(2)}, u32[]{:S(2)}) collective-permute-start(bf16[8,192,256]{2,1,0:T(8,128)(2,1)} %collective-permute-done.28.refs_1_), channel_id=1, source_target_pairs={{0,16},{16,0},{1,17},{17,1},{2,18},{18,2},{3,19},{19,3},{4,20},{20... | collective-permute-start | bytes 2359304 | tf_op jit(solution)/shard_map/ppermute | solution.py:87
  305.9 28.6 %collective-permute-start.66 = (bf16[8,192,256]{2,1,0:T(8,128)(2,1)S(1)}, bf16[8,192,256]{2,1,0:T(8,128)(2,1)S(1)}, u32[]{:S(2)}, u32[]{:S(2)}) collective-permute-start(bf16[8,192,256]{2,1,0:T(8,128)(2,1)S(1)} %get-tuple-element.417), channel_id=1, source_target_pairs={{0,1},{1,0},{2,3},{3,2},{4,5},{5,4},{6,7},{7,6},{8,9},{9,8},{10,11... | collective-permute-start | bytes 2359304 | tf_op jit(solution)/shard_map/ppermute | solution.py:49
  307.4 27.1 %collective-permute-start.67 = (bf16[8,192,256]{2,1,0:T(8,128)(2,1)S(1)}, bf16[8,192,256]{2,1,0:T(8,128)(2,1)S(1)}, u32[]{:S(2)}, u32[]{:S(2)}) collective-permute-start(bf16[8,192,256]{2,1,0:T(8,128)(2,1)S(1)} %get-tuple-element.419), channel_id=1, source_target_pairs={{0,2},{1,3},{2,0},{3,1},{4,6},{5,7},{6,4},{7,5},{8,10},{9,11},{10,... | collective-permute-start | bytes 2359304 | tf_op jit(solution)/shard_map/ppermute | solution.py:49
  335.8 12.4 %collective-permute-start.70 = (bf16[2048,1024]{1,0:T(8,128)(2,1)S(1)}, bf16[2048,1024]{1,0:T(8,128)(2,1)S(1)}, u32[]{:S(2)}, u32[]{:S(2)}) collective-permute-start(bf16[2048,1024]{1,0:T(8,128)(2,1)S(1)} %get-tuple-element.446), channel_id=1, source_target_pairs={{0,16},{16,0},{1,17},{17,1},{2,18},{18,2},{3,19},{19,3},{4,20},{20... | collective-permute-start | bytes 12582920 | tf_op jit(solution)/shard_map/ppermute | solution.py:87
  349.3 25.8 %collective-permute-start.78 = (bf16[8,64,1024]{2,1,0:T(8,128)(2,1)S(1)}, bf16[8,64,1024]{2,1,0:T(8,128)(2,1)S(1)}, u32[]{:S(2)}, u32[]{:S(2)}) collective-permute-start(bf16[8,64,1024]{2,1,0:T(8,128)(2,1)S(1)} %get-tuple-element.479), channel_id=1, source_target_pairs={{0,1},{1,0},{2,3},{3,2},{4,5},{5,4},{6,7},{7,6},{8,9},{9,8},{10,11... | collective-permute-start | bytes 3145736 | tf_op jit(solution)/shard_map/ppermute | solution.py:49
  350.9 24.2 %collective-permute-start.79 = (bf16[8,64,1024]{2,1,0:T(8,128)(2,1)S(1)}, bf16[8,64,1024]{2,1,0:T(8,128)(2,1)S(1)}, u32[]{:S(2)}, u32[]{:S(2)}) collective-permute-start(bf16[8,64,1024]{2,1,0:T(8,128)(2,1)S(1)} %get-tuple-element.480), channel_id=1, source_target_pairs={{0,2},{1,3},{2,0},{3,1},{4,6},{5,7},{6,4},{7,5},{8,10},{9,11},{10,... | collective-permute-start | bytes 3145736 | tf_op jit(solution)/shard_map/ppermute | solution.py:49
  352.0 18.9 %collective-permute-start.76 = (bf16[2,2,192,256]{3,2,1,0:T(8,128)(2,1)S(1)}, bf16[2,2,192,256]{3,2,1,0:T(8,128)(2,1)S(1)}, u32[]{:S(2)}, u32[]{:S(2)}) collective-permute-start(bf16[2,2,192,256]{3,2,1,0:T(8,128)(2,1)S(1)} %get-tuple-element.457), channel_id=1, source_target_pairs={{0,4},{1,5},{2,6},{3,7},{4,0},{5,1},{6,2},{7,3},{8,12},{9,13},{10,... | collective-permute-start | bytes 1179656 | tf_op jit(solution)/shard_map/ppermute | solution.py:49
  382.9 15.6 %collective-permute-start.80 = (bf16[6144,256]{1,0:T(8,128)(2,1)S(1)}, bf16[6144,256]{1,0:T(8,128)(2,1)S(1)}, u32[]{:S(2)}, u32[]{:S(2)}) collective-permute-start(bf16[6144,256]{1,0:T(8,128)(2,1)S(1)} %get-tuple-element.492), channel_id=1, source_target_pairs={{0,16},{16,0},{1,17},{17,1},{2,18},{18,2},{3,19},{19,3},{4,20},{20... | collective-permute-start | bytes 9437192 | tf_op jit(solution)/shard_map/ppermute | solution.py:87
  383.0 14.3 %collective-permute-start.81 = (bf16[4,64,1024]{2,1,0:T(8,128)(2,1)S(1)}, bf16[4,64,1024]{2,1,0:T(8,128)(2,1)S(1)}, u32[]{:S(2)}, u32[]{:S(2)}) collective-permute-start(bf16[4,64,1024]{2,1,0:T(8,128)(2,1)S(1)} %get-tuple-element.494), channel_id=1, source_target_pairs={{0,2},{1,3},{2,0},{3,1},{4,6},{5,7},{6,4},{7,5},{8,10},{9,11},{10,... | collective-permute-start | bytes 1572872 | tf_op jit(solution)/shard_map/ppermute | solution.py:49
  384.2 14.0 %collective-permute-start.82 = (bf16[4,64,1024]{2,1,0:T(8,128)(2,1)S(1)}, bf16[4,64,1024]{2,1,0:T(8,128)(2,1)S(1)}, u32[]{:S(2)}, u32[]{:S(2)}) collective-permute-start(bf16[4,64,1024]{2,1,0:T(8,128)(2,1)S(1)} %get-tuple-element.496), channel_id=1, source_target_pairs={{0,1},{1,0},{2,3},{3,2},{4,5},{5,4},{6,7},{7,6},{8,9},{9,8},{10,11... | collective-permute-start | bytes 1572872 | tf_op jit(solution)/shard_map/ppermute | solution.py:49
  385.7 12.8 %collective-permute-start.83 = (bf16[2,1,192,256]{3,2,1,0:T(8,128)(2,1)S(1)}, bf16[2,1,192,256]{3,2,1,0:T(8,128)(2,1)S(1)}, u32[]{:S(2)}, u32[]{:S(2)}) collective-permute-start(bf16[2,1,192,256]{3,2,1,0:T(8,128)(2,1)S(1)} %get-tuple-element.474), channel_id=1, source_target_pairs={{0,8},{1,9},{2,10},{3,11},{4,12},{5,13},{6,14},{7,15},{8,0},{9,1},... | collective-permute-start | bytes 589832 | tf_op jit(solution)/shard_map/ppermute | solution.py:49
  398.5 13.2 %collective-permute-start.86 = (bf16[2,2,64,1024]{3,2,1,0:T(8,128)(2,1)S(1)}, bf16[2,2,64,1024]{3,2,1,0:T(8,128)(2,1)S(1)}, u32[]{:S(2)}, u32[]{:S(2)}) collective-permute-start(bf16[2,2,64,1024]{3,2,1,0:T(8,128)(2,1)S(1)} %get-tuple-element.504), channel_id=1, source_target_pairs={{0,4},{1,5},{2,6},{3,7},{4,0},{5,1},{6,2},{7,3},{8,12},{9,13},{10,... | collective-permute-start | bytes 1572872 | tf_op jit(solution)/shard_map/ppermute | solution.py:49
  400.9 18.6 %collective-permute-start.84 = (bf16[8,192,256]{2,1,0:T(8,128)(2,1)S(1)}, bf16[8,192,256]{2,1,0:T(8,128)(2,1)S(1)}, u32[]{:S(2)}, u32[]{:S(2)}) collective-permute-start(bf16[8,192,256]{2,1,0:T(8,128)(2,1)S(1)} %get-tuple-element.501), channel_id=1, source_target_pairs={{0,1},{1,0},{2,3},{3,2},{4,5},{5,4},{6,7},{7,6},{8,9},{9,8},{10,11... | collective-permute-start | bytes 2359304 | tf_op jit(solution)/shard_map/ppermute | solution.py:49
  402.6 18.2 %collective-permute-start.85 = (bf16[8,192,256]{2,1,0:T(8,128)(2,1)S(1)}, bf16[8,192,256]{2,1,0:T(8,128)(2,1)S(1)}, u32[]{:S(2)}, u32[]{:S(2)}) collective-permute-start(bf16[8,192,256]{2,1,0:T(8,128)(2,1)S(1)} %get-tuple-element.502), channel_id=1, source_target_pairs={{0,2},{1,3},{2,0},{3,1},{4,6},{5,7},{6,4},{7,5},{8,10},{9,11},{10,... | collective-permute-start | bytes 2359304 | tf_op jit(solution)/shard_map/ppermute | solution.py:49
  418.1 17.2 %collective-permute-start.91 = (bf16[4,384,512]{2,1,0:T(8,128)(2,1)S(1)}, bf16[4,384,512]{2,1,0:T(8,128)(2,1)S(1)}, u32[]{:S(2)}, u32[]{:S(2)}) collective-permute-start(bf16[4,384,512]{2,1,0:T(8,128)(2,1)S(1)} %slice_bitcast_fusion), channel_id=1, source_target_pairs={{0,16},{16,0},{1,17},{17,1},{2,18},{18,2},{3,19},{19,3},{4,20},{20... | collective-permute-start | bytes 4718600 | tf_op jit(solution)/shard_map/ppermute | solution.py:87
  420.9 12.6 %collective-permute-start.89 = (bf16[2,1,64,1024]{3,2,1,0:T(8,128)(2,1)S(1)}, bf16[2,1,64,1024]{3,2,1,0:T(8,128)(2,1)S(1)}, u32[]{:S(2)}, u32[]{:S(2)}) collective-permute-start(bf16[2,1,64,1024]{3,2,1,0:T(8,128)(2,1)S(1)} %get-tuple-element.514), channel_id=1, source_target_pairs={{0,8},{1,9},{2,10},{3,11},{4,12},{5,13},{6,14},{7,15},{8,0},{9,1},... | collective-permute-start | bytes 786440 | tf_op jit(solution)/shard_map/ppermute | solution.py:49
  445.7 11.7 %collective-permute-start.92 = (bf16[2,1,192,256]{3,2,1,0:T(8,128)(2,1)S(1)}, bf16[2,1,192,256]{3,2,1,0:T(8,128)(2,1)S(1)}, u32[]{:S(2)}, u32[]{:S(2)}) collective-permute-start(bf16[2,1,192,256]{3,2,1,0:T(8,128)(2,1)S(1)} %get-tuple-element.526), channel_id=1, source_target_pairs={{0,8},{1,9},{2,10},{3,11},{4,12},{5,13},{6,14},{7,15},{8,0},{9,1},... | collective-permute-start | bytes 589832 | tf_op jit(solution)/shard_map/ppermute | solution.py:49
  447.8 12.4 %collective-permute-start.95 = (f32[8,512]{1,0:T(8,128)}, f32[8,512]{1,0:T(8,128)}, u32[]{:S(2)}, u32[]{:S(2)}) collective-permute-start(f32[8,512]{1,0:T(8,128)} %stack.10), channel_id=1, source_target_pairs={{0,16},{16,0},{1,17},{17,1},{2,18},{18,2},{3,19},{19,3},{4,20},{20... | collective-permute-start | bytes 49160 | tf_op jit(solution)/shard_map/ppermute | solution.py:87
  (104 other events, 1024.5 us)
Sparse Core Ops, SparseCore 0:
  51.3 80.8 all-gather.1

commit v5 on v4

--- a/solution.py
+++ b/solution.py
@@ -1252,7 +1252,7 @@
         [SCALARS, full_table, chunk, chunk, chunk, chunk_eight, chunk_eight, spec((6, TILE), lambda k: (0, k)), spec((6, TILE), lambda k: (0, k)), full_mask,
          spec((TILE, TILE), lambda k: (0, k)), full_mid, full_row, full_row],
         [chunk, chunk, full_mid, full_row],
-        [hbm_of((ROWS, C_OUT), BFLOAT), hbm_of((ROWS, C_OUT), BFLOAT), vmem_of((ROWS, C_MID)), shape_of((4, C_MID))],
+        [vmem_of((ROWS, C_OUT), BFLOAT), vmem_of((ROWS, C_OUT), BFLOAT), vmem_of((ROWS, C_MID)), shape_of((4, C_MID))],
         [pltpu.VMEM((ROWS, C_MID), SINGLE)],
         (core_row, base, gj, a3_kept, as_kept, *total3s.parts, *sum3.parts, mask, in_hbm(wide), a2, *total2.parts), vmem=11,
     )
@@ -1336,14 +1336,16 @@
             [full((ROWS, C_OUT)), spec((TILE, C_OUT), lambda k: (1 + k, 0)), ANYWHERE],
             spec((ROWS, TILE), lambda k: (0, k)),
             hbm_of((ROWS, C_IN)), [],
-            (in_hbm(gas), in_hbm(wide), token), vmem=8,
+            (gas, in_hbm(wide), token), vmem=8,
         )
 
     def first_w(token):
         if not fast:
             return token
         came = pin(held["came"], token)
-        return halved(split, came, False)
+        state = halved(split, came, False)
+        held["came_w"] = exchange(state[1], 2), exchange(state[3], 1)
+        return state
 
     held["a"] = bufs_a
     sum1, results1 = dp_sum(s1, [grad_two(0), grad_two(1), both_of(fourth_exchange_b, grad_two(2)), first_w], 4)
@@ -1376,7 +1378,7 @@
         return pair, swap_pipe(pair[1])
 
     if fast:
-        state_w = halved(state_w, (exchange(state_w[1], 2), exchange(state_w[3], 1)), True)
+        state_w = halved(state_w, held["came_w"], True)
         got_a, state_w, came_b = lax.optimization_barrier((got_a, state_w, held["came_b"]))
         came_w = exchange(state_w[1], 4)
         state_a = split_group("split_a", in_vmem(bufs_a[0]), got_a, part_n, by_rows)

time: 501 us -> 498 us (level)
  transfers between devices with their start and end apart: 103 -> 103, of which waited for: 69 -> 71; matrix products, arithmetic and copies ran while one was open for 1% -> 1% of each run, Pallas kernels for 23% -> 23%
where the time goes in v5:
time: 498 us; the launch traced here: 488 us
  waiting for transfers between devices  186 us (37%)
  Pallas kernels  161 us (32%)
  starting transfers between devices  115 us (23%)
  between operations  15.6 us (3%)
  other arithmetic  7.95 us (2%)
    ppermute x82, waiting for transfers between devices, exchange(): return lax.ppermute(value, 'dp', pairs(bit))  179 us
    pallas_call x70, Pallas kernels, call(): pl.pallas_call(kernel, out_shape=out_shape, grid_spec=pltpu.PrefetchScala...  161 us
    ppermute x82, starting transfers between devices, exchange(): return lax.ppermute(value, 'dp', pairs(bit))  111 us
  transfers between devices with their start and end apart: 103, of which 71 were waited for; matrix products, arithmetic and copies ran while one was open for 1% of the time, Pallas kernels for 23%

profile of v5, /device:TPU:0, one launch (start us, length us, event | category | flops | bytes accessed | tf_op | source)
XLA Modules:
  0.0 488.0 jit_solution(2316112071987857927)
XLA Ops:
  10.2 4.0 collective-permute-start.1
  14.2 9.4 %collective-permute-done.1.refs_1_ = bf16[2,1,192,256]{3,2,1,0:T(8,128)(2,1)S(1)} collective-permute-done((bf16[2,1,192,256]{3,2,1,0:T(8,128)(2,1)S(1)}, bf16[2,1,192,256]{3,2,1,0:T(8,128)(2,1)S(1)}, u32[]{:S(2)}, u32[]{:S(2)}) %collective-permute-start.1) | collective-permute-done | bytes 196640 | tf_op jit(solution)/shard_map/ppermute | solution.py:49
  25.0 9.9 %collective-permute-done.2.refs_1_ = bf16[2,2,192,256]{3,2,1,0:T(8,128)(2,1)S(1)} collective-permute-done((bf16[2,2,192,256]{3,2,1,0:T(8,128)(2,1)S(1)}, bf16[2,2,192,256]{3,2,1,0:T(8,128)(2,1)S(1)}, u32[]{:S(2)}, u32[]{:S(2)}) %collective-permute-start.2) | collective-permute-done | bytes 393248 | tf_op jit(solution)/shard_map/ppermute | solution.py:49
  42.5 7.5 %collective-permute-done.5.refs_1_.refs_2_ = bf16[2,1,192,256]{3,2,1,0:T(8,128)(2,1)S(1)} collective-permute-done((bf16[2,1,192,256]{3,2,1,0:T(8,128)(2,1)S(1)}, bf16[2,1,192,256]{3,2,1,0:T(8,128)(2,1)S(1)}, u32[]{:S(2)}, u32[]{:S(2)}) %collective-permute-start.5) | collective-permute-done | bytes 196640 | tf_op jit(solution)/shard_map/ppermute | solution.py:49
  54.4 4.9 %prep.1 = (bf16[4,384,1024]{2,1,0:T(8,128)(2,1)S(1)}, f32[384,1]{1,0:T(8,128)S(1)}, f32[4,512]{1,0:T(4,128)S(1)}) custom-call(s32[1]{0:T(128)} %bitcast.core_ref.refs_0_, s32[1,8]{1,0:T(1,128)S(1)} %copy-done.25, s32[8]{0:T(128)S(1)} %copy-done.28, s32[8]{0:T(128)S(1)} %copy-done.29, bf16[8,384,1024]{2,1,0:T(8,128)(2,1)} %bitcast.73, ...), custom_call_target="tpu_custom_call" | custom-call | bytes 3000000 | tf_op jit(solution)/shard_map/prep/pallas_call | solution.py:722
  59.9 7.5 %collective-permute-done.8.refs_1_.refs_2_ = bf16[2,2,192,256]{3,2,1,0:T(8,128)(2,1)S(1)} collective-permute-done((bf16[2,2,192,256]{3,2,1,0:T(8,128)(2,1)S(1)}, bf16[2,2,192,256]{3,2,1,0:T(8,128)(2,1)S(1)}, u32[]{:S(2)}, u32[]{:S(2)}) %collective-permute-start.8) | collective-permute-done | bytes 393248 | tf_op jit(solution)/shard_map/ppermute | solution.py:49
  67.4 4.6 collective-permute-done.6.refs_1_
  79.0 3.6 a1.1
  103.2 7.2 %collective-permute-done.17.refs_2_ = f32[40,512]{1,0:T(8,128)S(1)} collective-permute-done((f32[40,512]{1,0:T(8,128)S(1)}, f32[40,512]{1,0:T(8,128)S(1)}, u32[]{:S(2)}, u32[]{:S(2)}) %collective-permute-start.17) | collective-permute-done | bytes 81952 | tf_op jit(solution)/shard_map/ppermute | solution.py:49
  110.4 6.0 %a2.1 = (f32[384,512]{1,0:T(8,128)S(1)}, bf16[4,384,512]{2,1,0:T(8,128)(2,1)S(1)}, f32[4,512]{1,0:T(4,128)S(1)}) custom-call(s32[1]{0:T(128)} %bitcast.core_ref.refs_0_, f32[40,512]{1,0:T(8,128)S(1)} %add.229.refs_1_, f32[40,512]{1,0:T(8,128)S(1)} %collective-permute-done.17.refs_2_, ...), custom_call_target="tpu_custom_call" | custom-call | bytes 3000000 | tf_op jit(solution)/shard_map/a2/pallas_call | solution.py:722
  129.4 3.6 collective-permute-start.23
  133.1 4.5 as.1
  137.6 3.8 a3.1
  161.2 5.1 %a4.1 = (bf16[384,2048]{1,0:T(8,128)(2,1)S(1)}, f32[384,512]{1,0:T(8,128)S(1)}, f32[4,512]{1,0:T(4,128)S(1)}) custom-call(s32[1]{0:T(128)} %bitcast.core_ref.refs_0_, f32[40,512]{1,0:T(8,128)S(1)} %add.230.refs_1_.refs_2_, f32[8,2048]{1,0:T(8,128)S(1)} %add.236.refs_2_.refs_14_.refs_5_, f32[8,2048]{1,0:T(8,128)S(1)} %collective-permute-done.27.refs_3_.refs_15_.refs_6_, ...), custom_call_target="tpu_custom_call" | custom-call | bytes 2820000 | tf_op jit(solution)/shard_map/a4/pallas_call | solution.py:722
  181.9 3.6 a5.1
  201.7 3.8 a6.1
  222.3 5.6 %head.1 = (bf16[2,384,1024]{2,1,0:T(8,128)(2,1)S(1)}, f32[384,2048]{1,0:T(8,128)S(1)}, f32[4,2048]{1,0:T(4,128)S(1)}) custom-call(s32[1]{0:T(128)} %bitcast.core_ref.refs_0_, s32[1,8]{1,0:T(1,128)S(1)} %copy-done.25, f32[40,512]{1,0:T(8,128)S(1)} %add.230.refs_1_.refs_2_, f32[4,2048]{1,0:T(4,128)S(1)} %add.245.refs_3_.refs_4_, ...), custom_call_target="tpu_custom_call" | custom-call | bytes 3180000 | tf_op jit(solution)/shard_map/head/pallas_call | solution.py:722
  244.9 5.5 %g5.1 = (bf16[384,2048]{1,0:T(8,128)(2,1)S(1)}, f32[384,512]{1,0:T(8,128)S(1)}, f32[4,512]{1,0:T(4,128)S(1)}) custom-call(s32[1]{0:T(128)} %bitcast.core_ref.refs_0_, f32[40,512]{1,0:T(8,128)S(1)} %add.230.refs_1_.refs_2_, f32[384,2048]{1,0:T(8,128)S(1)} %get-tuple-element.363.refs_2_.refs_11_, f32[384,2048]{1,0:T(8,128)} %keep.13.refs_3_, ...), custom_call_target="tpu_custom_call" | custom-call | bytes 3120000 | tf_op jit(solution)/shard_map/g5/pallas_call | solution.py:722
  266.8 5.5 %g4.1 = (bf16[9,384,512]{2,1,0:T(8,128)(2,1)S(1)}, f32[384,512]{1,0:T(8,128)S(1)}, f32[4,512]{1,0:T(4,128)S(1)}) custom-call(s32[1]{0:T(128)} %bitcast.core_ref.refs_0_, f32[40,512]{1,0:T(8,128)S(1)} %add.230.refs_1_.refs_2_, f32[384,512]{1,0:T(8,128)S(1)} %get-tuple-element.381.refs_2_, f32[384,512]{1,0:T(8,128)S(1)} %get-tuple-element.356.refs_5_.refs_10_.refs_3_, ...), custom_call_target="tpu_custom_call" | custom-call | bytes 3240000 | tf_op jit(solution)/shard_map/g4/pallas_call | solution.py:722
  287.9 6.8 %gy.1 = (bf16[384,512]{1,0:T(8,128)(2,1)S(1)}, f32[384,2048]{1,0:T(8,128)S(1)}, f32[6,2048]{1,0:T(8,128)S(1)}) custom-call(s32[1]{0:T(128)} %bitcast.core_ref.refs_0_, f32[40,512]{1,0:T(8,128)S(1)} %add.230.refs_1_.refs_2_, f32[384,512]{1,0:T(8,128)S(1)} %get-tuple-element.384.refs_2_, f32[384,512]{1,0:T(8,128)S(1)} %get-tuple-element.348.refs_5_.refs_12_.refs_3_, ...), custom_call_target="tpu_custom_call" | custom-call | bytes 4200000 | tf_op jit(solution)/shard_map/gy/pallas_call | solution.py:722
  314.2 3.9 collective-permute-done.63.refs_8_
  318.0 7.0 %g2.1 = (bf16[384,2048]{1,0:T(8,128)(2,1)S(1)}, bf16[384,2048]{1,0:T(8,128)(2,1)S(1)}, f32[384,512]{1,0:T(8,128)S(1)}, f32[4,512]{1,0:T(4,128)S(1)}) custom-call(s32[1]{0:T(128)} %bitcast.core_ref.refs_0_, f32[40,512]{1,0:T(8,128)S(1)} %add.230.refs_1_.refs_2_, f32[384,2048]{1,0:T(8,128)S(1)} %get-tuple-element.399.refs_2_, ...), custom_call_target="tpu_custom_call" | custom-call | bytes 4380000 | tf_op jit(solution)/shard_map/g2/pallas_call | solution.py:722
  350.8 7.4 %g1.1 = (bf16[9,384,512]{2,1,0:T(8,128)(2,1)S(1)}, f32[4,384,512]{2,1,0:T(8,128)S(1)}, f32[4,512]{1,0:T(4,128)S(1)}) custom-call(s32[1]{0:T(128)} %bitcast.core_ref.refs_0_, f32[40,512]{1,0:T(8,128)S(1)} %add.230.refs_1_.refs_2_, f32[384,512]{1,0:T(8,128)S(1)} %get-tuple-element.419.refs_2_, f32[384,512]{1,0:T(8,128)S(1)} %copy-done.4, ...), custom_call_target="tpu_custom_call" | custom-call | bytes 4800000 | tf_op jit(solution)/shard_map/g1/pallas_call | solution.py:722
  384.2 10.2 %collective-permute-done.81.refs_2_.refs_3_ = bf16[4,64,1024]{2,1,0:T(8,128)(2,1)S(1)} collective-permute-done((bf16[4,64,1024]{2,1,0:T(8,128)(2,1)S(1)}, bf16[4,64,1024]{2,1,0:T(8,128)(2,1)S(1)}, u32[]{:S(2)}, u32[]{:S(2)}) %collective-permute-start.81) | collective-permute-done | bytes 524320 | tf_op jit(solution)/shard_map/ppermute | solution.py:49
  400.8 4.5 dxs.1.short_ref
  409.0 6.1 %gx.1.own_ref = bf16[2,4,384,512]{3,2,1,0:T(8,128)(2,1)S(1)} custom-call(s32[1]{0:T(128)} %bitcast.core_ref.refs_0_, bf16[4,384,512]{2,1,0:T(8,128)(2,1)S(1)} %g0.1.ga_ref, f32[384,1]{1,0:T(8,128)S(1)} %get-tuple-element.301.refs_3_.refs_4_.refs_5_.refs_8_.refs_9_.refs_6_.mask_ref, ...), custom_call_target="tpu_custom_call" | custom-call | bytes 3840000 | tf_op jit(solution)/shard_map/gx/pallas_call | solution.py:722
  422.1 8.5 %collective-permute-done.89 = bf16[2,1,64,1024]{3,2,1,0:T(8,128)(2,1)S(1)} collective-permute-done((bf16[2,1,64,1024]{3,2,1,0:T(8,128)(2,1)S(1)}, bf16[2,1,64,1024]{3,2,1,0:T(8,128)(2,1)S(1)}, u32[]{:S(2)}, u32[]{:S(2)}) %collective-permute-start.89) | collective-permute-done | bytes 262176 | tf_op jit(solution)/shard_map/ppermute | solution.py:49
  432.5 3.9 place_grad.1
  436.4 6.4 %collective-permute-done.90.came_ref = bf16[2,2,192,256]{3,2,1,0:T(8,128)(2,1)S(1)} collective-permute-done((bf16[2,2,192,256]{3,2,1,0:T(8,128)(2,1)S(1)}, bf16[2,2,192,256]{3,2,1,0:T(8,128)(2,1)S(1)}, u32[]{:S(2)}, u32[]{:S(2)}) %collective-permute-start.90) | collective-permute-done | bytes 393248 | tf_op jit(solution)/shard_map/ppermute | solution.py:49
  444.8 9.6 %collective-permute-done.92 = bf16[2,1,192,256]{3,2,1,0:T(8,128)(2,1)S(1)} collective-permute-done((bf16[2,1,192,256]{3,2,1,0:T(8,128)(2,1)S(1)}, bf16[2,1,192,256]{3,2,1,0:T(8,128)(2,1)S(1)}, u32[]{:S(2)}, u32[]{:S(2)}) %collective-permute-start.92) | collective-permute-done | bytes 196640 | tf_op jit(solution)/shard_map/ppermute | solution.py:49
  469.8 3.6 collective-permute-done.100
  474.3 3.6 collective-permute-done.101.refs_2_
  (392 shorter events, 285.1 us)
Async XLA Ops:
  7.2 125.9 %all-gather.2.cloned.1.call-start = ((), (), s32[]{:S(2)}) async-start(), calls=%async_computation | async-start | bytes 8650752 | tf_op jit(solution)/shard_map/all_gather | solution.py:897
  10.2 13.4 %collective-permute-start.1 = (bf16[2,1,192,256]{3,2,1,0:T(8,128)(2,1)S(1)}, bf16[2,1,192,256]{3,2,1,0:T(8,128)(2,1)S(1)}, u32[]{:S(2)}, u32[]{:S(2)}) collective-permute-start(bf16[2,1,192,256]{3,2,1,0:T(8,128)(2,1)S(1)} %bitcast.58), channel_id=1, source_target_pairs={{0,8},{1,9},{2,10},{3,11},{4,12},{5,13},{6,14},{7,15},{8,0},{9,1},... | collective-permute-start | bytes 589832 | tf_op jit(solution)/shard_map/ppermute | solution.py:49
  35.9 14.1 %collective-permute-start.3 = (bf16[4,192,256]{2,1,0:T(8,128)(2,1)S(1)}, bf16[4,192,256]{2,1,0:T(8,128)(2,1)S(1)}, u32[]{:S(2)}, u32[]{:S(2)}) collective-permute-start(bf16[4,192,256]{2,1,0:T(8,128)(2,1)S(1)} %get-tuple-element.280.refs_0_), channel_id=1, source_target_pairs={{0,2},{1,3},{2,0},{3,1},{4,6},{5,7},{6,4},{7,5},{8,10},{9,11},{10,... | collective-permute-start | bytes 1179656 | tf_op jit(solution)/shard_map/ppermute | solution.py:49
  37.2 12.8 %collective-permute-start.4 = (bf16[4,192,256]{2,1,0:T(8,128)(2,1)S(1)}, bf16[4,192,256]{2,1,0:T(8,128)(2,1)S(1)}, u32[]{:S(2)}, u32[]{:S(2)}) collective-permute-start(bf16[4,192,256]{2,1,0:T(8,128)(2,1)S(1)} %get-tuple-element.281.refs_1_), channel_id=1, source_target_pairs={{0,1},{1,0},{2,3},{3,2},{4,5},{5,4},{6,7},{7,6},{8,9},{9,8},{10,11... | collective-permute-start | bytes 1179656 | tf_op jit(solution)/shard_map/ppermute | solution.py:49
  51.2 20.8 %collective-permute-start.6 = (bf16[8,192,256]{2,1,0:T(8,128)(2,1)}, bf16[8,192,256]{2,1,0:T(8,128)(2,1)}, u32[]{:S(2)}, u32[]{:S(2)}) collective-permute-start(bf16[8,192,256]{2,1,0:T(8,128)(2,1)} %get-tuple-element.285.refs_0_), channel_id=1, source_target_pairs={{0,1},{1,0},{2,3},{3,2},{4,5},{5,4},{6,7},{7,6},{8,9},{9,8},{10,11... | collective-permute-start | bytes 2359304 | tf_op jit(solution)/shard_map/ppermute | solution.py:49
  51.8 20.4 %collective-permute-start.7 = (bf16[8,192,256]{2,1,0:T(8,128)(2,1)}, bf16[8,192,256]{2,1,0:T(8,128)(2,1)}, u32[]{:S(2)}, u32[]{:S(2)}) collective-permute-start(bf16[8,192,256]{2,1,0:T(8,128)(2,1)} %get-tuple-element.286.refs_2_), channel_id=1, source_target_pairs={{0,2},{1,3},{2,0},{3,1},{4,6},{5,7},{6,4},{7,5},{8,10},{9,11},{10,... | collective-permute-start | bytes 2359304 | tf_op jit(solution)/shard_map/ppermute | solution.py:49
  53.5 13.9 %collective-permute-start.8 = (bf16[2,2,192,256]{3,2,1,0:T(8,128)(2,1)S(1)}, bf16[2,2,192,256]{3,2,1,0:T(8,128)(2,1)S(1)}, u32[]{:S(2)}, u32[]{:S(2)}) collective-permute-start(bf16[2,2,192,256]{3,2,1,0:T(8,128)(2,1)S(1)} %join.9.refs_0_), channel_id=1, source_target_pairs={{0,4},{1,5},{2,6},{3,7},{4,0},{5,1},{6,2},{7,3},{8,12},{9,13},{10,... | collective-permute-start | bytes 1179656 | tf_op jit(solution)/shard_map/ppermute | solution.py:49
  59.3 13.5 %collective-permute-start.10 = (bf16[8,192,256]{2,1,0:T(8,128)(2,1)}, bf16[8,192,256]{2,1,0:T(8,128)(2,1)S(1)}, u32[]{:S(2)}, u32[]{:S(2)}) collective-permute-start(bf16[8,192,256]{2,1,0:T(8,128)(2,1)} %get-tuple-element.285.refs_0_), channel_id=1, source_target_pairs={{0,16},{16,0},{1,17},{17,1},{2,18},{18,2},{3,19},{19,3},{4,20},{20... | collective-permute-start | bytes 2359304 | tf_op jit(solution)/shard_map/ppermute | solution.py:87
  59.5 13.3 %collective-permute-start.12 = (bf16[8,192,256]{2,1,0:T(8,128)(2,1)}, bf16[8,192,256]{2,1,0:T(8,128)(2,1)S(1)}, u32[]{:S(2)}, u32[]{:S(2)}) collective-permute-start(bf16[8,192,256]{2,1,0:T(8,128)(2,1)} %get-tuple-element.286.refs_2_), channel_id=1, source_target_pairs={{0,16},{16,0},{1,17},{17,1},{2,18},{18,2},{3,19},{19,3},{4,20},{20... | collective-permute-start | bytes 2359304 | tf_op jit(solution)/shard_map/ppermute | solution.py:87
  94.0 27.5 %collective-permute-start.20 = (bf16[4,192,256]{2,1,0:T(8,128)(2,1)S(1)}, bf16[4,192,256]{2,1,0:T(8,128)(2,1)S(1)}, u32[]{:S(2)}, u32[]{:S(2)}) collective-permute-start(bf16[4,192,256]{2,1,0:T(8,128)(2,1)S(1)} %get-tuple-element.309.refs_0_), channel_id=1, source_target_pairs={{0,2},{1,3},{2,0},{3,1},{4,6},{5,7},{6,4},{7,5},{8,10},{9,11},{10,... | collective-permute-start | bytes 1179656 | tf_op jit(solution)/shard_map/ppermute | solution.py:49
  94.6 26.9 %collective-permute-start.21 = (bf16[4,192,256]{2,1,0:T(8,128)(2,1)S(1)}, bf16[4,192,256]{2,1,0:T(8,128)(2,1)S(1)}, u32[]{:S(2)}, u32[]{:S(2)}) collective-permute-start(bf16[4,192,256]{2,1,0:T(8,128)(2,1)S(1)} %get-tuple-element.310.refs_1_), channel_id=1, source_target_pairs={{0,1},{1,0},{2,3},{3,2},{4,5},{5,4},{6,7},{7,6},{8,9},{9,8},{10,11... | collective-permute-start | bytes 1179656 | tf_op jit(solution)/shard_map/ppermute | solution.py:49
  124.1 21.7 %collective-permute-start.28 = (bf16[8,192,256]{2,1,0:T(8,128)(2,1)}, bf16[8,192,256]{2,1,0:T(8,128)(2,1)}, u32[]{:S(2)}, u32[]{:S(2)}) collective-permute-start(bf16[8,192,256]{2,1,0:T(8,128)(2,1)} %get-tuple-element.331.refs_0_), channel_id=1, source_target_pairs={{0,1},{1,0},{2,3},{3,2},{4,5},{5,4},{6,7},{7,6},{8,9},{9,8},{10,11... | collective-permute-start | bytes 2359304 | tf_op jit(solution)/shard_map/ppermute | solution.py:49
  124.4 21.4 %collective-permute-start.29 = (bf16[8,192,256]{2,1,0:T(8,128)(2,1)}, bf16[8,192,256]{2,1,0:T(8,128)(2,1)}, u32[]{:S(2)}, u32[]{:S(2)}) collective-permute-start(bf16[8,192,256]{2,1,0:T(8,128)(2,1)} %get-tuple-element.333.refs_2_), channel_id=1, source_target_pairs={{0,2},{1,3},{2,0},{3,1},{4,6},{5,7},{6,4},{7,5},{8,10},{9,11},{10,... | collective-permute-start | bytes 2359304 | tf_op jit(solution)/shard_map/ppermute | solution.py:49
  145.8 12.2 %collective-permute-start.30 = (bf16[8,192,256]{2,1,0:T(8,128)(2,1)}, bf16[8,192,256]{2,1,0:T(8,128)(2,1)S(1)}, u32[]{:S(2)}, u32[]{:S(2)}) collective-permute-start(bf16[8,192,256]{2,1,0:T(8,128)(2,1)} %get-tuple-element.331.refs_0_), channel_id=1, source_target_pairs={{0,16},{16,0},{1,17},{17,1},{2,18},{18,2},{3,19},{19,3},{4,20},{20... | collective-permute-start | bytes 2359304 | tf_op jit(solution)/shard_map/ppermute | solution.py:87
  145.9 12.1 %collective-permute-start.31 = (bf16[8,192,256]{2,1,0:T(8,128)(2,1)}, bf16[8,192,256]{2,1,0:T(8,128)(2,1)S(1)}, u32[]{:S(2)}, u32[]{:S(2)}) collective-permute-start(bf16[8,192,256]{2,1,0:T(8,128)(2,1)} %collective-permute-done.28.refs_1_), channel_id=1, source_target_pairs={{0,16},{16,0},{1,17},{17,1},{2,18},{18,2},{3,19},{19,3},{4,20},{20... | collective-permute-start | bytes 2359304 | tf_op jit(solution)/shard_map/ppermute | solution.py:87
  305.8 25.8 %collective-permute-start.66 = (bf16[8,192,256]{2,1,0:T(8,128)(2,1)S(1)}, bf16[8,192,256]{2,1,0:T(8,128)(2,1)S(1)}, u32[]{:S(2)}, u32[]{:S(2)}) collective-permute-start(bf16[8,192,256]{2,1,0:T(8,128)(2,1)S(1)} %get-tuple-element.415), channel_id=1, source_target_pairs={{0,1},{1,0},{2,3},{3,2},{4,5},{5,4},{6,7},{7,6},{8,9},{9,8},{10,11... | collective-permute-start | bytes 2359304 | tf_op jit(solution)/shard_map/ppermute | solution.py:49
  307.4 24.3 %collective-permute-start.67 = (bf16[8,192,256]{2,1,0:T(8,128)(2,1)S(1)}, bf16[8,192,256]{2,1,0:T(8,128)(2,1)S(1)}, u32[]{:S(2)}, u32[]{:S(2)}) collective-permute-start(bf16[8,192,256]{2,1,0:T(8,128)(2,1)S(1)} %get-tuple-element.417), channel_id=1, source_target_pairs={{0,2},{1,3},{2,0},{3,1},{4,6},{5,7},{6,4},{7,5},{8,10},{9,11},{10,... | collective-permute-start | bytes 2359304 | tf_op jit(solution)/shard_map/ppermute | solution.py:49
  332.9 12.4 %collective-permute-start.70 = (bf16[2048,1024]{1,0:T(8,128)(2,1)S(1)}, bf16[2048,1024]{1,0:T(8,128)(2,1)S(1)}, u32[]{:S(2)}, u32[]{:S(2)}) collective-permute-start(bf16[2048,1024]{1,0:T(8,128)(2,1)S(1)} %get-tuple-element.444), channel_id=1, source_target_pairs={{0,16},{16,0},{1,17},{17,1},{2,18},{18,2},{3,19},{19,3},{4,20},{20... | collective-permute-start | bytes 12582920 | tf_op jit(solution)/shard_map/ppermute | solution.py:87
  346.4 25.8 %collective-permute-start.78 = (bf16[8,64,1024]{2,1,0:T(8,128)(2,1)S(1)}, bf16[8,64,1024]{2,1,0:T(8,128)(2,1)S(1)}, u32[]{:S(2)}, u32[]{:S(2)}) collective-permute-start(bf16[8,64,1024]{2,1,0:T(8,128)(2,1)S(1)} %get-tuple-element.477), channel_id=1, source_target_pairs={{0,1},{1,0},{2,3},{3,2},{4,5},{5,4},{6,7},{7,6},{8,9},{9,8},{10,11... | collective-permute-start | bytes 3145736 | tf_op jit(solution)/shard_map/ppermute | solution.py:49
  347.9 24.3 %collective-permute-start.79 = (bf16[8,64,1024]{2,1,0:T(8,128)(2,1)S(1)}, bf16[8,64,1024]{2,1,0:T(8,128)(2,1)S(1)}, u32[]{:S(2)}, u32[]{:S(2)}) collective-permute-start(bf16[8,64,1024]{2,1,0:T(8,128)(2,1)S(1)} %get-tuple-element.478), channel_id=1, source_target_pairs={{0,2},{1,3},{2,0},{3,1},{4,6},{5,7},{6,4},{7,5},{8,10},{9,11},{10,... | collective-permute-start | bytes 3145736 | tf_op jit(solution)/shard_map/ppermute | solution.py:49
  349.1 19.0 %collective-permute-start.76 = (bf16[2,2,192,256]{3,2,1,0:T(8,128)(2,1)S(1)}, bf16[2,2,192,256]{3,2,1,0:T(8,128)(2,1)S(1)}, u32[]{:S(2)}, u32[]{:S(2)}) collective-permute-start(bf16[2,2,192,256]{3,2,1,0:T(8,128)(2,1)S(1)} %get-tuple-element.455), channel_id=1, source_target_pairs={{0,4},{1,5},{2,6},{3,7},{4,0},{5,1},{6,2},{7,3},{8,12},{9,13},{10,... | collective-permute-start | bytes 1179656 | tf_op jit(solution)/shard_map/ppermute | solution.py:49
  380.0 15.6 %collective-permute-start.80 = (bf16[6144,256]{1,0:T(8,128)(2,1)S(1)}, bf16[6144,256]{1,0:T(8,128)(2,1)S(1)}, u32[]{:S(2)}, u32[]{:S(2)}) collective-permute-start(bf16[6144,256]{1,0:T(8,128)(2,1)S(1)} %get-tuple-element.490), channel_id=1, source_target_pairs={{0,16},{16,0},{1,17},{17,1},{2,18},{18,2},{3,19},{19,3},{4,20},{20... | collective-permute-start | bytes 9437192 | tf_op jit(solution)/shard_map/ppermute | solution.py:87
  380.1 14.3 %collective-permute-start.81 = (bf16[4,64,1024]{2,1,0:T(8,128)(2,1)S(1)}, bf16[4,64,1024]{2,1,0:T(8,128)(2,1)S(1)}, u32[]{:S(2)}, u32[]{:S(2)}) collective-permute-start(bf16[4,64,1024]{2,1,0:T(8,128)(2,1)S(1)} %get-tuple-element.483), channel_id=1, source_target_pairs={{0,2},{1,3},{2,0},{3,1},{4,6},{5,7},{6,4},{7,5},{8,10},{9,11},{10,... | collective-permute-start | bytes 1572872 | tf_op jit(solution)/shard_map/ppermute | solution.py:49
  381.3 14.0 %collective-permute-start.82 = (bf16[4,64,1024]{2,1,0:T(8,128)(2,1)S(1)}, bf16[4,64,1024]{2,1,0:T(8,128)(2,1)S(1)}, u32[]{:S(2)}, u32[]{:S(2)}) collective-permute-start(bf16[4,64,1024]{2,1,0:T(8,128)(2,1)S(1)} %get-tuple-element.485), channel_id=1, source_target_pairs={{0,1},{1,0},{2,3},{3,2},{4,5},{5,4},{6,7},{7,6},{8,9},{9,8},{10,11... | collective-permute-start | bytes 1572872 | tf_op jit(solution)/shard_map/ppermute | solution.py:49
  382.8 12.9 %collective-permute-start.83 = (bf16[2,1,192,256]{3,2,1,0:T(8,128)(2,1)S(1)}, bf16[2,1,192,256]{3,2,1,0:T(8,128)(2,1)S(1)}, u32[]{:S(2)}, u32[]{:S(2)}) collective-permute-start(bf16[2,1,192,256]{3,2,1,0:T(8,128)(2,1)S(1)} %get-tuple-element.472), channel_id=1, source_target_pairs={{0,8},{1,9},{2,10},{3,11},{4,12},{5,13},{6,14},{7,15},{8,0},{9,1},... | collective-permute-start | bytes 589832 | tf_op jit(solution)/shard_map/ppermute | solution.py:49
  395.7 13.2 %collective-permute-start.86 = (bf16[2,2,64,1024]{3,2,1,0:T(8,128)(2,1)S(1)}, bf16[2,2,64,1024]{3,2,1,0:T(8,128)(2,1)S(1)}, u32[]{:S(2)}, u32[]{:S(2)}) collective-permute-start(bf16[2,2,64,1024]{3,2,1,0:T(8,128)(2,1)S(1)} %get-tuple-element.500), channel_id=1, source_target_pairs={{0,4},{1,5},{2,6},{3,7},{4,0},{5,1},{6,2},{7,3},{8,12},{9,13},{10,... | collective-permute-start | bytes 1572872 | tf_op jit(solution)/shard_map/ppermute | solution.py:49
  398.0 18.6 %collective-permute-start.84 = (bf16[8,192,256]{2,1,0:T(8,128)(2,1)S(1)}, bf16[8,192,256]{2,1,0:T(8,128)(2,1)S(1)}, u32[]{:S(2)}, u32[]{:S(2)}) collective-permute-start(bf16[8,192,256]{2,1,0:T(8,128)(2,1)S(1)} %get-tuple-element.497), channel_id=1, source_target_pairs={{0,1},{1,0},{2,3},{3,2},{4,5},{5,4},{6,7},{7,6},{8,9},{9,8},{10,11... | collective-permute-start | bytes 2359304 | tf_op jit(solution)/shard_map/ppermute | solution.py:49
  399.8 18.2 %collective-permute-start.85 = (bf16[8,192,256]{2,1,0:T(8,128)(2,1)S(1)}, bf16[8,192,256]{2,1,0:T(8,128)(2,1)S(1)}, u32[]{:S(2)}, u32[]{:S(2)}) collective-permute-start(bf16[8,192,256]{2,1,0:T(8,128)(2,1)S(1)} %get-tuple-element.498), channel_id=1, source_target_pairs={{0,2},{1,3},{2,0},{3,1},{4,6},{5,7},{6,4},{7,5},{8,10},{9,11},{10,... | collective-permute-start | bytes 2359304 | tf_op jit(solution)/shard_map/ppermute | solution.py:49
  415.2 17.3 %collective-permute-start.91 = (bf16[4,384,512]{2,1,0:T(8,128)(2,1)S(1)}, bf16[4,384,512]{2,1,0:T(8,128)(2,1)S(1)}, u32[]{:S(2)}, u32[]{:S(2)}) collective-permute-start(bf16[4,384,512]{2,1,0:T(8,128)(2,1)S(1)} %slice_bitcast_fusion), channel_id=1, source_target_pairs={{0,16},{16,0},{1,17},{17,1},{2,18},{18,2},{3,19},{19,3},{4,20},{20... | collective-permute-start | bytes 4718600 | tf_op jit(solution)/shard_map/ppermute | solution.py:87
  418.0 12.6 %collective-permute-start.89 = (bf16[2,1,64,1024]{3,2,1,0:T(8,128)(2,1)S(1)}, bf16[2,1,64,1024]{3,2,1,0:T(8,128)(2,1)S(1)}, u32[]{:S(2)}, u32[]{:S(2)}) collective-permute-start(bf16[2,1,64,1024]{3,2,1,0:T(8,128)(2,1)S(1)} %get-tuple-element.510), channel_id=1, source_target_pairs={{0,8},{1,9},{2,10},{3,11},{4,12},{5,13},{6,14},{7,15},{8,0},{9,1},... | collective-permute-start | bytes 786440 | tf_op jit(solution)/shard_map/ppermute | solution.py:49
  442.8 11.7 %collective-permute-start.92 = (bf16[2,1,192,256]{3,2,1,0:T(8,128)(2,1)S(1)}, bf16[2,1,192,256]{3,2,1,0:T(8,128)(2,1)S(1)}, u32[]{:S(2)}, u32[]{:S(2)}) collective-permute-start(bf16[2,1,192,256]{3,2,1,0:T(8,128)(2,1)S(1)} %get-tuple-element.522), channel_id=1, source_target_pairs={{0,8},{1,9},{2,10},{3,11},{4,12},{5,13},{6,14},{7,15},{8,0},{9,1},... | collective-permute-start | bytes 589832 | tf_op jit(solution)/shard_map/ppermute | solution.py:49
  444.8 12.6 %collective-permute-start.95 = (f32[8,512]{1,0:T(8,128)}, f32[8,512]{1,0:T(8,128)}, u32[]{:S(2)}, u32[]{:S(2)}) collective-permute-start(f32[8,512]{1,0:T(8,128)} %stack.10), channel_id=1, source_target_pairs={{0,16},{16,0},{1,17},{17,1},{2,18},{18,2},{3,19},{19,3},{4,20},{20... | collective-permute-start | bytes 49160 | tf_op jit(solution)/shard_map/ppermute | solution.py:87
  (102 other events, 1016.1 us)
Sparse Core Ops, SparseCore 0:
  51.3 80.8 all-gather.1

commit v6 on v5

--- a/solution.py
+++ b/solution.py
@@ -1377,6 +1377,18 @@
         )
         return pair, swap_pipe(pair[1])
 
+    def table_grads(sums):
+        sum1, sum2, sum3, sum4, sum5, sum6 = (t.sum for t in sums)
+
+        def pair_sum(rows):
+            return rows[0] + rows[1]
+
+        mid_rows = jnp.stack([pair_sum(v) for t in (sum1, sum2, sum4, sum5) for v in (t[2:4], t[0:2])])
+        wide_rows = jnp.stack([pair_sum(v) for v in (sum3[2:4], sum3[0:2], sum3[4:6], sum3[0:2], sum6[2:4], sum6[0:2])])
+        mid_rows = mid_rows + swap_pipe(mid_rows)
+        wide_rows = wide_rows + swap_pipe(wide_rows)
+        return lax.dynamic_slice(mid_rows, (0, shard * mid_cols), (8, mid_cols)), lax.dynamic_slice(wide_rows, (0, shard * wide_cols), (6, wide_cols))
+
     if fast:
         state_w = halved(state_w, held["came_w"], True)
         got_a, state_w, came_b = lax.optimization_barrier((got_a, state_w, held["came_b"]))
@@ -1400,7 +1412,8 @@
         state_a = halved_both(state_a, came_a)
         came_a = exchange(state_a[1], 8)
         sums = pin(tuple(t.parts for t in sums), state_a[0])
-        sums = [Total(*parts) for parts in sums]
+        grad_mid, grad_table = table_grads([Total(*parts) for parts in sums])
+        came_a, grad_mid, grad_table = lax.optimization_barrier((came_a, grad_mid, grad_table))
         half_a = jnp.concatenate(added(state_a, came_a), axis=0)
     else:
         half_a = jnp.concatenate(scatter_plain(bufs_a[0], got_a, rows_n, True), axis=0)
@@ -1408,6 +1421,7 @@
         half_b = jnp.concatenate(scatter_plain(bufs_b[0], held["got_b"], rows_n, True), axis=0)
         pair, got_pair = image_grads(ga1, wide_back(ga1))
         grad_local = place("place_grad", pair, got_pair, ga1)
+        grad_mid, grad_table = table_grads(sums)
     grad_local = grad_local.reshape(IMG_DEV, 2 * HB, 2 * WB, C_IN // 2)
 
     def join_halves(first, second):
@@ -1417,18 +1431,6 @@
 
     grad_narrow = join_halves(half_a, half_b)
     grad_wide = join_halves(half_w0, half_w1)
-
-    sum1, sum2, sum3, sum4, sum5, sum6 = (t.sum for t in sums)
-
-    def pair_sum(rows):
-        return rows[0] + rows[1]
-
-    mid_rows = jnp.stack([pair_sum(v) for t in (sum1, sum2, sum4, sum5) for v in (t[2:4], t[0:2])])
-    wide_rows = jnp.stack([pair_sum(v) for v in (sum3[2:4], sum3[0:2], sum3[4:6], sum3[0:2], sum6[2:4], sum6[0:2])])
-    mid_rows = mid_rows + swap_pipe(mid_rows)
-    wide_rows = wide_rows + swap_pipe(wide_rows)
-    grad_mid = lax.dynamic_slice(mid_rows, (0, shard * mid_cols), (8, mid_cols))
-    grad_table = lax.dynamic_slice(wide_rows, (0, shard * wide_cols), (6, wide_cols))
 
     starts = (shard * jnp.array([rows_n, w_wide.shape[0]])).astype(jnp.int32)
     weights, grads = (w_narrow, w_wide, bn_mid, bn_wide), (grad_narrow, grad_wide, grad_mid, grad_table)

time: 498 us -> 494 us (level)
  transfers between devices with their start and end apart: 103 -> 103, of which waited for: 71 -> 69; matrix products, arithmetic and copies ran while one was open for 1% -> 1% of each run, Pallas kernels for 23% -> 23%
where the time goes in v6:
time: 494 us; the launch traced here: 484 us
  waiting for transfers between devices  187 us (38%)
  Pallas kernels  161 us (33%)
  starting transfers between devices  115 us (23%)
  between operations  15.7 us (3%)
    ppermute x82, waiting for transfers between devices, exchange(): return lax.ppermute(value, 'dp', pairs(bit))  179 us
    pallas_call x70, Pallas kernels, call(): pl.pallas_call(kernel, out_shape=out_shape, grid_spec=pltpu.PrefetchScala...  161 us
    ppermute x82, starting transfers between devices, exchange(): return lax.ppermute(value, 'dp', pairs(bit))  111 us
  transfers between devices with their start and end apart: 103, of which 69 were waited for; matrix products, arithmetic and copies ran while one was open for 1% of the time, Pallas kernels for 23%

profile of v6, /device:TPU:0, one launch (start us, length us, event | category | flops | bytes accessed | tf_op | source)
XLA Modules:
  0.0 484.0 jit_solution(13212298268243202591)
XLA Ops:
  10.2 4.0 collective-permute-start.1
  14.2 9.4 %collective-permute-done.1.refs_1_ = bf16[2,1,192,256]{3,2,1,0:T(8,128)(2,1)S(1)} collective-permute-done((bf16[2,1,192,256]{3,2,1,0:T(8,128)(2,1)S(1)}, bf16[2,1,192,256]{3,2,1,0:T(8,128)(2,1)S(1)}, u32[]{:S(2)}, u32[]{:S(2)}) %collective-permute-start.1) | collective-permute-done | bytes 196640 | tf_op jit(solution)/shard_map/ppermute | solution.py:49
  24.9 9.9 %collective-permute-done.2.refs_1_ = bf16[2,2,192,256]{3,2,1,0:T(8,128)(2,1)S(1)} collective-permute-done((bf16[2,2,192,256]{3,2,1,0:T(8,128)(2,1)S(1)}, bf16[2,2,192,256]{3,2,1,0:T(8,128)(2,1)S(1)}, u32[]{:S(2)}, u32[]{:S(2)}) %collective-permute-start.2) | collective-permute-done | bytes 393248 | tf_op jit(solution)/shard_map/ppermute | solution.py:49
  42.5 7.5 %collective-permute-done.5.refs_1_.refs_2_ = bf16[2,1,192,256]{3,2,1,0:T(8,128)(2,1)S(1)} collective-permute-done((bf16[2,1,192,256]{3,2,1,0:T(8,128)(2,1)S(1)}, bf16[2,1,192,256]{3,2,1,0:T(8,128)(2,1)S(1)}, u32[]{:S(2)}, u32[]{:S(2)}) %collective-permute-start.5) | collective-permute-done | bytes 196640 | tf_op jit(solution)/shard_map/ppermute | solution.py:49
  54.4 4.9 %prep.1 = (bf16[4,384,1024]{2,1,0:T(8,128)(2,1)S(1)}, f32[384,1]{1,0:T(8,128)S(1)}, f32[4,512]{1,0:T(4,128)S(1)}) custom-call(s32[1]{0:T(128)} %bitcast.core_ref.refs_0_, s32[1,8]{1,0:T(1,128)S(1)} %copy-done.25, s32[8]{0:T(128)S(1)} %copy-done.28, s32[8]{0:T(128)S(1)} %copy-done.29, bf16[8,384,1024]{2,1,0:T(8,128)(2,1)} %bitcast.73, ...), custom_call_target="tpu_custom_call" | custom-call | bytes 3000000 | tf_op jit(solution)/shard_map/prep/pallas_call | solution.py:722
  59.9 7.4 %collective-permute-done.8.refs_1_.refs_2_ = bf16[2,2,192,256]{3,2,1,0:T(8,128)(2,1)S(1)} collective-permute-done((bf16[2,2,192,256]{3,2,1,0:T(8,128)(2,1)S(1)}, bf16[2,2,192,256]{3,2,1,0:T(8,128)(2,1)S(1)}, u32[]{:S(2)}, u32[]{:S(2)}) %collective-permute-start.8) | collective-permute-done | bytes 393248 | tf_op jit(solution)/shard_map/ppermute | solution.py:49
  67.3 4.7 collective-permute-done.6.refs_1_
  79.0 3.6 a1.1
  103.2 7.2 %collective-permute-done.17.refs_2_ = f32[40,512]{1,0:T(8,128)S(1)} collective-permute-done((f32[40,512]{1,0:T(8,128)S(1)}, f32[40,512]{1,0:T(8,128)S(1)}, u32[]{:S(2)}, u32[]{:S(2)}) %collective-permute-start.17) | collective-permute-done | bytes 81952 | tf_op jit(solution)/shard_map/ppermute | solution.py:49
  110.4 6.0 %a2.1 = (f32[384,512]{1,0:T(8,128)S(1)}, bf16[4,384,512]{2,1,0:T(8,128)(2,1)S(1)}, f32[4,512]{1,0:T(4,128)S(1)}) custom-call(s32[1]{0:T(128)} %bitcast.core_ref.refs_0_, f32[40,512]{1,0:T(8,128)S(1)} %add.229.refs_1_, f32[40,512]{1,0:T(8,128)S(1)} %collective-permute-done.17.refs_2_, ...), custom_call_target="tpu_custom_call" | custom-call | bytes 3000000 | tf_op jit(solution)/shard_map/a2/pallas_call | solution.py:722
  129.4 3.5 collective-permute-start.23
  133.0 4.5 as.1
  137.5 3.8 a3.1
  161.1 5.1 %a4.1 = (bf16[384,2048]{1,0:T(8,128)(2,1)S(1)}, f32[384,512]{1,0:T(8,128)S(1)}, f32[4,512]{1,0:T(4,128)S(1)}) custom-call(s32[1]{0:T(128)} %bitcast.core_ref.refs_0_, f32[40,512]{1,0:T(8,128)S(1)} %add.230.refs_1_.refs_2_, f32[8,2048]{1,0:T(8,128)S(1)} %add.236.refs_2_.refs_14_.refs_5_, f32[8,2048]{1,0:T(8,128)S(1)} %collective-permute-done.27.refs_3_.refs_15_.refs_6_, ...), custom_call_target="tpu_custom_call" | custom-call | bytes 2820000 | tf_op jit(solution)/shard_map/a4/pallas_call | solution.py:722
  181.8 3.6 a5.1
  201.6 3.8 a6.1
  222.2 5.5 %head.1 = (bf16[2,384,1024]{2,1,0:T(8,128)(2,1)S(1)}, f32[384,2048]{1,0:T(8,128)S(1)}, f32[4,2048]{1,0:T(4,128)S(1)}) custom-call(s32[1]{0:T(128)} %bitcast.core_ref.refs_0_, s32[1,8]{1,0:T(1,128)S(1)} %copy-done.25, f32[40,512]{1,0:T(8,128)S(1)} %add.230.refs_1_.refs_2_, f32[4,2048]{1,0:T(4,128)S(1)} %add.245.refs_3_.refs_4_, ...), custom_call_target="tpu_custom_call" | custom-call | bytes 3180000 | tf_op jit(solution)/shard_map/head/pallas_call | solution.py:722
  244.8 5.5 %g5.1 = (bf16[384,2048]{1,0:T(8,128)(2,1)S(1)}, f32[384,512]{1,0:T(8,128)S(1)}, f32[4,512]{1,0:T(4,128)S(1)}) custom-call(s32[1]{0:T(128)} %bitcast.core_ref.refs_0_, f32[40,512]{1,0:T(8,128)S(1)} %add.230.refs_1_.refs_2_, f32[384,2048]{1,0:T(8,128)S(1)} %get-tuple-element.366.refs_2_.refs_11_, f32[384,2048]{1,0:T(8,128)} %keep.13.refs_3_, ...), custom_call_target="tpu_custom_call" | custom-call | bytes 3120000 | tf_op jit(solution)/shard_map/g5/pallas_call | solution.py:722
  266.6 5.5 %g4.1 = (bf16[9,384,512]{2,1,0:T(8,128)(2,1)S(1)}, f32[384,512]{1,0:T(8,128)S(1)}, f32[4,512]{1,0:T(4,128)S(1)}) custom-call(s32[1]{0:T(128)} %bitcast.core_ref.refs_0_, f32[40,512]{1,0:T(8,128)S(1)} %add.230.refs_1_.refs_2_, f32[384,512]{1,0:T(8,128)S(1)} %get-tuple-element.384.refs_2_, f32[384,512]{1,0:T(8,128)S(1)} %get-tuple-element.359.refs_5_.refs_10_.refs_3_, ...), custom_call_target="tpu_custom_call" | custom-call | bytes 3240000 | tf_op jit(solution)/shard_map/g4/pallas_call | solution.py:722
  287.8 6.8 %gy.1 = (bf16[384,512]{1,0:T(8,128)(2,1)S(1)}, f32[384,2048]{1,0:T(8,128)S(1)}, f32[6,2048]{1,0:T(8,128)S(1)}) custom-call(s32[1]{0:T(128)} %bitcast.core_ref.refs_0_, f32[40,512]{1,0:T(8,128)S(1)} %add.230.refs_1_.refs_2_, f32[384,512]{1,0:T(8,128)S(1)} %get-tuple-element.387.refs_2_, f32[384,512]{1,0:T(8,128)S(1)} %get-tuple-element.351.refs_5_.refs_12_.refs_3_, ...), custom_call_target="tpu_custom_call" | custom-call | bytes 4200000 | tf_op jit(solution)/shard_map/gy/pallas_call | solution.py:722
  314.0 3.9 collective-permute-done.63.refs_8_
  317.8 7.0 %g2.1 = (bf16[384,2048]{1,0:T(8,128)(2,1)S(1)}, bf16[384,2048]{1,0:T(8,128)(2,1)S(1)}, f32[384,512]{1,0:T(8,128)S(1)}, f32[4,512]{1,0:T(4,128)S(1)}) custom-call(s32[1]{0:T(128)} %bitcast.core_ref.refs_0_, f32[40,512]{1,0:T(8,128)S(1)} %add.230.refs_1_.refs_2_, f32[384,2048]{1,0:T(8,128)S(1)} %get-tuple-element.402.refs_2_, ...), custom_call_target="tpu_custom_call" | custom-call | bytes 4380000 | tf_op jit(solution)/shard_map/g2/pallas_call | solution.py:722
  350.6 7.4 %g1.1 = (bf16[9,384,512]{2,1,0:T(8,128)(2,1)S(1)}, f32[4,384,512]{2,1,0:T(8,128)S(1)}, f32[4,512]{1,0:T(4,128)S(1)}) custom-call(s32[1]{0:T(128)} %bitcast.core_ref.refs_0_, f32[40,512]{1,0:T(8,128)S(1)} %add.230.refs_1_.refs_2_, f32[384,512]{1,0:T(8,128)S(1)} %get-tuple-element.422.refs_2_, f32[384,512]{1,0:T(8,128)S(1)} %copy-done.4, ...), custom_call_target="tpu_custom_call" | custom-call | bytes 4800000 | tf_op jit(solution)/shard_map/g1/pallas_call | solution.py:722
  384.0 10.3 %collective-permute-done.81.refs_2_.refs_3_ = bf16[4,64,1024]{2,1,0:T(8,128)(2,1)S(1)} collective-permute-done((bf16[4,64,1024]{2,1,0:T(8,128)(2,1)S(1)}, bf16[4,64,1024]{2,1,0:T(8,128)(2,1)S(1)}, u32[]{:S(2)}, u32[]{:S(2)}) %collective-permute-start.81) | collective-permute-done | bytes 524320 | tf_op jit(solution)/shard_map/ppermute | solution.py:49
  400.6 4.5 dxs.1.short_ref
  405.2 3.6 collective-permute-done.86.came_ref
  408.9 6.0 %gx.1.own_ref = bf16[2,4,384,512]{3,2,1,0:T(8,128)(2,1)S(1)} custom-call(s32[1]{0:T(128)} %bitcast.core_ref.refs_0_, bf16[4,384,512]{2,1,0:T(8,128)(2,1)S(1)} %g0.1.ga_ref, f32[384,1]{1,0:T(8,128)S(1)} %get-tuple-element.304.refs_3_.refs_4_.refs_5_.refs_8_.refs_9_.refs_6_.mask_ref, ...), custom_call_target="tpu_custom_call" | custom-call | bytes 3840000 | tf_op jit(solution)/shard_map/gx/pallas_call | solution.py:722
  421.2 9.3 %collective-permute-done.89 = bf16[2,1,64,1024]{3,2,1,0:T(8,128)(2,1)S(1)} collective-permute-done((bf16[2,1,64,1024]{3,2,1,0:T(8,128)(2,1)S(1)}, bf16[2,1,64,1024]{3,2,1,0:T(8,128)(2,1)S(1)}, u32[]{:S(2)}, u32[]{:S(2)}) %collective-permute-start.89) | collective-permute-done | bytes 262176 | tf_op jit(solution)/shard_map/ppermute | solution.py:49
  431.2 3.8 place_grad.1
  435.0 6.1 %collective-permute-done.90.came_ref = bf16[2,2,192,256]{3,2,1,0:T(8,128)(2,1)S(1)} collective-permute-done((bf16[2,2,192,256]{3,2,1,0:T(8,128)(2,1)S(1)}, bf16[2,2,192,256]{3,2,1,0:T(8,128)(2,1)S(1)}, u32[]{:S(2)}, u32[]{:S(2)}) %collective-permute-start.90) | collective-permute-done | bytes 393248 | tf_op jit(solution)/shard_map/ppermute | solution.py:49
  444.2 10.0 %collective-permute-done.92 = bf16[2,1,192,256]{3,2,1,0:T(8,128)(2,1)S(1)} collective-permute-done((bf16[2,1,192,256]{3,2,1,0:T(8,128)(2,1)S(1)}, bf16[2,1,192,256]{3,2,1,0:T(8,128)(2,1)S(1)}, u32[]{:S(2)}, u32[]{:S(2)}) %collective-permute-start.92) | collective-permute-done | bytes 196640 | tf_op jit(solution)/shard_map/ppermute | solution.py:49
  465.8 3.6 collective-permute-done.100
  (392 shorter events, 280.6 us)
Async XLA Ops:
  7.2 125.8 %all-gather.2.cloned.1.call-start = ((), (), s32[]{:S(2)}) async-start(), calls=%async_computation | async-start | bytes 8650752 | tf_op jit(solution)/shard_map/all_gather | solution.py:897
  10.2 13.4 %collective-permute-start.1 = (bf16[2,1,192,256]{3,2,1,0:T(8,128)(2,1)S(1)}, bf16[2,1,192,256]{3,2,1,0:T(8,128)(2,1)S(1)}, u32[]{:S(2)}, u32[]{:S(2)}) collective-permute-start(bf16[2,1,192,256]{3,2,1,0:T(8,128)(2,1)S(1)} %bitcast.58), channel_id=1, source_target_pairs={{0,8},{1,9},{2,10},{3,11},{4,12},{5,13},{6,14},{7,15},{8,0},{9,1},... | collective-permute-start | bytes 589832 | tf_op jit(solution)/shard_map/ppermute | solution.py:49
  35.9 14.1 %collective-permute-start.3 = (bf16[4,192,256]{2,1,0:T(8,128)(2,1)S(1)}, bf16[4,192,256]{2,1,0:T(8,128)(2,1)S(1)}, u32[]{:S(2)}, u32[]{:S(2)}) collective-permute-start(bf16[4,192,256]{2,1,0:T(8,128)(2,1)S(1)} %get-tuple-element.283.refs_0_), channel_id=1, source_target_pairs={{0,2},{1,3},{2,0},{3,1},{4,6},{5,7},{6,4},{7,5},{8,10},{9,11},{10,... | collective-permute-start | bytes 1179656 | tf_op jit(solution)/shard_map/ppermute | solution.py:49
  37.2 12.8 %collective-permute-start.4 = (bf16[4,192,256]{2,1,0:T(8,128)(2,1)S(1)}, bf16[4,192,256]{2,1,0:T(8,128)(2,1)S(1)}, u32[]{:S(2)}, u32[]{:S(2)}) collective-permute-start(bf16[4,192,256]{2,1,0:T(8,128)(2,1)S(1)} %get-tuple-element.284.refs_1_), channel_id=1, source_target_pairs={{0,1},{1,0},{2,3},{3,2},{4,5},{5,4},{6,7},{7,6},{8,9},{9,8},{10,11... | collective-permute-start | bytes 1179656 | tf_op jit(solution)/shard_map/ppermute | solution.py:49
  51.2 20.8 %collective-permute-start.6 = (bf16[8,192,256]{2,1,0:T(8,128)(2,1)}, bf16[8,192,256]{2,1,0:T(8,128)(2,1)}, u32[]{:S(2)}, u32[]{:S(2)}) collective-permute-start(bf16[8,192,256]{2,1,0:T(8,128)(2,1)} %get-tuple-element.288.refs_0_), channel_id=1, source_target_pairs={{0,1},{1,0},{2,3},{3,2},{4,5},{5,4},{6,7},{7,6},{8,9},{9,8},{10,11... | collective-permute-start | bytes 2359304 | tf_op jit(solution)/shard_map/ppermute | solution.py:49
  51.8 20.4 %collective-permute-start.7 = (bf16[8,192,256]{2,1,0:T(8,128)(2,1)}, bf16[8,192,256]{2,1,0:T(8,128)(2,1)}, u32[]{:S(2)}, u32[]{:S(2)}) collective-permute-start(bf16[8,192,256]{2,1,0:T(8,128)(2,1)} %get-tuple-element.289.refs_2_), channel_id=1, source_target_pairs={{0,2},{1,3},{2,0},{3,1},{4,6},{5,7},{6,4},{7,5},{8,10},{9,11},{10,... | collective-permute-start | bytes 2359304 | tf_op jit(solution)/shard_map/ppermute | solution.py:49
  53.5 13.8 %collective-permute-start.8 = (bf16[2,2,192,256]{3,2,1,0:T(8,128)(2,1)S(1)}, bf16[2,2,192,256]{3,2,1,0:T(8,128)(2,1)S(1)}, u32[]{:S(2)}, u32[]{:S(2)}) collective-permute-start(bf16[2,2,192,256]{3,2,1,0:T(8,128)(2,1)S(1)} %join.9.refs_0_), channel_id=1, source_target_pairs={{0,4},{1,5},{2,6},{3,7},{4,0},{5,1},{6,2},{7,3},{8,12},{9,13},{10,... | collective-permute-start | bytes 1179656 | tf_op jit(solution)/shard_map/ppermute | solution.py:49
  59.3 13.5 %collective-permute-start.10 = (bf16[8,192,256]{2,1,0:T(8,128)(2,1)}, bf16[8,192,256]{2,1,0:T(8,128)(2,1)S(1)}, u32[]{:S(2)}, u32[]{:S(2)}) collective-permute-start(bf16[8,192,256]{2,1,0:T(8,128)(2,1)} %get-tuple-element.288.refs_0_), channel_id=1, source_target_pairs={{0,16},{16,0},{1,17},{17,1},{2,18},{18,2},{3,19},{19,3},{4,20},{20... | collective-permute-start | bytes 2359304 | tf_op jit(solution)/shard_map/ppermute | solution.py:87
  59.5 13.3 %collective-permute-start.12 = (bf16[8,192,256]{2,1,0:T(8,128)(2,1)}, bf16[8,192,256]{2,1,0:T(8,128)(2,1)S(1)}, u32[]{:S(2)}, u32[]{:S(2)}) collective-permute-start(bf16[8,192,256]{2,1,0:T(8,128)(2,1)} %get-tuple-element.289.refs_2_), channel_id=1, source_target_pairs={{0,16},{16,0},{1,17},{17,1},{2,18},{18,2},{3,19},{19,3},{4,20},{20... | collective-permute-start | bytes 2359304 | tf_op jit(solution)/shard_map/ppermute | solution.py:87
  94.0 27.6 %collective-permute-start.20 = (bf16[4,192,256]{2,1,0:T(8,128)(2,1)S(1)}, bf16[4,192,256]{2,1,0:T(8,128)(2,1)S(1)}, u32[]{:S(2)}, u32[]{:S(2)}) collective-permute-start(bf16[4,192,256]{2,1,0:T(8,128)(2,1)S(1)} %get-tuple-element.312.refs_0_), channel_id=1, source_target_pairs={{0,2},{1,3},{2,0},{3,1},{4,6},{5,7},{6,4},{7,5},{8,10},{9,11},{10,... | collective-permute-start | bytes 1179656 | tf_op jit(solution)/shard_map/ppermute | solution.py:49
  94.5 27.0 %collective-permute-start.21 = (bf16[4,192,256]{2,1,0:T(8,128)(2,1)S(1)}, bf16[4,192,256]{2,1,0:T(8,128)(2,1)S(1)}, u32[]{:S(2)}, u32[]{:S(2)}) collective-permute-start(bf16[4,192,256]{2,1,0:T(8,128)(2,1)S(1)} %get-tuple-element.313.refs_1_), channel_id=1, source_target_pairs={{0,1},{1,0},{2,3},{3,2},{4,5},{5,4},{6,7},{7,6},{8,9},{9,8},{10,11... | collective-permute-start | bytes 1179656 | tf_op jit(solution)/shard_map/ppermute | solution.py:49
  124.1 21.7 %collective-permute-start.28 = (bf16[8,192,256]{2,1,0:T(8,128)(2,1)}, bf16[8,192,256]{2,1,0:T(8,128)(2,1)}, u32[]{:S(2)}, u32[]{:S(2)}) collective-permute-start(bf16[8,192,256]{2,1,0:T(8,128)(2,1)} %get-tuple-element.334.refs_0_), channel_id=1, source_target_pairs={{0,1},{1,0},{2,3},{3,2},{4,5},{5,4},{6,7},{7,6},{8,9},{9,8},{10,11... | collective-permute-start | bytes 2359304 | tf_op jit(solution)/shard_map/ppermute | solution.py:49
  124.4 21.4 %collective-permute-start.29 = (bf16[8,192,256]{2,1,0:T(8,128)(2,1)}, bf16[8,192,256]{2,1,0:T(8,128)(2,1)}, u32[]{:S(2)}, u32[]{:S(2)}) collective-permute-start(bf16[8,192,256]{2,1,0:T(8,128)(2,1)} %get-tuple-element.336.refs_2_), channel_id=1, source_target_pairs={{0,2},{1,3},{2,0},{3,1},{4,6},{5,7},{6,4},{7,5},{8,10},{9,11},{10,... | collective-permute-start | bytes 2359304 | tf_op jit(solution)/shard_map/ppermute | solution.py:49
  145.8 12.2 %collective-permute-start.30 = (bf16[8,192,256]{2,1,0:T(8,128)(2,1)}, bf16[8,192,256]{2,1,0:T(8,128)(2,1)S(1)}, u32[]{:S(2)}, u32[]{:S(2)}) collective-permute-start(bf16[8,192,256]{2,1,0:T(8,128)(2,1)} %get-tuple-element.334.refs_0_), channel_id=1, source_target_pairs={{0,16},{16,0},{1,17},{17,1},{2,18},{18,2},{3,19},{19,3},{4,20},{20... | collective-permute-start | bytes 2359304 | tf_op jit(solution)/shard_map/ppermute | solution.py:87
  145.8 12.1 %collective-permute-start.31 = (bf16[8,192,256]{2,1,0:T(8,128)(2,1)}, bf16[8,192,256]{2,1,0:T(8,128)(2,1)S(1)}, u32[]{:S(2)}, u32[]{:S(2)}) collective-permute-start(bf16[8,192,256]{2,1,0:T(8,128)(2,1)} %collective-permute-done.28.refs_1_), channel_id=1, source_target_pairs={{0,16},{16,0},{1,17},{17,1},{2,18},{18,2},{3,19},{19,3},{4,20},{20... | collective-permute-start | bytes 2359304 | tf_op jit(solution)/shard_map/ppermute | solution.py:87
  305.6 25.8 %collective-permute-start.66 = (bf16[8,192,256]{2,1,0:T(8,128)(2,1)S(1)}, bf16[8,192,256]{2,1,0:T(8,128)(2,1)S(1)}, u32[]{:S(2)}, u32[]{:S(2)}) collective-permute-start(bf16[8,192,256]{2,1,0:T(8,128)(2,1)S(1)} %get-tuple-element.418), channel_id=1, source_target_pairs={{0,1},{1,0},{2,3},{3,2},{4,5},{5,4},{6,7},{7,6},{8,9},{9,8},{10,11... | collective-permute-start | bytes 2359304 | tf_op jit(solution)/shard_map/ppermute | solution.py:49
  307.2 24.3 %collective-permute-start.67 = (bf16[8,192,256]{2,1,0:T(8,128)(2,1)S(1)}, bf16[8,192,256]{2,1,0:T(8,128)(2,1)S(1)}, u32[]{:S(2)}, u32[]{:S(2)}) collective-permute-start(bf16[8,192,256]{2,1,0:T(8,128)(2,1)S(1)} %get-tuple-element.420), channel_id=1, source_target_pairs={{0,2},{1,3},{2,0},{3,1},{4,6},{5,7},{6,4},{7,5},{8,10},{9,11},{10,... | collective-permute-start | bytes 2359304 | tf_op jit(solution)/shard_map/ppermute | solution.py:49
  332.7 12.4 %collective-permute-start.70 = (bf16[2048,1024]{1,0:T(8,128)(2,1)S(1)}, bf16[2048,1024]{1,0:T(8,128)(2,1)S(1)}, u32[]{:S(2)}, u32[]{:S(2)}) collective-permute-start(bf16[2048,1024]{1,0:T(8,128)(2,1)S(1)} %get-tuple-element.447), channel_id=1, source_target_pairs={{0,16},{16,0},{1,17},{17,1},{2,18},{18,2},{3,19},{19,3},{4,20},{20... | collective-permute-start | bytes 12582920 | tf_op jit(solution)/shard_map/ppermute | solution.py:87
  346.2 25.8 %collective-permute-start.78 = (bf16[8,64,1024]{2,1,0:T(8,128)(2,1)S(1)}, bf16[8,64,1024]{2,1,0:T(8,128)(2,1)S(1)}, u32[]{:S(2)}, u32[]{:S(2)}) collective-permute-start(bf16[8,64,1024]{2,1,0:T(8,128)(2,1)S(1)} %get-tuple-element.480), channel_id=1, source_target_pairs={{0,1},{1,0},{2,3},{3,2},{4,5},{5,4},{6,7},{7,6},{8,9},{9,8},{10,11... | collective-permute-start | bytes 3145736 | tf_op jit(solution)/shard_map/ppermute | solution.py:49
  347.8 24.2 %collective-permute-start.79 = (bf16[8,64,1024]{2,1,0:T(8,128)(2,1)S(1)}, bf16[8,64,1024]{2,1,0:T(8,128)(2,1)S(1)}, u32[]{:S(2)}, u32[]{:S(2)}) collective-permute-start(bf16[8,64,1024]{2,1,0:T(8,128)(2,1)S(1)} %get-tuple-element.481), channel_id=1, source_target_pairs={{0,2},{1,3},{2,0},{3,1},{4,6},{5,7},{6,4},{7,5},{8,10},{9,11},{10,... | collective-permute-start | bytes 3145736 | tf_op jit(solution)/shard_map/ppermute | solution.py:49
  348.9 19.0 %collective-permute-start.76 = (bf16[2,2,192,256]{3,2,1,0:T(8,128)(2,1)S(1)}, bf16[2,2,192,256]{3,2,1,0:T(8,128)(2,1)S(1)}, u32[]{:S(2)}, u32[]{:S(2)}) collective-permute-start(bf16[2,2,192,256]{3,2,1,0:T(8,128)(2,1)S(1)} %get-tuple-element.458), channel_id=1, source_target_pairs={{0,4},{1,5},{2,6},{3,7},{4,0},{5,1},{6,2},{7,3},{8,12},{9,13},{10,... | collective-permute-start | bytes 1179656 | tf_op jit(solution)/shard_map/ppermute | solution.py:49
  379.9 15.6 %collective-permute-start.80 = (bf16[6144,256]{1,0:T(8,128)(2,1)S(1)}, bf16[6144,256]{1,0:T(8,128)(2,1)S(1)}, u32[]{:S(2)}, u32[]{:S(2)}) collective-permute-start(bf16[6144,256]{1,0:T(8,128)(2,1)S(1)} %get-tuple-element.493), channel_id=1, source_target_pairs={{0,16},{16,0},{1,17},{17,1},{2,18},{18,2},{3,19},{19,3},{4,20},{20... | collective-permute-start | bytes 9437192 | tf_op jit(solution)/shard_map/ppermute | solution.py:87
  380.0 14.3 %collective-permute-start.81 = (bf16[4,64,1024]{2,1,0:T(8,128)(2,1)S(1)}, bf16[4,64,1024]{2,1,0:T(8,128)(2,1)S(1)}, u32[]{:S(2)}, u32[]{:S(2)}) collective-permute-start(bf16[4,64,1024]{2,1,0:T(8,128)(2,1)S(1)} %get-tuple-element.486), channel_id=1, source_target_pairs={{0,2},{1,3},{2,0},{3,1},{4,6},{5,7},{6,4},{7,5},{8,10},{9,11},{10,... | collective-permute-start | bytes 1572872 | tf_op jit(solution)/shard_map/ppermute | solution.py:49
  381.2 14.0 %collective-permute-start.82 = (bf16[4,64,1024]{2,1,0:T(8,128)(2,1)S(1)}, bf16[4,64,1024]{2,1,0:T(8,128)(2,1)S(1)}, u32[]{:S(2)}, u32[]{:S(2)}) collective-permute-start(bf16[4,64,1024]{2,1,0:T(8,128)(2,1)S(1)} %get-tuple-element.488), channel_id=1, source_target_pairs={{0,1},{1,0},{2,3},{3,2},{4,5},{5,4},{6,7},{7,6},{8,9},{9,8},{10,11... | collective-permute-start | bytes 1572872 | tf_op jit(solution)/shard_map/ppermute | solution.py:49
  382.6 12.9 %collective-permute-start.83 = (bf16[2,1,192,256]{3,2,1,0:T(8,128)(2,1)S(1)}, bf16[2,1,192,256]{3,2,1,0:T(8,128)(2,1)S(1)}, u32[]{:S(2)}, u32[]{:S(2)}) collective-permute-start(bf16[2,1,192,256]{3,2,1,0:T(8,128)(2,1)S(1)} %get-tuple-element.475), channel_id=1, source_target_pairs={{0,8},{1,9},{2,10},{3,11},{4,12},{5,13},{6,14},{7,15},{8,0},{9,1},... | collective-permute-start | bytes 589832 | tf_op jit(solution)/shard_map/ppermute | solution.py:49
  395.5 13.2 %collective-permute-start.86 = (bf16[2,2,64,1024]{3,2,1,0:T(8,128)(2,1)S(1)}, bf16[2,2,64,1024]{3,2,1,0:T(8,128)(2,1)S(1)}, u32[]{:S(2)}, u32[]{:S(2)}) collective-permute-start(bf16[2,2,64,1024]{3,2,1,0:T(8,128)(2,1)S(1)} %get-tuple-element.503), channel_id=1, source_target_pairs={{0,4},{1,5},{2,6},{3,7},{4,0},{5,1},{6,2},{7,3},{8,12},{9,13},{10,... | collective-permute-start | bytes 1572872 | tf_op jit(solution)/shard_map/ppermute | solution.py:49
  397.9 18.6 %collective-permute-start.84 = (bf16[8,192,256]{2,1,0:T(8,128)(2,1)S(1)}, bf16[8,192,256]{2,1,0:T(8,128)(2,1)S(1)}, u32[]{:S(2)}, u32[]{:S(2)}) collective-permute-start(bf16[8,192,256]{2,1,0:T(8,128)(2,1)S(1)} %get-tuple-element.500), channel_id=1, source_target_pairs={{0,1},{1,0},{2,3},{3,2},{4,5},{5,4},{6,7},{7,6},{8,9},{9,8},{10,11... | collective-permute-start | bytes 2359304 | tf_op jit(solution)/shard_map/ppermute | solution.py:49
  399.6 18.2 %collective-permute-start.85 = (bf16[8,192,256]{2,1,0:T(8,128)(2,1)S(1)}, bf16[8,192,256]{2,1,0:T(8,128)(2,1)S(1)}, u32[]{:S(2)}, u32[]{:S(2)}) collective-permute-start(bf16[8,192,256]{2,1,0:T(8,128)(2,1)S(1)} %get-tuple-element.501), channel_id=1, source_target_pairs={{0,2},{1,3},{2,0},{3,1},{4,6},{5,7},{6,4},{7,5},{8,10},{9,11},{10,... | collective-permute-start | bytes 2359304 | tf_op jit(solution)/shard_map/ppermute | solution.py:49
  415.0 16.1 %collective-permute-start.91 = (bf16[4,384,512]{2,1,0:T(8,128)(2,1)S(1)}, bf16[4,384,512]{2,1,0:T(8,128)(2,1)S(1)}, u32[]{:S(2)}, u32[]{:S(2)}) collective-permute-start(bf16[4,384,512]{2,1,0:T(8,128)(2,1)S(1)} %slice_bitcast_fusion), channel_id=1, source_target_pairs={{0,16},{16,0},{1,17},{17,1},{2,18},{18,2},{3,19},{19,3},{4,20},{20... | collective-permute-start | bytes 4718600 | tf_op jit(solution)/shard_map/ppermute | solution.py:87
  417.9 12.6 %collective-permute-start.89 = (bf16[2,1,64,1024]{3,2,1,0:T(8,128)(2,1)S(1)}, bf16[2,1,64,1024]{3,2,1,0:T(8,128)(2,1)S(1)}, u32[]{:S(2)}, u32[]{:S(2)}) collective-permute-start(bf16[2,1,64,1024]{3,2,1,0:T(8,128)(2,1)S(1)} %get-tuple-element.513), channel_id=1, source_target_pairs={{0,8},{1,9},{2,10},{3,11},{4,12},{5,13},{6,14},{7,15},{8,0},{9,1},... | collective-permute-start | bytes 786440 | tf_op jit(solution)/shard_map/ppermute | solution.py:49
  431.0 23.4 %collective-permute-start.96 = (f32[64,1024]{1,0:T(8,128)S(1)}, f32[64,1024]{1,0:T(8,128)S(1)}, u32[]{:S(2)}, u32[]{:S(2)}) collective-permute-start(f32[64,1024]{1,0:T(8,128)S(1)} %get-tuple-element.557), channel_id=1, source_target_pairs={{0,16},{16,0},{1,17},{17,1},{2,18},{18,2},{3,19},{19,3},{4,20},{20... | collective-permute-start | bytes 786440 | tf_op jit(solution)/shard_map/ppermute | solution.py:87
  442.2 12.0 %collective-permute-start.92 = (bf16[2,1,192,256]{3,2,1,0:T(8,128)(2,1)S(1)}, bf16[2,1,192,256]{3,2,1,0:T(8,128)(2,1)S(1)}, u32[]{:S(2)}, u32[]{:S(2)}) collective-permute-start(bf16[2,1,192,256]{3,2,1,0:T(8,128)(2,1)S(1)} %get-tuple-element.525), channel_id=1, source_target_pairs={{0,8},{1,9},{2,10},{3,11},{4,12},{5,13},{6,14},{7,15},{8,0},{9,1},... | collective-permute-start | bytes 589832 | tf_op jit(solution)/shard_map/ppermute | solution.py:49
  (102 other events, 963.4 us)
Sparse Core Ops, SparseCore 0:
  51.3 80.8 all-gather.1

commit v7 on v6

--- a/solution.py
+++ b/solution.py
@@ -660,6 +660,16 @@
 def group_of(rows, start, bounds):
     index = lax.broadcasted_iota(jnp.int32, (rows, 1), 0) + start
     return sum((index >= bound).astype(jnp.int32) for bound in bounds)
+
+
+def k_load(*refs):
+    count = (len(refs) - 2) // 2
+    ins, outs, sems = refs[:count], refs[count + 1 : -1], refs[-1]
+    copies = [pltpu.make_async_copy(source, target, sems.at[k]) for k, (source, target) in enumerate(zip(ins, outs))]
+    for copy in copies:
+        copy.start()
+    for copy in copies:
+        copy.wait()
 
 
 def k_squares(start_ref, *refs):
@@ -1438,12 +1448,21 @@
     squares = call(
         k_squares, "squares", (1,), whole_specs * 2, full((8, 128)), shape_of((8, 128)), [], (starts, *weights, *grads), prefetch=1, vmem=10,
     )
-    squares, _unused = dp_sum(squares + swap_pipe(squares))
+    big = (w_narrow, w_wide, mom_narrow, mom_wide)
+
+    def load(token):
+        return call(
+            k_load, "load", (), [ANYWHERE] * 5, [ANYWHERE] * 4, [vmem_of(v.shape) for v in big], [pltpu.SemaphoreType.DMA((4,))],
+            (*(in_hbm(v) for v in big), token), vmem=2,
+        )
+
+    squares, (loaded,) = dp_sum(squares + swap_pipe(squares), [load])
+    near_narrow, near_wide, near_mom_narrow, near_mom_wide = (in_vmem(v) for v in loaded)
     parts = 4 if rows_n % 64 == 0 and w_wide.shape[0] % 64 == 0 else 1
     specs = [spec((v.shape[0] // parts, v.shape[1]), lambda k, *_: (k, 0)) for v in weights[:2]] + whole_specs[2:]
     updated = call(
         paired(k_update, {1: ONE}), "update", (parts,), [full((8, 128))] * 2 + specs * 3, specs * 2, [shape_of(v.shape) for v in weights] * 2, [],
-        (starts, *squares.parts, *weights, *grads, mom_narrow, mom_wide, mom_bn_mid, mom_bn_wide), prefetch=1, vmem=12,
+        (starts, *squares.parts, near_narrow, near_wide, bn_mid, bn_wide, *grads, near_mom_narrow, near_mom_wide, mom_bn_mid, mom_bn_wide), prefetch=1, vmem=12,
     )
     new_mom_narrow, new_mom_wide, new_mom_mid, new_mom_table, new_narrow, new_wide, new_mid, new_table = updated
     return (

time: 494 us -> 494 us (level)
    pallas_call x70 -> x71, Pallas kernels: 161 us -> 163 us  [call(): pl.pallas_call(kernel, out_shape=out_shape, grid_spec=pltpu.PrefetchScala...]
  transfers between devices with their start and end apart: 103 -> 103, of which waited for: 69 -> 68; matrix products, arithmetic and copies ran while one was open for 1% -> 1% of each run, Pallas kernels for 23% -> 23%
where the time goes in v7:
time: 494 us; the launch traced here: 484 us
  waiting for transfers between devices  187 us (38%)
  Pallas kernels  163 us (33%)
  starting transfers between devices  115 us (23%)
  between operations  15.7 us (3%)
    ppermute x82, waiting for transfers between devices, exchange(): return lax.ppermute(value, 'dp', pairs(bit))  179 us
    pallas_call x71, Pallas kernels, call(): pl.pallas_call(kernel, out_shape=out_shape, grid_spec=pltpu.PrefetchScala...  163 us
    ppermute x82, starting transfers between devices, exchange(): return lax.ppermute(value, 'dp', pairs(bit))  111 us
  transfers between devices with their start and end apart: 103, of which 68 were waited for; matrix products, arithmetic and copies ran while one was open for 1% of the time, Pallas kernels for 23%

profile of v7, /device:TPU:0, one launch (start us, length us, event | category | flops | bytes accessed | tf_op | source)
XLA Modules:
  0.0 484.0 jit_solution(17272112002691027031)
XLA Ops:
  10.2 4.0 collective-permute-start.1
  14.2 9.4 %collective-permute-done.1.refs_1_ = bf16[2,1,192,256]{3,2,1,0:T(8,128)(2,1)S(1)} collective-permute-done((bf16[2,1,192,256]{3,2,1,0:T(8,128)(2,1)S(1)}, bf16[2,1,192,256]{3,2,1,0:T(8,128)(2,1)S(1)}, u32[]{:S(2)}, u32[]{:S(2)}) %collective-permute-start.1) | collective-permute-done | bytes 196640 | tf_op jit(solution)/shard_map/ppermute | solution.py:49
  24.9 9.9 %collective-permute-done.2.refs_1_ = bf16[2,2,192,256]{3,2,1,0:T(8,128)(2,1)S(1)} collective-permute-done((bf16[2,2,192,256]{3,2,1,0:T(8,128)(2,1)S(1)}, bf16[2,2,192,256]{3,2,1,0:T(8,128)(2,1)S(1)}, u32[]{:S(2)}, u32[]{:S(2)}) %collective-permute-start.2) | collective-permute-done | bytes 393248 | tf_op jit(solution)/shard_map/ppermute | solution.py:49
  42.5 7.5 %collective-permute-done.5.refs_1_.refs_2_ = bf16[2,1,192,256]{3,2,1,0:T(8,128)(2,1)S(1)} collective-permute-done((bf16[2,1,192,256]{3,2,1,0:T(8,128)(2,1)S(1)}, bf16[2,1,192,256]{3,2,1,0:T(8,128)(2,1)S(1)}, u32[]{:S(2)}, u32[]{:S(2)}) %collective-permute-start.5) | collective-permute-done | bytes 196640 | tf_op jit(solution)/shard_map/ppermute | solution.py:49
  54.4 4.9 %prep.1 = (bf16[4,384,1024]{2,1,0:T(8,128)(2,1)S(1)}, f32[384,1]{1,0:T(8,128)S(1)}, f32[4,512]{1,0:T(4,128)S(1)}) custom-call(s32[1]{0:T(128)} %bitcast.core_ref.refs_0_, s32[1,8]{1,0:T(1,128)S(1)} %copy-done.23, s32[8]{0:T(128)S(1)} %copy-done.26, s32[8]{0:T(128)S(1)} %copy-done.27, bf16[8,384,1024]{2,1,0:T(8,128)(2,1)} %bitcast.73, ...), custom_call_target="tpu_custom_call" | custom-call | bytes 3000000 | tf_op jit(solution)/shard_map/prep/pallas_call | solution.py:732
  59.9 7.4 %collective-permute-done.8.refs_1_.refs_2_ = bf16[2,2,192,256]{3,2,1,0:T(8,128)(2,1)S(1)} collective-permute-done((bf16[2,2,192,256]{3,2,1,0:T(8,128)(2,1)S(1)}, bf16[2,2,192,256]{3,2,1,0:T(8,128)(2,1)S(1)}, u32[]{:S(2)}, u32[]{:S(2)}) %collective-permute-start.8) | collective-permute-done | bytes 393248 | tf_op jit(solution)/shard_map/ppermute | solution.py:49
  67.3 4.7 collective-permute-done.6.refs_1_
  79.0 3.6 a1.1
  103.2 7.2 %collective-permute-done.17.refs_2_ = f32[40,512]{1,0:T(8,128)S(1)} collective-permute-done((f32[40,512]{1,0:T(8,128)S(1)}, f32[40,512]{1,0:T(8,128)S(1)}, u32[]{:S(2)}, u32[]{:S(2)}) %collective-permute-start.17) | collective-permute-done | bytes 81952 | tf_op jit(solution)/shard_map/ppermute | solution.py:49
  110.4 6.0 %a2.1 = (f32[384,512]{1,0:T(8,128)S(1)}, bf16[4,384,512]{2,1,0:T(8,128)(2,1)S(1)}, f32[4,512]{1,0:T(4,128)S(1)}) custom-call(s32[1]{0:T(128)} %bitcast.core_ref.refs_0_, f32[40,512]{1,0:T(8,128)S(1)} %add.229.refs_1_, f32[40,512]{1,0:T(8,128)S(1)} %collective-permute-done.17.refs_2_, ...), custom_call_target="tpu_custom_call" | custom-call | bytes 3000000 | tf_op jit(solution)/shard_map/a2/pallas_call | solution.py:732
  129.5 3.5 collective-permute-start.23
  133.0 4.5 as.1
  137.6 3.8 a3.1
  161.1 5.1 %a4.1 = (bf16[384,2048]{1,0:T(8,128)(2,1)S(1)}, f32[384,512]{1,0:T(8,128)S(1)}, f32[4,512]{1,0:T(4,128)S(1)}) custom-call(s32[1]{0:T(128)} %bitcast.core_ref.refs_0_, f32[40,512]{1,0:T(8,128)S(1)} %add.230.refs_1_.refs_2_, f32[8,2048]{1,0:T(8,128)S(1)} %add.236.refs_2_.refs_14_.refs_5_, f32[8,2048]{1,0:T(8,128)S(1)} %collective-permute-done.27.refs_3_.refs_15_.refs_6_, ...), custom_call_target="tpu_custom_call" | custom-call | bytes 2820000 | tf_op jit(solution)/shard_map/a4/pallas_call | solution.py:732
  181.8 3.6 a5.1
  201.6 3.8 a6.1
  222.3 5.5 %head.1 = (bf16[2,384,1024]{2,1,0:T(8,128)(2,1)S(1)}, f32[384,2048]{1,0:T(8,128)S(1)}, f32[4,2048]{1,0:T(4,128)S(1)}) custom-call(s32[1]{0:T(128)} %bitcast.core_ref.refs_0_, s32[1,8]{1,0:T(1,128)S(1)} %copy-done.23, f32[40,512]{1,0:T(8,128)S(1)} %add.230.refs_1_.refs_2_, f32[4,2048]{1,0:T(4,128)S(1)} %add.245.refs_3_.refs_4_, ...), custom_call_target="tpu_custom_call" | custom-call | bytes 3180000 | tf_op jit(solution)/shard_map/head/pallas_call | solution.py:732
  244.8 5.5 %g5.1 = (bf16[384,2048]{1,0:T(8,128)(2,1)S(1)}, f32[384,512]{1,0:T(8,128)S(1)}, f32[4,512]{1,0:T(4,128)S(1)}) custom-call(s32[1]{0:T(128)} %bitcast.core_ref.refs_0_, f32[40,512]{1,0:T(8,128)S(1)} %add.230.refs_1_.refs_2_, f32[384,2048]{1,0:T(8,128)S(1)} %get-tuple-element.375.refs_2_.refs_11_, f32[384,2048]{1,0:T(8,128)} %keep.13.refs_3_, ...), custom_call_target="tpu_custom_call" | custom-call | bytes 3120000 | tf_op jit(solution)/shard_map/g5/pallas_call | solution.py:732
  266.7 5.5 %g4.1 = (bf16[9,384,512]{2,1,0:T(8,128)(2,1)S(1)}, f32[384,512]{1,0:T(8,128)S(1)}, f32[4,512]{1,0:T(4,128)S(1)}) custom-call(s32[1]{0:T(128)} %bitcast.core_ref.refs_0_, f32[40,512]{1,0:T(8,128)S(1)} %add.230.refs_1_.refs_2_, f32[384,512]{1,0:T(8,128)S(1)} %get-tuple-element.393.refs_2_, f32[384,512]{1,0:T(8,128)S(1)} %get-tuple-element.368.refs_5_.refs_10_.refs_3_, ...), custom_call_target="tpu_custom_call" | custom-call | bytes 3240000 | tf_op jit(solution)/shard_map/g4/pallas_call | solution.py:732
  287.8 6.8 %gy.1 = (bf16[384,512]{1,0:T(8,128)(2,1)S(1)}, f32[384,2048]{1,0:T(8,128)S(1)}, f32[6,2048]{1,0:T(8,128)S(1)}) custom-call(s32[1]{0:T(128)} %bitcast.core_ref.refs_0_, f32[40,512]{1,0:T(8,128)S(1)} %add.230.refs_1_.refs_2_, f32[384,512]{1,0:T(8,128)S(1)} %get-tuple-element.396.refs_2_, f32[384,512]{1,0:T(8,128)S(1)} %get-tuple-element.360.refs_5_.refs_12_.refs_3_, ...), custom_call_target="tpu_custom_call" | custom-call | bytes 4200000 | tf_op jit(solution)/shard_map/gy/pallas_call | solution.py:732
  314.0 3.9 collective-permute-done.63.refs_8_
  317.9 7.0 %g2.1 = (bf16[384,2048]{1,0:T(8,128)(2,1)S(1)}, bf16[384,2048]{1,0:T(8,128)(2,1)S(1)}, f32[384,512]{1,0:T(8,128)S(1)}, f32[4,512]{1,0:T(4,128)S(1)}) custom-call(s32[1]{0:T(128)} %bitcast.core_ref.refs_0_, f32[40,512]{1,0:T(8,128)S(1)} %add.230.refs_1_.refs_2_, f32[384,2048]{1,0:T(8,128)S(1)} %get-tuple-element.411.refs_2_, ...), custom_call_target="tpu_custom_call" | custom-call | bytes 4380000 | tf_op jit(solution)/shard_map/g2/pallas_call | solution.py:732
  350.6 7.4 %g1.1 = (bf16[9,384,512]{2,1,0:T(8,128)(2,1)S(1)}, f32[4,384,512]{2,1,0:T(8,128)S(1)}, f32[4,512]{1,0:T(4,128)S(1)}) custom-call(s32[1]{0:T(128)} %bitcast.core_ref.refs_0_, f32[40,512]{1,0:T(8,128)S(1)} %add.230.refs_1_.refs_2_, f32[384,512]{1,0:T(8,128)S(1)} %get-tuple-element.431.refs_2_, f32[384,512]{1,0:T(8,128)S(1)} %copy-done.4, ...), custom_call_target="tpu_custom_call" | custom-call | bytes 4800000 | tf_op jit(solution)/shard_map/g1/pallas_call | solution.py:732
  384.0 10.3 %collective-permute-done.81.refs_2_.refs_3_ = bf16[4,64,1024]{2,1,0:T(8,128)(2,1)S(1)} collective-permute-done((bf16[4,64,1024]{2,1,0:T(8,128)(2,1)S(1)}, bf16[4,64,1024]{2,1,0:T(8,128)(2,1)S(1)}, u32[]{:S(2)}, u32[]{:S(2)}) %collective-permute-start.81) | collective-permute-done | bytes 524320 | tf_op jit(solution)/shard_map/ppermute | solution.py:49
  400.6 4.5 dxs.1.short_ref
  405.2 3.6 collective-permute-done.86.came_ref
  408.9 6.0 %gx.1.own_ref = bf16[2,4,384,512]{3,2,1,0:T(8,128)(2,1)S(1)} custom-call(s32[1]{0:T(128)} %bitcast.core_ref.refs_0_, bf16[4,384,512]{2,1,0:T(8,128)(2,1)S(1)} %g0.1.ga_ref, f32[384,1]{1,0:T(8,128)S(1)} %get-tuple-element.313.refs_3_.refs_4_.refs_5_.refs_8_.refs_9_.refs_6_.mask_ref, ...), custom_call_target="tpu_custom_call" | custom-call | bytes 3840000 | tf_op jit(solution)/shard_map/gx/pallas_call | solution.py:732
  421.2 9.3 %collective-permute-done.89 = bf16[2,1,64,1024]{3,2,1,0:T(8,128)(2,1)S(1)} collective-permute-done((bf16[2,1,64,1024]{3,2,1,0:T(8,128)(2,1)S(1)}, bf16[2,1,64,1024]{3,2,1,0:T(8,128)(2,1)S(1)}, u32[]{:S(2)}, u32[]{:S(2)}) %collective-permute-start.89) | collective-permute-done | bytes 262176 | tf_op jit(solution)/shard_map/ppermute | solution.py:49
  431.2 3.8 place_grad.1
  435.0 6.1 %collective-permute-done.90.came_ref = bf16[2,2,192,256]{3,2,1,0:T(8,128)(2,1)S(1)} collective-permute-done((bf16[2,2,192,256]{3,2,1,0:T(8,128)(2,1)S(1)}, bf16[2,2,192,256]{3,2,1,0:T(8,128)(2,1)S(1)}, u32[]{:S(2)}, u32[]{:S(2)}) %collective-permute-start.90) | collective-permute-done | bytes 393248 | tf_op jit(solution)/shard_map/ppermute | solution.py:49
  444.2 10.1 %collective-permute-done.92 = bf16[2,1,192,256]{3,2,1,0:T(8,128)(2,1)S(1)} collective-permute-done((bf16[2,1,192,256]{3,2,1,0:T(8,128)(2,1)S(1)}, bf16[2,1,192,256]{3,2,1,0:T(8,128)(2,1)S(1)}, u32[]{:S(2)}, u32[]{:S(2)}) %collective-permute-start.92) | collective-permute-done | bytes 196640 | tf_op jit(solution)/shard_map/ppermute | solution.py:49
  465.9 3.6 collective-permute-done.100
  (389 shorter events, 280.3 us)
Async XLA Ops:
  7.2 125.8 %all-gather.2.cloned.1.call-start = ((), (), s32[]{:S(2)}) async-start(), calls=%async_computation | async-start | bytes 8650752 | tf_op jit(solution)/shard_map/all_gather | solution.py:907
  10.2 13.4 %collective-permute-start.1 = (bf16[2,1,192,256]{3,2,1,0:T(8,128)(2,1)S(1)}, bf16[2,1,192,256]{3,2,1,0:T(8,128)(2,1)S(1)}, u32[]{:S(2)}, u32[]{:S(2)}) collective-permute-start(bf16[2,1,192,256]{3,2,1,0:T(8,128)(2,1)S(1)} %bitcast.58), channel_id=1, source_target_pairs={{0,8},{1,9},{2,10},{3,11},{4,12},{5,13},{6,14},{7,15},{8,0},{9,1},... | collective-permute-start | bytes 589832 | tf_op jit(solution)/shard_map/ppermute | solution.py:49
  35.9 14.1 %collective-permute-start.3 = (bf16[4,192,256]{2,1,0:T(8,128)(2,1)S(1)}, bf16[4,192,256]{2,1,0:T(8,128)(2,1)S(1)}, u32[]{:S(2)}, u32[]{:S(2)}) collective-permute-start(bf16[4,192,256]{2,1,0:T(8,128)(2,1)S(1)} %get-tuple-element.292.refs_0_), channel_id=1, source_target_pairs={{0,2},{1,3},{2,0},{3,1},{4,6},{5,7},{6,4},{7,5},{8,10},{9,11},{10,... | collective-permute-start | bytes 1179656 | tf_op jit(solution)/shard_map/ppermute | solution.py:49
  37.2 12.8 %collective-permute-start.4 = (bf16[4,192,256]{2,1,0:T(8,128)(2,1)S(1)}, bf16[4,192,256]{2,1,0:T(8,128)(2,1)S(1)}, u32[]{:S(2)}, u32[]{:S(2)}) collective-permute-start(bf16[4,192,256]{2,1,0:T(8,128)(2,1)S(1)} %get-tuple-element.293.refs_1_), channel_id=1, source_target_pairs={{0,1},{1,0},{2,3},{3,2},{4,5},{5,4},{6,7},{7,6},{8,9},{9,8},{10,11... | collective-permute-start | bytes 1179656 | tf_op jit(solution)/shard_map/ppermute | solution.py:49
  51.2 20.8 %collective-permute-start.6 = (bf16[8,192,256]{2,1,0:T(8,128)(2,1)}, bf16[8,192,256]{2,1,0:T(8,128)(2,1)}, u32[]{:S(2)}, u32[]{:S(2)}) collective-permute-start(bf16[8,192,256]{2,1,0:T(8,128)(2,1)} %get-tuple-element.297.refs_0_), channel_id=1, source_target_pairs={{0,1},{1,0},{2,3},{3,2},{4,5},{5,4},{6,7},{7,6},{8,9},{9,8},{10,11... | collective-permute-start | bytes 2359304 | tf_op jit(solution)/shard_map/ppermute | solution.py:49
  51.8 20.4 %collective-permute-start.7 = (bf16[8,192,256]{2,1,0:T(8,128)(2,1)}, bf16[8,192,256]{2,1,0:T(8,128)(2,1)}, u32[]{:S(2)}, u32[]{:S(2)}) collective-permute-start(bf16[8,192,256]{2,1,0:T(8,128)(2,1)} %get-tuple-element.298.refs_2_), channel_id=1, source_target_pairs={{0,2},{1,3},{2,0},{3,1},{4,6},{5,7},{6,4},{7,5},{8,10},{9,11},{10,... | collective-permute-start | bytes 2359304 | tf_op jit(solution)/shard_map/ppermute | solution.py:49
  53.5 13.8 %collective-permute-start.8 = (bf16[2,2,192,256]{3,2,1,0:T(8,128)(2,1)S(1)}, bf16[2,2,192,256]{3,2,1,0:T(8,128)(2,1)S(1)}, u32[]{:S(2)}, u32[]{:S(2)}) collective-permute-start(bf16[2,2,192,256]{3,2,1,0:T(8,128)(2,1)S(1)} %join.9.refs_0_), channel_id=1, source_target_pairs={{0,4},{1,5},{2,6},{3,7},{4,0},{5,1},{6,2},{7,3},{8,12},{9,13},{10,... | collective-permute-start | bytes 1179656 | tf_op jit(solution)/shard_map/ppermute | solution.py:49
  59.3 13.5 %collective-permute-start.10 = (bf16[8,192,256]{2,1,0:T(8,128)(2,1)}, bf16[8,192,256]{2,1,0:T(8,128)(2,1)S(1)}, u32[]{:S(2)}, u32[]{:S(2)}) collective-permute-start(bf16[8,192,256]{2,1,0:T(8,128)(2,1)} %get-tuple-element.297.refs_0_), channel_id=1, source_target_pairs={{0,16},{16,0},{1,17},{17,1},{2,18},{18,2},{3,19},{19,3},{4,20},{20... | collective-permute-start | bytes 2359304 | tf_op jit(solution)/shard_map/ppermute | solution.py:87
  59.5 13.3 %collective-permute-start.12 = (bf16[8,192,256]{2,1,0:T(8,128)(2,1)}, bf16[8,192,256]{2,1,0:T(8,128)(2,1)S(1)}, u32[]{:S(2)}, u32[]{:S(2)}) collective-permute-start(bf16[8,192,256]{2,1,0:T(8,128)(2,1)} %get-tuple-element.298.refs_2_), channel_id=1, source_target_pairs={{0,16},{16,0},{1,17},{17,1},{2,18},{18,2},{3,19},{19,3},{4,20},{20... | collective-permute-start | bytes 2359304 | tf_op jit(solution)/shard_map/ppermute | solution.py:87
  94.0 27.6 %collective-permute-start.20 = (bf16[4,192,256]{2,1,0:T(8,128)(2,1)S(1)}, bf16[4,192,256]{2,1,0:T(8,128)(2,1)S(1)}, u32[]{:S(2)}, u32[]{:S(2)}) collective-permute-start(bf16[4,192,256]{2,1,0:T(8,128)(2,1)S(1)} %get-tuple-element.321.refs_0_), channel_id=1, source_target_pairs={{0,2},{1,3},{2,0},{3,1},{4,6},{5,7},{6,4},{7,5},{8,10},{9,11},{10,... | collective-permute-start | bytes 1179656 | tf_op jit(solution)/shard_map/ppermute | solution.py:49
  94.5 27.0 %collective-permute-start.21 = (bf16[4,192,256]{2,1,0:T(8,128)(2,1)S(1)}, bf16[4,192,256]{2,1,0:T(8,128)(2,1)S(1)}, u32[]{:S(2)}, u32[]{:S(2)}) collective-permute-start(bf16[4,192,256]{2,1,0:T(8,128)(2,1)S(1)} %get-tuple-element.322.refs_1_), channel_id=1, source_target_pairs={{0,1},{1,0},{2,3},{3,2},{4,5},{5,4},{6,7},{7,6},{8,9},{9,8},{10,11... | collective-permute-start | bytes 1179656 | tf_op jit(solution)/shard_map/ppermute | solution.py:49
  124.1 21.7 %collective-permute-start.28 = (bf16[8,192,256]{2,1,0:T(8,128)(2,1)}, bf16[8,192,256]{2,1,0:T(8,128)(2,1)}, u32[]{:S(2)}, u32[]{:S(2)}) collective-permute-start(bf16[8,192,256]{2,1,0:T(8,128)(2,1)} %get-tuple-element.343.refs_0_), channel_id=1, source_target_pairs={{0,1},{1,0},{2,3},{3,2},{4,5},{5,4},{6,7},{7,6},{8,9},{9,8},{10,11... | collective-permute-start | bytes 2359304 | tf_op jit(solution)/shard_map/ppermute | solution.py:49
  124.4 21.4 %collective-permute-start.29 = (bf16[8,192,256]{2,1,0:T(8,128)(2,1)}, bf16[8,192,256]{2,1,0:T(8,128)(2,1)}, u32[]{:S(2)}, u32[]{:S(2)}) collective-permute-start(bf16[8,192,256]{2,1,0:T(8,128)(2,1)} %get-tuple-element.345.refs_2_), channel_id=1, source_target_pairs={{0,2},{1,3},{2,0},{3,1},{4,6},{5,7},{6,4},{7,5},{8,10},{9,11},{10,... | collective-permute-start | bytes 2359304 | tf_op jit(solution)/shard_map/ppermute | solution.py:49
  145.8 12.2 %collective-permute-start.30 = (bf16[8,192,256]{2,1,0:T(8,128)(2,1)}, bf16[8,192,256]{2,1,0:T(8,128)(2,1)S(1)}, u32[]{:S(2)}, u32[]{:S(2)}) collective-permute-start(bf16[8,192,256]{2,1,0:T(8,128)(2,1)} %get-tuple-element.343.refs_0_), channel_id=1, source_target_pairs={{0,16},{16,0},{1,17},{17,1},{2,18},{18,2},{3,19},{19,3},{4,20},{20... | collective-permute-start | bytes 2359304 | tf_op jit(solution)/shard_map/ppermute | solution.py:87
  145.9 12.1 %collective-permute-start.31 = (bf16[8,192,256]{2,1,0:T(8,128)(2,1)}, bf16[8,192,256]{2,1,0:T(8,128)(2,1)S(1)}, u32[]{:S(2)}, u32[]{:S(2)}) collective-permute-start(bf16[8,192,256]{2,1,0:T(8,128)(2,1)} %collective-permute-done.28.refs_1_), channel_id=1, source_target_pairs={{0,16},{16,0},{1,17},{17,1},{2,18},{18,2},{3,19},{19,3},{4,20},{20... | collective-permute-start | bytes 2359304 | tf_op jit(solution)/shard_map/ppermute | solution.py:87
  305.7 25.8 %collective-permute-start.66 = (bf16[8,192,256]{2,1,0:T(8,128)(2,1)S(1)}, bf16[8,192,256]{2,1,0:T(8,128)(2,1)S(1)}, u32[]{:S(2)}, u32[]{:S(2)}) collective-permute-start(bf16[8,192,256]{2,1,0:T(8,128)(2,1)S(1)} %get-tuple-element.427), channel_id=1, source_target_pairs={{0,1},{1,0},{2,3},{3,2},{4,5},{5,4},{6,7},{7,6},{8,9},{9,8},{10,11... | collective-permute-start | bytes 2359304 | tf_op jit(solution)/shard_map/ppermute | solution.py:49
  307.2 24.2 %collective-permute-start.67 = (bf16[8,192,256]{2,1,0:T(8,128)(2,1)S(1)}, bf16[8,192,256]{2,1,0:T(8,128)(2,1)S(1)}, u32[]{:S(2)}, u32[]{:S(2)}) collective-permute-start(bf16[8,192,256]{2,1,0:T(8,128)(2,1)S(1)} %get-tuple-element.429), channel_id=1, source_target_pairs={{0,2},{1,3},{2,0},{3,1},{4,6},{5,7},{6,4},{7,5},{8,10},{9,11},{10,... | collective-permute-start | bytes 2359304 | tf_op jit(solution)/shard_map/ppermute | solution.py:49
  332.7 12.4 %collective-permute-start.70 = (bf16[2048,1024]{1,0:T(8,128)(2,1)S(1)}, bf16[2048,1024]{1,0:T(8,128)(2,1)S(1)}, u32[]{:S(2)}, u32[]{:S(2)}) collective-permute-start(bf16[2048,1024]{1,0:T(8,128)(2,1)S(1)} %get-tuple-element.456), channel_id=1, source_target_pairs={{0,16},{16,0},{1,17},{17,1},{2,18},{18,2},{3,19},{19,3},{4,20},{20... | collective-permute-start | bytes 12582920 | tf_op jit(solution)/shard_map/ppermute | solution.py:87
  346.3 25.8 %collective-permute-start.78 = (bf16[8,64,1024]{2,1,0:T(8,128)(2,1)S(1)}, bf16[8,64,1024]{2,1,0:T(8,128)(2,1)S(1)}, u32[]{:S(2)}, u32[]{:S(2)}) collective-permute-start(bf16[8,64,1024]{2,1,0:T(8,128)(2,1)S(1)} %get-tuple-element.489), channel_id=1, source_target_pairs={{0,1},{1,0},{2,3},{3,2},{4,5},{5,4},{6,7},{7,6},{8,9},{9,8},{10,11... | collective-permute-start | bytes 3145736 | tf_op jit(solution)/shard_map/ppermute | solution.py:49
  347.8 24.2 %collective-permute-start.79 = (bf16[8,64,1024]{2,1,0:T(8,128)(2,1)S(1)}, bf16[8,64,1024]{2,1,0:T(8,128)(2,1)S(1)}, u32[]{:S(2)}, u32[]{:S(2)}) collective-permute-start(bf16[8,64,1024]{2,1,0:T(8,128)(2,1)S(1)} %get-tuple-element.490), channel_id=1, source_target_pairs={{0,2},{1,3},{2,0},{3,1},{4,6},{5,7},{6,4},{7,5},{8,10},{9,11},{10,... | collective-permute-start | bytes 3145736 | tf_op jit(solution)/shard_map/ppermute | solution.py:49
  349.0 19.0 %collective-permute-start.76 = (bf16[2,2,192,256]{3,2,1,0:T(8,128)(2,1)S(1)}, bf16[2,2,192,256]{3,2,1,0:T(8,128)(2,1)S(1)}, u32[]{:S(2)}, u32[]{:S(2)}) collective-permute-start(bf16[2,2,192,256]{3,2,1,0:T(8,128)(2,1)S(1)} %get-tuple-element.467), channel_id=1, source_target_pairs={{0,4},{1,5},{2,6},{3,7},{4,0},{5,1},{6,2},{7,3},{8,12},{9,13},{10,... | collective-permute-start | bytes 1179656 | tf_op jit(solution)/shard_map/ppermute | solution.py:49
  379.9 15.6 %collective-permute-start.80 = (bf16[6144,256]{1,0:T(8,128)(2,1)S(1)}, bf16[6144,256]{1,0:T(8,128)(2,1)S(1)}, u32[]{:S(2)}, u32[]{:S(2)}) collective-permute-start(bf16[6144,256]{1,0:T(8,128)(2,1)S(1)} %get-tuple-element.502), channel_id=1, source_target_pairs={{0,16},{16,0},{1,17},{17,1},{2,18},{18,2},{3,19},{19,3},{4,20},{20... | collective-permute-start | bytes 9437192 | tf_op jit(solution)/shard_map/ppermute | solution.py:87
  380.0 14.3 %collective-permute-start.81 = (bf16[4,64,1024]{2,1,0:T(8,128)(2,1)S(1)}, bf16[4,64,1024]{2,1,0:T(8,128)(2,1)S(1)}, u32[]{:S(2)}, u32[]{:S(2)}) collective-permute-start(bf16[4,64,1024]{2,1,0:T(8,128)(2,1)S(1)} %get-tuple-element.495), channel_id=1, source_target_pairs={{0,2},{1,3},{2,0},{3,1},{4,6},{5,7},{6,4},{7,5},{8,10},{9,11},{10,... | collective-permute-start | bytes 1572872 | tf_op jit(solution)/shard_map/ppermute | solution.py:49
  381.2 14.0 %collective-permute-start.82 = (bf16[4,64,1024]{2,1,0:T(8,128)(2,1)S(1)}, bf16[4,64,1024]{2,1,0:T(8,128)(2,1)S(1)}, u32[]{:S(2)}, u32[]{:S(2)}) collective-permute-start(bf16[4,64,1024]{2,1,0:T(8,128)(2,1)S(1)} %get-tuple-element.497), channel_id=1, source_target_pairs={{0,1},{1,0},{2,3},{3,2},{4,5},{5,4},{6,7},{7,6},{8,9},{9,8},{10,11... | collective-permute-start | bytes 1572872 | tf_op jit(solution)/shard_map/ppermute | solution.py:49
  382.7 12.8 %collective-permute-start.83 = (bf16[2,1,192,256]{3,2,1,0:T(8,128)(2,1)S(1)}, bf16[2,1,192,256]{3,2,1,0:T(8,128)(2,1)S(1)}, u32[]{:S(2)}, u32[]{:S(2)}) collective-permute-start(bf16[2,1,192,256]{3,2,1,0:T(8,128)(2,1)S(1)} %get-tuple-element.484), channel_id=1, source_target_pairs={{0,8},{1,9},{2,10},{3,11},{4,12},{5,13},{6,14},{7,15},{8,0},{9,1},... | collective-permute-start | bytes 589832 | tf_op jit(solution)/shard_map/ppermute | solution.py:49
  395.6 13.2 %collective-permute-start.86 = (bf16[2,2,64,1024]{3,2,1,0:T(8,128)(2,1)S(1)}, bf16[2,2,64,1024]{3,2,1,0:T(8,128)(2,1)S(1)}, u32[]{:S(2)}, u32[]{:S(2)}) collective-permute-start(bf16[2,2,64,1024]{3,2,1,0:T(8,128)(2,1)S(1)} %get-tuple-element.512), channel_id=1, source_target_pairs={{0,4},{1,5},{2,6},{3,7},{4,0},{5,1},{6,2},{7,3},{8,12},{9,13},{10,... | collective-permute-start | bytes 1572872 | tf_op jit(solution)/shard_map/ppermute | solution.py:49
  397.9 18.6 %collective-permute-start.84 = (bf16[8,192,256]{2,1,0:T(8,128)(2,1)S(1)}, bf16[8,192,256]{2,1,0:T(8,128)(2,1)S(1)}, u32[]{:S(2)}, u32[]{:S(2)}) collective-permute-start(bf16[8,192,256]{2,1,0:T(8,128)(2,1)S(1)} %get-tuple-element.509), channel_id=1, source_target_pairs={{0,1},{1,0},{2,3},{3,2},{4,5},{5,4},{6,7},{7,6},{8,9},{9,8},{10,11... | collective-permute-start | bytes 2359304 | tf_op jit(solution)/shard_map/ppermute | solution.py:49
  399.7 18.2 %collective-permute-start.85 = (bf16[8,192,256]{2,1,0:T(8,128)(2,1)S(1)}, bf16[8,192,256]{2,1,0:T(8,128)(2,1)S(1)}, u32[]{:S(2)}, u32[]{:S(2)}) collective-permute-start(bf16[8,192,256]{2,1,0:T(8,128)(2,1)S(1)} %get-tuple-element.510), channel_id=1, source_target_pairs={{0,2},{1,3},{2,0},{3,1},{4,6},{5,7},{6,4},{7,5},{8,10},{9,11},{10,... | collective-permute-start | bytes 2359304 | tf_op jit(solution)/shard_map/ppermute | solution.py:49
  415.1 16.1 %collective-permute-start.91 = (bf16[4,384,512]{2,1,0:T(8,128)(2,1)S(1)}, bf16[4,384,512]{2,1,0:T(8,128)(2,1)S(1)}, u32[]{:S(2)}, u32[]{:S(2)}) collective-permute-start(bf16[4,384,512]{2,1,0:T(8,128)(2,1)S(1)} %slice_bitcast_fusion), channel_id=1, source_target_pairs={{0,16},{16,0},{1,17},{17,1},{2,18},{18,2},{3,19},{19,3},{4,20},{20... | collective-permute-start | bytes 4718600 | tf_op jit(solution)/shard_map/ppermute | solution.py:87
  417.9 12.6 %collective-permute-start.89 = (bf16[2,1,64,1024]{3,2,1,0:T(8,128)(2,1)S(1)}, bf16[2,1,64,1024]{3,2,1,0:T(8,128)(2,1)S(1)}, u32[]{:S(2)}, u32[]{:S(2)}) collective-permute-start(bf16[2,1,64,1024]{3,2,1,0:T(8,128)(2,1)S(1)} %get-tuple-element.522), channel_id=1, source_target_pairs={{0,8},{1,9},{2,10},{3,11},{4,12},{5,13},{6,14},{7,15},{8,0},{9,1},... | collective-permute-start | bytes 786440 | tf_op jit(solution)/shard_map/ppermute | solution.py:49
  431.1 23.4 %collective-permute-start.96 = (f32[64,1024]{1,0:T(8,128)S(1)}, f32[64,1024]{1,0:T(8,128)S(1)}, u32[]{:S(2)}, u32[]{:S(2)}) collective-permute-start(f32[64,1024]{1,0:T(8,128)S(1)} %get-tuple-element.575), channel_id=1, source_target_pairs={{0,16},{16,0},{1,17},{17,1},{2,18},{18,2},{3,19},{19,3},{4,20},{20... | collective-permute-start | bytes 786440 | tf_op jit(solution)/shard_map/ppermute | solution.py:87
  442.3 12.0 %collective-permute-start.92 = (bf16[2,1,192,256]{3,2,1,0:T(8,128)(2,1)S(1)}, bf16[2,1,192,256]{3,2,1,0:T(8,128)(2,1)S(1)}, u32[]{:S(2)}, u32[]{:S(2)}) collective-permute-start(bf16[2,1,192,256]{3,2,1,0:T(8,128)(2,1)S(1)} %get-tuple-element.534), channel_id=1, source_target_pairs={{0,8},{1,9},{2,10},{3,11},{4,12},{5,13},{6,14},{7,15},{8,0},{9,1},... | collective-permute-start | bytes 589832 | tf_op jit(solution)/shard_map/ppermute | solution.py:49
  (100 other events, 917.3 us)
Sparse Core Ops, SparseCore 0:
  51.3 80.7 all-gather.1
